TPU v7x, 512 devices: a whole 4x4x16 slice. The times are simulated.
512 devices in a mesh: dp: 64 (over y, z), tensor: 8 (over x, core).
Axes of the slice: x: 4, y: 4, z: 16, core: 2. Of those that a mesh axis runs over, the one named last changes fastest.
Arguments:
- residual: bfloat16 [16384, 4096], P(('dp', 'tensor')), as said below
- context: bfloat16 [16384, 5120], P('dp', 'tensor'), may hold values from -6 to 6
- out_proj: bfloat16 [5120, 4096], P('tensor', 'dp'), may hold values from -0.078125 to 0.078125
- norm_gain: float32 [4096], replicated, may hold values from 0.1 to 1.9
- colbert_head: bfloat16 [4096, 128], P('tensor'), may hold values from -0.09375 to 0.09375
- candidates: int32 [512, 64], P(('dp', 'tensor')), may hold values from 0 to 4095, as said below
- lengths: int32 [4096], P('dp'), may hold values from 16 to 64, as said below
- centroid_ids: int32 [4096, 64], P('dp'), may hold values from 0 to 8191
- residual_codes: int32 [4096, 1024], P('dp'), may hold values from 0 to 65535
- centroids: bfloat16 [8192, 128], replicated, may hold values from -0.5 to 0.5
- buckets: float32 [4], replicated, may hold values from -0.1 to 0.1
Outputs:
- scores: float32 [512, 64], P(('dp', 'tensor'))
- context_grad: bfloat16 [16384, 5120], P('dp', 'tensor')
- residual_grad: bfloat16 [16384, 4096], P(('dp', 'tensor'))
- head_grad: float32 [4096, 128], P('tensor')
- gain_grad: float32 [4096], replicated
Inputs may be any that keep to these rules, and one draw needn't show every extreme that they name: `candidates`: passage p lies in shard floor(p / 64). Of the 64 entries of one device's rows of dp+tensor, at most 2 name passages of one shard, and some shard has exactly 2 of them. Ids may repeat. `lengths`: each shard has a passage of exactly 64 tokens. `residual`: row scales and feature scales vary.
All inputs are finite; a program needn't handle non-finite values.
Results may differ from a plain program's by a relative error of at most 0.029.
Values may be sent and summed in bfloat16 or wider, within the bound.
No kernel may reach another device: no remote copies, remote signals or barrier semaphores. Data moves between devices by JAX's collectives and lax.ppermute only.
A program may use at most 128 MiB of HBM per device.

v0:
```python
import jax
import jax.numpy as jnp
from jax import lax
from jax.sharding import PartitionSpec as P

EPS = 1e-06
TEMPER = 0.1
LOSS_SCALE = 64.0


def decompress(cell_ids, packed, centroids, buckets):
    leading = cell_ids.shape
    packed = packed.reshape(leading + (packed.shape[-1] // leading[-1], 1))
    shifts = 2 * jnp.arange(8, dtype=jnp.int32)
    code_vals = jnp.bitwise_and(jnp.right_shift(packed, shifts), 3)
    code_vals = code_vals.reshape(leading + (-1,))
    low_bit = jnp.bitwise_and(code_vals, 1).astype(jnp.float32)
    high_bit = jnp.right_shift(code_vals, 1).astype(jnp.float32)
    levels = (
        buckets[0]
        + low_bit * (buckets[1] - buckets[0])
        + high_bit * (buckets[2] - buckets[0])
        + low_bit * high_bit * (buckets[3] - buckets[2] - buckets[1] + buckets[0])
    )
    vectors = jnp.take(centroids, cell_ids, axis=0).astype(jnp.float32) + levels
    unit_scale = lax.rsqrt(jnp.sum(vectors * vectors, axis=-1, keepdims=True) + EPS)
    return (vectors * unit_scale).astype(jnp.bfloat16)


def fetch_passages(wanted, lengths, centroid_ids, residual_codes, centroids, buckets):
    documents = decompress(
        jnp.take(centroid_ids, wanted, axis=0),
        jnp.take(residual_codes, wanted, axis=0),
        centroids,
        buckets,
    )
    return (documents, jnp.take(lengths, wanted, axis=0))


def soft_parts(similar, doc_spans):
    in_range = jnp.arange(similar.shape[-1])[None, None, :] < doc_spans[..., None, None]
    weights = jnp.where(in_range, jnp.exp(similar / TEMPER), 0.0)
    totals = jnp.sum(weights, axis=-1)
    scores = TEMPER * jnp.sum(jnp.log(totals), axis=-1)
    return (weights, totals, scores)


def seeds_of(scores):
    exponent = jnp.exp(scores)
    softmax_w = exponent / jnp.sum(exponent, axis=-1, keepdims=True)
    positive = jnp.arange(scores.shape[-1]) == 0
    return LOSS_SCALE * (softmax_w - jnp.where(positive, 1.0, 0.0))


def score_fetched(grouped, got_docs, got_spans, position, query_count, cand_count):
    feature_dim = grouped.shape[2]
    doc_len = got_docs.shape[2]
    slot_docs = jnp.take(got_docs.reshape(-1, doc_len, feature_dim), position, axis=0)
    slot_docs = slot_docs.reshape(query_count, cand_count, doc_len, feature_dim)
    slot_spans = jnp.take(got_spans.reshape(-1), position, axis=0).reshape(query_count, cand_count)
    similar = jnp.einsum("nid,nctd->ncit", grouped, slot_docs, preferred_element_type=jnp.float32)
    weights, totals, scores = soft_parts(similar, slot_spans)
    score_seeds = seeds_of(scores)
    mixing = (score_seeds[:, :, None, None] * weights / totals[..., None]).astype(jnp.bfloat16)
    grad_queries = jnp.einsum(
        "ncit,nctd->nid", mixing, slot_docs, preferred_element_type=jnp.float32
    )
    return (scores, grad_queries)


def local(
    residual,
    context,
    out_proj,
    norm_gain,
    colbert_head,
    candidates,
    lengths,
    centroid_ids,
    residual_codes,
    centroids,
    buckets,
):
    shard_total = lax.axis_size("dp")
    tensor_total = lax.axis_size("tensor")
    proj_full = lax.all_gather(out_proj, "dp", axis=1, tiled=True)
    seq_rows = residual.shape[0]
    attended = lax.psum_scatter(
        jnp.dot(context, proj_full, preferred_element_type=jnp.float32).astype(jnp.bfloat16),
        "tensor",
        scatter_dimension=0,
        tiled=True,
    ).astype(jnp.float32)
    summed = residual.astype(jnp.float32) + attended
    inv_rms = lax.rsqrt(jnp.mean(summed * summed, axis=-1, keepdims=True) + EPS)
    normed = (summed * inv_rms * norm_gain).astype(jnp.bfloat16)
    head_full = lax.all_gather(colbert_head, "tensor", axis=0, tiled=True)
    embedded = jnp.dot(normed, head_full, preferred_element_type=jnp.float32)
    inverse = lax.rsqrt(jnp.sum(embedded * embedded, axis=-1, keepdims=True) + EPS)
    queries = (embedded * inverse).astype(jnp.bfloat16)
    query_count = candidates.shape[0]
    cand_count = candidates.shape[1]
    query_len = seq_rows // query_count
    feature_dim = queries.shape[1]
    grouped = queries.reshape(query_count, query_len, feature_dim)
    slot_ids = candidates.reshape(-1)
    slot_count = slot_ids.shape[0]
    per_shard = lengths.shape[0]
    owners = slot_ids // per_shard
    local_ids = slot_ids - owners * per_shard
    capacity = 2 * slot_count // shard_total
    slot_order = jnp.arange(slot_count, dtype=jnp.int32)
    earlier = (owners[None, :] == owners[:, None]) & (slot_order[None, :] < slot_order[:, None])
    slot_rank = jnp.sum(earlier.astype(jnp.int32), axis=1)
    position = owners * capacity + slot_rank
    placed = position[None, :] == jnp.arange(shard_total * capacity, dtype=jnp.int32)[:, None]
    request = jnp.sum(jnp.where(placed, local_ids[None, :], 0), axis=1).reshape(
        shard_total, capacity
    )
    documents, doc_spans = fetch_passages(
        lax.all_to_all(request, "dp", split_axis=0, concat_axis=0, tiled=True),
        lengths,
        centroid_ids,
        residual_codes,
        centroids,
        buckets,
    )
    got_docs = lax.all_to_all(documents, "dp", split_axis=0, concat_axis=0, tiled=True)
    got_spans = lax.all_to_all(doc_spans, "dp", split_axis=0, concat_axis=0, tiled=True)
    scores, grad_queries = score_fetched(
        grouped, got_docs, got_spans, position, query_count, cand_count
    )
    grad_q = grad_queries.reshape(seq_rows, feature_dim)
    grad_embedded = (
        inverse * grad_q
        - inverse**3 * embedded * jnp.sum(embedded * grad_q, axis=-1, keepdims=True)
    ).astype(jnp.bfloat16)
    head_term = lax.dot_general(
        normed, grad_embedded, (((0,), (0,)), ((), ())), preferred_element_type=jnp.float32
    )
    grad_normed = lax.dot_general(
        grad_embedded, head_full, (((1,), (1,)), ((), ())), preferred_element_type=jnp.float32
    )
    gain_term = jnp.sum(grad_normed * summed * inv_rms, axis=0)
    scaled = grad_normed * norm_gain
    residual_grad = (
        inv_rms * scaled - summed * inv_rms**3 * jnp.mean(summed * scaled, axis=-1, keepdims=True)
    ).astype(jnp.bfloat16)
    context_grad = lax.dot_general(
        lax.all_gather(residual_grad, "tensor", axis=0, tiled=True),
        proj_full,
        (((1,), (1,)), ((), ())),
        preferred_element_type=jnp.float32,
    ).astype(jnp.bfloat16)
    head_total, gain_grad = lax.psum((head_term, gain_term), ("dp", "tensor"))
    head_count = head_total.shape[0] // tensor_total
    head_grad = lax.dynamic_slice_in_dim(
        head_total, lax.axis_index("tensor") * head_count, head_count, 0
    )
    return (scores, context_grad, residual_grad, head_grad, gain_grad)


def solution(mesh):
    in_specs = (
        P(("dp", "tensor"), None),
        P("dp", "tensor"),
        P("tensor", "dp"),
        P(),
        P("tensor", None),
        P(("dp", "tensor"), None),
        P("dp"),
        P("dp", None),
        P("dp", None),
        P(),
        P(),
    )
    out_specs = (
        P(("dp", "tensor"), None),
        P("dp", "tensor"),
        P(("dp", "tensor"), None),
        P("tensor", None),
        P(),
    )
    return jax.shard_map(local, mesh=mesh, in_specs=in_specs, out_specs=out_specs, check_vma=False)
```

profile of v0, /device:TPU:1, one launch (start us, length us, event | category | flops | bytes accessed | tf_op | source)
XLA Modules:
  0.0 817.6 jit_solution(13815733177478389366)
XLA Ops:
  7.2 0.7 all-gather.4.cloned.1.call-update
  7.9 0.7 subtract_bitcast_fusion
  8.6 0.7 and_select_fusion.3
  9.2 0.2 convert_reduce_fusion
  9.4 0.1 select_reduce_fusion
  9.5 0.8 all_to_all.17
  10.3 19.3 %all-to-all-start = ((s32[64,1,2]{2,1,0:T(1,128)}), s32[64,1,2]{2,1,0:T(1,128)S(1)}, u32[]{:S(2)}, u32[]{:S(2)}) async-start(s32[64,1,2]{2,1,0:T(1,128)} %bitcast.5), calls=%async_computation | async-start | bytes 65536 | tf_op jit(solution)/shard_map/all_to_all | solution.py:121
  29.6 1.4 fusion.18
  36.2 0.1 shift_right_arithmetic.34
  36.3 6.5 all-to-all-done
  42.8 0.1 copy.71
  42.9 0.1 copy.72
  43.0 0.1 reshape.391
  43.1 0.1 copy.75
  43.3 1.4 gather_fusion.2
  44.7 0.1 compare_select_fusion
  44.8 0.1 reshape.415
  44.9 2.0 gather_fusion.4
  46.9 2.8 gather.37
  49.7 4.5 broadcast_select_fusion
  54.2 2.8 copy.78
  57.0 4.4 broadcast_bitcast_fusion
  61.4 6.8 copy.79
  68.2 1.2 gather_fusion
  69.4 0.1 gather.31
  69.6 0.6 and_select_fusion
  70.2 8.0 all-to-all-start.1
  78.3 29.2 %gather_fusion.3 = bf16[8192,128]{1,0:T(8,128)(2,1)} fusion(bf16[8192,128]{1,0:T(8,128)(2,1)S(1)} %copy-done, s32[8192]{0:T(1024)S(1)} %broadcast_clamp_fusion), kind=kCustom, calls=%fused_computation.3 | custom fusion | bytes 4227072 | tf_op jit(solution)/shard_map/jit(_take)/gather | solution.py:25
  107.5 0.2 compare_and_fusion
  107.7 7.0 multiply_reduce_fusion
  114.7 5.5 multiply_convert_fusion
  120.3 15.0 %all-to-all-start.2 = ((bf16[64,2,64,128]{3,2,1,0:T(8,128)(2,1)}), bf16[64,2,64,128]{3,2,1,0:T(8,128)(2,1)}, u32[]{:S(2)}, u32[]{:S(2)}) async-start(bf16[64,2,64,128]{3,2,1,0:T(8,128)(2,1)} %multiply_convert_fusion), calls=%async_computation.2 | async-start | bytes 4194304 | tf_op jit(solution)/shard_map/all_to_all | solution.py:128
  135.3 0.0 reduce-scatter.2.cloned.1.call-start
  135.3 62.1 %all-gather.4.cloned.1.call-done = bf16[640,4096]{0,1:T(8,128)(2,1)} async-done(((bf16[640,64]{0,1:T(8,128)(2,1)}), bf16[640,4096]{0,1:T(8,128)(2,1)}) %all-gather.4.cloned.1.call-update) | async-done | bytes 5242896 | tf_op jit(solution)/shard_map/all_gather | solution.py:86
  197.5 5.6 convolution_convert_fusion
  203.1 0.0 all-gather.6.cloned.1.call-start
  203.2 0.7 all-gather.6.cloned.1.call-update
  203.9 0.2 all-reduce.2.cloned.1.call-start
  204.1 0.5 broadcast.519
  204.7 0.7 reduce.12
  205.4 0.1 reshape.385
  205.5 0.8 gather_fusion.1
  206.3 0.1 iota_compare_fusion.2
  206.4 31.9 %all-to-all-done.2 = bf16[64,2,64,128]{3,2,1,0:T(8,128)(2,1)} async-done(((bf16[64,2,64,128]{3,2,1,0:T(8,128)(2,1)}), bf16[64,2,64,128]{3,2,1,0:T(8,128)(2,1)}, u32[]{:S(2)}, u32[]{:S(2)}) %all-to-all-start.2) | async-done | bytes 2097184 | tf_op jit(solution)/shard_map/all_to_all | solution.py:128
  238.3 3.3 gather_fusion.5
  241.6 11.2 %reduce-scatter.2.cloned.1.call-done = bf16[32,4096]{1,0:T(8,128)(2,1)} async-done(((bf16[256,4096]{1,0:T(8,128)(2,1)}), bf16[32,4096]{1,0:T(8,128)(2,1)}) %reduce-scatter.2.cloned.1.call-update) | async-done | bytes 262160 | tf_op jit(solution)/shard_map/reduce_scatter | solution.py:88
  252.8 1.2 multiply_reduce_fusion.3
  254.0 33.0 %all-gather.6.cloned.1.call-done = bf16[4096,128]{1,0:T(8,128)(2,1)} async-done(((bf16[512,128]{1,0:T(8,128)(2,1)}), bf16[4096,128]{1,0:T(8,128)(2,1)}) %all-gather.6.cloned.1.call-update) | async-done | bytes 1048592 | tf_op jit(solution)/shard_map/all_gather | solution.py:97
  287.0 1.8 multiply_reduce_fusion.5
  288.9 2.5 fusion.19
  291.4 0.1 log_reduce_fusion
  291.5 0.6 exponential_reduce_fusion
  292.2 1.2 fusion.12
  293.3 0.8 multiply_reduce_fusion.4
  294.1 0.1 subtract_convert_fusion.1
  294.2 1.9 fusion.16
  296.1 0.0 all-gather.8.cloned.1.call-start
  296.2 1.8 multiply_reduce_fusion.1
  298.0 0.9 subtract_convert_fusion
  298.9 104.6 %psum.15 = f32[4096]{0:T(1024)} all-reduce(f32[4096]{0:T(1024)S(1)} %get-tuple-element.5), channel_id=1, replica_groups=mesh['dp'=64,'tensor'=8] {'dp','tensor'}, use_global_device_ids=true, to_apply=%region_13.14 | all-reduce | flops 4096 | bytes 32768 | tf_op jit(solution)/shard_map/psum | solution.py:155
  403.5 368.7 %all-reduce.2.cloned.1.call-done = f32[4096,128]{1,0:T(8,128)} async-done(((f32[4096,128]{1,0:T(8,128)}), f32[4096,128]{1,0:T(8,128)}) %all-reduce.2.cloned.1.call-update) | async-done | bytes 2097168 | tf_op jit(solution)/shard_map/psum | solution.py:155
  772.3 1.7 constant_dynamic-slice_fusion
  773.9 31.5 %all-gather.8.cloned.1.call-done = bf16[256,4096]{1,0:T(8,128)(2,1)} async-done(((bf16[32,4096]{1,0:T(8,128)(2,1)}), bf16[256,4096]{1,0:T(8,128)(2,1)}) %all-gather.8.cloned.1.call-update) | async-done | bytes 2097168 | tf_op jit(solution)/shard_map/all_gather | solution.py:150
  805.5 5.6 convolution_convert_fusion.1
  (39 shorter events, 0.3 us)
Async XLA Ops:
  7.2 71.1 %copy-start = (bf16[8192,128]{1,0:T(8,128)(2,1)S(1)}, bf16[8192,128]{1,0:T(8,128)(2,1)}, u32[]{:S(2)}) copy-start(bf16[8192,128]{1,0:T(8,128)(2,1)} %param.20) | copy-start | bytes 6291460
  7.2 190.3 %all-gather.4.cloned.1.call-start = ((), (), s32[]{:S(2)}) async-start(), calls=%async_computation.4 | async-start | bytes 5324800 | tf_op jit(solution)/shard_map/all_gather | solution.py:86
  10.3 32.5 %all-to-all-start = ((s32[64,1,2]{2,1,0:T(1,128)}), s32[64,1,2]{2,1,0:T(1,128)S(1)}, u32[]{:S(2)}, u32[]{:S(2)}) async-start(s32[64,1,2]{2,1,0:T(1,128)} %bitcast.5), calls=%async_computation | async-start | bytes 65536 | tf_op jit(solution)/shard_map/all_to_all | solution.py:121
  61.4 6.8 copy-start.1
  70.2 50.1 %all-to-all-start.1 = ((s32[64,1,2]{2,1,0:T(1,128)}), s32[64,1,2]{2,1,0:T(1,128)S(1)}, u32[]{:S(2)}, u32[]{:S(2)}) async-start(s32[64,1,2]{2,1,0:T(1,128)} %bitcast.10), calls=%async_computation.1 | async-start | bytes 65536 | tf_op jit(solution)/shard_map/all_to_all | solution.py:129
  107.5 7.2 copy-start.2
  107.5 7.2 copy-start.3
  120.3 77.2 %copy-start.9 = (bf16[256,640]{1,0:T(8,128)(2,1)S(1)}, bf16[256,640]{1,0:T(8,128)(2,1)}, u32[]{:S(2)}) copy-start(bf16[256,640]{1,0:T(8,128)(2,1)} %param.12) | copy-start | bytes 983044
  120.3 118.1 %all-to-all-start.2 = ((bf16[64,2,64,128]{3,2,1,0:T(8,128)(2,1)}), bf16[64,2,64,128]{3,2,1,0:T(8,128)(2,1)}, u32[]{:S(2)}, u32[]{:S(2)}) async-start(bf16[64,2,64,128]{3,2,1,0:T(8,128)(2,1)} %multiply_convert_fusion), calls=%async_computation.2 | async-start | bytes 4194304 | tf_op jit(solution)/shard_map/all_to_all | solution.py:128
  135.3 68.8 %copy-start.8 = (s32[1,64]{1,0:T(1,128)S(1)}, s32[1,64]{1,0:T(1,128)}, u32[]{:S(2)}) copy-start(s32[1,64]{1,0:T(1,128)} %param.16) | copy-start | bytes 772
  135.3 117.5 %reduce-scatter.2.cloned.1.call-start = ((), (), s32[]{:S(2)}) async-start(), calls=%async_computation.5 | async-start | bytes 2359296 | tf_op jit(solution)/shard_map/reduce_scatter | solution.py:88
  203.1 49.7 %copy-start.4 = (bf16[32,4096]{1,0:T(8,128)(2,1)S(1)}, bf16[32,4096]{1,0:T(8,128)(2,1)}, u32[]{:S(2)}) copy-start(bf16[32,4096]{1,0:T(8,128)(2,1)} %param.11) | copy-start | bytes 786436
  203.1 83.9 %copy-start.7 = (f32[4096]{0:T(1024)S(1)}, f32[4096]{0:T(1024)}, u32[]{:S(2)}) copy-start(f32[4096]{0:T(1024)} %param.14) | copy-start | bytes 49156
  203.1 83.9 %all-gather.6.cloned.1.call-start = ((), (), s32[]{:S(2)}) async-start(), calls=%async_computation.6 | async-start | bytes 1179648 | tf_op jit(solution)/shard_map/all_gather | solution.py:97
  203.9 568.4 %all-reduce.2.cloned.1.call-start = ((), (), s32[]{:S(2)}) async-start(), calls=%async_computation.8 | async-start | bytes 4194304 | tf_op jit(solution)/shard_map/psum | solution.py:155
  287.0 6.3 copy-start.6
  288.9 5.3 copy-start.5
  296.1 509.3 %all-gather.8.cloned.1.call-start = ((), (), s32[]{:S(2)}) async-start(), calls=%async_computation.7 | async-start | bytes 2359296 | tf_op jit(solution)/shard_map/all_gather | solution.py:150
Sparse Core Ops, SparseCore 0:
  11.0 186.4 all-gather.3
  203.2 49.5 reduce-scatter.1
  255.0 31.9 all-gather.5
  296.2 475.9 all-reduce.1
  774.8 30.5 all-gather.7
where the time goes:
time: 819 us; the launch traced here: 818 us
  waiting for transfers between devices  547 us (67%)
  blocking collectives  105 us (13%)
  local copies, waits for them, and re-layouts  60 us (7%)
  starting transfers between devices  42.7 us (5%)
  other arithmetic  24.5 us (3%)
  matrix products  20.1 us (2%)
  between operations  19.2 us (2%)
    psum x1, waiting for transfers between devices, local(): head_total, gain_grad = lax.psum((head_term, gain_term), ('dp', 'tensor'))  369 us
    psum x1, blocking collectives, local(): head_total, gain_grad = lax.psum((head_term, gain_term), ('dp', 'tensor'))  105 us
    all_gather x1, waiting for transfers between devices, local(): proj_full = lax.all_gather(out_proj, 'dp', axis=1, tiled=True)  62.1 us
    all_gather x1, waiting for transfers between devices, local(): head_full = lax.all_gather(colbert_head, 'tensor', axis=0, tiled=True)  33 us
    all_to_all x1, waiting for transfers between devices, local(): lax.all_to_all(documents, 'dp', split_axis=0, concat_axis=0, tiled=True)  31.9 us
    all_gather x1, waiting for transfers between devices, local(): lax.all_gather(residual_grad, 'tensor', axis=0, tiled=True)  31.5 us
    gather x1, local copies, waits for them, and re-layouts, decompress(): vectors = jnp.take(centroids, cell_ids, axis=0).astype(jnp.float32) + levels  29.2 us
    all_to_all x1, starting transfers between devices, local(): lax.all_to_all(request, 'dp', split_axis=0, concat_axis=0, tiled=True)  19.3 us
  transfers between devices with their start and end apart: 8, of which 7 were waited for; matrix products, arithmetic and copies ran while one was open for 11% of the time, Pallas kernels for 0%

commit v1 on v0

v1 whole, which is shorter than its diff:
```python
import jax
import jax.numpy as jnp
from jax import lax
from jax.sharding import Mesh, PartitionSpec as P

EPS = 1e-06
TEMPER = 0.1
LOSS_SCALE = 64.0

Y, Z, X, C = 4, 16, 4, 2
DP = ("y", "z")
TENSOR = ("x", "c")
PLANE = ("y", "x", "c")

BF16 = jnp.bfloat16
F32 = jnp.float32


def decode_all(cell_ids, packed, centroids, buckets):
    passages, tokens = cell_ids.shape
    words = packed.shape[1] // tokens
    features = centroids.shape[1]
    rows = passages * tokens
    packed = packed.reshape(rows, words)
    bytes_of = jnp.concatenate([packed & 255, (packed >> 8) & 255], axis=1).astype(BF16)
    feature = jnp.arange(features, dtype=jnp.int32)[None, :]
    source = jnp.arange(2 * words, dtype=jnp.int32)[:, None]
    spread = (source == (feature // 8) + words * ((feature % 8) // 4)).astype(BF16)
    code_bytes = jnp.dot(bytes_of, spread, preferred_element_type=F32).astype(jnp.int32)
    codes = (code_bytes >> (2 * (feature % 4))) & 3
    low = (codes & 1).astype(F32)
    high = (codes >> 1).astype(F32)
    levels = (
        buckets[0]
        + low * (buckets[1] - buckets[0])
        + high * (buckets[2] - buckets[0])
        + low * high * (buckets[3] - buckets[2] - buckets[1] + buckets[0])
    )
    vectors = jnp.take(centroids, cell_ids.reshape(rows), axis=0).astype(F32) + levels
    scale = lax.rsqrt(jnp.sum(vectors * vectors, axis=-1, keepdims=True) + EPS)
    return (vectors * scale).astype(BF16)


def halves(values):
    top = values.astype(BF16)
    return top, (values - top.astype(F32)).astype(BF16)


def local(
    residual,
    context,
    out_proj,
    norm_gain,
    colbert_head,
    candidates,
    lengths,
    centroid_ids,
    residual_codes,
    centroids,
    buckets,
):
    shards = Y * Z
    seq_rows, width = residual.shape
    cand_count = candidates.shape[1]
    per_shard, doc_len = centroid_ids.shape
    feature_dim = centroids.shape[1]
    cap = 2 * cand_count // shards
    slots = shards * cap

    slot_ids = candidates.reshape(-1)
    owners = slot_ids // per_shard
    local_ids = slot_ids - owners * per_shard
    order = jnp.arange(cand_count, dtype=jnp.int32)
    earlier = (owners[None, :] == owners[:, None]) & (order[None, :] < order[:, None])
    rank = jnp.sum(earlier.astype(jnp.int32), axis=1)
    position = owners * cap + rank
    placed = position[None, :] == jnp.arange(slots, dtype=jnp.int32)[:, None]
    request = jnp.sum(jnp.where(placed, local_ids[None, :], 0), axis=1).reshape(shards, cap)
    filled = jnp.any(placed, axis=1)
    note = jnp.concatenate(
        [
            jnp.broadcast_to(lengths[None, :], (shards, per_shard)),
            request,
            jnp.zeros((shards, 128 - per_shard - cap), jnp.int32),
        ],
        axis=1,
    )
    notes = lax.all_to_all(note, DP, 0, 0, tiled=True)

    proj_z = lax.all_gather(out_proj, "z", axis=1, tiled=True)
    context_y = lax.all_to_all(
        jnp.broadcast_to(context[None], (Y,) + context.shape), "y", 0, 0, tiled=True
    ).reshape(Y * context.shape[0], context.shape[1])

    documents = decode_all(centroid_ids, residual_codes, centroids, buckets)
    wanted = notes[:, per_shard : per_shard + cap].reshape(slots)
    chosen = jnp.take(documents.reshape(per_shard, doc_len, feature_dim), wanted, axis=0)
    got_docs = lax.all_to_all(
        chosen.reshape(shards, cap * doc_len, feature_dim), DP, 0, 0, tiled=True
    ).reshape(slots * doc_len, feature_dim)
    all_lengths = notes[:, None, :per_shard]
    spans = jnp.sum(
        jnp.where(
            jnp.arange(per_shard, dtype=jnp.int32)[None, None, :] == request[:, :, None],
            all_lengths,
            0,
        ),
        axis=2,
    ).reshape(slots)

    terms = jnp.dot(context_y, proj_z, preferred_element_type=F32).astype(BF16)
    parts = lax.all_to_all(terms, PLANE, 0, 0, tiled=True)
    parts = parts.reshape(Y, X * C, seq_rows, width // Y).astype(F32)
    attended = jnp.sum(parts, axis=1).transpose(1, 0, 2).reshape(seq_rows, width)
    summed = residual.astype(F32) + attended
    inv_rms = lax.rsqrt(jnp.mean(summed * summed, axis=-1, keepdims=True) + EPS)
    scaled_sum = summed * inv_rms
    normed = (scaled_sum * norm_gain).astype(BF16)

    proj_z_later, head_blk = lax.optimization_barrier((proj_z, colbert_head))
    head_full = lax.all_gather(head_blk, TENSOR, axis=0, tiled=True)
    proj_full = lax.all_gather(proj_z_later, "y", axis=1, tiled=True)
    unit_all = lax.all_gather(scaled_sum.astype(BF16), TENSOR, axis=0, tiled=True)

    embedded = jnp.dot(normed, head_full, preferred_element_type=F32)
    inverse = lax.rsqrt(jnp.sum(embedded * embedded, axis=-1, keepdims=True) + EPS)
    queries = (embedded * inverse).astype(BF16)

    similar = lax.dot_general(
        got_docs, queries, (((1,), (1,)), ((), ())), preferred_element_type=F32
    ).reshape(slots, doc_len, seq_rows)
    in_range = jnp.arange(doc_len, dtype=jnp.int32)[None, :, None] < spans[:, None, None]
    weights = jnp.where(in_range, jnp.exp(similar / TEMPER), 0.0)
    totals = jnp.sum(weights, axis=1)
    slot_scores = TEMPER * jnp.sum(jnp.log(totals), axis=-1)
    scores = jnp.sum(jnp.where(placed, slot_scores[:, None], 0.0), axis=0)[None, :]
    exponent = jnp.where(filled, jnp.exp(jnp.where(filled, slot_scores, 0.0)), 0.0)
    positive = jnp.arange(slots, dtype=jnp.int32) == position[0]
    seeds = LOSS_SCALE * (exponent / jnp.sum(exponent) - jnp.where(positive, 1.0, 0.0))
    mixing = (weights * (seeds[:, None] / totals)[:, None, :]).astype(BF16)
    grad_q = lax.dot_general(
        mixing.reshape(slots * doc_len, seq_rows),
        got_docs,
        (((0,), (0,)), ((), ())),
        preferred_element_type=F32,
    )

    along = jnp.sum(embedded * grad_q, axis=-1, keepdims=True)
    grad_embedded = (inverse * grad_q - inverse**3 * embedded * along).astype(BF16)
    pull = (
        inv_rms
        * jnp.sum(grad_embedded.astype(F32) * embedded, axis=-1, keepdims=True)
        * (1.0 / width)
    )
    packet = jnp.concatenate(
        [
            grad_embedded,
            *halves(pull),
            *halves(inv_rms),
            jnp.zeros((seq_rows, feature_dim - 4), BF16),
        ],
        axis=1,
    )
    packets = lax.all_gather(packet, TENSOR, axis=0, tiled=True)
    ge_all = packets[:, :feature_dim]
    extra = packets[:, feature_dim : feature_dim + 4].astype(F32)
    pull_all = extra[:, 0:1] + extra[:, 1:2]
    inv_all = extra[:, 2:3] + extra[:, 3:4]

    moments = lax.dot_general(
        unit_all, ge_all, (((0,), (0,)), ((), ())), preferred_element_type=F32
    )
    gain_term = jnp.sum(moments * head_full.astype(F32), axis=1).reshape(shards, width // shards)
    head_rows = colbert_head.shape[0]
    mine = (lax.axis_index("x") * C + lax.axis_index("c")) * head_rows
    head_term = lax.dynamic_slice_in_dim(moments, mine, head_rows, 0)
    share = head_rows // shards

    def bundle(head_part, gain_part):
        count = head_part.shape[0]
        return jnp.concatenate(
            [
                head_part.astype(BF16),
                jnp.concatenate(halves(gain_part), axis=1).reshape(count, 1, feature_dim),
                jnp.zeros((count, share - 1, feature_dim), BF16),
            ],
            axis=1,
        )

    def unbundle(rows):
        rows = rows.astype(F32)
        pair = rows[:, share]
        return rows[:, :share], pair[:, : width // shards] + pair[:, width // shards :]

    first = lax.all_to_all(
        bundle(head_term.reshape(shards, share, feature_dim), gain_term), DP, 0, 0, tiled=True
    )
    head_got, gain_got = unbundle(first)
    second = bundle(
        jnp.sum(head_got, axis=0, keepdims=True), jnp.sum(gain_got, axis=0, keepdims=True)
    )
    second = lax.all_to_all(
        jnp.broadcast_to(second, (shards,) + second.shape[1:]), DP, 0, 0, tiled=True
    )
    head_got, gain_got = unbundle(second)
    gain_blk = lax.dynamic_slice_in_dim(norm_gain, mine, head_rows, 0)
    head_grad = head_got.reshape(head_rows, feature_dim) * gain_blk[:, None]
    gain_grad = gain_got.reshape(width)

    grad_normed = lax.dot_general(
        grad_embedded, head_full, (((1,), (1,)), ((), ())), preferred_element_type=F32
    )
    scaled = grad_normed * norm_gain
    residual_grad = (
        inv_rms * scaled - summed * inv_rms**3 * jnp.mean(summed * scaled, axis=-1, keepdims=True)
    ).astype(BF16)
    gained_head = (head_full.astype(F32) * norm_gain[:, None]).astype(BF16)
    mixed_head = jnp.dot(proj_full, gained_head, preferred_element_type=F32).astype(BF16)
    pulled = lax.dot_general(
        unit_all, proj_full, (((1,), (1,)), ((), ())), preferred_element_type=F32
    )
    context_grad = (
        inv_all
        * lax.dot_general(
            ge_all, mixed_head, (((1,), (1,)), ((), ())), preferred_element_type=F32
        )
        - pull_all * pulled
    ).astype(BF16)
    return (scores, context_grad, residual_grad, head_grad, gain_grad)


def solution(mesh):
    split = Mesh(mesh.devices.reshape(Y, Z, X, C), ("y", "z", "x", "c"))
    both = DP + TENSOR
    in_specs = (
        P(both, None),
        P(DP, TENSOR),
        P(TENSOR, DP),
        P(),
        P(TENSOR, None),
        P(both, None),
        P(DP),
        P(DP, None),
        P(DP, None),
        P(),
        P(),
    )
    out_specs = (
        P(both, None),
        P(DP, TENSOR),
        P(both, None),
        P(TENSOR, None),
        P(),
    )
    return jax.shard_map(local, mesh=split, in_specs=in_specs, out_specs=out_specs, check_vma=False)
```

time: 819 us -> 368 us (0.45)
  waiting for transfers between devices: 547 us -> 181 us
  blocking collectives: 105 us -> 15.9 us
  local copies, waits for them, and re-layouts: 60 us -> 27.1 us
  starting transfers between devices: 42.7 us -> 74.4 us
  matrix products: 20.1 us -> 31.4 us
    psum x1 -> x0, waiting for transfers between devices: 369 us -> none  [local(): head_total, gain_grad = lax.psum((head_term, gain_term), ('dp', 'tensor'))]
    psum x1 -> x0, blocking collectives: 105 us -> none  [local(): head_total, gain_grad = lax.psum((head_term, gain_term), ('dp', 'tensor'))]
    all_to_all x3 -> x6, waiting for transfers between devices: 38.5 us -> 97.6 us  [the longest x1 60.4 us: local(): lax.all_to_all(chosen.reshape(shards, cap * doc_len, feature_dim), DP, 0,...]
    all_gather x3 -> x4, waiting for transfers between devices: 127 us -> 81.4 us  [the longest x1 28.9 us: local(): head_full = lax.all_gather(head_blk, TENSOR, axis=0, tiled=True)]
    all_to_all x3 -> x6, starting transfers between devices: 42.3 us -> 74 us  [the longest x1 18.6 us: local(): notes = lax.all_to_all(note, DP, 0, 0, tiled=True)]
    gather x8 -> x2, local copies, waits for them, and re-layouts: 40.8 us -> 14.3 us  [the longest x1 12.1 us: decode_all(): jnp.take(centroids, cell_ids.reshape(rows), axis=0).astype(F32) + levels]
    all_gather x0 -> x1, blocking collectives: none -> 15.9 us  [local(): packets = lax.all_gather(packet, TENSOR, axis=0, tiled=True)]
    dot_general x6 -> x8, matrix products: 18.3 us -> 30.8 us  [the longest x1 5.93 us: local(): lax.dot_general(unit_all, proj_full, (((1,), (1,)), ((), ())), preferred_...]
  transfers between devices with their start and end apart: 8 -> 10, of which waited for: 7 -> 7; matrix products, arithmetic and copies ran while one was open for 11% -> 17% of each run, Pallas kernels for 0% -> 0%
where the time goes in v1:
time: 368 us; the launch traced here: 367 us
  waiting for transfers between devices  181 us (49%)
  starting transfers between devices  74.4 us (20%)
  matrix products  31.4 us (9%)
  local copies, waits for them, and re-layouts  27.1 us (7%)
  between operations  19.4 us (5%)
  other arithmetic  18.3 us (5%)
  blocking collectives  15.9 us (4%)
    all_to_all x1, waiting for transfers between devices, local(): lax.all_to_all(chosen.reshape(shards, cap * doc_len, feature_dim), DP, 0,...  60.4 us
    all_gather x1, waiting for transfers between devices, local(): head_full = lax.all_gather(head_blk, TENSOR, axis=0, tiled=True)  28.9 us
    all_gather x1, waiting for transfers between devices, local(): proj_full = lax.all_gather(proj_z_later, 'y', axis=1, tiled=True)  23 us
    all_to_all x1, waiting for transfers between devices, local(): parts = lax.all_to_all(terms, PLANE, 0, 0, tiled=True)  18.8 us
    all_to_all x1, starting transfers between devices, local(): notes = lax.all_to_all(note, DP, 0, 0, tiled=True)  18.6 us
    all_to_all x1, waiting for transfers between devices, local(): lax.all_to_all(bundle(head_term.reshape(shards, share, feature_dim), gain...  18.3 us
    all_gather x1, waiting for transfers between devices, local(): proj_z = lax.all_gather(out_proj, 'z', axis=1, tiled=True)  18.3 us
    all_to_all x1, starting transfers between devices, local(): parts = lax.all_to_all(terms, PLANE, 0, 0, tiled=True)  17 us
  transfers between devices with their start and end apart: 10, of which 7 were waited for; matrix products, arithmetic and copies ran while one was open for 17% of the time, Pallas kernels for 0%

profile of v1, /device:TPU:1, one launch (start us, length us, event | category | flops | bytes accessed | tf_op | source)
XLA Modules:
  0.0 367.3 jit_solution(2887058261421002134)
XLA Ops:
  7.2 0.7 all-gather.5.cloned.1.call-update
  8.0 2.2 broadcast_in_dim.160
  10.2 5.0 %all-to-all-start.2 = ((bf16[4,256,640]{2,1,0:T(8,128)(2,1)}), bf16[4,256,640]{2,1,0:T(8,128)(2,1)}, u32[]{:S(2)}, u32[]{:S(2)}) async-start(bf16[4,256,640]{2,1,0:T(8,128)(2,1)} %broadcast_in_dim.160), calls=%async_computation.2 | async-start | bytes 2621440 | tf_op jit(solution)/shard_map/all_to_all | solution.py:91
  15.2 0.2 convert_reduce_fusion.1
  15.7 0.6 fusion.52
  16.4 0.1 eq.80
  21.8 0.8 and.124
  22.6 0.3 copy.60
  23.0 0.8 and.122
  23.8 0.3 copy.59
  24.1 12.1 %gather_fusion = bf16[4096,128]{1,0:T(8,128)(2,1)S(1)} fusion(bf16[8192,128]{1,0:T(8,128)(2,1)S(1)} %copy-done, s32[4096]{0:T(1024)S(1)} %broadcast_clamp_fusion), kind=kCustom, calls=%fused_computation | custom fusion | bytes 2113536 | tf_op jit(solution)/shard_map/jit(_take)/gather | solution.py:39
  36.3 0.7 add_add_fusion.1
  37.0 4.1 %multiply_reduce_fusion = (f32[4096]{0:T(1024)S(1)}, f32[4096,128]{1,0:T(8,128)}) fusion(f32[]{:T(128)S(6)} %add.202, f32[]{:T(128)S(6)} %sub.92, f32[]{:T(128)S(6)} %sub.91, s32[128]{0:T(128)S(1)} %get-tuple-element.47, s32[128]{0:T(128)S(1)} %get-tuple-element.46, bf16[4096,16]{0,1:T(8,128)(2,1)S(1)} %copy.60, bf16[4096,16]{0,1:T(8,128)(2,1)S(1)} %copy.59, ...), kind=kOutput, calls=%fused_computation.15 | convolution fusion | flops 44040192 | bytes 3429392 | tf_op jit(solution)/shard_map/dot_general | solution.py:29
  41.1 18.6 %all-to-all-start = ((s32[64,1,128]{2,1,0:T(1,128)}), s32[64,1,128]{2,1,0:T(1,128)S(1)}, u32[]{:S(2)}, u32[]{:S(2)}) async-start(s32[64,1,128]{2,1,0:T(1,128)} %bitcast.5), calls=%async_computation | async-start | bytes 65536 | tf_op jit(solution)/shard_map/all_to_all | solution.py:88
  59.6 18.3 %all-gather.5.cloned.1.call-done = bf16[640,1024]{0,1:T(8,128)(2,1)} async-done(((bf16[640,64]{0,1:T(8,128)(2,1)}), bf16[640,1024]{0,1:T(8,128)(2,1)}) %all-gather.5.cloned.1.call-update) | async-done | bytes 1310736 | tf_op jit(solution)/shard_map/all_gather | solution.py:90
  77.9 4.8 %convolution_convert_fusion.1 = bf16[1024,1024]{1,0:T(8,128)(2,1)} fusion(bf16[1024,640]{1,0:T(8,128)(2,1)} %bitcast.17, bf16[640,1024]{0,1:T(8,128)(2,1)} %all-gather.5.cloned.1.call-done), kind=kOutput, calls=%fused_computation.17 | convolution fusion | flops 1343225856 | bytes 4718592 | tf_op jit(solution)/shard_map/dot_general | solution.py:111
  82.8 17.0 %all-to-all-start.3 = ((bf16[32,32,1024]{2,1,0:T(8,128)(2,1)}), bf16[32,32,1024]{2,1,0:T(8,128)(2,1)}, u32[]{:S(2)}, u32[]{:S(2)}) async-start(bf16[32,32,1024]{2,1,0:T(8,128)(2,1)} %bitcast.116), calls=%async_computation.3 | async-start | bytes 4194304 | tf_op jit(solution)/shard_map/all_to_all | solution.py:112
  99.8 1.9 multiply_convert_fusion
  102.0 0.1 copy.58
  102.1 0.1 reshape.497
  102.3 2.2 gather_fusion.1
  104.5 4.4 %bitcast_select_fusion = bf16[64,128,128]{2,1,0:T(8,128)(2,1)} fusion(pred[64,128]{1,0:T(8,128)(4,1)S(1)} %copy.58, bf16[64,128,128]{2,1,0:T(8,128)(2,1)} %bitcast.114), kind=kLoop, calls=%fused_computation.11 | loop fusion | flops 1048576 | bytes 4202496 | tf_op jit(solution)/shard_map/jit(_take)/select_n | solution.py:97
  108.9 18.8 %all-to-all-done.3 = bf16[32,32,1024]{2,1,0:T(8,128)(2,1)} async-done(((bf16[32,32,1024]{2,1,0:T(8,128)(2,1)}), bf16[32,32,1024]{2,1,0:T(8,128)(2,1)}, u32[]{:S(2)}, u32[]{:S(2)}) %all-to-all-start.3) | async-done | bytes 2097184 | tf_op jit(solution)/shard_map/all_to_all | solution.py:112
  127.7 10.9 %all-to-all-start.1 = ((bf16[64,128,128]{2,1,0:T(8,128)(2,1)}), bf16[64,128,128]{2,1,0:T(8,128)(2,1)}, u32[]{:S(2)}, u32[]{:S(2)}) async-start(bf16[64,128,128]{2,1,0:T(8,128)(2,1)} %bitcast_select_fusion), calls=%async_computation.1 | async-start | bytes 4194304 | tf_op jit(solution)/shard_map/all_to_all | solution.py:98
  138.7 0.7 all-gather.7.cloned.1.call-update
  139.4 0.2 all-gather.11.cloned.1.call-start
  139.8 0.2 select_reduce_fusion
  140.1 0.1 lt.94
  140.2 2.0 convert_reduce_fusion
  142.3 0.2 multiply_reduce_fusion.2
  142.5 28.9 %all-gather.7.cloned.1.call-done = bf16[4096,128]{1,0:T(8,128)(2,1)} async-done(((bf16[512,128]{1,0:T(8,128)(2,1)}), bf16[4096,128]{1,0:T(8,128)(2,1)}) %all-gather.7.cloned.1.call-update) | async-done | bytes 1048592 | tf_op jit(solution)/shard_map/all_gather | solution.py:121
  171.4 1.7 multiply_reduce_fusion.5
  173.1 60.4 %all-to-all-done.1 = bf16[64,128,128]{2,1,0:T(8,128)(2,1)} async-done(((bf16[64,128,128]{2,1,0:T(8,128)(2,1)}), bf16[64,128,128]{2,1,0:T(8,128)(2,1)}, u32[]{:S(2)}, u32[]{:S(2)}) %all-to-all-start.1) | async-done | bytes 2097184 | tf_op jit(solution)/shard_map/all_to_all | solution.py:98
  233.6 3.1 fusion.53
  236.7 0.6 fusion.51
  237.3 1.2 fusion.48
  238.5 0.1 multiply_convert_fusion.1
  238.6 1.6 copy.63
  240.2 2.1 reshape.500
  242.3 2.2 multiply_reduce_fusion.4
  244.5 0.2 multiply_reduce_fusion.3
  244.7 0.6 multiply_reduce_fusion.1
  245.3 1.0 subtract_convert_fusion
  246.3 0.5 all-gather.9.cloned.1.call-update
  247.0 0.1 copy.66
  247.1 0.1 copy.64
  247.2 0.1 copy.65
  247.3 0.1 copy.67
  247.5 15.9 %all_gather.17 = bf16[256,256]{1,0:T(8,128)(2,1)S(1)} all-gather(bf16[32,256]{1,0:T(8,128)(2,1)S(1)} %concatenate.24), channel_id=1, replica_groups=mesh['y'=4,'z'=16,'x'=4,'c'=2] {'x','c'}, dimensions={0}, use_global_device_ids=true | all-gather | bytes 147456 | tf_op jit(solution)/shard_map/all_gather | solution.py:164
  263.4 11.2 %all-gather.11.cloned.1.call-done = bf16[256,4096]{1,0:T(8,128)(2,1)} async-done(((bf16[32,4096]{1,0:T(8,128)(2,1)}), bf16[256,4096]{1,0:T(8,128)(2,1)}) %all-gather.11.cloned.1.call-update) | async-done | bytes 2097168 | tf_op jit(solution)/shard_map/all_gather | solution.py:123
  274.6 3.2 fusion.3
  278.0 0.8 maximum_maximum_fusion
  278.8 15.4 %all-to-all-start.4 = ((bf16[64,16,128]{2,1,0:T(8,128)(2,1)}), bf16[64,16,128]{2,1,0:T(8,128)(2,1)S(1)}, u32[]{:S(2)}, u32[]{:S(2)}) async-start(bf16[64,16,128]{2,1,0:T(8,128)(2,1)} %maximum_maximum_fusion), calls=%async_computation.4 | async-start | bytes 524288 | tf_op jit(solution)/shard_map/all_to_all | solution.py:195
  294.2 0.7 dynamic_slice.7
  294.9 0.8 fusion.30
  295.7 18.3 %all-to-all-done.4 = bf16[64,16,128]{2,1,0:T(8,128)(2,1)S(1)} async-done(((bf16[64,16,128]{2,1,0:T(8,128)(2,1)}), bf16[64,16,128]{2,1,0:T(8,128)(2,1)S(1)}, u32[]{:S(2)}, u32[]{:S(2)}) %all-to-all-start.4) | async-done | bytes 262176 | tf_op jit(solution)/shard_map/all_to_all | solution.py:195
  314.5 0.7 broadcast_in_dim.171
  315.2 7.2 %all-to-all-start.5 = ((bf16[64,16,128]{2,1,0:T(8,128)(2,1)}), bf16[64,16,128]{2,1,0:T(8,128)(2,1)S(1)}, u32[]{:S(2)}, u32[]{:S(2)}) async-start(bf16[64,16,128]{2,1,0:T(8,128)(2,1)} %broadcast_in_dim.171), calls=%async_computation.5 | async-start | bytes 524288 | tf_op jit(solution)/shard_map/all_to_all | solution.py:202
  322.4 1.4 select_reduce_fusion.1
  323.7 23.0 %all-gather.9.cloned.1.call-done = bf16[640,4096]{0,1:T(8,128)(2,1)} async-done(((bf16[640,1024]{0,1:T(8,128)(2,1)}), bf16[640,4096]{0,1:T(8,128)(2,1)}) %all-gather.9.cloned.1.call-update) | async-done | bytes 5242896 | tf_op jit(solution)/shard_map/all_gather | solution.py:122
  346.7 5.9 %convolution_multiply_fusion.1 = f32[256,640]{1,0:T(8,128)} fusion(bf16[256,4096]{1,0:T(8,128)(2,1)} %all-gather.11.cloned.1.call-done, bf16[640,4096]{0,1:T(8,128)(2,1)} %all-gather.9.cloned.1.call-done, f32[256]{0:T(256)} %get-tuple-element.10), kind=kOutput, calls=%fused_computation.21 | convolution fusion | flops 1342341120 | bytes 7996416 | tf_op jit(solution)/shard_map/dot_general | solution.py:219
  352.7 5.8 %fusion.16 = bf16[256,640]{1,0:T(8,128)(2,1)} fusion(f32[256,640]{1,0:T(8,128)} %convolution_multiply_fusion.1, bf16[640,4096]{0,1:T(8,128)(2,1)} %all-gather.9.cloned.1.call-done, bf16[4096,128]{1,0:T(8,128)(2,1)S(1)} %copy-done.2, f32[4096]{0:T(1024)S(1)} %copy-done.6, f32[256]{0:T(256)} %get-tuple-element.9, bf16[256,256]{1,0:T(8,128)(2,1)S(1)} %all_gather.17), kind=kOutput, calls=%fused_computation.24 | convolution fusion | flops 715177984 | bytes 7357440 | tf_op jit(solution)/shard_map/dot_general | solution.py:224
  358.6 0.7 reshape.506
  359.3 1.5 fusion.22
  (84 shorter events, 2.3 us)
Async XLA Ops:
  7.2 17.0 %copy-start = (bf16[8192,128]{1,0:T(8,128)(2,1)S(1)}, bf16[8192,128]{1,0:T(8,128)(2,1)}, u32[]{:S(2)}) copy-start(bf16[8192,128]{1,0:T(8,128)(2,1)} %param.20) | copy-start | bytes 6291460
  7.2 70.8 %all-gather.5.cloned.1.call-start = ((), (), s32[]{:S(2)}) async-start(), calls=%async_computation.6 | async-start | bytes 1392640 | tf_op jit(solution)/shard_map/all_gather | solution.py:90
  7.9 7.3 %copy-start.9 = (s32[1,64]{1,0:T(1,128)S(1)}, s32[1,64]{1,0:T(1,128)}, u32[]{:S(2)}) copy-start(s32[1,64]{1,0:T(1,128)} %param.16) | copy-start | bytes 772
  7.9 7.5 %copy-start.5 = (s32[64,64]{1,0:T(8,128)S(1)}, s32[64,64]{1,0:T(8,128)}, u32[]{:S(2)}) copy-start(s32[64,64]{1,0:T(8,128)} %param.18) | copy-start | bytes 49156
  7.9 7.7 %copy-start.4 = (s32[64,1024]{1,0:T(8,128)S(1)}, s32[64,1024]{1,0:T(8,128)}, u32[]{:S(2)}) copy-start(s32[64,1024]{1,0:T(8,128)} %param.19) | copy-start | bytes 786436
  7.9 7.8 %copy-start.7 = (f32[4]{0:T(128)S(1)}, f32[4]{0:T(128)}, u32[]{:S(2)}) copy-start(f32[4]{0:T(128)} %param.21) | copy-start | bytes 52
  8.0 8.7 %copy-start.8 = (s32[64]{0:T(128)S(1)}, s32[64]{0:T(128)}, u32[]{:S(2)}) copy-start(s32[64]{0:T(128)} %param.17) | copy-start | bytes 772
  10.2 30.9 %all-to-all-start.2 = ((bf16[4,256,640]{2,1,0:T(8,128)(2,1)}), bf16[4,256,640]{2,1,0:T(8,128)(2,1)}, u32[]{:S(2)}, u32[]{:S(2)}) async-start(bf16[4,256,640]{2,1,0:T(8,128)(2,1)} %broadcast_in_dim.160), calls=%async_computation.2 | async-start | bytes 2621440 | tf_op jit(solution)/shard_map/all_to_all | solution.py:91
  15.4 124.3 %copy-start.10 = (s32[64]{0:T(128)}, s32[64]{0:T(128)S(1)}, u32[]{:S(2)}) copy-start(s32[64]{0:T(128)S(1)} %fusion.47) | copy-start | bytes 772
  41.1 41.7 %all-to-all-start = ((s32[64,1,128]{2,1,0:T(1,128)}), s32[64,1,128]{2,1,0:T(1,128)S(1)}, u32[]{:S(2)}, u32[]{:S(2)}) async-start(s32[64,1,128]{2,1,0:T(1,128)} %bitcast.5), calls=%async_computation | async-start | bytes 65536 | tf_op jit(solution)/shard_map/all_to_all | solution.py:88
  82.8 44.9 %all-to-all-start.3 = ((bf16[32,32,1024]{2,1,0:T(8,128)(2,1)}), bf16[32,32,1024]{2,1,0:T(8,128)(2,1)}, u32[]{:S(2)}, u32[]{:S(2)}) async-start(bf16[32,32,1024]{2,1,0:T(8,128)(2,1)} %bitcast.116), calls=%async_computation.3 | async-start | bytes 4194304 | tf_op jit(solution)/shard_map/all_to_all | solution.py:112
  127.7 105.9 %all-to-all-start.1 = ((bf16[64,128,128]{2,1,0:T(8,128)(2,1)}), bf16[64,128,128]{2,1,0:T(8,128)(2,1)}, u32[]{:S(2)}, u32[]{:S(2)}) async-start(bf16[64,128,128]{2,1,0:T(8,128)(2,1)} %bitcast_select_fusion), calls=%async_computation.1 | async-start | bytes 4194304 | tf_op jit(solution)/shard_map/all_to_all | solution.py:98
  138.6 3.7 %copy-start.3 = (bf16[32,4096]{1,0:T(8,128)(2,1)S(1)}, bf16[32,4096]{1,0:T(8,128)(2,1)}, u32[]{:S(2)}) copy-start(bf16[32,4096]{1,0:T(8,128)(2,1)} %param.11) | copy-start | bytes 786436
  138.6 32.8 %all-gather.7.cloned.1.call-start = ((), (), s32[]{:S(2)}) async-start(), calls=%async_computation.7 | async-start | bytes 1179648 | tf_op jit(solution)/shard_map/all_gather | solution.py:121
  139.4 135.2 %all-gather.11.cloned.1.call-start = ((), (), s32[]{:S(2)}) async-start(), calls=%async_computation.9 | async-start | bytes 2359296 | tf_op jit(solution)/shard_map/all_gather | solution.py:123
  140.2 31.2 %copy-start.6 = (f32[4096]{0:T(1024)S(1)}, f32[4096]{0:T(1024)}, u32[]{:S(2)}) copy-start(f32[4096]{0:T(1024)} %param.14) | copy-start | bytes 49156
  242.3 2.4 copy-start.1
  246.3 100.4 %all-gather.9.cloned.1.call-start = ((), (), s32[]{:S(2)}) async-start(), calls=%async_computation.8 | async-start | bytes 6553600 | tf_op jit(solution)/shard_map/all_gather | solution.py:122
  278.8 35.2 %all-to-all-start.4 = ((bf16[64,16,128]{2,1,0:T(8,128)(2,1)}), bf16[64,16,128]{2,1,0:T(8,128)(2,1)S(1)}, u32[]{:S(2)}, u32[]{:S(2)}) async-start(bf16[64,16,128]{2,1,0:T(8,128)(2,1)} %maximum_maximum_fusion), calls=%async_computation.4 | async-start | bytes 524288 | tf_op jit(solution)/shard_map/all_to_all | solution.py:195
  315.2 43.3 %all-to-all-start.5 = ((bf16[64,16,128]{2,1,0:T(8,128)(2,1)}), bf16[64,16,128]{2,1,0:T(8,128)(2,1)S(1)}, u32[]{:S(2)}, u32[]{:S(2)}) async-start(bf16[64,16,128]{2,1,0:T(8,128)(2,1)} %broadcast_in_dim.171), calls=%async_computation.5 | async-start | bytes 524288 | tf_op jit(solution)/shard_map/all_to_all | solution.py:202
  346.7 5.9 %copy-start.2 = (bf16[4096,128]{1,0:T(8,128)(2,1)S(1)}, bf16[4096,128]{1,0:T(8,128)(2,1)}, u32[]{:S(2)}) copy-start(bf16[4096,128]{1,0:T(8,128)(2,1)} %all-gather.7.cloned.1.call-done) | copy-start | bytes 3145732
Sparse Core Ops, SparseCore 0:
  10.1 67.7 all-gather.4
  141.6 29.7 all-gather.6
  246.4 28.1 all-gather.10
  276.6 70.1 all-gather.8

commit v2 on v1

--- a/solution.py
+++ b/solution.py
@@ -39,6 +39,15 @@
     vectors = jnp.take(centroids, cell_ids.reshape(rows), axis=0).astype(F32) + levels
     scale = lax.rsqrt(jnp.sum(vectors * vectors, axis=-1, keepdims=True) + EPS)
     return (vectors * scale).astype(BF16)
+
+
+def swap(values, axis, size, step):
+    return lax.ppermute(values, axis, [(i, i ^ step) for i in range(size)])
+
+
+def unxor(blocks, place):
+    order = jnp.arange(blocks.shape[0], dtype=jnp.int32) ^ place
+    return jnp.take(blocks, order, axis=0)
 
 
 def halves(values):
@@ -88,13 +97,10 @@
     notes = lax.all_to_all(note, DP, 0, 0, tiled=True)
 
     proj_z = lax.all_gather(out_proj, "z", axis=1, tiled=True)
-    context_y = lax.all_to_all(
-        jnp.broadcast_to(context[None], (Y,) + context.shape), "y", 0, 0, tiled=True
-    ).reshape(Y * context.shape[0], context.shape[1])
-
     documents = decode_all(centroid_ids, residual_codes, centroids, buckets)
     wanted = notes[:, per_shard : per_shard + cap].reshape(slots)
     chosen = jnp.take(documents.reshape(per_shard, doc_len, feature_dim), wanted, axis=0)
+    chosen, context, colbert_head = lax.optimization_barrier((chosen, context, colbert_head))
     got_docs = lax.all_to_all(
         chosen.reshape(shards, cap * doc_len, feature_dim), DP, 0, 0, tiled=True
     ).reshape(slots * doc_len, feature_dim)
@@ -108,23 +114,47 @@
         axis=2,
     ).reshape(slots)
 
-    terms = jnp.dot(context_y, proj_z, preferred_element_type=F32).astype(BF16)
-    parts = lax.all_to_all(terms, PLANE, 0, 0, tiled=True)
-    parts = parts.reshape(Y, X * C, seq_rows, width // Y).astype(F32)
-    attended = jnp.sum(parts, axis=1).transpose(1, 0, 2).reshape(seq_rows, width)
+    here_x, here_c, here_y = lax.axis_index("x"), lax.axis_index("c"), lax.axis_index("y")
+    blocks = context.reshape(X, C, seq_rows, context.shape[1])
+    blocks = jnp.where(here_c == 0, blocks, blocks[:, ::-1])
+    blocks = unxor(blocks, here_x).transpose(1, 0, 2, 3)
+    by_y = jnp.stack([blocks] + [swap(blocks, "y", Y, step) for step in range(1, Y)], axis=2)
+    by_y = by_y.reshape(C, X * Y * seq_rows, context.shape[1])
+
+    head_pair = swap(colbert_head, "c", C, 1)
+    head_pair = jnp.where(
+        here_c == 0,
+        jnp.stack([colbert_head, head_pair]),
+        jnp.stack([head_pair, colbert_head]),
+    )
+    head_full = unxor(
+        jnp.stack([head_pair] + [swap(head_pair, "x", X, step) for step in range(1, X)]), here_x
+    ).reshape(width, feature_dim)
+
+    by_y, head_full = lax.optimization_barrier((by_y, head_full))
+
+    away = jnp.dot(by_y[1], proj_z, preferred_element_type=F32).astype(BF16)
+    away = swap(away, "c", C, 1)
+    stay = jnp.dot(by_y[0], proj_z, preferred_element_type=F32).astype(BF16)
+    pair = (stay.astype(F32) + away.astype(F32)).reshape(X, Y, seq_rows, width // Y)
+    for_x = pair.astype(BF16)
+    row = pair[0]
+    for step in range(1, X):
+        row = row + swap(for_x[step], "x", X, step).astype(F32)
+    for_y = row.astype(BF16)
+    columns = [for_y[0]] + [swap(for_y[step], "y", Y, step) for step in range(1, Y)]
+    columns = unxor(jnp.stack(columns), here_y)
+    attended = columns.transpose(1, 0, 2).reshape(seq_rows, width).astype(F32)
     summed = residual.astype(F32) + attended
     inv_rms = lax.rsqrt(jnp.mean(summed * summed, axis=-1, keepdims=True) + EPS)
     scaled_sum = summed * inv_rms
     normed = (scaled_sum * norm_gain).astype(BF16)
-
-    proj_z_later, head_blk = lax.optimization_barrier((proj_z, colbert_head))
-    head_full = lax.all_gather(head_blk, TENSOR, axis=0, tiled=True)
-    proj_full = lax.all_gather(proj_z_later, "y", axis=1, tiled=True)
+    proj_full = lax.all_gather(proj_z, "y", axis=1, tiled=True)
     unit_all = lax.all_gather(scaled_sum.astype(BF16), TENSOR, axis=0, tiled=True)
-
     embedded = jnp.dot(normed, head_full, preferred_element_type=F32)
     inverse = lax.rsqrt(jnp.sum(embedded * embedded, axis=-1, keepdims=True) + EPS)
     queries = (embedded * inverse).astype(BF16)
+    got_docs, unit_all = lax.optimization_barrier((got_docs, unit_all))
 
     similar = lax.dot_general(
         got_docs, queries, (((1,), (1,)), ((), ())), preferred_element_type=F32
@@ -161,7 +191,9 @@
         ],
         axis=1,
     )
-    packets = lax.all_gather(packet, TENSOR, axis=0, tiled=True)
+    packets = lax.all_to_all(
+        jnp.broadcast_to(packet, (X * C,) + packet.shape), TENSOR, 0, 0, tiled=True
+    ).reshape(X * C * seq_rows, 2 * feature_dim)
     ge_all = packets[:, :feature_dim]
     extra = packets[:, feature_dim : feature_dim + 4].astype(F32)
     pull_all = extra[:, 0:1] + extra[:, 1:2]
@@ -189,20 +221,22 @@
 
     def unbundle(rows):
         rows = rows.astype(F32)
-        pair = rows[:, share]
-        return rows[:, :share], pair[:, : width // shards] + pair[:, width // shards :]
-
-    first = lax.all_to_all(
-        bundle(head_term.reshape(shards, share, feature_dim), gain_term), DP, 0, 0, tiled=True
-    )
-    head_got, gain_got = unbundle(first)
-    second = bundle(
-        jnp.sum(head_got, axis=0, keepdims=True), jnp.sum(gain_got, axis=0, keepdims=True)
-    )
-    second = lax.all_to_all(
-        jnp.broadcast_to(second, (shards,) + second.shape[1:]), DP, 0, 0, tiled=True
-    )
-    head_got, gain_got = unbundle(second)
+        pair = rows[..., share, :]
+        return rows[..., :share, :], pair[..., : width // shards] + pair[..., width // shards :]
+
+    rows = bundle(head_term.reshape(shards, share, feature_dim), gain_term)
+    rows = lax.all_to_all(rows, "y", 0, 0, tiled=True)
+    rows = unbundle(rows.reshape(Y, Z, 2 * share, feature_dim))
+    rows = bundle(*[jnp.sum(part, axis=0) for part in rows])
+    rows = unbundle(lax.all_to_all(rows, "z", 0, 0, tiled=True))
+    rows = bundle(*[jnp.sum(part, axis=0, keepdims=True) for part in rows])
+    rows = lax.all_to_all(
+        jnp.broadcast_to(rows, (Z,) + rows.shape[1:]), "z", 0, 0, tiled=True
+    )
+    rows = lax.all_to_all(
+        jnp.broadcast_to(rows[None], (Y,) + rows.shape), "y", 0, 0, tiled=True
+    )
+    head_got, gain_got = unbundle(rows.reshape(shards, 2 * share, feature_dim))
     gain_blk = lax.dynamic_slice_in_dim(norm_gain, mine, head_rows, 0)
     head_grad = head_got.reshape(head_rows, feature_dim) * gain_blk[:, None]
     gain_grad = gain_got.reshape(width)

time: 368 us -> 357 us (0.970); the launches traced: 367 us -> 351 us
  waiting for transfers between devices: 181 us -> 100 us
  starting transfers between devices: 74.4 us -> 110 us
  local copies, waits for them, and re-layouts: 27.1 us -> 47.1 us
  other arithmetic: 18.3 us -> 36.5 us
  blocking collectives: 15.9 us -> 0 us
  matrix products: 31.4 us -> 37.8 us
    all_gather x2 -> x1, waiting for transfers between devices: 51.9 us -> 0.01 us  [local(): proj_full = lax.all_gather(proj_z, 'y', axis=1, tiled=True)]
    all_to_all x1, waiting for transfers between devices: 60.4 us -> 15.3 us  [local(): lax.all_to_all(chosen.reshape(shards, cap * doc_len, feature_dim), DP, 0,...]
    ppermute x0 -> x14, starting transfers between devices: none -> 44.1 us  [swap(): return lax.ppermute(values, axis, [(i, i ^ step) for i in range(size)])]
    ppermute x0 -> x14, waiting for transfers between devices: none -> 24.4 us  [swap(): return lax.ppermute(values, axis, [(i, i ^ step) for i in range(size)])]
    all_gather x1, waiting for transfers between devices: 18.3 us -> 0.02 us  [local(): proj_z = lax.all_gather(out_proj, 'z', axis=1, tiled=True)]
    all_gather x1, waiting for transfers between devices: 11.2 us -> 28.6 us  [local(): lax.all_gather(scaled_sum.astype(BF16), TENSOR, axis=0, tiled=True)]
    all_gather x1 -> x0, blocking collectives: 15.9 us -> none  [local(): packets = lax.all_gather(packet, TENSOR, axis=0, tiled=True)]
    all_to_all x4 -> x5, starting transfers between devices: 44.6 us -> 31.4 us  [the longest x1 10.3 us: local(): rows = unbundle(lax.all_to_all(rows, 'z', 0, 0, tiled=True))]
  transfers between devices with their start and end apart: 10 -> 24, of which waited for: 7 -> 14; matrix products, arithmetic and copies ran while one was open for 17% -> 29% of each run, Pallas kernels for 0% -> 0%
where the time goes in v2:
time: 357 us; the launch traced here: 351 us
  starting transfers between devices  110 us (31%)
  waiting for transfers between devices  100 us (28%)
  local copies, waits for them, and re-layouts  47.1 us (13%)
  matrix products  37.8 us (11%)
  other arithmetic  36.5 us (10%)
  between operations  19.6 us (5%)
    ppermute x14, starting transfers between devices, swap(): return lax.ppermute(values, axis, [(i, i ^ step) for i in range(size)])  44.1 us
    all_gather x1, waiting for transfers between devices, local(): lax.all_gather(scaled_sum.astype(BF16), TENSOR, axis=0, tiled=True)  28.6 us
    ppermute x14, waiting for transfers between devices, swap(): return lax.ppermute(values, axis, [(i, i ^ step) for i in range(size)])  24.4 us
    all_to_all x1, starting transfers between devices, local(): notes = lax.all_to_all(note, DP, 0, 0, tiled=True)  19.3 us
    all_to_all x1, waiting for transfers between devices, local(): lax.all_to_all(chosen.reshape(shards, cap * doc_len, feature_dim), DP, 0,...  15.3 us
    all_to_all x1, starting transfers between devices, local(): lax.all_to_all(chosen.reshape(shards, cap * doc_len, feature_dim), DP, 0,...  14.9 us
    gather x1, local copies, waits for them, and re-layouts, decode_all(): jnp.take(centroids, cell_ids.reshape(rows), axis=0).astype(F32) + levels  12.1 us
    all_to_all x1, starting transfers between devices, local(): rows = unbundle(lax.all_to_all(rows, 'z', 0, 0, tiled=True))  10.3 us
  transfers between devices with their start and end apart: 24, of which 14 were waited for; matrix products, arithmetic and copies ran while one was open for 29% of the time, Pallas kernels for 0%

profile of v2, /device:TPU:1, one launch (start us, length us, event | category | flops | bytes accessed | tf_op | source)
XLA Modules:
  0.0 351.2 jit_solution(12670395035446790083)
XLA Ops:
  11.1 19.3 %all-to-all-start = ((s32[64,1,128]{2,1,0:T(1,128)}), s32[64,1,128]{2,1,0:T(1,128)S(1)}, u32[]{:S(2)}, u32[]{:S(2)}) async-start(s32[64,1,128]{2,1,0:T(1,128)} %bitcast.5), calls=%async_computation | async-start | bytes 65536 | tf_op jit(solution)/shard_map/all_to_all | solution.py:97
  32.8 1.4 fusion.55
  42.8 12.1 %gather_fusion = bf16[4096,128]{1,0:T(8,128)(2,1)S(1)} fusion(bf16[8192,128]{1,0:T(8,128)(2,1)S(1)} %copy-done, s32[4096]{0:T(1024)S(1)} %broadcast_clamp_fusion), kind=kCustom, calls=%fused_computation | custom fusion | bytes 2113536 | tf_op jit(solution)/shard_map/jit(_take)/gather | solution.py:39
  54.9 4.0 %multiply_reduce_fusion = (f32[4096]{0:T(1024)S(1)}, f32[4096,128]{1,0:T(8,128)}) fusion(f32[]{:T(128)S(6)} %add.248, f32[]{:T(128)S(6)} %sub.95, f32[]{:T(128)S(6)} %sub.94, s32[128]{0:T(128)S(1)} %get-tuple-element.66, s32[128]{0:T(128)S(1)} %get-tuple-element.65, bf16[4096,16]{0,1:T(8,128)(2,1)S(1)} %copy.77, bf16[4096,16]{0,1:T(8,128)(2,1)S(1)} %copy.76, ...), kind=kOutput, calls=%fused_computation.18 | convolution fusion | flops 44040192 | bytes 3429392 | tf_op jit(solution)/shard_map/dot_general | solution.py:29
  59.0 1.9 multiply_convert_fusion
  61.4 2.1 gather_fusion.1
  63.5 3.2 broadcast_select_fusion
  67.6 2.9 collective-permute-start
  70.5 3.4 collective-permute-start.3
  73.9 4.5 %collective-permute-start.1 = (bf16[2,4,32,640]{3,2,0,1:T(8,128)(2,1)S(1)}, bf16[2,4,32,640]{3,2,0,1:T(8,128)(2,1)}, u32[]{:S(2)}, u32[]{:S(2)}) collective-permute-start(bf16[2,4,32,640]{3,2,0,1:T(8,128)(2,1)S(1)} %get-tuple-element.35), channel_id=1, source_target_pairs={{0,256},{128,384},{256,0},{384,128},{1,257},{129,385},{257,1},{385... | collective-permute-start | bytes 983048 | tf_op jit(solution)/shard_map/ppermute | solution.py:45
  78.4 1.9 collective-permute-start.2
  80.5 3.1 collective-permute-start.4
  83.7 4.4 %collective-permute-start.5 = (bf16[2,512,128]{2,1,0:T(8,128)(2,1)S(1)}, bf16[2,512,128]{2,1,0:T(8,128)(2,1)S(1)}, u32[]{:S(2)}, u32[]{:S(2)}) collective-permute-start(bf16[2,512,128]{2,1,0:T(8,128)(2,1)S(1)} %maximum_select_fusion.1), channel_id=1, source_target_pairs={{0,4},{2,6},{4,0},{6,2},{1,5},{3,7},{5,1},{7,3},{8,12},{10,14},{12... | collective-permute-start | bytes 786440 | tf_op jit(solution)/shard_map/ppermute | solution.py:45
  88.0 2.1 collective-permute-start.6
  90.2 5.2 %collective-permute-done.2 = bf16[2,4,32,640]{3,2,0,1:T(8,128)(2,1)} collective-permute-done((bf16[2,4,32,640]{3,2,0,1:T(8,128)(2,1)S(1)}, bf16[2,4,32,640]{3,2,0,1:T(8,128)(2,1)}, u32[]{:S(2)}, u32[]{:S(2)}) %collective-permute-start.2) | collective-permute-done | bytes 327712 | tf_op jit(solution)/shard_map/ppermute | solution.py:45
  95.4 1.3 pad_maximum_fusion
  96.7 1.2 copy.78
  97.9 6.1 %collective-permute-done.6 = bf16[2,512,128]{2,1,0:T(8,128)(2,1)S(1)} collective-permute-done((bf16[2,512,128]{2,1,0:T(8,128)(2,1)S(1)}, bf16[2,512,128]{2,1,0:T(8,128)(2,1)S(1)}, u32[]{:S(2)}, u32[]{:S(2)}) %collective-permute-start.6) | collective-permute-done | bytes 262176 | tf_op jit(solution)/shard_map/ppermute | solution.py:45
  104.1 1.7 gather_fusion.3
  105.8 3.4 bitcast_select_fusion
  109.2 3.5 %convolution_convert_fusion.1 = bf16[512,1024]{1,0:T(8,128)(2,1)} fusion(bf16[640,1024]{0,1:T(8,128)(2,1)} %all-gather.4.cloned.1.call-done, bf16[2,512,640]{2,1,0:T(8,128)(2,1)} %bitcast.159), kind=kOutput, calls=%fused_computation.21 | convolution fusion | flops 671612928 | bytes 3014656 | tf_op jit(solution)/shard_map/dot_general | solution.py:136
  112.7 2.4 collective-permute-start.7
  115.2 14.9 %all-to-all-start.1 = ((bf16[64,128,128]{2,1,0:T(8,128)(2,1)}), bf16[64,128,128]{2,1,0:T(8,128)(2,1)}, u32[]{:S(2)}, u32[]{:S(2)}) async-start(bf16[64,128,128]{2,1,0:T(8,128)(2,1)} %bitcast.158), calls=%async_computation.1 | async-start | bytes 4194304 | tf_op jit(solution)/shard_map/all_to_all | solution.py:104
  130.1 4.2 %fusion.56 = (bf16[512,1024]{1,0:T(8,128)(2,1)S(1)}, f32[512,1024]{1,0:T(8,128)}) fusion(bf16[512,1024]{1,0:T(8,128)(2,1)} %collective-permute-done.7, bf16[640,1024]{0,1:T(8,128)(2,1)} %all-gather.4.cloned.1.call-done, bf16[2,512,640]{2,1,0:T(8,128)(2,1)} %bitcast.160), kind=kOutput, calls=%fused_computation.188 | convolution fusion | flops 673710080 | bytes 6160384 | tf_op jit(solution)/shard_map/dot_general | solution.py:138
  135.1 2.1 collective-permute-start.10
  137.2 1.9 collective-permute-start.8
  139.1 5.6 %collective-permute-start.9 = (bf16[4,32,1024]{2,1,0:T(8,128)(2,1)S(1)}, bf16[4,32,1024]{2,1,0:T(8,128)(2,1)}, u32[]{:S(2)}, u32[]{:S(2)}) collective-permute-start(bf16[4,32,1024]{2,1,0:T(8,128)(2,1)S(1)} %bitcast.175), channel_id=1, source_target_pairs={{0,4},{2,6},{4,0},{6,2},{1,5},{3,7},{5,1},{7,3},{8,12},{10,14},{12... | collective-permute-start | bytes 786440 | tf_op jit(solution)/shard_map/ppermute | solution.py:45
  146.7 7.8 %collective-permute-done.9 = bf16[4,32,1024]{2,1,0:T(8,128)(2,1)} collective-permute-done((bf16[4,32,1024]{2,1,0:T(8,128)(2,1)S(1)}, bf16[4,32,1024]{2,1,0:T(8,128)(2,1)}, u32[]{:S(2)}, u32[]{:S(2)}) %collective-permute-start.9) | collective-permute-done | bytes 262176 | tf_op jit(solution)/shard_map/ppermute | solution.py:45
  154.5 1.3 add_convert_fusion
  155.8 2.7 collective-permute-start.11
  158.5 4.5 %collective-permute-start.12 = (bf16[32,1024]{1,0:T(8,128)(2,1)S(1)}, bf16[32,1024]{1,0:T(8,128)(2,1)S(1)}, u32[]{:S(2)}, u32[]{:S(2)}) collective-permute-start(bf16[32,1024]{1,0:T(8,128)(2,1)S(1)} %get-tuple-element.38), channel_id=1, source_target_pairs={{0,256},{128,384},{256,0},{384,128},{1,257},{129,385},{257,1},{385... | collective-permute-start | bytes 196616 | tf_op jit(solution)/shard_map/ppermute | solution.py:45
  163.0 2.6 collective-permute-start.13
  166.4 3.5 collective-permute-done.13
  170.6 2.2 gather_fusion.4
  176.9 1.5 multiply_reduce_fusion.5
  178.4 28.6 %all-gather.6.cloned.1.call-done = bf16[256,4096]{1,0:T(8,128)(2,1)} async-done(((bf16[32,4096]{1,0:T(8,128)(2,1)}), bf16[256,4096]{1,0:T(8,128)(2,1)}) %all-gather.6.cloned.1.call-update) | async-done | bytes 2097168 | tf_op jit(solution)/shard_map/all_gather | solution.py:153
  207.0 15.3 %all-to-all-done.1 = bf16[64,128,128]{2,1,0:T(8,128)(2,1)} async-done(((bf16[64,128,128]{2,1,0:T(8,128)(2,1)}), bf16[64,128,128]{2,1,0:T(8,128)(2,1)}, u32[]{:S(2)}, u32[]{:S(2)}) %all-to-all-start.1) | async-done | bytes 2097184 | tf_op jit(solution)/shard_map/all_to_all | solution.py:104
  222.3 3.5 fusion
  225.8 3.2 exp.15
  229.0 2.4 select_reduce_fusion
  233.2 1.9 mul.297
  235.1 2.9 mul.298
  238.0 2.8 multiply_reduce_fusion.4
  242.2 9.5 %all-to-all-start.2 = ((bf16[8,32,256]{2,1,0:T(8,128)(2,1)}), bf16[8,32,256]{2,1,0:T(8,128)(2,1)S(1)}, u32[]{:S(2)}, u32[]{:S(2)}) async-start(bf16[8,32,256]{2,1,0:T(8,128)(2,1)} %broadcast_in_dim.212), calls=%async_computation.2 | async-start | bytes 262144 | tf_op jit(solution)/shard_map/all_to_all | solution.py:194
  252.3 4.7 %all-to-all-done.2 = bf16[8,32,256]{2,1,0:T(8,128)(2,1)S(1)} async-done(((bf16[8,32,256]{2,1,0:T(8,128)(2,1)}), bf16[8,32,256]{2,1,0:T(8,128)(2,1)S(1)}, u32[]{:S(2)}, u32[]{:S(2)}) %all-to-all-start.2) | async-done | bytes 131104 | tf_op jit(solution)/shard_map/all_to_all | solution.py:194
  257.0 4.5 %fusion.4 = (f32[4096]{0:T(1024)}, bf16[4096,128]{1,0:T(8,128)(2,1)}) fusion(bf16[4096,128]{1,0:T(8,128)(2,1)S(1)} %bitcast_select_fusion, bf16[256,4096]{1,0:T(8,128)(2,1)} %all-gather.6.cloned.1.call-done, bf16[256,256]{1,0:T(8,128)(2,1)S(1)} %bitcast.162), kind=kOutput, calls=%fused_computation.14 | convolution fusion | flops 270528512 | bytes 4276224 | tf_op jit(solution)/shard_map/dot_general | solution.py:202
  261.5 1.4 reshape.632
  264.8 1.4 maximum_maximum_fusion
  266.3 4.1 %all-to-all-start.3 = ((bf16[64,16,128]{2,1,0:T(8,128)(2,1)}), bf16[64,16,128]{2,1,0:T(8,128)(2,1)}, u32[]{:S(2)}, u32[]{:S(2)}) async-start(bf16[64,16,128]{2,1,0:T(8,128)(2,1)} %maximum_maximum_fusion), calls=%async_computation.3 | async-start | bytes 524288 | tf_op jit(solution)/shard_map/all_to_all | solution.py:228
  271.0 5.0 %all-to-all-done.3 = bf16[64,16,128]{2,1,0:T(8,128)(2,1)} async-done(((bf16[64,16,128]{2,1,0:T(8,128)(2,1)}), bf16[64,16,128]{2,1,0:T(8,128)(2,1)}, u32[]{:S(2)}, u32[]{:S(2)}) %all-to-all-start.3) | async-done | bytes 262176 | tf_op jit(solution)/shard_map/all_to_all | solution.py:228
  277.2 1.3 maximum_maximum_fusion.1
  278.5 10.3 %all-to-all-start.4 = ((bf16[16,16,128]{2,1,0:T(8,128)(2,1)}), bf16[16,16,128]{2,1,0:T(8,128)(2,1)}, u32[]{:S(2)}, u32[]{:S(2)}) async-start(bf16[16,16,128]{2,1,0:T(8,128)(2,1)} %maximum_maximum_fusion.1), calls=%async_computation.4 | async-start | bytes 131072 | tf_op jit(solution)/shard_map/all_to_all | solution.py:231
  288.9 2.5 multiply_reduce_fusion.1
  291.9 8.6 %all-to-all-done.4 = bf16[16,16,128]{2,1,0:T(8,128)(2,1)} async-done(((bf16[16,16,128]{2,1,0:T(8,128)(2,1)}), bf16[16,16,128]{2,1,0:T(8,128)(2,1)}, u32[]{:S(2)}, u32[]{:S(2)}) %all-to-all-start.4) | async-done | bytes 65568 | tf_op jit(solution)/shard_map/all_to_all | solution.py:231
  303.6 4.2 %all-to-all-start.5 = ((bf16[16,16,128]{2,1,0:T(8,128)(2,1)}), bf16[16,16,128]{2,1,0:T(8,128)(2,1)}, u32[]{:S(2)}, u32[]{:S(2)}) async-start(bf16[16,16,128]{2,1,0:T(8,128)(2,1)} %broadcast_in_dim.217), calls=%async_computation.5 | async-start | bytes 131072 | tf_op jit(solution)/shard_map/all_to_all | solution.py:233
  307.8 2.1 subtract_convert_fusion
  309.9 1.3 select_reduce_fusion.2
  311.2 8.2 %all-to-all-done.5 = bf16[16,16,128]{2,1,0:T(8,128)(2,1)} async-done(((bf16[16,16,128]{2,1,0:T(8,128)(2,1)}), bf16[16,16,128]{2,1,0:T(8,128)(2,1)}, u32[]{:S(2)}, u32[]{:S(2)}) %all-to-all-start.5) | async-done | bytes 65568 | tf_op jit(solution)/shard_map/all_to_all | solution.py:233
  319.5 1.6 broadcast_in_dim.218
  321.0 3.4 all-to-all-start.6
  325.3 4.6 %all-to-all-done.6 = bf16[4,16,16,128]{3,2,1,0:T(8,128)(2,1)S(1)} async-done(((bf16[4,16,16,128]{3,2,1,0:T(8,128)(2,1)}), bf16[4,16,16,128]{3,2,1,0:T(8,128)(2,1)S(1)}, u32[]{:S(2)}, u32[]{:S(2)}) %all-to-all-start.6) | async-done | bytes 262176 | tf_op jit(solution)/shard_map/all_to_all | solution.py:236
  331.6 1.8 fusion.19
  333.4 5.8 %convolution_multiply_fusion.2 = f32[256,640]{1,0:T(8,128)} fusion(bf16[256,4096]{1,0:T(8,128)(2,1)} %all-gather.6.cloned.1.call-done, bf16[640,4096]{0,1:T(8,128)(2,1)} %all-gather.8.cloned.1.call-done, f32[256]{0:T(256)} %get-tuple-element.20), kind=kOutput, calls=%fused_computation.24 | convolution fusion | flops 1342341120 | bytes 7996416 | tf_op jit(solution)/shard_map/dot_general | solution.py:253
  339.2 5.5 %fusion.6 = bf16[256,640]{1,0:T(8,128)(2,1)} fusion(f32[256,640]{1,0:T(8,128)} %convolution_multiply_fusion.2, bf16[640,4096]{0,1:T(8,128)(2,1)} %all-gather.8.cloned.1.call-done, bf16[4096,128]{1,0:T(8,128)(2,1)S(1)} %bitcast_select_fusion, f32[4096]{0:T(1024)S(1)} %copy-done.10, f32[256]{0:T(256)S(1)} %copy-done.13, bf16[256,256]{1,0:T(8,128)(2,1)S(1)} %bitcast.164), kind=kOutput, calls=%fused_computation.27 | convolution fusion | flops 715177984 | bytes 7357440 | tf_op jit(solution)/shard_map/dot_general | solution.py:258
  (161 shorter events, 33.2 us)
Async XLA Ops:
  7.2 35.6 %copy-start = (bf16[8192,128]{1,0:T(8,128)(2,1)S(1)}, bf16[8192,128]{1,0:T(8,128)(2,1)}, u32[]{:S(2)}) copy-start(bf16[8192,128]{1,0:T(8,128)(2,1)} %param.20) | copy-start | bytes 6291460
  8.8 0.5 copy-start.17
  8.9 0.5 copy-start.15
  9.6 30.8 %copy-start.6 = (s32[64,2]{1,0:T(8,128)}, s32[64,2]{1,0:T(8,128)S(1)}, u32[]{:S(2)}) copy-start(s32[64,2]{1,0:T(8,128)S(1)} %eq.84) | copy-start | bytes 1540
  11.1 49.9 %all-to-all-start = ((s32[64,1,128]{2,1,0:T(1,128)}), s32[64,1,128]{2,1,0:T(1,128)S(1)}, u32[]{:S(2)}, u32[]{:S(2)}) async-start(s32[64,1,128]{2,1,0:T(1,128)} %bitcast.5), calls=%async_computation | async-start | bytes 65536 | tf_op jit(solution)/shard_map/all_to_all | solution.py:97
  30.4 78.8 %all-gather.4.cloned.1.call-start = ((), (), s32[]{:S(2)}) async-start(), calls=%async_computation.7 | async-start | bytes 1392640 | tf_op jit(solution)/shard_map/all_gather | solution.py:99
  61.0 2.5 copy-start.8
  63.5 3.2 copy-start.5
  66.8 3.7 %copy-start.4 = (bf16[512,128]{1,0:T(8,128)(2,1)S(1)}, bf16[512,128]{1,0:T(8,128)(2,1)}, u32[]{:S(2)}) copy-start(bf16[512,128]{1,0:T(8,128)(2,1)} %param.15) | copy-start | bytes 393220
  67.6 20.5 %collective-permute-start = (bf16[2,4,32,640]{3,2,0,1:T(8,128)(2,1)S(1)}, bf16[2,4,32,640]{3,2,0,1:T(8,128)(2,1)S(1)}, u32[]{:S(2)}, u32[]{:S(2)}) collective-permute-start(bf16[2,4,32,640]{3,2,0,1:T(8,128)(2,1)S(1)} %get-tuple-element.35), channel_id=1, source_target_pairs={{0,128},{128,0},{256,384},{384,256},{1,129},{129,1},{257,385},{385... | collective-permute-start | bytes 983048 | tf_op jit(solution)/shard_map/ppermute | solution.py:45
  70.5 10.0 %collective-permute-start.3 = (bf16[512,128]{1,0:T(8,128)(2,1)S(1)}, bf16[512,128]{1,0:T(8,128)(2,1)S(1)}, u32[]{:S(2)}, u32[]{:S(2)}) collective-permute-start(bf16[512,128]{1,0:T(8,128)(2,1)S(1)} %copy-done.4), channel_id=1, source_target_pairs={{0,1},{1,0},{2,3},{3,2},{4,5},{5,4},{6,7},{7,6},{8,9},{9,8},{10,11... | collective-permute-start | bytes 393224 | tf_op jit(solution)/shard_map/ppermute | solution.py:45
  73.9 16.2 %collective-permute-start.1 = (bf16[2,4,32,640]{3,2,0,1:T(8,128)(2,1)S(1)}, bf16[2,4,32,640]{3,2,0,1:T(8,128)(2,1)}, u32[]{:S(2)}, u32[]{:S(2)}) collective-permute-start(bf16[2,4,32,640]{3,2,0,1:T(8,128)(2,1)S(1)} %get-tuple-element.35), channel_id=1, source_target_pairs={{0,256},{128,384},{256,0},{384,128},{1,257},{129,385},{257,1},{385... | collective-permute-start | bytes 983048 | tf_op jit(solution)/shard_map/ppermute | solution.py:45
  78.4 17.0 %collective-permute-start.2 = (bf16[2,4,32,640]{3,2,0,1:T(8,128)(2,1)S(1)}, bf16[2,4,32,640]{3,2,0,1:T(8,128)(2,1)}, u32[]{:S(2)}, u32[]{:S(2)}) collective-permute-start(bf16[2,4,32,640]{3,2,0,1:T(8,128)(2,1)S(1)} %get-tuple-element.35), channel_id=1, source_target_pairs={{0,384},{128,256},{256,128},{384,0},{1,385},{129,257},{257,129},{3... | collective-permute-start | bytes 983048 | tf_op jit(solution)/shard_map/ppermute | solution.py:45
  80.5 17.4 %collective-permute-start.4 = (bf16[2,512,128]{2,1,0:T(8,128)(2,1)S(1)}, bf16[2,512,128]{2,1,0:T(8,128)(2,1)S(1)}, u32[]{:S(2)}, u32[]{:S(2)}) collective-permute-start(bf16[2,512,128]{2,1,0:T(8,128)(2,1)S(1)} %maximum_select_fusion.1), channel_id=1, source_target_pairs={{0,2},{2,0},{4,6},{6,4},{1,3},{3,1},{5,7},{7,5},{8,10},{10,8},{12,... | collective-permute-start | bytes 786440 | tf_op jit(solution)/shard_map/ppermute | solution.py:45
  83.7 14.2 %collective-permute-start.5 = (bf16[2,512,128]{2,1,0:T(8,128)(2,1)S(1)}, bf16[2,512,128]{2,1,0:T(8,128)(2,1)S(1)}, u32[]{:S(2)}, u32[]{:S(2)}) collective-permute-start(bf16[2,512,128]{2,1,0:T(8,128)(2,1)S(1)} %maximum_select_fusion.1), channel_id=1, source_target_pairs={{0,4},{2,6},{4,0},{6,2},{1,5},{3,7},{5,1},{7,3},{8,12},{10,14},{12... | collective-permute-start | bytes 786440 | tf_op jit(solution)/shard_map/ppermute | solution.py:45
  88.0 16.0 %collective-permute-start.6 = (bf16[2,512,128]{2,1,0:T(8,128)(2,1)S(1)}, bf16[2,512,128]{2,1,0:T(8,128)(2,1)S(1)}, u32[]{:S(2)}, u32[]{:S(2)}) collective-permute-start(bf16[2,512,128]{2,1,0:T(8,128)(2,1)S(1)} %maximum_select_fusion.1), channel_id=1, source_target_pairs={{0,6},{2,4},{4,2},{6,0},{1,7},{3,5},{5,3},{7,1},{8,14},{10,12},{12... | collective-permute-start | bytes 786440 | tf_op jit(solution)/shard_map/ppermute | solution.py:45
  112.7 17.4 %collective-permute-start.7 = (bf16[512,1024]{1,0:T(8,128)(2,1)}, bf16[512,1024]{1,0:T(8,128)(2,1)}, u32[]{:S(2)}, u32[]{:S(2)}) collective-permute-start(bf16[512,1024]{1,0:T(8,128)(2,1)} %convolution_convert_fusion.1), channel_id=1, source_target_pairs={{0,1},{1,0},{2,3},{3,2},{4,5},{5,4},{6,7},{7,6},{8,9},{9,8},{10,11... | collective-permute-start | bytes 3145736 | tf_op jit(solution)/shard_map/ppermute | solution.py:45
  115.2 107.2 %all-to-all-start.1 = ((bf16[64,128,128]{2,1,0:T(8,128)(2,1)}), bf16[64,128,128]{2,1,0:T(8,128)(2,1)}, u32[]{:S(2)}, u32[]{:S(2)}) async-start(bf16[64,128,128]{2,1,0:T(8,128)(2,1)} %bitcast.158), calls=%async_computation.1 | async-start | bytes 4194304 | tf_op jit(solution)/shard_map/all_to_all | solution.py:104
  130.0 77.0 %all-gather.6.cloned.1.call-start = ((), (), s32[]{:S(2)}) async-start(), calls=%async_computation.8 | async-start | bytes 2359296 | tf_op jit(solution)/shard_map/all_gather | solution.py:153
  135.1 11.0 %collective-permute-start.10 = (bf16[4,32,1024]{2,1,0:T(8,128)(2,1)}, bf16[4,32,1024]{2,1,0:T(8,128)(2,1)}, u32[]{:S(2)}, u32[]{:S(2)}) collective-permute-start(bf16[4,32,1024]{2,1,0:T(8,128)(2,1)} %bitcast.37), channel_id=1, source_target_pairs={{0,6},{2,4},{4,2},{6,0},{1,7},{3,5},{5,3},{7,1},{8,14},{10,12},{12... | collective-permute-start | bytes 786440 | tf_op jit(solution)/shard_map/ppermute | solution.py:45
  137.2 9.5 %collective-permute-start.8 = (bf16[4,32,1024]{2,1,0:T(8,128)(2,1)}, bf16[4,32,1024]{2,1,0:T(8,128)(2,1)}, u32[]{:S(2)}, u32[]{:S(2)}) collective-permute-start(bf16[4,32,1024]{2,1,0:T(8,128)(2,1)} %bitcast.35), channel_id=1, source_target_pairs={{0,2},{2,0},{4,6},{6,4},{1,3},{3,1},{5,7},{7,5},{8,10},{10,8},{12,... | collective-permute-start | bytes 786440 | tf_op jit(solution)/shard_map/ppermute | solution.py:45
  139.1 15.4 %collective-permute-start.9 = (bf16[4,32,1024]{2,1,0:T(8,128)(2,1)S(1)}, bf16[4,32,1024]{2,1,0:T(8,128)(2,1)}, u32[]{:S(2)}, u32[]{:S(2)}) collective-permute-start(bf16[4,32,1024]{2,1,0:T(8,128)(2,1)S(1)} %bitcast.175), channel_id=1, source_target_pairs={{0,4},{2,6},{4,0},{6,2},{1,5},{3,7},{5,1},{7,3},{8,12},{10,14},{12... | collective-permute-start | bytes 786440 | tf_op jit(solution)/shard_map/ppermute | solution.py:45
  155.8 18.3 %copy-start.2 = (bf16[32,4096]{1,0:T(8,128)(2,1)S(1)}, bf16[32,4096]{1,0:T(8,128)(2,1)}, u32[]{:S(2)}) copy-start(bf16[32,4096]{1,0:T(8,128)(2,1)} %param.11) | copy-start | bytes 786436
  155.8 9.8 %collective-permute-start.11 = (bf16[32,1024]{1,0:T(8,128)(2,1)S(1)}, bf16[32,1024]{1,0:T(8,128)(2,1)S(1)}, u32[]{:S(2)}, u32[]{:S(2)}) collective-permute-start(bf16[32,1024]{1,0:T(8,128)(2,1)S(1)} %get-tuple-element.39), channel_id=1, source_target_pairs={{0,128},{128,0},{256,384},{384,256},{1,129},{129,1},{257,385},{385... | collective-permute-start | bytes 196616 | tf_op jit(solution)/shard_map/ppermute | solution.py:45
  158.5 7.9 %collective-permute-start.12 = (bf16[32,1024]{1,0:T(8,128)(2,1)S(1)}, bf16[32,1024]{1,0:T(8,128)(2,1)S(1)}, u32[]{:S(2)}, u32[]{:S(2)}) collective-permute-start(bf16[32,1024]{1,0:T(8,128)(2,1)S(1)} %get-tuple-element.38), channel_id=1, source_target_pairs={{0,256},{128,384},{256,0},{384,128},{1,257},{129,385},{257,1},{385... | collective-permute-start | bytes 196616 | tf_op jit(solution)/shard_map/ppermute | solution.py:45
  163.0 6.9 %collective-permute-start.13 = (bf16[32,1024]{1,0:T(8,128)(2,1)S(1)}, bf16[32,1024]{1,0:T(8,128)(2,1)S(1)}, u32[]{:S(2)}, u32[]{:S(2)}) collective-permute-start(bf16[32,1024]{1,0:T(8,128)(2,1)S(1)} %get-tuple-element.37), channel_id=1, source_target_pairs={{0,384},{128,256},{256,128},{384,0},{1,385},{129,257},{257,129},{3... | collective-permute-start | bytes 196616 | tf_op jit(solution)/shard_map/ppermute | solution.py:45
  172.9 3.1 copy-start.7
  172.9 3.1 copy-start.16
  172.9 3.2 copy-start.14
  172.9 3.3 copy-start.18
  172.9 3.3 copy-start.9
  174.0 2.9 copy-start.10
  174.0 0.8 copy-start.1
  174.8 66.3 %copy-start.12 = (f32[32]{0:T(128)}, f32[32]{0:T(128)S(1)}, u32[]{:S(2)}) copy-start(f32[32]{0:T(128)S(1)} %get-tuple-element.26) | copy-start | bytes 388
  175.7 157.7 %all-gather.8.cloned.1.call-start = ((), (), s32[]{:S(2)}) async-start(), calls=%async_computation.9 | async-start | bytes 6553600 | tf_op jit(solution)/shard_map/all_gather | solution.py:152
  241.1 1.1 copy-start.11
  242.2 14.8 %all-to-all-start.2 = ((bf16[8,32,256]{2,1,0:T(8,128)(2,1)}), bf16[8,32,256]{2,1,0:T(8,128)(2,1)S(1)}, u32[]{:S(2)}, u32[]{:S(2)}) async-start(bf16[8,32,256]{2,1,0:T(8,128)(2,1)} %broadcast_in_dim.212), calls=%async_computation.2 | async-start | bytes 262144 | tf_op jit(solution)/shard_map/all_to_all | solution.py:194
  266.3 9.7 %all-to-all-start.3 = ((bf16[64,16,128]{2,1,0:T(8,128)(2,1)}), bf16[64,16,128]{2,1,0:T(8,128)(2,1)}, u32[]{:S(2)}, u32[]{:S(2)}) async-start(bf16[64,16,128]{2,1,0:T(8,128)(2,1)} %maximum_maximum_fusion), calls=%async_computation.3 | async-start | bytes 524288 | tf_op jit(solution)/shard_map/all_to_all | solution.py:228
  278.5 21.9 %all-to-all-start.4 = ((bf16[16,16,128]{2,1,0:T(8,128)(2,1)}), bf16[16,16,128]{2,1,0:T(8,128)(2,1)}, u32[]{:S(2)}, u32[]{:S(2)}) async-start(bf16[16,16,128]{2,1,0:T(8,128)(2,1)} %maximum_maximum_fusion.1), calls=%async_computation.4 | async-start | bytes 131072 | tf_op jit(solution)/shard_map/all_to_all | solution.py:231
  303.6 15.8 %all-to-all-start.5 = ((bf16[16,16,128]{2,1,0:T(8,128)(2,1)}), bf16[16,16,128]{2,1,0:T(8,128)(2,1)}, u32[]{:S(2)}, u32[]{:S(2)}) async-start(bf16[16,16,128]{2,1,0:T(8,128)(2,1)} %broadcast_in_dim.217), calls=%async_computation.5 | async-start | bytes 131072 | tf_op jit(solution)/shard_map/all_to_all | solution.py:233
  321.0 8.9 %all-to-all-start.6 = ((bf16[4,16,16,128]{3,2,1,0:T(8,128)(2,1)}), bf16[4,16,16,128]{3,2,1,0:T(8,128)(2,1)S(1)}, u32[]{:S(2)}, u32[]{:S(2)}) async-start(bf16[4,16,16,128]{3,2,1,0:T(8,128)(2,1)} %broadcast_in_dim.218), calls=%async_computation.6 | async-start | bytes 524288 | tf_op jit(solution)/shard_map/all_to_all | solution.py:236
  330.0 0.8 copy-start.3
  333.4 5.8 %copy-start.13 = (f32[256]{0:T(256)S(1)}, f32[256]{0:T(256)}, u32[]{:S(2)}) copy-start(f32[256]{0:T(256)} %get-tuple-element.19) | copy-start | bytes 3076
Sparse Core Ops, SparseCore 0:
  33.3 63.7 all-gather.3
  175.8 31.1 all-gather.5
  209.1 64.6 all-gather.7

commit v3 on v2

v3 whole, which is shorter than its diff:
```python
import jax
import jax.numpy as jnp
from jax import lax
from jax.experimental import pallas as pl
from jax.experimental.pallas import tpu as pltpu
from jax.sharding import Mesh, PartitionSpec as P

EPS = 1e-06
TEMPER = 0.1
LOSS_SCALE = 64.0

Y, Z, X, C = 4, 16, 4, 2
DP = ("y", "z")
TENSOR = ("x", "c")

BF16 = jnp.bfloat16
F32 = jnp.float32
I32 = jnp.int32
VMEM = pl.BlockSpec(memory_space=pltpu.VMEM)
SMEM = pl.BlockSpec(memory_space=pltpu.SMEM)


def swap(values, axis, size, step):
    return lax.ppermute(values, axis, [(i, i ^ step) for i in range(size)])


def rows_of(values, index):
    return values.at[index].get(mode="promise_in_bounds")


def unxor(blocks, place):
    return rows_of(blocks, jnp.arange(blocks.shape[0], dtype=I32) ^ place)


def halves(values):
    top = values.astype(BF16)
    return top, (values - top.astype(F32)).astype(BF16)


def decode_kernel(buckets, low_bytes, high_bytes, rows, out):
    words = low_bytes.shape[1]
    features = out.shape[1]
    feature = lax.broadcasted_iota(I32, (words, features), 1)
    word = lax.broadcasted_iota(I32, (words, features), 0)
    here = (feature >> 3) == word
    first = (feature & 7) < 4
    spread_low = jnp.where(here & first, 1.0, 0.0).astype(BF16)
    spread_high = jnp.where(here & ~first, 1.0, 0.0).astype(BF16)
    code_bytes = jnp.dot(low_bytes[...], spread_low, preferred_element_type=F32) + jnp.dot(
        high_bytes[...], spread_high, preferred_element_type=F32
    )
    shift = 2 * (lax.broadcasted_iota(I32, code_bytes.shape, 1) & 3)
    codes = (code_bytes.astype(I32) >> shift) & 3
    low = (codes & 1).astype(F32)
    high = (codes >> 1).astype(F32)
    zero, one, two, three = [buckets[k] for k in range(4)]
    levels = zero + low * (one - zero) + high * (two - zero)
    levels = levels + low * high * (three - two - one + zero)
    vectors = rows[...].astype(F32) + levels
    scale = lax.rsqrt(jnp.sum(vectors * vectors, axis=1, keepdims=True) + EPS)
    out[...] = (vectors * scale).astype(BF16)


def decode_all(cell_ids, packed, centroids, buckets):
    count = cell_ids.size
    words = packed.size // count
    features = centroids.shape[1]
    low_bytes = (packed & 255).astype(BF16).reshape(count, words)
    high_bytes = ((packed >> 8) & 255).astype(BF16).reshape(count, words)
    rows = rows_of(centroids, cell_ids.reshape(count))
    step = min(count, 512)
    return pl.pallas_call(
        decode_kernel,
        grid=(count // step,),
        in_specs=[
            SMEM,
            pl.BlockSpec((step, words), lambda i: (i, 0)),
            pl.BlockSpec((step, words), lambda i: (i, 0)),
            pl.BlockSpec((step, features), lambda i: (i, 0)),
        ],
        out_specs=pl.BlockSpec((step, features), lambda i: (i, 0)),
        out_shape=jax.ShapeDtypeStruct((count, features), BF16),
        name="decode",
    )(buckets, low_bytes, high_bytes, rows)


def score_kernel(docs_a, docs_b, embedded_ref, inv_rms_ref, spans, flags, scores, packet, weights, totals):
    slots, queries_n = totals.shape
    half = slots // 2
    tokens = docs_a.shape[0] // half
    features = docs_a.shape[1]
    embedded = embedded_ref[...]
    inv_rms = inv_rms_ref[...]
    inverse = lax.rsqrt(jnp.sum(embedded * embedded, axis=1, keepdims=True) + EPS)
    queries = (embedded * inverse).astype(BF16)
    group = 8
    token = lax.broadcasted_iota(I32, (tokens, queries_n), 0)

    for part, docs in enumerate((docs_a, docs_b)):

        @pl.loop(0, half // group)
        def _(i, part=part, docs=docs):
            at = pl.multiple_of(i * (group * tokens), group * tokens)
            slot0 = pl.multiple_of(part * half + i * group, group)
            similar = lax.dot_general(
                docs[pl.ds(at, group * tokens), :],
                queries,
                (((1,), (1,)), ((), ())),
                preferred_element_type=F32,
            )
            sizes = spans[pl.ds(slot0, group), :]
            sums = []
            for g in range(group):
                one = jnp.exp(similar[g * tokens : (g + 1) * tokens] / TEMPER)
                one = jnp.where(token < sizes[g : g + 1, :], one, 0.0)
                weights[pl.ds(slot0 * tokens + g * tokens, tokens), :] = one
                sums.append(jnp.sum(one, axis=0, keepdims=True))
            totals[pl.ds(slot0, group), :] = jnp.concatenate(sums, axis=0)

    all_totals = totals[...]
    slot_scores = TEMPER * jnp.sum(jnp.log(all_totals), axis=1, keepdims=True)
    scores[...] = slot_scores
    filled = flags[:, 0:1] > 0
    positive = flags[:, 1:2] > 0
    exponent = jnp.where(filled, jnp.exp(slot_scores), 0.0)
    share = exponent / jnp.sum(exponent, axis=0, keepdims=True)
    seeds = LOSS_SCALE * (share - jnp.where(positive, 1.0, 0.0))
    totals[...] = seeds / all_totals

    grad_q = jnp.zeros((queries_n, features), F32)
    for part, docs in enumerate((docs_a, docs_b)):

        def add(i, total, part=part, docs=docs):
            at = pl.multiple_of(i * (group * tokens), group * tokens)
            slot0 = pl.multiple_of(part * half + i * group, group)
            factors = totals[pl.ds(slot0, group), :]
            mixing = [
                weights[pl.ds(slot0 * tokens + g * tokens, tokens), :] * factors[g : g + 1, :]
                for g in range(group)
            ]
            mixing = jnp.concatenate(mixing, axis=0).astype(BF16)
            return total + lax.dot_general(
                mixing,
                docs[pl.ds(at, group * tokens), :],
                (((0,), (0,)), ((), ())),
                preferred_element_type=F32,
            )

        grad_q = lax.fori_loop(0, half // group, add, grad_q)

    along = jnp.sum(embedded * grad_q, axis=1, keepdims=True)
    grad_embedded = (inverse * grad_q - inverse * inverse * inverse * embedded * along).astype(BF16)
    packet[:, 0:features] = grad_embedded
    pull = inv_rms * jnp.sum(grad_embedded.astype(F32) * embedded, axis=1, keepdims=True)
    lane = lax.broadcasted_iota(I32, (queries_n, features), 1)
    extra = jnp.zeros((queries_n, features), F32)
    column = 0
    for value in (pull, inv_rms):
        for piece in halves(value):
            extra = jnp.where(lane == column, piece.astype(F32), extra)
            column += 1
    packet[:, features : 2 * features] = extra.astype(BF16)


def score(docs_a, docs_b, embedded, inv_rms, spans, flags):
    slots = flags.shape[0]
    queries_n, features = embedded.shape
    count = docs_a.shape[0] + docs_b.shape[0]
    return pl.pallas_call(
        score_kernel,
        in_specs=[VMEM] * 6,
        out_specs=[VMEM] * 2,
        out_shape=[
            jax.ShapeDtypeStruct((slots, 1), F32),
            jax.ShapeDtypeStruct((queries_n, 2 * features), BF16),
        ],
        scratch_shapes=[
            pltpu.VMEM((count, queries_n), F32),
            pltpu.VMEM((slots, queries_n), F32),
        ],
        compiler_params=pltpu.CompilerParams(vmem_limit_bytes=32 * 1024 * 1024),
        name="score",
    )(docs_a, docs_b, embedded, inv_rms, spans, flags)


def local(
    residual,
    context,
    out_proj,
    norm_gain,
    colbert_head,
    candidates,
    lengths,
    centroid_ids,
    residual_codes,
    centroids,
    buckets,
):
    shards = Y * Z
    seq_rows, width = residual.shape
    cand_count = candidates.shape[1]
    per_shard, doc_len = centroid_ids.shape
    feature_dim = centroids.shape[1]
    cap = 2
    slots = shards * cap

    slot_ids = candidates.reshape(-1)
    owners = slot_ids // per_shard
    local_ids = slot_ids - owners * per_shard
    order = jnp.arange(cand_count, dtype=I32)
    earlier = (owners[None, :] == owners[:, None]) & (order[None, :] < order[:, None])
    rank = jnp.sum(earlier.astype(I32), axis=1)
    position = rank * shards + owners
    slot_at = jnp.arange(slots, dtype=I32)
    placed = position[None, :] == slot_at[:, None]
    request = jnp.sum(jnp.where(placed, local_ids[None, :], 0), axis=1)
    filled = jnp.any(placed, axis=1)
    flags = jnp.stack([filled, slot_at == position[0]], axis=1).astype(I32)
    note = jnp.concatenate(
        [
            jnp.broadcast_to(lengths[None, :], (shards, per_shard)),
            request.reshape(cap, shards).T,
            jnp.zeros((shards, 128 - per_shard - cap), I32),
        ],
        axis=1,
    )

    proj_z = lax.all_gather(out_proj, "z", axis=1, tiled=True)
    documents = decode_all(centroid_ids, residual_codes, centroids, buckets)
    note, documents = lax.optimization_barrier((note, documents))
    notes = lax.all_to_all(note, DP, 0, 0, tiled=True)
    documents = documents.reshape(per_shard, doc_len, feature_dim)
    chosen_a = rows_of(documents, notes[:, per_shard])
    chosen_b = rows_of(documents, notes[:, per_shard + 1])
    chosen_a, chosen_b, context, colbert_head = lax.optimization_barrier(
        (chosen_a, chosen_b, context, colbert_head)
    )
    got_a = lax.all_to_all(chosen_a, DP, 0, 0, tiled=True).reshape(shards * doc_len, feature_dim)
    spans = jnp.sum(
        jnp.where(
            jnp.arange(per_shard, dtype=I32)[None, None, :]
            == request.reshape(cap, shards)[:, :, None],
            notes[None, :, :per_shard],
            0,
        ),
        axis=2,
    ).reshape(slots, 1)
    spans = jnp.broadcast_to(spans, (slots, seq_rows))

    here_x, here_c, here_y = lax.axis_index("x"), lax.axis_index("c"), lax.axis_index("y")
    blocks = context.reshape(X, C, seq_rows, context.shape[1])
    blocks = jnp.where(here_c == 0, blocks, blocks[:, ::-1])
    blocks = unxor(blocks, here_x).transpose(1, 0, 2, 3)
    by_y = jnp.stack([blocks] + [swap(blocks, "y", Y, step) for step in range(1, Y)], axis=2)
    by_y = by_y.reshape(C, X * Y * seq_rows, context.shape[1])

    head_pair = swap(colbert_head, "c", C, 1)
    head_pair = jnp.where(
        here_c == 0,
        jnp.stack([colbert_head, head_pair]),
        jnp.stack([head_pair, colbert_head]),
    )
    head_full = unxor(
        jnp.stack([head_pair] + [swap(head_pair, "x", X, step) for step in range(1, X)]), here_x
    ).reshape(width, feature_dim)
    by_y, head_full, got_a, proj_z = lax.optimization_barrier((by_y, head_full, got_a, proj_z))

    got_b = lax.all_to_all(chosen_b, DP, 0, 0, tiled=True).reshape(shards * doc_len, feature_dim)
    away = jnp.dot(by_y[1], proj_z, preferred_element_type=F32).astype(BF16)
    away = swap(away, "c", C, 1)
    stay = jnp.dot(by_y[0], proj_z, preferred_element_type=F32).astype(BF16)
    pair = (stay.astype(F32) + away.astype(F32)).reshape(X, Y, seq_rows, width // Y)
    for_x = pair.astype(BF16)
    row = pair[0]
    for step in range(1, X):
        row = row + swap(for_x[step], "x", X, step).astype(F32)
    for_y = row.astype(BF16)
    columns = [for_y[0]] + [swap(for_y[step], "y", Y, step) for step in range(1, Y)]
    columns = unxor(jnp.stack(columns), here_y)
    attended = columns.transpose(1, 0, 2).reshape(seq_rows, width).astype(F32)
    summed = residual.astype(F32) + attended
    inv_rms = lax.rsqrt(jnp.mean(summed * summed, axis=-1, keepdims=True) + EPS)
    scaled_sum = summed * inv_rms
    normed = (scaled_sum * norm_gain).astype(BF16)
    proj_full = lax.all_gather(proj_z, "y", axis=1, tiled=True)
    unit, proj_full = lax.optimization_barrier((scaled_sum.astype(BF16), proj_full))
    unit_all = lax.all_gather(unit, TENSOR, axis=0, tiled=True)
    embedded = jnp.dot(normed, head_full, preferred_element_type=F32)

    slot_scores, packet = score(got_a, got_b, embedded, inv_rms, spans, flags)
    scores = jnp.sum(jnp.where(placed, slot_scores, 0.0), axis=0)[None, :]
    packets = lax.all_to_all(
        jnp.broadcast_to(packet, (X * C,) + packet.shape), TENSOR, 0, 0, tiled=True
    ).reshape(X * C * seq_rows, 2 * feature_dim)
    ge_all = packets[:, :feature_dim]
    extra = packets[:, feature_dim : feature_dim + 4].astype(F32)
    pull_all = (extra[:, 0:1] + extra[:, 1:2]) * (1.0 / width)
    inv_all = extra[:, 2:3] + extra[:, 3:4]

    head_rows = colbert_head.shape[0]
    mine = (here_x * C + here_c) * head_rows
    head_term = lax.dot_general(
        lax.dynamic_slice_in_dim(unit_all, mine, head_rows, 1),
        ge_all,
        (((0,), (0,)), ((), ())),
        preferred_element_type=F32,
    )
    gain_term = jnp.sum(
        lax.dot_general(
            ge_all, head_full, (((1,), (1,)), ((), ())), preferred_element_type=F32
        )
        * unit_all.astype(F32),
        axis=0,
    )
    share = head_rows // shards
    lines = width // feature_dim

    def bundle(head_part, gain_part):
        return jnp.concatenate(
            [head_part.astype(BF16)] + [piece[:, None, :] for piece in halves(gain_part)], axis=1
        )

    def unbundle(rows):
        rows = rows.astype(F32)
        return rows[:, :share], rows[:, share] + rows[:, share + 1]

    gain_term = jnp.concatenate(
        [gain_term.reshape(lines, feature_dim), jnp.zeros((shards - lines, feature_dim), F32)]
    )
    first = bundle(head_term.reshape(shards, share, feature_dim), gain_term)
    first = unbundle(lax.all_to_all(first, DP, 0, 0, tiled=True))
    second = bundle(*[jnp.sum(part, axis=0, keepdims=True) for part in first])

    grad_embedded = packet[:, :feature_dim]
    grad_normed = lax.dot_general(
        grad_embedded, head_full, (((1,), (1,)), ((), ())), preferred_element_type=F32
    )
    scaled = grad_normed * norm_gain
    residual_grad = (
        inv_rms * scaled - summed * inv_rms**3 * jnp.mean(summed * scaled, axis=-1, keepdims=True)
    ).astype(BF16)
    gained_head = (head_full.astype(F32) * norm_gain[:, None]).astype(BF16)
    mixed_head = jnp.dot(proj_full, gained_head, preferred_element_type=F32).astype(BF16)
    pulled = lax.dot_general(
        unit_all, proj_full, (((1,), (1,)), ((), ())), preferred_element_type=F32
    )
    context_grad = (
        inv_all
        * lax.dot_general(
            ge_all, mixed_head, (((1,), (1,)), ((), ())), preferred_element_type=F32
        )
        - pull_all * pulled
    ).astype(BF16)
    second, context_grad = lax.optimization_barrier((second, context_grad))

    second = lax.all_to_all(
        jnp.broadcast_to(second, (shards,) + second.shape[1:]), DP, 0, 0, tiled=True
    )
    head_got, gain_got = unbundle(second)
    gain_blk = lax.dynamic_slice_in_dim(norm_gain, mine, head_rows, 0)
    head_grad = head_got.reshape(head_rows, feature_dim) * gain_blk[:, None]
    gain_grad = gain_got[:lines].reshape(width)
    return (scores, context_grad, residual_grad, head_grad, gain_grad)


def solution(mesh):
    split = Mesh(mesh.devices.reshape(Y, Z, X, C), ("y", "z", "x", "c"))
    both = DP + TENSOR
    in_specs = (
        P(both, None),
        P(DP, TENSOR),
        P(TENSOR, DP),
        P(),
        P(TENSOR, None),
        P(both, None),
        P(DP),
        P(DP, None),
        P(DP, None),
        P(),
        P(),
    )
    out_specs = (
        P(both, None),
        P(DP, TENSOR),
        P(both, None),
        P(TENSOR, None),
        P(),
    )
    return jax.shard_map(local, mesh=split, in_specs=in_specs, out_specs=out_specs, check_vma=False)
```

time: 357 us -> 355 us (level)
  blocking collectives: 0 us -> 32.5 us
  other arithmetic: 36.5 us -> 16.3 us
  waiting for transfers between devices: 100 us -> 117 us
  starting transfers between devices: 110 us -> 93.9 us
  Pallas kernels: 0 us -> 15.6 us
  matrix products: 37.8 us -> 23.4 us
  local copies, waits for them, and re-layouts: 47.1 us -> 38.5 us
  between operations: 19.6 us -> 14.4 us
    all_gather x1, waiting for transfers between devices: 0.02 us -> 40.1 us  [local(): proj_z = lax.all_gather(out_proj, 'z', axis=1, tiled=True)]
    all_to_all x0 -> x1, blocking collectives: none -> 32.5 us  [local(): notes = lax.all_to_all(note, DP, 0, 0, tiled=True)]
    all_to_all x6 -> x4, starting transfers between devices: 56.1 us -> 37.7 us  [the longest x1 15.4 us: local(): first = unbundle(lax.all_to_all(first, DP, 0, 0, tiled=True))]
    all_to_all x6 -> x4, waiting for transfers between devices: 41.8 us -> 25.6 us  [the longest x1 17.3 us: local(): lax.all_to_all(jnp.broadcast_to(second, (shards,) + second.shape[1:]), DP...]
    pallas_call x0 -> x2, Pallas kernels: none -> 15.6 us  [the longest x1 8.42 us: score(): pl.pallas_call(score_kernel, in_specs=[VMEM] * 6, out_specs=[VMEM] * 2, o...]
    dot_general x4 -> x2, matrix products: 14.8 us -> 3.53 us  [the longest x1 2.31 us: local(): lax.dot_general(ge_all, head_full, (((1,), (1,)), ((), ())), preferred_el...]
    gather x5 -> x6, local copies, waits for them, and re-layouts: 18.8 us -> 26.3 us  [rows_of(): return values.at[index].get(mode='promise_in_bounds')]
    select_n x6 -> x4, other arithmetic: 6.65 us -> 0.21 us  [rows_of(): return values.at[index].get(mode='promise_in_bounds')]
  transfers between devices with their start and end apart: 24 -> 22, of which waited for: 14 -> 12; matrix products, arithmetic and copies ran while one was open for 29% -> 12% of each run, Pallas kernels for 0% -> 2%
where the time goes in v3:
time: 355 us; the launch traced here: 352 us
  waiting for transfers between devices  117 us (33%)
  starting transfers between devices  93.9 us (26%)
  local copies, waits for them, and re-layouts  38.5 us (11%)
  blocking collectives  32.5 us (9%)
  matrix products  23.4 us (7%)
  other arithmetic  16.3 us (5%)
  Pallas kernels  15.6 us (4%)
  between operations  14.4 us (4%)
    ppermute x14, starting transfers between devices, swap(): return lax.ppermute(values, axis, [(i, i ^ step) for i in range(size)])  49.4 us
    all_gather x1, waiting for transfers between devices, local(): proj_z = lax.all_gather(out_proj, 'z', axis=1, tiled=True)  40.1 us
    all_to_all x1, blocking collectives, local(): notes = lax.all_to_all(note, DP, 0, 0, tiled=True)  32.5 us
    gather x6, local copies, waits for them, and re-layouts, rows_of(): return values.at[index].get(mode='promise_in_bounds')  26.3 us
    all_gather x1, waiting for transfers between devices, local(): unit_all = lax.all_gather(unit, TENSOR, axis=0, tiled=True)  22.8 us
    ppermute x14, waiting for transfers between devices, swap(): return lax.ppermute(values, axis, [(i, i ^ step) for i in range(size)])  22.6 us
    all_to_all x1, waiting for transfers between devices, local(): lax.all_to_all(jnp.broadcast_to(second, (shards,) + second.shape[1:]), DP...  17.3 us
    all_to_all x1, starting transfers between devices, local(): first = unbundle(lax.all_to_all(first, DP, 0, 0, tiled=True))  15.4 us
  transfers between devices with their start and end apart: 22, of which 12 were waited for; matrix products, arithmetic and copies ran while one was open for 12% of the time, Pallas kernels for 2%

profile of v3, /device:TPU:1, one launch (start us, length us, event | category | flops | bytes accessed | tf_op | source)
XLA Modules:
  0.0 351.5 jit_solution(16820303350285304979)
XLA Ops:
  7.2 0.8 subtract_bitcast_fusion
  10.3 1.0 and_convert_fusion
  11.3 1.8 reshape.315.low_bytes
  13.1 1.8 reshape.316.high_bytes
  15.1 15.0 %gather_fusion = bf16[4096,128]{1,0:T(8,128)(2,1)} fusion(bf16[8192,128]{1,0:T(8,128)(2,1)S(1)} %copy-done, s32[4096]{0:T(1024)S(1)} %broadcast_clamp_fusion), kind=kCustom, calls=%fused_computation | custom fusion | bytes 2113536 | tf_op jit(solution)/shard_map/gather | solution.py:28
  30.2 7.2 %decode.1 = bf16[4096,128]{1,0:T(8,128)(2,1)} custom-call(f32[4]{0:T(128)} %buckets.1, bf16[4096,16]{1,0:T(8,128)(2,1)} %reshape.315.low_bytes, bf16[4096,16]{1,0:T(8,128)(2,1)} %reshape.316.high_bytes, bf16[4096,128]{1,0:T(8,128)(2,1)} %gather_fusion), custom_call_target="tpu_custom_call" | custom-call | tf_op jit(solution)/shard_map/decode/pallas_call | solution.py:72
  37.4 32.5 %all_to_all.37 = s32[64,1,128]{2,1,0:T(1,128)S(1)} all-to-all(s32[64,1,128]{2,1,0:T(1,128)S(1)} %bitcast.145), channel_id=1, replica_groups=mesh['y'=4,'z'=16,'x'=4,'c'=2] {'y','z'}, dimensions={0} | all-to-all | bytes 65536 | tf_op jit(solution)/shard_map/all_to_all | solution.py:231
  70.7 2.9 gather_fusion.1
  73.6 1.7 gather_fusion.2
  75.3 4.7 %all-to-all-start.1 = ((bf16[64,64,128]{2,1,0:T(8,128)(2,1)}), bf16[64,64,128]{2,1,0:T(8,128)(2,1)S(1)}, u32[]{:S(2)}, u32[]{:S(2)}) async-start(bf16[64,64,128]{2,1,0:T(8,128)(2,1)} %gather_fusion.1), calls=%async_computation.1 | async-start | bytes 2097152 | tf_op jit(solution)/shard_map/all_to_all | solution.py:238
  81.5 1.6 gather_fusion.3
  83.1 4.3 %collective-permute-start.2 = (bf16[2,4,32,640]{3,2,0,1:T(8,128)(2,1)S(1)}, bf16[2,4,32,640]{3,2,0,1:T(8,128)(2,1)S(1)}, u32[]{:S(2)}, u32[]{:S(2)}) collective-permute-start(bf16[2,4,32,640]{3,2,0,1:T(8,128)(2,1)S(1)} %bitcast.123), channel_id=1, source_target_pairs={{0,384},{128,256},{256,128},{384,0},{1,385},{129,257},{257,129},{3... | collective-permute-start | bytes 983048 | tf_op jit(solution)/shard_map/ppermute | solution.py:24
  87.5 4.6 %collective-permute-start.3 = (bf16[512,128]{1,0:T(8,128)(2,1)}, bf16[512,128]{1,0:T(8,128)(2,1)S(1)}, u32[]{:S(2)}, u32[]{:S(2)}) collective-permute-start(bf16[512,128]{1,0:T(8,128)(2,1)} %param.15), channel_id=1, source_target_pairs={{0,1},{1,0},{2,3},{3,2},{4,5},{5,4},{6,7},{7,6},{8,9},{9,8},{10,11... | collective-permute-start | bytes 393224 | tf_op jit(solution)/shard_map/ppermute | solution.py:24
  92.0 2.3 collective-permute-start.1
  94.3 2.1 collective-permute-start
  96.4 1.0 maximum_select_fusion.1
  97.4 4.4 %collective-permute-start.6 = (bf16[2,512,128]{2,1,0:T(8,128)(2,1)S(1)}, bf16[2,512,128]{2,1,0:T(8,128)(2,1)S(1)}, u32[]{:S(2)}, u32[]{:S(2)}) collective-permute-start(bf16[2,512,128]{2,1,0:T(8,128)(2,1)S(1)} %maximum_select_fusion.1), channel_id=1, source_target_pairs={{0,6},{2,4},{4,2},{6,0},{1,7},{3,5},{5,3},{7,1},{8,14},{10,12},{12... | collective-permute-start | bytes 786440 | tf_op jit(solution)/shard_map/ppermute | solution.py:24
  101.8 2.4 collective-permute-start.5
  104.3 2.2 collective-permute-start.4
  106.5 1.0 maximum_select_fusion
  107.5 5.3 %collective-permute-done = bf16[2,4,32,640]{3,2,0,1:T(8,128)(2,1)S(1)} collective-permute-done((bf16[2,4,32,640]{3,2,0,1:T(8,128)(2,1)S(1)}, bf16[2,4,32,640]{3,2,0,1:T(8,128)(2,1)S(1)}, u32[]{:S(2)}, u32[]{:S(2)}) %collective-permute-start) | collective-permute-done | bytes 327712 | tf_op jit(solution)/shard_map/ppermute | solution.py:24
  113.0 1.2 copy.60
  114.2 1.6 collective-permute-done.4
  115.8 1.1 pad_maximum_fusion.1
  116.9 2.9 gather_fusion.4
  119.8 40.1 %all-gather.4.cloned.1.call-done = bf16[640,1024]{0,1:T(8,128)(2,1)} async-done(((bf16[640,64]{0,1:T(8,128)(2,1)}), bf16[640,1024]{0,1:T(8,128)(2,1)}) %all-gather.4.cloned.1.call-update) | async-done | bytes 1310736 | tf_op jit(solution)/shard_map/all_gather | solution.py:228
  160.0 10.8 %all-to-all-start.2 = ((bf16[64,64,128]{2,1,0:T(8,128)(2,1)}), bf16[64,64,128]{2,1,0:T(8,128)(2,1)}, u32[]{:S(2)}, u32[]{:S(2)}) async-start(bf16[64,64,128]{2,1,0:T(8,128)(2,1)} %gather_fusion.2), calls=%async_computation.2 | async-start | bytes 2097152 | tf_op jit(solution)/shard_map/all_to_all | solution.py:268
  170.8 2.7 convolution_convert_fusion
  173.5 9.2 %collective-permute-start.7 = (bf16[512,1024]{1,0:T(8,128)(2,1)S(1)}, bf16[512,1024]{1,0:T(8,128)(2,1)S(1)}, u32[]{:S(2)}, u32[]{:S(2)}) collective-permute-start(bf16[512,1024]{1,0:T(8,128)(2,1)S(1)} %convolution_convert_fusion), channel_id=1, source_target_pairs={{0,1},{1,0},{2,3},{3,2},{4,5},{5,4},{6,7},{7,6},{8,9},{9,8},{10,11... | collective-permute-start | bytes 3145736 | tf_op jit(solution)/shard_map/ppermute | solution.py:24
  182.9 2.1 collective-permute-done.7
  185.0 2.4 fusion.38
  187.3 0.8 fusion.35
  188.2 4.2 %collective-permute-start.10 = (bf16[4,32,1024]{2,1,0:T(8,128)(2,1)}, bf16[4,32,1024]{2,1,0:T(8,128)(2,1)}, u32[]{:S(2)}, u32[]{:S(2)}) collective-permute-start(bf16[4,32,1024]{2,1,0:T(8,128)(2,1)} %bitcast.33), channel_id=1, source_target_pairs={{0,6},{2,4},{4,2},{6,0},{1,7},{3,5},{5,3},{7,1},{8,14},{10,12},{12... | collective-permute-start | bytes 786440 | tf_op jit(solution)/shard_map/ppermute | solution.py:24
  192.4 2.6 collective-permute-start.9
  195.0 2.2 collective-permute-start.8
  197.3 1.1 slice.131
  198.4 5.5 %collective-permute-done.10 = bf16[4,32,1024]{2,1,0:T(8,128)(2,1)} collective-permute-done((bf16[4,32,1024]{2,1,0:T(8,128)(2,1)}, bf16[4,32,1024]{2,1,0:T(8,128)(2,1)}, u32[]{:S(2)}, u32[]{:S(2)}) %collective-permute-start.10) | collective-permute-done | bytes 262176 | tf_op jit(solution)/shard_map/ppermute | solution.py:24
  203.9 3.1 collective-permute-done.8
  207.0 1.3 add_convert_fusion
  209.0 4.5 %collective-permute-start.13 = (bf16[32,1024]{1,0:T(8,128)(2,1)}, bf16[32,1024]{1,0:T(8,128)(2,1)}, u32[]{:S(2)}, u32[]{:S(2)}) collective-permute-start(bf16[32,1024]{1,0:T(8,128)(2,1)} %get-tuple-element.53), channel_id=1, source_target_pairs={{0,384},{128,256},{256,128},{384,0},{1,385},{129,257},{257,129},{3... | collective-permute-start | bytes 196616 | tf_op jit(solution)/shard_map/ppermute | solution.py:24
  213.5 2.3 collective-permute-start.12
  215.8 2.2 collective-permute-start.11
  218.3 4.1 %collective-permute-done.12 = bf16[32,1024]{1,0:T(8,128)(2,1)} collective-permute-done((bf16[32,1024]{1,0:T(8,128)(2,1)}, bf16[32,1024]{1,0:T(8,128)(2,1)}, u32[]{:S(2)}, u32[]{:S(2)}) %collective-permute-start.12) | collective-permute-done | bytes 65568 | tf_op jit(solution)/shard_map/ppermute | solution.py:24
  222.4 0.9 collective-permute-done.11
  223.3 1.7 pad_maximum_fusion.2
  225.0 2.2 gather_fusion.5
  227.2 1.0 convert_bitcast_fusion
  229.1 1.8 fusion.10.embedded_ref
  231.0 8.4 %score.1 = (f32[128,1]{1,0:T(8,128)S(1)}, bf16[32,256]{1,0:T(8,128)(2,1)S(1)}) custom-call(bf16[4096,128]{1,0:T(8,128)(2,1)S(1)} %bitcast.109, bf16[4096,128]{1,0:T(8,128)(2,1)} %bitcast.27.docs_b, f32[32,128]{1,0:T(8,128)S(1)} %fusion.10.embedded_ref, f32[32,1]{1,0:T(8,128)S(1)} %copy.62.inv_rms_ref, s32[128,32]{1,0:T(8,128)S(1)} %broadcast_in_dim.109.spans, ...), custom_call_target="tpu_custom_call" | custom-call | tf_op jit(solution)/shard_map/score/pallas_call | solution.py:169
  239.5 1.5 multiply_reduce_fusion
  241.0 1.0 subtract_convert_fusion
  242.7 6.6 %all-to-all-start.3 = ((bf16[8,32,256]{2,1,0:T(8,128)(2,1)}), bf16[8,32,256]{2,1,0:T(8,128)(2,1)S(1)}, u32[]{:S(2)}, u32[]{:S(2)}) async-start(bf16[8,32,256]{2,1,0:T(8,128)(2,1)} %broadcast_in_dim.114), calls=%async_computation.3 | async-start | bytes 262144 | tf_op jit(solution)/shard_map/all_to_all | solution.py:292
  249.3 5.3 %all-to-all-done.3 = bf16[8,32,256]{2,1,0:T(8,128)(2,1)S(1)} async-done(((bf16[8,32,256]{2,1,0:T(8,128)(2,1)}), bf16[8,32,256]{2,1,0:T(8,128)(2,1)S(1)}, u32[]{:S(2)}, u32[]{:S(2)}) %all-to-all-start.3) | async-done | bytes 131104 | tf_op jit(solution)/shard_map/all_to_all | solution.py:292
  254.9 22.8 %all-gather.8.cloned.1.call-done = bf16[256,4096]{1,0:T(8,128)(2,1)} async-done(((bf16[32,4096]{1,0:T(8,128)(2,1)}), bf16[256,4096]{1,0:T(8,128)(2,1)}) %all-gather.8.cloned.1.call-update) | async-done | bytes 2097168 | tf_op jit(solution)/shard_map/all_gather | solution.py:287
  277.7 2.3 fusion
  280.1 1.2 fusion.3
  281.3 0.8 pad_maximum_fusion.3
  282.1 15.4 %all-to-all-start.4 = ((bf16[64,10,128]{2,1,0:T(8,128)(2,1)}), bf16[64,10,128]{2,1,0:T(8,128)(2,1)S(1)}, u32[]{:S(2)}, u32[]{:S(2)}) async-start(bf16[64,10,128]{2,1,0:T(8,128)(2,1)} %pad_maximum_fusion.3), calls=%async_computation.4 | async-start | bytes 524288 | tf_op jit(solution)/shard_map/all_to_all | solution.py:331
  297.5 5.8 %convolution_multiply_fusion.2 = f32[256,640]{1,0:T(8,128)} fusion(bf16[256,4096]{1,0:T(8,128)(2,1)} %all-gather.8.cloned.1.call-done, bf16[640,4096]{0,1:T(8,128)(2,1)} %all-gather.6.cloned.1.call-done, f32[256]{0:T(256)S(1)} %get-tuple-element.38), kind=kOutput, calls=%fused_computation.14 | convolution fusion | flops 1342341120 | bytes 7996416 | tf_op jit(solution)/shard_map/dot_general | solution.py:344
  303.3 5.8 %fusion.2 = bf16[256,640]{1,0:T(8,128)(2,1)} fusion(f32[256,640]{1,0:T(8,128)} %convolution_multiply_fusion.2, bf16[640,4096]{0,1:T(8,128)(2,1)} %all-gather.6.cloned.1.call-done, bf16[4096,128]{1,0:T(8,128)(2,1)S(1)} %bitcast.119, f32[4096]{0:T(1024)S(1)} %copy-done.14, f32[256]{0:T(256)S(1)} %get-tuple-element.37, bf16[256,256]{1,0:T(8,128)(2,1)} %bitcast.134), kind=kOutput, calls=%fused_computation.17 | convolution fusion | flops 715177984 | bytes 7357440 | tf_op jit(solution)/shard_map/dot_general | solution.py:349
  309.1 8.3 %all-to-all-done.4 = bf16[64,10,128]{2,1,0:T(8,128)(2,1)S(1)} async-done(((bf16[64,10,128]{2,1,0:T(8,128)(2,1)}), bf16[64,10,128]{2,1,0:T(8,128)(2,1)S(1)}, u32[]{:S(2)}, u32[]{:S(2)}) %all-to-all-start.4) | async-done | bytes 163872 | tf_op jit(solution)/shard_map/all_to_all | solution.py:331
  318.3 6.9 %all-to-all-start.5 = ((bf16[64,10,128]{2,1,0:T(8,128)(2,1)}), bf16[64,10,128]{2,1,0:T(8,128)(2,1)S(1)}, u32[]{:S(2)}, u32[]{:S(2)}) async-start(bf16[64,10,128]{2,1,0:T(8,128)(2,1)} %broadcast_in_dim.118), calls=%async_computation.5 | async-start | bytes 524288 | tf_op jit(solution)/shard_map/all_to_all | solution.py:356
  326.2 17.3 %all-to-all-done.5 = bf16[64,10,128]{2,1,0:T(8,128)(2,1)S(1)} async-done(((bf16[64,10,128]{2,1,0:T(8,128)(2,1)}), bf16[64,10,128]{2,1,0:T(8,128)(2,1)S(1)}, u32[]{:S(2)}, u32[]{:S(2)}) %all-to-all-start.5) | async-done | bytes 163872 | tf_op jit(solution)/shard_map/all_to_all | solution.py:356
  343.5 0.8 fusion.11
  (113 shorter events, 11.0 us)
Async XLA Ops:
  7.2 7.9 %copy-start = (bf16[8192,128]{1,0:T(8,128)(2,1)S(1)}, bf16[8192,128]{1,0:T(8,128)(2,1)}, u32[]{:S(2)}) copy-start(bf16[8192,128]{1,0:T(8,128)(2,1)} %param.20) | copy-start | bytes 6291460
  7.2 7.8 %copy-start.15 = (s32[64,64]{1,0:T(8,128)S(1)}, s32[64,64]{1,0:T(8,128)}, u32[]{:S(2)}) copy-start(s32[64,64]{1,0:T(8,128)} %param.18) | copy-start | bytes 49156
  8.9 173.9 %copy-start.19 = (s32[64]{0:T(128)}, s32[64]{0:T(128)S(1)}, u32[]{:S(2)}) copy-start(s32[64]{0:T(128)S(1)} %fusion.33) | copy-start | bytes 772
  9.1 0.6 copy-start.16
  37.4 36.2 %copy-start.3 = (bf16[4096,128]{1,0:T(8,128)(2,1)S(1)}, bf16[4096,128]{1,0:T(8,128)(2,1)}, u32[]{:S(2)}) copy-start(bf16[4096,128]{1,0:T(8,128)(2,1)} %decode.1) | copy-start | bytes 3145732
  69.9 0.6 copy-start.11
  73.6 7.2 %copy-start.13 = (bf16[256,640]{1,0:T(8,128)(2,1)S(1)}, bf16[256,640]{1,0:T(8,128)(2,1)}, u32[]{:S(2)}) copy-start(bf16[256,640]{1,0:T(8,128)(2,1)} %param.12) | copy-start | bytes 983044
  75.3 84.7 %all-to-all-start.1 = ((bf16[64,64,128]{2,1,0:T(8,128)(2,1)}), bf16[64,64,128]{2,1,0:T(8,128)(2,1)S(1)}, u32[]{:S(2)}, u32[]{:S(2)}) async-start(bf16[64,64,128]{2,1,0:T(8,128)(2,1)} %gather_fusion.1), calls=%async_computation.1 | async-start | bytes 2097152 | tf_op jit(solution)/shard_map/all_to_all | solution.py:238
  79.9 80.0 %all-gather.4.cloned.1.call-start = ((), (), s32[]{:S(2)}) async-start(), calls=%async_computation.6 | async-start | bytes 1392640 | tf_op jit(solution)/shard_map/all_gather | solution.py:228
  80.7 161.3 %all-gather.6.cloned.1.call-start = ((), (), s32[]{:S(2)}) async-start(), calls=%async_computation.7 | async-start | bytes 6553600 | tf_op jit(solution)/shard_map/all_gather | solution.py:285
  83.1 21.2 %collective-permute-start.2 = (bf16[2,4,32,640]{3,2,0,1:T(8,128)(2,1)S(1)}, bf16[2,4,32,640]{3,2,0,1:T(8,128)(2,1)S(1)}, u32[]{:S(2)}, u32[]{:S(2)}) collective-permute-start(bf16[2,4,32,640]{3,2,0,1:T(8,128)(2,1)S(1)} %bitcast.123), channel_id=1, source_target_pairs={{0,384},{128,256},{256,128},{384,0},{1,385},{129,257},{257,129},{3... | collective-permute-start | bytes 983048 | tf_op jit(solution)/shard_map/ppermute | solution.py:24
  87.5 8.9 %collective-permute-start.3 = (bf16[512,128]{1,0:T(8,128)(2,1)}, bf16[512,128]{1,0:T(8,128)(2,1)S(1)}, u32[]{:S(2)}, u32[]{:S(2)}) collective-permute-start(bf16[512,128]{1,0:T(8,128)(2,1)} %param.15), channel_id=1, source_target_pairs={{0,1},{1,0},{2,3},{3,2},{4,5},{5,4},{6,7},{7,6},{8,9},{9,8},{10,11... | collective-permute-start | bytes 393224 | tf_op jit(solution)/shard_map/ppermute | solution.py:24
  92.0 15.5 %collective-permute-start.1 = (bf16[2,4,32,640]{3,2,0,1:T(8,128)(2,1)S(1)}, bf16[2,4,32,640]{3,2,0,1:T(8,128)(2,1)S(1)}, u32[]{:S(2)}, u32[]{:S(2)}) collective-permute-start(bf16[2,4,32,640]{3,2,0,1:T(8,128)(2,1)S(1)} %bitcast.124), channel_id=1, source_target_pairs={{0,256},{128,384},{256,0},{384,128},{1,257},{129,385},{257,1},{385... | collective-permute-start | bytes 983048 | tf_op jit(solution)/shard_map/ppermute | solution.py:24
  94.3 18.5 %collective-permute-start = (bf16[2,4,32,640]{3,2,0,1:T(8,128)(2,1)S(1)}, bf16[2,4,32,640]{3,2,0,1:T(8,128)(2,1)S(1)}, u32[]{:S(2)}, u32[]{:S(2)}) collective-permute-start(bf16[2,4,32,640]{3,2,0,1:T(8,128)(2,1)S(1)} %bitcast.125), channel_id=1, source_target_pairs={{0,128},{128,0},{256,384},{384,256},{1,129},{129,1},{257,385},{385... | collective-permute-start | bytes 983048 | tf_op jit(solution)/shard_map/ppermute | solution.py:24
  97.4 16.8 %collective-permute-start.6 = (bf16[2,512,128]{2,1,0:T(8,128)(2,1)S(1)}, bf16[2,512,128]{2,1,0:T(8,128)(2,1)S(1)}, u32[]{:S(2)}, u32[]{:S(2)}) collective-permute-start(bf16[2,512,128]{2,1,0:T(8,128)(2,1)S(1)} %maximum_select_fusion.1), channel_id=1, source_target_pairs={{0,6},{2,4},{4,2},{6,0},{1,7},{3,5},{5,3},{7,1},{8,14},{10,12},{12... | collective-permute-start | bytes 786440 | tf_op jit(solution)/shard_map/ppermute | solution.py:24
  101.8 12.4 %collective-permute-start.5 = (bf16[2,512,128]{2,1,0:T(8,128)(2,1)S(1)}, bf16[2,512,128]{2,1,0:T(8,128)(2,1)S(1)}, u32[]{:S(2)}, u32[]{:S(2)}) collective-permute-start(bf16[2,512,128]{2,1,0:T(8,128)(2,1)S(1)} %maximum_select_fusion.1), channel_id=1, source_target_pairs={{0,4},{2,6},{4,0},{6,2},{1,5},{3,7},{5,1},{7,3},{8,12},{10,14},{12... | collective-permute-start | bytes 786440 | tf_op jit(solution)/shard_map/ppermute | solution.py:24
  104.3 11.5 %collective-permute-start.4 = (bf16[2,512,128]{2,1,0:T(8,128)(2,1)S(1)}, bf16[2,512,128]{2,1,0:T(8,128)(2,1)S(1)}, u32[]{:S(2)}, u32[]{:S(2)}) collective-permute-start(bf16[2,512,128]{2,1,0:T(8,128)(2,1)S(1)} %maximum_select_fusion.1), channel_id=1, source_target_pairs={{0,2},{2,0},{4,6},{6,4},{1,3},{3,1},{5,7},{7,5},{8,10},{10,8},{12,... | collective-permute-start | bytes 786440 | tf_op jit(solution)/shard_map/ppermute | solution.py:24
  160.0 71.0 %all-to-all-start.2 = ((bf16[64,64,128]{2,1,0:T(8,128)(2,1)}), bf16[64,64,128]{2,1,0:T(8,128)(2,1)}, u32[]{:S(2)}, u32[]{:S(2)}) async-start(bf16[64,64,128]{2,1,0:T(8,128)(2,1)} %gather_fusion.2), calls=%async_computation.2 | async-start | bytes 2097152 | tf_op jit(solution)/shard_map/all_to_all | solution.py:268
  170.7 12.0 %copy-start.18 = (s32[1,64]{1,0:T(1,128)S(1)}, s32[1,64]{1,0:T(1,128)}, u32[]{:S(2)}) copy-start(s32[1,64]{1,0:T(1,128)} %param.16) | copy-start | bytes 772
  170.7 106.9 %all-gather.8.cloned.1.call-start = ((), (), s32[]{:S(2)}) async-start(), calls=%async_computation.8 | async-start | bytes 2359296 | tf_op jit(solution)/shard_map/all_gather | solution.py:287
  170.8 14.2 %copy-start.6 = (bf16[640,1024]{0,1:T(8,128)(2,1)S(1)}, bf16[640,1024]{0,1:T(8,128)(2,1)}, u32[]{:S(2)}) copy-start(bf16[640,1024]{0,1:T(8,128)(2,1)} %all-gather.4.cloned.1.call-done) | copy-start | bytes 3932164
  170.8 14.2 %copy-start.9 = (bf16[2,4,4,32,640]{4,3,2,1,0:T(8,128)(2,1)S(1)}, bf16[2,4,4,32,640]{4,3,2,1,0:T(8,128)(2,1)}, u32[]{:S(2)}) copy-start(bf16[2,4,4,32,640]{4,3,2,1,0:T(8,128)(2,1)} %copy.60) | copy-start | bytes 3932164
  173.5 11.5 %collective-permute-start.7 = (bf16[512,1024]{1,0:T(8,128)(2,1)S(1)}, bf16[512,1024]{1,0:T(8,128)(2,1)S(1)}, u32[]{:S(2)}, u32[]{:S(2)}) collective-permute-start(bf16[512,1024]{1,0:T(8,128)(2,1)S(1)} %convolution_convert_fusion), channel_id=1, source_target_pairs={{0,1},{1,0},{2,3},{3,2},{4,5},{5,4},{6,7},{7,6},{8,9},{9,8},{10,11... | collective-permute-start | bytes 3145736 | tf_op jit(solution)/shard_map/ppermute | solution.py:24
  187.3 30.6 %copy-start.12 = (s32[64,1,128]{2,1,0:T(1,128)S(1)}, s32[64,1,128]{2,1,0:T(1,128)}, u32[]{:S(2)}) copy-start(s32[64,1,128]{2,1,0:T(1,128)} %copy-done.11) | copy-start | bytes 98308
  187.3 30.7 %copy-start.17 = (s32[2,64]{1,0:T(2,128)S(1)}, s32[2,64]{1,0:T(2,128)}, u32[]{:S(2)}) copy-start(s32[2,64]{1,0:T(2,128)} %copy-done.16) | copy-start | bytes 1540
  188.2 15.7 %collective-permute-start.10 = (bf16[4,32,1024]{2,1,0:T(8,128)(2,1)}, bf16[4,32,1024]{2,1,0:T(8,128)(2,1)}, u32[]{:S(2)}, u32[]{:S(2)}) collective-permute-start(bf16[4,32,1024]{2,1,0:T(8,128)(2,1)} %bitcast.33), channel_id=1, source_target_pairs={{0,6},{2,4},{4,2},{6,0},{1,7},{3,5},{5,3},{7,1},{8,14},{10,12},{12... | collective-permute-start | bytes 786440 | tf_op jit(solution)/shard_map/ppermute | solution.py:24
  192.4 11.5 %collective-permute-start.9 = (bf16[4,32,1024]{2,1,0:T(8,128)(2,1)}, bf16[4,32,1024]{2,1,0:T(8,128)(2,1)}, u32[]{:S(2)}, u32[]{:S(2)}) collective-permute-start(bf16[4,32,1024]{2,1,0:T(8,128)(2,1)} %bitcast.32), channel_id=1, source_target_pairs={{0,4},{2,6},{4,0},{6,2},{1,5},{3,7},{5,1},{7,3},{8,12},{10,14},{12... | collective-permute-start | bytes 786440 | tf_op jit(solution)/shard_map/ppermute | solution.py:24
  195.0 12.0 %collective-permute-start.8 = (bf16[4,32,1024]{2,1,0:T(8,128)(2,1)S(1)}, bf16[4,32,1024]{2,1,0:T(8,128)(2,1)}, u32[]{:S(2)}, u32[]{:S(2)}) collective-permute-start(bf16[4,32,1024]{2,1,0:T(8,128)(2,1)S(1)} %bitcast.141), channel_id=1, source_target_pairs={{0,2},{2,0},{4,6},{6,4},{1,3},{3,1},{5,7},{7,5},{8,10},{10,8},{12,... | collective-permute-start | bytes 786440 | tf_op jit(solution)/shard_map/ppermute | solution.py:24
  208.3 20.0 %copy-start.7 = (bf16[32,4096]{1,0:T(8,128)(2,1)S(1)}, bf16[32,4096]{1,0:T(8,128)(2,1)}, u32[]{:S(2)}) copy-start(bf16[32,4096]{1,0:T(8,128)(2,1)} %param.11) | copy-start | bytes 786436
  208.3 20.8 %copy-start.14 = (f32[4096]{0:T(1024)S(1)}, f32[4096]{0:T(1024)}, u32[]{:S(2)}) copy-start(f32[4096]{0:T(1024)} %param.14) | copy-start | bytes 49156
  209.0 9.3 %collective-permute-start.13 = (bf16[32,1024]{1,0:T(8,128)(2,1)}, bf16[32,1024]{1,0:T(8,128)(2,1)}, u32[]{:S(2)}, u32[]{:S(2)}) collective-permute-start(bf16[32,1024]{1,0:T(8,128)(2,1)} %get-tuple-element.53), channel_id=1, source_target_pairs={{0,384},{128,256},{256,128},{384,0},{1,385},{129,257},{257,129},{3... | collective-permute-start | bytes 196616 | tf_op jit(solution)/shard_map/ppermute | solution.py:24
  213.5 8.8 %collective-permute-start.12 = (bf16[32,1024]{1,0:T(8,128)(2,1)}, bf16[32,1024]{1,0:T(8,128)(2,1)}, u32[]{:S(2)}, u32[]{:S(2)}) collective-permute-start(bf16[32,1024]{1,0:T(8,128)(2,1)} %get-tuple-element.54), channel_id=1, source_target_pairs={{0,256},{128,384},{256,0},{384,128},{1,257},{129,385},{257,1},{385... | collective-permute-start | bytes 196616 | tf_op jit(solution)/shard_map/ppermute | solution.py:24
  215.8 7.5 %collective-permute-start.11 = (bf16[32,1024]{1,0:T(8,128)(2,1)}, bf16[32,1024]{1,0:T(8,128)(2,1)}, u32[]{:S(2)}, u32[]{:S(2)}) collective-permute-start(bf16[32,1024]{1,0:T(8,128)(2,1)} %get-tuple-element.55), channel_id=1, source_target_pairs={{0,128},{128,0},{256,384},{384,256},{1,129},{129,1},{257,385},{385... | collective-permute-start | bytes 196616 | tf_op jit(solution)/shard_map/ppermute | solution.py:24
  228.2 0.8 copy-start.1
  230.9 8.5 %copy-start.2 = (f32[4,4,8,1024]{3,2,0,1:T(8,128)S(1)}, f32[4,4,8,1024]{3,2,0,1:T(8,128)}, u32[]{:S(2)}) copy-start(f32[4,4,8,1024]{3,2,0,1:T(8,128)} %copy-done.1) | copy-start | bytes 1572868
  230.9 8.5 %copy-start.4 = (bf16[4,2,512,128]{3,2,1,0:T(8,128)(2,1)S(1)}, bf16[4,2,512,128]{3,2,1,0:T(8,128)(2,1)}, u32[]{:S(2)}) copy-start(bf16[4,2,512,128]{3,2,1,0:T(8,128)(2,1)} %gather_fusion.4) | copy-start | bytes 3145732
  231.0 10.0 %copy-start.8 = (bf16[32,4096]{1,0:T(8,128)(2,1)S(1)}, bf16[32,4096]{1,0:T(8,128)(2,1)}, u32[]{:S(2)}) copy-start(bf16[32,4096]{1,0:T(8,128)(2,1)} %param.11) | copy-start | bytes 786436
  241.0 36.7 %copy-start.5 = (bf16[4,2,512,128]{3,2,1,0:T(8,128)(2,1)S(1)}, bf16[4,2,512,128]{3,2,1,0:T(8,128)(2,1)}, u32[]{:S(2)}) copy-start(bf16[4,2,512,128]{3,2,1,0:T(8,128)(2,1)} %gather_fusion.4) | copy-start | bytes 3145732
  242.7 11.9 %all-to-all-start.3 = ((bf16[8,32,256]{2,1,0:T(8,128)(2,1)}), bf16[8,32,256]{2,1,0:T(8,128)(2,1)S(1)}, u32[]{:S(2)}, u32[]{:S(2)}) async-start(bf16[8,32,256]{2,1,0:T(8,128)(2,1)} %broadcast_in_dim.114), calls=%async_computation.3 | async-start | bytes 262144 | tf_op jit(solution)/shard_map/all_to_all | solution.py:292
  254.6 25.5 %copy-start.10 = (bf16[8,32,256]{2,1,0:T(8,128)(2,1)}, bf16[8,32,256]{2,1,0:T(8,128)(2,1)S(1)}, u32[]{:S(2)}) copy-start(bf16[8,32,256]{2,1,0:T(8,128)(2,1)S(1)} %all-to-all-done.3) | copy-start | bytes 393220
  282.1 35.2 %all-to-all-start.4 = ((bf16[64,10,128]{2,1,0:T(8,128)(2,1)}), bf16[64,10,128]{2,1,0:T(8,128)(2,1)S(1)}, u32[]{:S(2)}, u32[]{:S(2)}) async-start(bf16[64,10,128]{2,1,0:T(8,128)(2,1)} %pad_maximum_fusion.3), calls=%async_computation.4 | async-start | bytes 524288 | tf_op jit(solution)/shard_map/all_to_all | solution.py:331
  303.3 22.2 %copy-start.20 = (s32[64]{0:T(128)S(1)}, s32[64]{0:T(128)}, u32[]{:S(2)}) copy-start(s32[64]{0:T(128)} %copy-done.19) | copy-start | bytes 772
  318.3 25.1 %all-to-all-start.5 = ((bf16[64,10,128]{2,1,0:T(8,128)(2,1)}), bf16[64,10,128]{2,1,0:T(8,128)(2,1)S(1)}, u32[]{:S(2)}, u32[]{:S(2)}) async-start(bf16[64,10,128]{2,1,0:T(8,128)(2,1)} %broadcast_in_dim.118), calls=%async_computation.5 | async-start | bytes 524288 | tf_op jit(solution)/shard_map/all_to_all | solution.py:356
Sparse Core Ops, SparseCore 0:
  82.8 77.0 all-gather.3
  162.0 78.6 all-gather.5
  243.4 34.1 all-gather.7

commit v4 on v3

--- a/solution.py
+++ b/solution.py
@@ -84,11 +84,10 @@
     )(buckets, low_bytes, high_bytes, rows)
 
 
-def score_kernel(docs_a, docs_b, embedded_ref, inv_rms_ref, spans, flags, scores, packet, weights, totals):
+def score_kernel(docs, embedded_ref, inv_rms_ref, spans, flags, scores, packet, weights, totals):
     slots, queries_n = totals.shape
-    half = slots // 2
-    tokens = docs_a.shape[0] // half
-    features = docs_a.shape[1]
+    tokens = docs.shape[0] // slots
+    features = docs.shape[1]
     embedded = embedded_ref[...]
     inv_rms = inv_rms_ref[...]
     inverse = lax.rsqrt(jnp.sum(embedded * embedded, axis=1, keepdims=True) + EPS)
@@ -96,26 +95,24 @@
     group = 8
     token = lax.broadcasted_iota(I32, (tokens, queries_n), 0)
 
-    for part, docs in enumerate((docs_a, docs_b)):
-
-        @pl.loop(0, half // group)
-        def _(i, part=part, docs=docs):
-            at = pl.multiple_of(i * (group * tokens), group * tokens)
-            slot0 = pl.multiple_of(part * half + i * group, group)
-            similar = lax.dot_general(
-                docs[pl.ds(at, group * tokens), :],
-                queries,
-                (((1,), (1,)), ((), ())),
-                preferred_element_type=F32,
-            )
-            sizes = spans[pl.ds(slot0, group), :]
-            sums = []
-            for g in range(group):
-                one = jnp.exp(similar[g * tokens : (g + 1) * tokens] / TEMPER)
-                one = jnp.where(token < sizes[g : g + 1, :], one, 0.0)
-                weights[pl.ds(slot0 * tokens + g * tokens, tokens), :] = one
-                sums.append(jnp.sum(one, axis=0, keepdims=True))
-            totals[pl.ds(slot0, group), :] = jnp.concatenate(sums, axis=0)
+    @pl.loop(0, slots // group)
+    def _(i):
+        at = pl.multiple_of(i * (group * tokens), group * tokens)
+        slot0 = pl.multiple_of(i * group, group)
+        similar = lax.dot_general(
+            docs[pl.ds(at, group * tokens), :],
+            queries,
+            (((1,), (1,)), ((), ())),
+            preferred_element_type=F32,
+        )
+        sizes = spans[pl.ds(slot0, group), :]
+        sums = []
+        for g in range(group):
+            one = jnp.exp(similar[g * tokens : (g + 1) * tokens] / TEMPER)
+            one = jnp.where(token < sizes[g : g + 1, :], one, 0.0)
+            weights[pl.ds(at + g * tokens, tokens), :] = one
+            sums.append(jnp.sum(one, axis=0, keepdims=True))
+        totals[pl.ds(slot0, group), :] = jnp.concatenate(sums, axis=0)
 
     all_totals = totals[...]
     slot_scores = TEMPER * jnp.sum(jnp.log(all_totals), axis=1, keepdims=True)
@@ -127,27 +124,23 @@
     seeds = LOSS_SCALE * (share - jnp.where(positive, 1.0, 0.0))
     totals[...] = seeds / all_totals
 
-    grad_q = jnp.zeros((queries_n, features), F32)
-    for part, docs in enumerate((docs_a, docs_b)):
-
-        def add(i, total, part=part, docs=docs):
-            at = pl.multiple_of(i * (group * tokens), group * tokens)
-            slot0 = pl.multiple_of(part * half + i * group, group)
-            factors = totals[pl.ds(slot0, group), :]
-            mixing = [
-                weights[pl.ds(slot0 * tokens + g * tokens, tokens), :] * factors[g : g + 1, :]
-                for g in range(group)
-            ]
-            mixing = jnp.concatenate(mixing, axis=0).astype(BF16)
-            return total + lax.dot_general(
-                mixing,
-                docs[pl.ds(at, group * tokens), :],
-                (((0,), (0,)), ((), ())),
-                preferred_element_type=F32,
-            )
-
-        grad_q = lax.fori_loop(0, half // group, add, grad_q)
-
+    def add(i, total):
+        at = pl.multiple_of(i * (group * tokens), group * tokens)
+        slot0 = pl.multiple_of(i * group, group)
+        factors = totals[pl.ds(slot0, group), :]
+        mixing = [
+            weights[pl.ds(at + g * tokens, tokens), :] * factors[g : g + 1, :]
+            for g in range(group)
+        ]
+        mixing = jnp.concatenate(mixing, axis=0).astype(BF16)
+        return total + lax.dot_general(
+            mixing,
+            docs[pl.ds(at, group * tokens), :],
+            (((0,), (0,)), ((), ())),
+            preferred_element_type=F32,
+        )
+
+    grad_q = lax.fori_loop(0, slots // group, add, jnp.zeros((queries_n, features), F32))
     along = jnp.sum(embedded * grad_q, axis=1, keepdims=True)
     grad_embedded = (inverse * grad_q - inverse * inverse * inverse * embedded * along).astype(BF16)
     packet[:, 0:features] = grad_embedded
@@ -162,13 +155,13 @@
     packet[:, features : 2 * features] = extra.astype(BF16)
 
 
-def score(docs_a, docs_b, embedded, inv_rms, spans, flags):
+def score(docs, embedded, inv_rms, spans, flags):
     slots = flags.shape[0]
     queries_n, features = embedded.shape
-    count = docs_a.shape[0] + docs_b.shape[0]
+    count = docs.shape[0]
     return pl.pallas_call(
         score_kernel,
-        in_specs=[VMEM] * 6,
+        in_specs=[VMEM] * 5,
         out_specs=[VMEM] * 2,
         out_shape=[
             jax.ShapeDtypeStruct((slots, 1), F32),
@@ -179,8 +172,13 @@
             pltpu.VMEM((slots, queries_n), F32),
         ],
         compiler_params=pltpu.CompilerParams(vmem_limit_bytes=32 * 1024 * 1024),
+        cost_estimate=pl.CostEstimate(
+            flops=4 * count * queries_n * features,
+            bytes_accessed=30_000_000,
+            transcendentals=count * queries_n,
+        ),
         name="score",
-    )(docs_a, docs_b, embedded, inv_rms, spans, flags)
+    )(docs, embedded, inv_rms, spans, flags)
 
 
 def local(
@@ -210,7 +208,7 @@
     order = jnp.arange(cand_count, dtype=I32)
     earlier = (owners[None, :] == owners[:, None]) & (order[None, :] < order[:, None])
     rank = jnp.sum(earlier.astype(I32), axis=1)
-    position = rank * shards + owners
+    position = owners * cap + rank
     slot_at = jnp.arange(slots, dtype=I32)
     placed = position[None, :] == slot_at[:, None]
     request = jnp.sum(jnp.where(placed, local_ids[None, :], 0), axis=1)
@@ -219,7 +217,7 @@
     note = jnp.concatenate(
         [
             jnp.broadcast_to(lengths[None, :], (shards, per_shard)),
-            request.reshape(cap, shards).T,
+            request.reshape(shards, cap),
             jnp.zeros((shards, 128 - per_shard - cap), I32),
         ],
         axis=1,
@@ -227,20 +225,18 @@
 
     proj_z = lax.all_gather(out_proj, "z", axis=1, tiled=True)
     documents = decode_all(centroid_ids, residual_codes, centroids, buckets)
-    note, documents = lax.optimization_barrier((note, documents))
     notes = lax.all_to_all(note, DP, 0, 0, tiled=True)
     documents = documents.reshape(per_shard, doc_len, feature_dim)
-    chosen_a = rows_of(documents, notes[:, per_shard])
-    chosen_b = rows_of(documents, notes[:, per_shard + 1])
-    chosen_a, chosen_b, context, colbert_head = lax.optimization_barrier(
-        (chosen_a, chosen_b, context, colbert_head)
-    )
-    got_a = lax.all_to_all(chosen_a, DP, 0, 0, tiled=True).reshape(shards * doc_len, feature_dim)
+    chosen = rows_of(documents, notes[:, per_shard : per_shard + cap].reshape(slots))
+    chosen, context, colbert_head = lax.optimization_barrier((chosen, context, colbert_head))
+    got_docs = lax.all_to_all(
+        chosen.reshape(shards, cap * doc_len, feature_dim), DP, 0, 0, tiled=True
+    ).reshape(slots * doc_len, feature_dim)
     spans = jnp.sum(
         jnp.where(
             jnp.arange(per_shard, dtype=I32)[None, None, :]
-            == request.reshape(cap, shards)[:, :, None],
-            notes[None, :, :per_shard],
+            == request.reshape(shards, cap)[:, :, None],
+            notes[:, None, :per_shard],
             0,
         ),
         axis=2,
@@ -263,17 +259,15 @@
     head_full = unxor(
         jnp.stack([head_pair] + [swap(head_pair, "x", X, step) for step in range(1, X)]), here_x
     ).reshape(width, feature_dim)
-    by_y, head_full, got_a, proj_z = lax.optimization_barrier((by_y, head_full, got_a, proj_z))
-
-    got_b = lax.all_to_all(chosen_b, DP, 0, 0, tiled=True).reshape(shards * doc_len, feature_dim)
+    by_y, head_full, proj_z = lax.optimization_barrier((by_y, head_full, proj_z))
+
     away = jnp.dot(by_y[1], proj_z, preferred_element_type=F32).astype(BF16)
     away = swap(away, "c", C, 1)
     stay = jnp.dot(by_y[0], proj_z, preferred_element_type=F32).astype(BF16)
     pair = (stay.astype(F32) + away.astype(F32)).reshape(X, Y, seq_rows, width // Y)
-    for_x = pair.astype(BF16)
-    row = pair[0]
+    pieces, row = [pair[step].astype(BF16) for step in range(1, X)], pair[0]
     for step in range(1, X):
-        row = row + swap(for_x[step], "x", X, step).astype(F32)
+        row = row + swap(pieces[step - 1], "x", X, step).astype(F32)
     for_y = row.astype(BF16)
     columns = [for_y[0]] + [swap(for_y[step], "y", Y, step) for step in range(1, Y)]
     columns = unxor(jnp.stack(columns), here_y)
@@ -283,15 +277,25 @@
     scaled_sum = summed * inv_rms
     normed = (scaled_sum * norm_gain).astype(BF16)
     proj_full = lax.all_gather(proj_z, "y", axis=1, tiled=True)
-    unit, proj_full = lax.optimization_barrier((scaled_sum.astype(BF16), proj_full))
-    unit_all = lax.all_gather(unit, TENSOR, axis=0, tiled=True)
+    unit = scaled_sum.astype(BF16)
+    unit = jnp.stack([unit, swap(unit, "c", C, 1)])
+    units = [unit] + [swap(unit, "x", X, step) for step in range(1, X)]
+    scaled_sum, normed, got_docs = lax.optimization_barrier((scaled_sum, normed, got_docs))
     embedded = jnp.dot(normed, head_full, preferred_element_type=F32)
 
-    slot_scores, packet = score(got_a, got_b, embedded, inv_rms, spans, flags)
+    slot_scores, packet = score(got_docs, embedded, inv_rms, spans, flags)
     scores = jnp.sum(jnp.where(placed, slot_scores, 0.0), axis=0)[None, :]
+    packet, units, proj_full = lax.optimization_barrier((packet, units, proj_full))
+    unit_all = jnp.stack(units).reshape(X * C * seq_rows, width)
     packets = lax.all_to_all(
         jnp.broadcast_to(packet, (X * C,) + packet.shape), TENSOR, 0, 0, tiled=True
-    ).reshape(X * C * seq_rows, 2 * feature_dim)
+    )
+
+    def reorder(rows):
+        rows = rows.reshape(X * C, seq_rows, rows.shape[-1])
+        return unxor(rows, here_x * C + here_c).reshape(X * C * seq_rows, rows.shape[-1])
+
+    packets = reorder(packets)
     ge_all = packets[:, :feature_dim]
     extra = packets[:, feature_dim : feature_dim + 4].astype(F32)
     pull_all = (extra[:, 0:1] + extra[:, 1:2]) * (1.0 / width)
@@ -321,8 +325,8 @@
         )
 
     def unbundle(rows):
-        rows = rows.astype(F32)
-        return rows[:, :share], rows[:, share] + rows[:, share + 1]
+        pair = rows[:, share].astype(F32) + rows[:, share + 1].astype(F32)
+        return rows[:, :share].astype(F32), pair
 
     gain_term = jnp.concatenate(
         [gain_term.reshape(lines, feature_dim), jnp.zeros((shards - lines, feature_dim), F32)]
@@ -331,6 +335,7 @@
     first = unbundle(lax.all_to_all(first, DP, 0, 0, tiled=True))
     second = bundle(*[jnp.sum(part, axis=0, keepdims=True) for part in first])
 
+    packet, packets = lax.optimization_barrier((packet, packets))
     grad_embedded = packet[:, :feature_dim]
     grad_normed = lax.dot_general(
         grad_embedded, head_full, (((1,), (1,)), ((), ())), preferred_element_type=F32
@@ -351,6 +356,7 @@
         )
         - pull_all * pulled
     ).astype(BF16)
+    context_grad = reorder(context_grad)
     second, context_grad = lax.optimization_barrier((second, context_grad))
 
     second = lax.all_to_all(

time: 355 us -> 312 us (0.88)
  waiting for transfers between devices: 117 us -> 62.4 us
  starting transfers between devices: 93.9 us -> 131 us
  blocking collectives: 32.5 us -> 0 us
  other arithmetic: 16.3 us -> 22.4 us
    all_gather x1, waiting for transfers between devices: 40.1 us -> 2.17 us  [local(): proj_z = lax.all_gather(out_proj, 'z', axis=1, tiled=True)]
    all_to_all x1 -> x0, blocking collectives: 32.5 us -> none  [local(): notes = lax.all_to_all(note, DP, 0, 0, tiled=True)]
    all_gather x1 -> x0, waiting for transfers between devices: 22.8 us -> none  [local(): unit_all = lax.all_gather(unit, TENSOR, axis=0, tiled=True)]
    ppermute x14 -> x18, starting transfers between devices: 49.4 us -> 70.1 us  [swap(): return lax.ppermute(values, axis, [(i, i ^ step) for i in range(size)])]
    all_to_all x2, starting transfers between devices: 15.4 us -> 34.3 us  [the longest x1 19.3 us: local(): notes = lax.all_to_all(note, DP, 0, 0, tiled=True)]
    ppermute x14 -> x18, waiting for transfers between devices: 22.6 us -> 36.1 us  [swap(): return lax.ppermute(values, axis, [(i, i ^ step) for i in range(size)])]
    another operation x0 -> x2, other arithmetic: none -> 5.05 us  [the longest x1 3.12 us: local(): unit_all = jnp.stack(units).reshape(X * C * seq_rows, width)]
    all_to_all x1, waiting for transfers between devices: 8.29 us -> 4.11 us  [local(): first = unbundle(lax.all_to_all(first, DP, 0, 0, tiled=True))]
  transfers between devices with their start and end apart: 22 -> 25, of which waited for: 12 -> 12; matrix products, arithmetic and copies ran while one was open for 12% -> 22% of each run, Pallas kernels for 2% -> 5%
where the time goes in v4:
time: 312 us; the launch traced here: 309 us
  starting transfers between devices  131 us (42%)
  waiting for transfers between devices  62.4 us (20%)
  local copies, waits for them, and re-layouts  36.1 us (12%)
  matrix products  25.6 us (8%)
  other arithmetic  22.4 us (7%)
  Pallas kernels  15.9 us (5%)
  between operations  14.8 us (5%)
    ppermute x18, starting transfers between devices, swap(): return lax.ppermute(values, axis, [(i, i ^ step) for i in range(size)])  70.1 us
    ppermute x18, waiting for transfers between devices, swap(): return lax.ppermute(values, axis, [(i, i ^ step) for i in range(size)])  36.1 us
    gather x7, local copies, waits for them, and re-layouts, rows_of(): return values.at[index].get(mode='promise_in_bounds')  23 us
    all_to_all x1, starting transfers between devices, local(): notes = lax.all_to_all(note, DP, 0, 0, tiled=True)  19.3 us
    all_to_all x1, waiting for transfers between devices, local(): lax.all_to_all(jnp.broadcast_to(second, (shards,) + second.shape[1:]), DP...  17.1 us
    all_to_all x1, starting transfers between devices, local(): lax.all_to_all(chosen.reshape(shards, cap * doc_len, feature_dim), DP, 0,...  15 us
    all_to_all x1, starting transfers between devices, local(): first = unbundle(lax.all_to_all(first, DP, 0, 0, tiled=True))  11.5 us
    all_to_all x1, starting transfers between devices, local(): lax.all_to_all(jnp.broadcast_to(second, (shards,) + second.shape[1:]), DP...  10.7 us
  transfers between devices with their start and end apart: 25, of which 12 were waited for; matrix products, arithmetic and copies ran while one was open for 22% of the time, Pallas kernels for 5%

profile of v4, /device:TPU:1, one launch (start us, length us, event | category | flops | bytes accessed | tf_op | source)
XLA Modules:
  0.0 308.5 jit_solution(17310922069033969708)
XLA Ops:
  10.5 19.3 %all-to-all-start = ((s32[64,1,128]{2,1,0:T(1,128)}), s32[64,1,128]{2,1,0:T(1,128)S(1)}, u32[]{:S(2)}, u32[]{:S(2)}) async-start(s32[64,1,128]{2,1,0:T(1,128)} %bitcast.7), calls=%async_computation | async-start | bytes 65536 | tf_op jit(solution)/shard_map/all_to_all | solution.py:228
  30.6 0.8 reshape.373
  31.5 1.0 and_convert_fusion
  32.5 1.9 reshape.371.low_bytes
  34.4 1.8 reshape.372.high_bytes
  36.2 14.9 %gather_fusion = bf16[4096,128]{1,0:T(8,128)(2,1)} fusion(bf16[8192,128]{1,0:T(8,128)(2,1)S(1)} %copy-done, s32[4096]{0:T(1024)S(1)} %broadcast_clamp_fusion), kind=kCustom, calls=%fused_computation | custom fusion | bytes 2113536 | tf_op jit(solution)/shard_map/gather | solution.py:28
  51.1 7.2 %decode.1 = bf16[4096,128]{1,0:T(8,128)(2,1)} custom-call(f32[4]{0:T(128)} %buckets.1, bf16[4096,16]{1,0:T(8,128)(2,1)} %reshape.371.low_bytes, bf16[4096,16]{1,0:T(8,128)(2,1)} %reshape.372.high_bytes, bf16[4096,128]{1,0:T(8,128)(2,1)} %gather_fusion), custom_call_target="tpu_custom_call" | custom-call | tf_op jit(solution)/shard_map/decode/pallas_call | solution.py:72
  58.6 3.4 %gather_fusion.1 = bf16[128,64,128]{2,1,0:T(8,128)(2,1)} fusion(bf16[64,64,128]{2,1,0:T(8,128)(2,1)} %bitcast.125, s32[1024]{0:T(1024)S(1)} %pad_clamp_fusion.3), kind=kCustom, calls=%fused_computation.1 | custom fusion | bytes 4194816 | tf_op jit(solution)/shard_map/gather | solution.py:28
  61.9 15.0 %all-to-all-start.1 = ((bf16[64,128,128]{2,1,0:T(8,128)(2,1)}), bf16[64,128,128]{2,1,0:T(8,128)(2,1)}, u32[]{:S(2)}, u32[]{:S(2)}) async-start(bf16[64,128,128]{2,1,0:T(8,128)(2,1)} %bitcast.130), calls=%async_computation.1 | async-start | bytes 4194304 | tf_op jit(solution)/shard_map/all_to_all | solution.py:232
  77.7 4.3 %collective-permute-start.2 = (bf16[2,4,32,640]{3,2,0,1:T(8,128)(2,1)S(1)}, bf16[2,4,32,640]{3,2,0,1:T(8,128)(2,1)S(1)}, u32[]{:S(2)}, u32[]{:S(2)}) collective-permute-start(bf16[2,4,32,640]{3,2,0,1:T(8,128)(2,1)S(1)} %bitcast.137), channel_id=1, source_target_pairs={{0,384},{128,256},{256,128},{384,0},{1,385},{129,257},{257,129},{3... | collective-permute-start | bytes 983048 | tf_op jit(solution)/shard_map/ppermute | solution.py:24
  82.0 4.0 %collective-permute-start.3 = (bf16[512,128]{1,0:T(8,128)(2,1)S(1)}, bf16[512,128]{1,0:T(8,128)(2,1)S(1)}, u32[]{:S(2)}, u32[]{:S(2)}) collective-permute-start(bf16[512,128]{1,0:T(8,128)(2,1)S(1)} %copy-done.3), channel_id=1, source_target_pairs={{0,1},{1,0},{2,3},{3,2},{4,5},{5,4},{6,7},{7,6},{8,9},{9,8},{10,11... | collective-permute-start | bytes 393224 | tf_op jit(solution)/shard_map/ppermute | solution.py:24
  85.9 2.3 collective-permute-start.1
  88.2 2.1 collective-permute-start
  90.4 4.4 %collective-permute-start.6 = (bf16[2,512,128]{2,1,0:T(8,128)(2,1)S(1)}, bf16[2,512,128]{2,1,0:T(8,128)(2,1)S(1)}, u32[]{:S(2)}, u32[]{:S(2)}) collective-permute-start(bf16[2,512,128]{2,1,0:T(8,128)(2,1)S(1)} %maximum_select_fusion.1), channel_id=1, source_target_pairs={{0,6},{2,4},{4,2},{6,0},{1,7},{3,5},{5,3},{7,1},{8,14},{10,12},{12... | collective-permute-start | bytes 786440 | tf_op jit(solution)/shard_map/ppermute | solution.py:24
  94.8 2.4 collective-permute-start.5
  97.3 3.3 %collective-permute-start.4 = (bf16[2,512,128]{2,1,0:T(8,128)(2,1)S(1)}, bf16[2,512,128]{2,1,0:T(8,128)(2,1)S(1)}, u32[]{:S(2)}, u32[]{:S(2)}) collective-permute-start(bf16[2,512,128]{2,1,0:T(8,128)(2,1)S(1)} %maximum_select_fusion.1), channel_id=1, source_target_pairs={{0,2},{2,0},{4,6},{6,4},{1,3},{3,1},{5,7},{7,5},{8,10},{10,8},{12,... | collective-permute-start | bytes 786440 | tf_op jit(solution)/shard_map/ppermute | solution.py:24
  100.6 7.0 %collective-permute-done = bf16[2,4,32,640]{3,2,0,1:T(8,128)(2,1)S(1)} collective-permute-done((bf16[2,4,32,640]{3,2,0,1:T(8,128)(2,1)S(1)}, bf16[2,4,32,640]{3,2,0,1:T(8,128)(2,1)S(1)}, u32[]{:S(2)}, u32[]{:S(2)}) %collective-permute-start) | collective-permute-done | bytes 327712 | tf_op jit(solution)/shard_map/ppermute | solution.py:24
  107.8 1.2 copy.48
  109.2 1.6 gather_fusion.3
  110.8 2.2 all-gather.3.cloned.1.call-done
  113.0 3.6 %convolution_convert_fusion = bf16[512,1024]{1,0:T(8,128)(2,1)} fusion(bf16[640,1024]{0,1:T(8,128)(2,1)} %all-gather.3.cloned.1.call-done, bf16[2,512,640]{2,1,0:T(8,128)(2,1)} %bitcast.131), kind=kOutput, calls=%fused_computation.13 | convolution fusion | flops 671612928 | bytes 3014656 | tf_op jit(solution)/shard_map/dot_general | solution.py:264
  116.7 13.3 %collective-permute-start.7 = (bf16[512,1024]{1,0:T(8,128)(2,1)}, bf16[512,1024]{1,0:T(8,128)(2,1)}, u32[]{:S(2)}, u32[]{:S(2)}) collective-permute-start(bf16[512,1024]{1,0:T(8,128)(2,1)} %convolution_convert_fusion), channel_id=1, source_target_pairs={{0,1},{1,0},{2,3},{3,2},{4,5},{5,4},{6,7},{7,6},{8,9},{9,8},{10,11... | collective-permute-start | bytes 3145736 | tf_op jit(solution)/shard_map/ppermute | solution.py:24
  130.0 2.6 collective-permute-done.7
  132.6 3.7 %fusion.37 = (bf16[512,1024]{1,0:T(8,128)(2,1)S(1)}, f32[512,1024]{1,0:T(8,128)}) fusion(bf16[512,1024]{1,0:T(8,128)(2,1)} %collective-permute-done.7, bf16[640,1024]{0,1:T(8,128)(2,1)S(1)} %copy-done.1, bf16[2,512,640]{2,1,0:T(8,128)(2,1)} %bitcast.132), kind=kOutput, calls=%fused_computation.125 | convolution fusion | flops 673710080 | bytes 6160384 | tf_op jit(solution)/shard_map/dot_general | solution.py:266
  136.4 5.2 %collective-permute-start.10 = (bf16[4,32,1024]{2,1,0:T(8,128)(2,1)S(1)}, bf16[4,32,1024]{2,1,0:T(8,128)(2,1)S(1)}, u32[]{:S(2)}, u32[]{:S(2)}) collective-permute-start(bf16[4,32,1024]{2,1,0:T(8,128)(2,1)S(1)} %bitcast.159), channel_id=1, source_target_pairs={{0,6},{2,4},{4,2},{6,0},{1,7},{3,5},{5,3},{7,1},{8,14},{10,12},{12... | collective-permute-start | bytes 786440 | tf_op jit(solution)/shard_map/ppermute | solution.py:24
  141.6 2.4 collective-permute-start.9
  143.9 2.0 collective-permute-start.8
  146.1 1.1 slice.131
  147.2 5.5 %collective-permute-done.10 = bf16[4,32,1024]{2,1,0:T(8,128)(2,1)S(1)} collective-permute-done((bf16[4,32,1024]{2,1,0:T(8,128)(2,1)S(1)}, bf16[4,32,1024]{2,1,0:T(8,128)(2,1)S(1)}, u32[]{:S(2)}, u32[]{:S(2)}) %collective-permute-start.10) | collective-permute-done | bytes 262176 | tf_op jit(solution)/shard_map/ppermute | solution.py:24
  152.8 3.1 %collective-permute-done.8 = bf16[4,32,1024]{2,1,0:T(8,128)(2,1)} collective-permute-done((bf16[4,32,1024]{2,1,0:T(8,128)(2,1)S(1)}, bf16[4,32,1024]{2,1,0:T(8,128)(2,1)}, u32[]{:S(2)}, u32[]{:S(2)}) %collective-permute-start.8) | collective-permute-done | bytes 262176 | tf_op jit(solution)/shard_map/ppermute | solution.py:24
  155.9 1.1 add_convert_fusion
  157.0 5.9 %collective-permute-start.13 = (bf16[32,1024]{1,0:T(8,128)(2,1)S(1)}, bf16[32,1024]{1,0:T(8,128)(2,1)S(1)}, u32[]{:S(2)}, u32[]{:S(2)}) collective-permute-start(bf16[32,1024]{1,0:T(8,128)(2,1)S(1)} %get-tuple-element.57), channel_id=1, source_target_pairs={{0,384},{128,256},{256,128},{384,0},{1,385},{129,257},{257,129},{3... | collective-permute-start | bytes 196616 | tf_op jit(solution)/shard_map/ppermute | solution.py:24
  162.9 2.0 collective-permute-start.12
  164.9 2.4 collective-permute-start.11
  167.9 4.6 %collective-permute-done.12 = bf16[32,1024]{1,0:T(8,128)(2,1)S(1)} collective-permute-done((bf16[32,1024]{1,0:T(8,128)(2,1)S(1)}, bf16[32,1024]{1,0:T(8,128)(2,1)S(1)}, u32[]{:S(2)}, u32[]{:S(2)}) %collective-permute-start.12) | collective-permute-done | bytes 65568 | tf_op jit(solution)/shard_map/ppermute | solution.py:24
  172.5 1.2 collective-permute-done.11
  176.0 3.9 %collective-permute-start.14 = (bf16[32,4096]{1,0:T(8,128)(2,1)}, bf16[32,4096]{1,0:T(8,128)(2,1)}, u32[]{:S(2)}, u32[]{:S(2)}) collective-permute-start(bf16[32,4096]{1,0:T(8,128)(2,1)} %get-tuple-element.47), channel_id=1, source_target_pairs={{0,1},{1,0},{2,3},{3,2},{4,5},{5,4},{6,7},{7,6},{8,9},{9,8},{10,11... | collective-permute-start | bytes 786440 | tf_op jit(solution)/shard_map/ppermute | solution.py:24
  182.6 0.9 select_reduce_fusion
  183.7 1.9 pad_maximum_fusion.3
  185.6 4.1 %collective-permute-start.15 = (bf16[2,32,4096]{2,1,0:T(8,128)(2,1)}, bf16[2,32,4096]{2,1,0:T(8,128)(2,1)}, u32[]{:S(2)}, u32[]{:S(2)}) collective-permute-start(bf16[2,32,4096]{2,1,0:T(8,128)(2,1)} %pad_maximum_fusion.3), channel_id=1, source_target_pairs={{0,2},{2,0},{4,6},{6,4},{1,3},{3,1},{5,7},{7,5},{8,10},{10,8},{12,... | collective-permute-start | bytes 1572872 | tf_op jit(solution)/shard_map/ppermute | solution.py:24
  189.7 3.5 %collective-permute-start.16 = (bf16[2,32,4096]{2,1,0:T(8,128)(2,1)}, bf16[2,32,4096]{2,1,0:T(8,128)(2,1)}, u32[]{:S(2)}, u32[]{:S(2)}) collective-permute-start(bf16[2,32,4096]{2,1,0:T(8,128)(2,1)} %pad_maximum_fusion.3), channel_id=1, source_target_pairs={{0,4},{2,6},{4,0},{6,2},{1,5},{3,7},{5,1},{7,3},{8,12},{10,14},{12... | collective-permute-start | bytes 1572872 | tf_op jit(solution)/shard_map/ppermute | solution.py:24
  193.2 2.8 collective-permute-start.17
  197.4 1.6 fusion.38.embedded_ref
  199.0 8.7 %score.1 = (f32[128,1]{1,0:T(8,128)S(1)}, bf16[32,256]{1,0:T(8,128)(2,1)S(1)}) custom-call(bf16[8192,128]{1,0:T(8,128)(2,1)} %bitcast.41.docs, f32[32,128]{1,0:T(8,128)S(1)} %fusion.38.embedded_ref, f32[32,1]{1,0:T(8,128)S(1)} %copy.52.inv_rms_ref, s32[128,32]{1,0:T(8,128)S(1)} %broadcast_in_dim.110.spans, s32[128,2]{1,0:T(8,128)S(1)} %copy.53.flags), custom_call_target="tpu_custom_call" | custom-call | flops 134217728 | bytes 30000000 | tf_op jit(solution)/shard_map/score/pallas_call | solution.py:162
  208.6 6.3 %collective-permute-done.16 = bf16[2,32,4096]{2,1,0:T(8,128)(2,1)} collective-permute-done((bf16[2,32,4096]{2,1,0:T(8,128)(2,1)}, bf16[2,32,4096]{2,1,0:T(8,128)(2,1)}, u32[]{:S(2)}, u32[]{:S(2)}) %collective-permute-start.16) | collective-permute-done | bytes 524320 | tf_op jit(solution)/shard_map/ppermute | solution.py:24
  214.9 5.8 %collective-permute-done.17 = bf16[2,32,4096]{2,1,0:T(8,128)(2,1)} collective-permute-done((bf16[2,32,4096]{2,1,0:T(8,128)(2,1)}, bf16[2,32,4096]{2,1,0:T(8,128)(2,1)}, u32[]{:S(2)}, u32[]{:S(2)}) %collective-permute-start.17) | collective-permute-done | bytes 524320 | tf_op jit(solution)/shard_map/ppermute | solution.py:24
  221.4 4.7 %all-to-all-start.2 = ((bf16[8,32,256]{2,1,0:T(8,128)(2,1)}), bf16[8,32,256]{2,1,0:T(8,128)(2,1)S(1)}, u32[]{:S(2)}, u32[]{:S(2)}) async-start(bf16[8,32,256]{2,1,0:T(8,128)(2,1)} %broadcast_in_dim.115), calls=%async_computation.2 | async-start | bytes 262144 | tf_op jit(solution)/shard_map/all_to_all | solution.py:290
  226.1 3.1 %pad_maximum_fusion = bf16[4,2,32,4096]{3,2,1,0:T(8,128)(2,1)} fusion(bf16[1,2,32,4096]{3,2,1,0:T(8,128)(2,1)} %bitcast.51, bf16[1,2,32,4096]{3,2,1,0:T(8,128)(2,1)} %bitcast.50, bf16[1,2,32,4096]{3,2,1,0:T(8,128)(2,1)} %bitcast.49, bf16[1,2,32,4096]{3,2,1,0:T(8,128)(2,1)} %bitcast.48), kind=kLoop, calls=%fused_computation.9 | loop fusion | flops 3145728 | bytes 4194304 | tf_op jit(solution)/shard_map/stack | solution.py:289
  229.2 2.2 all-to-all-done.2
  232.0 2.6 fusion
  234.6 1.2 fusion.3
  236.8 11.5 %all-to-all-start.3 = ((bf16[64,10,128]{2,1,0:T(8,128)(2,1)}), bf16[64,10,128]{2,1,0:T(8,128)(2,1)}, u32[]{:S(2)}, u32[]{:S(2)}) async-start(bf16[64,10,128]{2,1,0:T(8,128)(2,1)} %pad_maximum_fusion.5), calls=%async_computation.3 | async-start | bytes 524288 | tf_op jit(solution)/shard_map/all_to_all | solution.py:335
  248.5 6.0 %convolution_multiply_fusion.3 = f32[256,640]{1,0:T(8,128)} fusion(bf16[640,4096]{0,1:T(8,128)(2,1)} %all-gather.5.cloned.1.call-done, bf16[4096,128]{1,0:T(8,128)(2,1)} %bitcast.128, f32[4096]{0:T(1024)S(1)} %copy-done.6, f32[256]{0:T(256)S(1)} %get-tuple-element.44, bf16[256,256]{1,0:T(8,128)(2,1)S(1)} %bitcast.148), kind=kOutput, calls=%fused_computation.17 | convolution fusion | flops 714850304 | bytes 7029760 | tf_op jit(solution)/shard_map/dot_general | solution.py:354
  254.5 5.0 %fusion.2 = bf16[256,640]{1,0:T(8,128)(2,1)S(1)} fusion(f32[256,640]{1,0:T(8,128)} %convolution_multiply_fusion.3, bf16[256,4096]{1,0:T(8,128)(2,1)} %bitcast.135, bf16[640,4096]{0,1:T(8,128)(2,1)} %all-gather.5.cloned.1.call-done, f32[256]{0:T(256)S(1)} %get-tuple-element.43), kind=kOutput, calls=%fused_computation.19 | convolution fusion | flops 1342668800 | bytes 8324096 | tf_op jit(solution)/shard_map/dot_general | solution.py:349
  259.6 1.3 gather_fusion.6
  260.9 1.8 multiply_reduce_fusion
  262.7 4.1 %all-to-all-done.3 = bf16[64,10,128]{2,1,0:T(8,128)(2,1)} async-done(((bf16[64,10,128]{2,1,0:T(8,128)(2,1)}), bf16[64,10,128]{2,1,0:T(8,128)(2,1)}, u32[]{:S(2)}, u32[]{:S(2)}) %all-to-all-start.3) | async-done | bytes 163872 | tf_op jit(solution)/shard_map/all_to_all | solution.py:335
  266.8 1.1 fusion.21
  267.9 1.0 slice_reduce_fusion
  269.6 10.7 %all-to-all-start.4 = ((bf16[64,10,128]{2,1,0:T(8,128)(2,1)}), bf16[64,10,128]{2,1,0:T(8,128)(2,1)}, u32[]{:S(2)}, u32[]{:S(2)}) async-start(bf16[64,10,128]{2,1,0:T(8,128)(2,1)} %broadcast_in_dim.119), calls=%async_computation.4 | async-start | bytes 524288 | tf_op jit(solution)/shard_map/all_to_all | solution.py:362
  280.3 0.9 subtract_convert_fusion
  281.2 17.1 %all-to-all-done.4 = bf16[64,10,128]{2,1,0:T(8,128)(2,1)} async-done(((bf16[64,10,128]{2,1,0:T(8,128)(2,1)}), bf16[64,10,128]{2,1,0:T(8,128)(2,1)}, u32[]{:S(2)}, u32[]{:S(2)}) %all-to-all-start.4) | async-done | bytes 163872 | tf_op jit(solution)/shard_map/all_to_all | solution.py:362
  298.3 1.0 fusion.35
  300.0 1.7 convert_multiply_fusion
  (109 shorter events, 17.6 us)
Async XLA Ops:
  7.2 29.0 %copy-start = (bf16[8192,128]{1,0:T(8,128)(2,1)S(1)}, bf16[8192,128]{1,0:T(8,128)(2,1)}, u32[]{:S(2)}) copy-start(bf16[8192,128]{1,0:T(8,128)(2,1)} %param.20) | copy-start | bytes 6291460
  8.8 137.2 %copy-start.11 = (s32[64]{0:T(128)}, s32[64]{0:T(128)S(1)}, u32[]{:S(2)}) copy-start(s32[64]{0:T(128)S(1)} %fusion.31) | copy-start | bytes 772
  10.5 47.8 %all-to-all-start = ((s32[64,1,128]{2,1,0:T(1,128)}), s32[64,1,128]{2,1,0:T(1,128)S(1)}, u32[]{:S(2)}, u32[]{:S(2)}) async-start(s32[64,1,128]{2,1,0:T(1,128)} %bitcast.7), calls=%async_computation | async-start | bytes 65536 | tf_op jit(solution)/shard_map/all_to_all | solution.py:228
  29.8 83.2 %all-gather.3.cloned.1.call-start = ((), (), s32[]{:S(2)}) async-start(), calls=%async_computation.5 | async-start | bytes 1392640 | tf_op jit(solution)/shard_map/all_gather | solution.py:226
  61.9 15.0 %copy-start.4 = (bf16[256,640]{1,0:T(8,128)(2,1)S(1)}, bf16[256,640]{1,0:T(8,128)(2,1)}, u32[]{:S(2)}) copy-start(bf16[256,640]{1,0:T(8,128)(2,1)} %param.12) | copy-start | bytes 983044
  61.9 20.0 %copy-start.3 = (bf16[512,128]{1,0:T(8,128)(2,1)S(1)}, bf16[512,128]{1,0:T(8,128)(2,1)}, u32[]{:S(2)}) copy-start(bf16[512,128]{1,0:T(8,128)(2,1)} %param.15) | copy-start | bytes 393220
  61.9 135.4 %all-to-all-start.1 = ((bf16[64,128,128]{2,1,0:T(8,128)(2,1)}), bf16[64,128,128]{2,1,0:T(8,128)(2,1)}, u32[]{:S(2)}, u32[]{:S(2)}) async-start(bf16[64,128,128]{2,1,0:T(8,128)(2,1)} %bitcast.130), calls=%async_computation.1 | async-start | bytes 4194304 | tf_op jit(solution)/shard_map/all_to_all | solution.py:232
  76.9 143.8 %all-gather.5.cloned.1.call-start = ((), (), s32[]{:S(2)}) async-start(), calls=%async_computation.6 | async-start | bytes 6553600 | tf_op jit(solution)/shard_map/all_gather | solution.py:279
  77.7 19.6 %collective-permute-start.2 = (bf16[2,4,32,640]{3,2,0,1:T(8,128)(2,1)S(1)}, bf16[2,4,32,640]{3,2,0,1:T(8,128)(2,1)S(1)}, u32[]{:S(2)}, u32[]{:S(2)}) collective-permute-start(bf16[2,4,32,640]{3,2,0,1:T(8,128)(2,1)S(1)} %bitcast.137), channel_id=1, source_target_pairs={{0,384},{128,256},{256,128},{384,0},{1,385},{129,257},{257,129},{3... | collective-permute-start | bytes 983048 | tf_op jit(solution)/shard_map/ppermute | solution.py:24
  82.0 8.4 %collective-permute-start.3 = (bf16[512,128]{1,0:T(8,128)(2,1)S(1)}, bf16[512,128]{1,0:T(8,128)(2,1)S(1)}, u32[]{:S(2)}, u32[]{:S(2)}) collective-permute-start(bf16[512,128]{1,0:T(8,128)(2,1)S(1)} %copy-done.3), channel_id=1, source_target_pairs={{0,1},{1,0},{2,3},{3,2},{4,5},{5,4},{6,7},{7,6},{8,9},{9,8},{10,11... | collective-permute-start | bytes 393224 | tf_op jit(solution)/shard_map/ppermute | solution.py:24
  85.9 14.6 %collective-permute-start.1 = (bf16[2,4,32,640]{3,2,0,1:T(8,128)(2,1)S(1)}, bf16[2,4,32,640]{3,2,0,1:T(8,128)(2,1)S(1)}, u32[]{:S(2)}, u32[]{:S(2)}) collective-permute-start(bf16[2,4,32,640]{3,2,0,1:T(8,128)(2,1)S(1)} %bitcast.138), channel_id=1, source_target_pairs={{0,256},{128,384},{256,0},{384,128},{1,257},{129,385},{257,1},{385... | collective-permute-start | bytes 983048 | tf_op jit(solution)/shard_map/ppermute | solution.py:24
  88.2 19.4 %collective-permute-start = (bf16[2,4,32,640]{3,2,0,1:T(8,128)(2,1)S(1)}, bf16[2,4,32,640]{3,2,0,1:T(8,128)(2,1)S(1)}, u32[]{:S(2)}, u32[]{:S(2)}) collective-permute-start(bf16[2,4,32,640]{3,2,0,1:T(8,128)(2,1)S(1)} %bitcast.139), channel_id=1, source_target_pairs={{0,128},{128,0},{256,384},{384,256},{1,129},{129,1},{257,385},{385... | collective-permute-start | bytes 983048 | tf_op jit(solution)/shard_map/ppermute | solution.py:24
  90.4 18.6 %collective-permute-start.6 = (bf16[2,512,128]{2,1,0:T(8,128)(2,1)S(1)}, bf16[2,512,128]{2,1,0:T(8,128)(2,1)S(1)}, u32[]{:S(2)}, u32[]{:S(2)}) collective-permute-start(bf16[2,512,128]{2,1,0:T(8,128)(2,1)S(1)} %maximum_select_fusion.1), channel_id=1, source_target_pairs={{0,6},{2,4},{4,2},{6,0},{1,7},{3,5},{5,3},{7,1},{8,14},{10,12},{12... | collective-permute-start | bytes 786440 | tf_op jit(solution)/shard_map/ppermute | solution.py:24
  94.8 14.2 %collective-permute-start.5 = (bf16[2,512,128]{2,1,0:T(8,128)(2,1)S(1)}, bf16[2,512,128]{2,1,0:T(8,128)(2,1)S(1)}, u32[]{:S(2)}, u32[]{:S(2)}) collective-permute-start(bf16[2,512,128]{2,1,0:T(8,128)(2,1)S(1)} %maximum_select_fusion.1), channel_id=1, source_target_pairs={{0,4},{2,6},{4,0},{6,2},{1,5},{3,7},{5,1},{7,3},{8,12},{10,14},{12... | collective-permute-start | bytes 786440 | tf_op jit(solution)/shard_map/ppermute | solution.py:24
  97.3 11.8 %collective-permute-start.4 = (bf16[2,512,128]{2,1,0:T(8,128)(2,1)S(1)}, bf16[2,512,128]{2,1,0:T(8,128)(2,1)S(1)}, u32[]{:S(2)}, u32[]{:S(2)}) collective-permute-start(bf16[2,512,128]{2,1,0:T(8,128)(2,1)S(1)} %maximum_select_fusion.1), channel_id=1, source_target_pairs={{0,2},{2,0},{4,6},{6,4},{1,3},{3,1},{5,7},{7,5},{8,10},{10,8},{12,... | collective-permute-start | bytes 786440 | tf_op jit(solution)/shard_map/ppermute | solution.py:24
  113.0 16.9 %copy-start.10 = (s32[1,64]{1,0:T(1,128)S(1)}, s32[1,64]{1,0:T(1,128)}, u32[]{:S(2)}) copy-start(s32[1,64]{1,0:T(1,128)} %param.16) | copy-start | bytes 772
  113.0 19.5 %copy-start.1 = (bf16[640,1024]{0,1:T(8,128)(2,1)S(1)}, bf16[640,1024]{0,1:T(8,128)(2,1)}, u32[]{:S(2)}) copy-start(bf16[640,1024]{0,1:T(8,128)(2,1)} %all-gather.3.cloned.1.call-done) | copy-start | bytes 3932164
  116.7 15.9 %collective-permute-start.7 = (bf16[512,1024]{1,0:T(8,128)(2,1)}, bf16[512,1024]{1,0:T(8,128)(2,1)}, u32[]{:S(2)}, u32[]{:S(2)}) collective-permute-start(bf16[512,1024]{1,0:T(8,128)(2,1)} %convolution_convert_fusion), channel_id=1, source_target_pairs={{0,1},{1,0},{2,3},{3,2},{4,5},{5,4},{6,7},{7,6},{8,9},{9,8},{10,11... | collective-permute-start | bytes 3145736 | tf_op jit(solution)/shard_map/ppermute | solution.py:24
  136.4 16.4 %collective-permute-start.10 = (bf16[4,32,1024]{2,1,0:T(8,128)(2,1)S(1)}, bf16[4,32,1024]{2,1,0:T(8,128)(2,1)S(1)}, u32[]{:S(2)}, u32[]{:S(2)}) collective-permute-start(bf16[4,32,1024]{2,1,0:T(8,128)(2,1)S(1)} %bitcast.159), channel_id=1, source_target_pairs={{0,6},{2,4},{4,2},{6,0},{1,7},{3,5},{5,3},{7,1},{8,14},{10,12},{12... | collective-permute-start | bytes 786440 | tf_op jit(solution)/shard_map/ppermute | solution.py:24
  141.6 11.2 %collective-permute-start.9 = (bf16[4,32,1024]{2,1,0:T(8,128)(2,1)S(1)}, bf16[4,32,1024]{2,1,0:T(8,128)(2,1)S(1)}, u32[]{:S(2)}, u32[]{:S(2)}) collective-permute-start(bf16[4,32,1024]{2,1,0:T(8,128)(2,1)S(1)} %bitcast.158), channel_id=1, source_target_pairs={{0,4},{2,6},{4,0},{6,2},{1,5},{3,7},{5,1},{7,3},{8,12},{10,14},{12... | collective-permute-start | bytes 786440 | tf_op jit(solution)/shard_map/ppermute | solution.py:24
  143.9 11.9 %collective-permute-start.8 = (bf16[4,32,1024]{2,1,0:T(8,128)(2,1)S(1)}, bf16[4,32,1024]{2,1,0:T(8,128)(2,1)}, u32[]{:S(2)}, u32[]{:S(2)}) collective-permute-start(bf16[4,32,1024]{2,1,0:T(8,128)(2,1)S(1)} %bitcast.157), channel_id=1, source_target_pairs={{0,2},{2,0},{4,6},{6,4},{1,3},{3,1},{5,7},{7,5},{8,10},{10,8},{12,... | collective-permute-start | bytes 786440 | tf_op jit(solution)/shard_map/ppermute | solution.py:24
  157.0 17.4 %copy-start.2 = (bf16[32,4096]{1,0:T(8,128)(2,1)S(1)}, bf16[32,4096]{1,0:T(8,128)(2,1)}, u32[]{:S(2)}) copy-start(bf16[32,4096]{1,0:T(8,128)(2,1)} %param.11) | copy-start | bytes 786436
  157.0 10.9 %collective-permute-start.13 = (bf16[32,1024]{1,0:T(8,128)(2,1)S(1)}, bf16[32,1024]{1,0:T(8,128)(2,1)S(1)}, u32[]{:S(2)}, u32[]{:S(2)}) collective-permute-start(bf16[32,1024]{1,0:T(8,128)(2,1)S(1)} %get-tuple-element.57), channel_id=1, source_target_pairs={{0,384},{128,256},{256,128},{384,0},{1,385},{129,257},{257,129},{3... | collective-permute-start | bytes 196616 | tf_op jit(solution)/shard_map/ppermute | solution.py:24
  162.9 9.6 %collective-permute-start.12 = (bf16[32,1024]{1,0:T(8,128)(2,1)S(1)}, bf16[32,1024]{1,0:T(8,128)(2,1)S(1)}, u32[]{:S(2)}, u32[]{:S(2)}) collective-permute-start(bf16[32,1024]{1,0:T(8,128)(2,1)S(1)} %get-tuple-element.58), channel_id=1, source_target_pairs={{0,256},{128,384},{256,0},{384,128},{1,257},{129,385},{257,1},{385... | collective-permute-start | bytes 196616 | tf_op jit(solution)/shard_map/ppermute | solution.py:24
  164.9 8.8 %collective-permute-start.11 = (bf16[32,1024]{1,0:T(8,128)(2,1)S(1)}, bf16[32,1024]{1,0:T(8,128)(2,1)S(1)}, u32[]{:S(2)}, u32[]{:S(2)}) collective-permute-start(bf16[32,1024]{1,0:T(8,128)(2,1)S(1)} %get-tuple-element.59), channel_id=1, source_target_pairs={{0,128},{128,0},{256,384},{384,256},{1,129},{129,1},{257,385},{385... | collective-permute-start | bytes 196616 | tf_op jit(solution)/shard_map/ppermute | solution.py:24
  174.3 7.5 %copy-start.5 = (f32[4096]{0:T(1024)S(1)}, f32[4096]{0:T(1024)}, u32[]{:S(2)}) copy-start(f32[4096]{0:T(1024)} %param.14) | copy-start | bytes 49156
  175.2 5.3 %copy-start.7 = (f32[32]{0:T(128)}, f32[32]{0:T(128)S(1)}, u32[]{:S(2)}) copy-start(f32[32]{0:T(128)S(1)} %get-tuple-element.46) | copy-start | bytes 388
  176.0 7.7 %collective-permute-start.14 = (bf16[32,4096]{1,0:T(8,128)(2,1)}, bf16[32,4096]{1,0:T(8,128)(2,1)}, u32[]{:S(2)}, u32[]{:S(2)}) collective-permute-start(bf16[32,4096]{1,0:T(8,128)(2,1)} %get-tuple-element.47), channel_id=1, source_target_pairs={{0,1},{1,0},{2,3},{3,2},{4,5},{5,4},{6,7},{7,6},{8,9},{9,8},{10,11... | collective-permute-start | bytes 786440 | tf_op jit(solution)/shard_map/ppermute | solution.py:24
  185.6 23.0 %collective-permute-start.15 = (bf16[2,32,4096]{2,1,0:T(8,128)(2,1)}, bf16[2,32,4096]{2,1,0:T(8,128)(2,1)}, u32[]{:S(2)}, u32[]{:S(2)}) collective-permute-start(bf16[2,32,4096]{2,1,0:T(8,128)(2,1)} %pad_maximum_fusion.3), channel_id=1, source_target_pairs={{0,2},{2,0},{4,6},{6,4},{1,3},{3,1},{5,7},{7,5},{8,10},{10,8},{12,... | collective-permute-start | bytes 1572872 | tf_op jit(solution)/shard_map/ppermute | solution.py:24
  189.7 25.2 %collective-permute-start.16 = (bf16[2,32,4096]{2,1,0:T(8,128)(2,1)}, bf16[2,32,4096]{2,1,0:T(8,128)(2,1)}, u32[]{:S(2)}, u32[]{:S(2)}) collective-permute-start(bf16[2,32,4096]{2,1,0:T(8,128)(2,1)} %pad_maximum_fusion.3), channel_id=1, source_target_pairs={{0,4},{2,6},{4,0},{6,2},{1,5},{3,7},{5,1},{7,3},{8,12},{10,14},{12... | collective-permute-start | bytes 1572872 | tf_op jit(solution)/shard_map/ppermute | solution.py:24
  193.2 27.6 %collective-permute-start.17 = (bf16[2,32,4096]{2,1,0:T(8,128)(2,1)}, bf16[2,32,4096]{2,1,0:T(8,128)(2,1)}, u32[]{:S(2)}, u32[]{:S(2)}) collective-permute-start(bf16[2,32,4096]{2,1,0:T(8,128)(2,1)} %pad_maximum_fusion.3), channel_id=1, source_target_pairs={{0,6},{2,4},{4,2},{6,0},{1,7},{3,5},{5,3},{7,1},{8,14},{10,12},{12... | collective-permute-start | bytes 1572872 | tf_op jit(solution)/shard_map/ppermute | solution.py:24
  195.9 12.0 %copy-start.12 = (s32[64]{0:T(128)S(1)}, s32[64]{0:T(128)}, u32[]{:S(2)}) copy-start(s32[64]{0:T(128)} %copy-done.11) | copy-start | bytes 772
  221.4 10.0 %all-to-all-start.2 = ((bf16[8,32,256]{2,1,0:T(8,128)(2,1)}), bf16[8,32,256]{2,1,0:T(8,128)(2,1)S(1)}, u32[]{:S(2)}, u32[]{:S(2)}) async-start(bf16[8,32,256]{2,1,0:T(8,128)(2,1)} %broadcast_in_dim.115), calls=%async_computation.2 | async-start | bytes 262144 | tf_op jit(solution)/shard_map/all_to_all | solution.py:290
  232.0 16.6 %copy-start.6 = (f32[4096]{0:T(1024)S(1)}, f32[4096]{0:T(1024)}, u32[]{:S(2)}) copy-start(f32[4096]{0:T(1024)} %param.14) | copy-start | bytes 49156
  236.8 30.0 %all-to-all-start.3 = ((bf16[64,10,128]{2,1,0:T(8,128)(2,1)}), bf16[64,10,128]{2,1,0:T(8,128)(2,1)}, u32[]{:S(2)}, u32[]{:S(2)}) async-start(bf16[64,10,128]{2,1,0:T(8,128)(2,1)} %pad_maximum_fusion.5), calls=%async_computation.3 | async-start | bytes 524288 | tf_op jit(solution)/shard_map/all_to_all | solution.py:335
  259.6 20.7 %copy-start.8 = (f32[32]{0:T(128)S(1)}, f32[32]{0:T(128)}, u32[]{:S(2)}) copy-start(f32[32]{0:T(128)} %copy-done.7) | copy-start | bytes 388
  259.6 20.7 %copy-start.9 = (f32[32]{0:T(128)S(1)}, f32[32]{0:T(128)}, u32[]{:S(2)}) copy-start(f32[32]{0:T(128)} %get-tuple-element.45) | copy-start | bytes 388
  269.6 28.7 %all-to-all-start.4 = ((bf16[64,10,128]{2,1,0:T(8,128)(2,1)}), bf16[64,10,128]{2,1,0:T(8,128)(2,1)}, u32[]{:S(2)}, u32[]{:S(2)}) async-start(bf16[64,10,128]{2,1,0:T(8,128)(2,1)} %broadcast_in_dim.119), calls=%async_computation.4 | async-start | bytes 524288 | tf_op jit(solution)/shard_map/all_to_all | solution.py:362
Sparse Core Ops, SparseCore 0:
  32.7 80.2 all-gather.2
  115.1 85.1 all-gather.4

commit v5 on v4

--- a/solution.py
+++ b/solution.py
@@ -12,6 +12,7 @@
 Y, Z, X, C = 4, 16, 4, 2
 DP = ("y", "z")
 TENSOR = ("x", "c")
+PLANE = ("y", "x", "c")
 
 BF16 = jnp.bfloat16
 F32 = jnp.float32
@@ -32,13 +33,8 @@
     return rows_of(blocks, jnp.arange(blocks.shape[0], dtype=I32) ^ place)
 
 
-def halves(values):
-    top = values.astype(BF16)
-    return top, (values - top.astype(F32)).astype(BF16)
-
-
-def decode_kernel(buckets, low_bytes, high_bytes, rows, out):
-    words = low_bytes.shape[1]
+def decode_kernel(buckets, packed, rows, out):
+    words = packed.shape[1]
     features = out.shape[1]
     feature = lax.broadcasted_iota(I32, (words, features), 1)
     word = lax.broadcasted_iota(I32, (words, features), 0)
@@ -46,50 +42,48 @@
     first = (feature & 7) < 4
     spread_low = jnp.where(here & first, 1.0, 0.0).astype(BF16)
     spread_high = jnp.where(here & ~first, 1.0, 0.0).astype(BF16)
-    code_bytes = jnp.dot(low_bytes[...], spread_low, preferred_element_type=F32) + jnp.dot(
-        high_bytes[...], spread_high, preferred_element_type=F32
-    )
-    shift = 2 * (lax.broadcasted_iota(I32, code_bytes.shape, 1) & 3)
-    codes = (code_bytes.astype(I32) >> shift) & 3
-    low = (codes & 1).astype(F32)
-    high = (codes >> 1).astype(F32)
+    step = 256
+    shift = 2 * (lax.broadcasted_iota(I32, (step, features), 1) & 3)
     zero, one, two, three = [buckets[k] for k in range(4)]
-    levels = zero + low * (one - zero) + high * (two - zero)
-    levels = levels + low * high * (three - two - one + zero)
-    vectors = rows[...].astype(F32) + levels
-    scale = lax.rsqrt(jnp.sum(vectors * vectors, axis=1, keepdims=True) + EPS)
-    out[...] = (vectors * scale).astype(BF16)
+
+    @pl.loop(0, out.shape[0] // step)
+    def _(i):
+        at = pl.ds(pl.multiple_of(i * step, step), step)
+        codes = packed[at, :]
+        code_bytes = jnp.dot(
+            (codes & 255).astype(F32).astype(BF16), spread_low, preferred_element_type=F32
+        ) + jnp.dot(
+            ((codes >> 8) & 255).astype(F32).astype(BF16), spread_high, preferred_element_type=F32
+        )
+        codes = (code_bytes.astype(I32) >> shift) & 3
+        low = (codes & 1).astype(F32)
+        high = (codes >> 1).astype(F32)
+        levels = zero + low * (one - zero) + high * (two - zero)
+        levels = levels + low * high * (three - two - one + zero)
+        vectors = rows[at, :].astype(F32) + levels
+        scale = lax.rsqrt(jnp.sum(vectors * vectors, axis=1, keepdims=True) + EPS)
+        out[at, :] = (vectors * scale).astype(BF16)
 
 
 def decode_all(cell_ids, packed, centroids, buckets):
     count = cell_ids.size
-    words = packed.size // count
-    features = centroids.shape[1]
-    low_bytes = (packed & 255).astype(BF16).reshape(count, words)
-    high_bytes = ((packed >> 8) & 255).astype(BF16).reshape(count, words)
+    packed = packed.reshape(count, packed.size // count)
     rows = rows_of(centroids, cell_ids.reshape(count))
-    step = min(count, 512)
     return pl.pallas_call(
         decode_kernel,
-        grid=(count // step,),
-        in_specs=[
-            SMEM,
-            pl.BlockSpec((step, words), lambda i: (i, 0)),
-            pl.BlockSpec((step, words), lambda i: (i, 0)),
-            pl.BlockSpec((step, features), lambda i: (i, 0)),
-        ],
-        out_specs=pl.BlockSpec((step, features), lambda i: (i, 0)),
-        out_shape=jax.ShapeDtypeStruct((count, features), BF16),
+        in_specs=[SMEM, VMEM, VMEM],
+        out_specs=VMEM,
+        out_shape=jax.ShapeDtypeStruct((count, centroids.shape[1]), BF16),
+        compiler_params=pltpu.CompilerParams(vmem_limit_bytes=32 * 1024 * 1024),
         name="decode",
-    )(buckets, low_bytes, high_bytes, rows)
-
-
-def score_kernel(docs, embedded_ref, inv_rms_ref, spans, flags, scores, packet, weights, totals):
+    )(buckets, packed, rows)
+
+
+def score_kernel(docs, embedded_ref, spans, flags, unit, head, scores, packet, weights, totals):
     slots, queries_n = totals.shape
     tokens = docs.shape[0] // slots
     features = docs.shape[1]
     embedded = embedded_ref[...]
-    inv_rms = inv_rms_ref[...]
     inverse = lax.rsqrt(jnp.sum(embedded * embedded, axis=1, keepdims=True) + EPS)
     queries = (embedded * inverse).astype(BF16)
     group = 8
@@ -143,29 +137,32 @@
     grad_q = lax.fori_loop(0, slots // group, add, jnp.zeros((queries_n, features), F32))
     along = jnp.sum(embedded * grad_q, axis=1, keepdims=True)
     grad_embedded = (inverse * grad_q - inverse * inverse * inverse * embedded * along).astype(BF16)
-    packet[:, 0:features] = grad_embedded
-    pull = inv_rms * jnp.sum(grad_embedded.astype(F32) * embedded, axis=1, keepdims=True)
-    lane = lax.broadcasted_iota(I32, (queries_n, features), 1)
-    extra = jnp.zeros((queries_n, features), F32)
-    column = 0
-    for value in (pull, inv_rms):
-        for piece in halves(value):
-            extra = jnp.where(lane == column, piece.astype(F32), extra)
-            column += 1
-    packet[:, features : 2 * features] = extra.astype(BF16)
-
-
-def score(docs, embedded, inv_rms, spans, flags):
+    packet[0:queries_n, :] = grad_embedded
+
+    block = 8
+    for i in range(head.shape[0] // (block * features)):
+        sums = []
+        for k in range(i * block, (i + 1) * block):
+            at = slice(k * features, (k + 1) * features)
+            grad_normed = lax.dot_general(
+                grad_embedded, head[at, :], (((1,), (1,)), ((), ())), preferred_element_type=F32
+            )
+            sums.append(jnp.sum(grad_normed * unit[:, at], axis=0, keepdims=True))
+        line = queries_n + i * block
+        packet[line : line + block, :] = jnp.concatenate(sums, axis=0).astype(BF16)
+
+
+def score(docs, embedded, spans, flags, unit, head):
     slots = flags.shape[0]
     queries_n, features = embedded.shape
     count = docs.shape[0]
     return pl.pallas_call(
         score_kernel,
-        in_specs=[VMEM] * 5,
+        in_specs=[VMEM] * 6,
         out_specs=[VMEM] * 2,
         out_shape=[
             jax.ShapeDtypeStruct((slots, 1), F32),
-            jax.ShapeDtypeStruct((queries_n, 2 * features), BF16),
+            jax.ShapeDtypeStruct((queries_n + head.shape[0] // features, features), BF16),
         ],
         scratch_shapes=[
             pltpu.VMEM((count, queries_n), F32),
@@ -178,7 +175,7 @@
             transcendentals=count * queries_n,
         ),
         name="score",
-    )(docs, embedded, inv_rms, spans, flags)
+    )(docs, embedded, spans, flags, unit, head)
 
 
 def local(
@@ -264,6 +261,7 @@
     away = jnp.dot(by_y[1], proj_z, preferred_element_type=F32).astype(BF16)
     away = swap(away, "c", C, 1)
     stay = jnp.dot(by_y[0], proj_z, preferred_element_type=F32).astype(BF16)
+    stay = lax.optimization_barrier(stay)
     pair = (stay.astype(F32) + away.astype(F32)).reshape(X, Y, seq_rows, width // Y)
     pieces, row = [pair[step].astype(BF16) for step in range(1, X)], pair[0]
     for step in range(1, X):
@@ -276,67 +274,53 @@
     inv_rms = lax.rsqrt(jnp.mean(summed * summed, axis=-1, keepdims=True) + EPS)
     scaled_sum = summed * inv_rms
     normed = (scaled_sum * norm_gain).astype(BF16)
+    embedded = jnp.dot(normed, head_full, preferred_element_type=F32)
+
+    head_rows = colbert_head.shape[0]
+    unit = scaled_sum.astype(BF16).reshape(seq_rows, X * C, head_rows).transpose(1, 0, 2)
+    unit, got_docs = lax.optimization_barrier((unit, got_docs))
+    unit_plane = lax.all_to_all(
+        jnp.concatenate([unit] * Y), PLANE, 0, 0, tiled=True
+    ).reshape(Y * X * C * seq_rows, head_rows)
+
+    slot_scores, packet = score(got_docs, embedded, spans, flags, scaled_sum, head_full)
+    scores = jnp.sum(jnp.where(placed, slot_scores, 0.0), axis=0)[None, :]
+    packet, unit_plane = lax.optimization_barrier((packet, unit_plane))
+    packets = lax.all_to_all(
+        jnp.broadcast_to(packet, (Y * X * C,) + packet.shape), PLANE, 0, 0, tiled=True
+    )
+    ge_plane = packets[:, :seq_rows]
+
     proj_full = lax.all_gather(proj_z, "y", axis=1, tiled=True)
-    unit = scaled_sum.astype(BF16)
-    unit = jnp.stack([unit, swap(unit, "c", C, 1)])
-    units = [unit] + [swap(unit, "x", X, step) for step in range(1, X)]
-    scaled_sum, normed, got_docs = lax.optimization_barrier((scaled_sum, normed, got_docs))
-    embedded = jnp.dot(normed, head_full, preferred_element_type=F32)
-
-    slot_scores, packet = score(got_docs, embedded, inv_rms, spans, flags)
-    scores = jnp.sum(jnp.where(placed, slot_scores, 0.0), axis=0)[None, :]
-    packet, units, proj_full = lax.optimization_barrier((packet, units, proj_full))
-    unit_all = jnp.stack(units).reshape(X * C * seq_rows, width)
-    packets = lax.all_to_all(
-        jnp.broadcast_to(packet, (X * C,) + packet.shape), TENSOR, 0, 0, tiled=True
-    )
-
-    def reorder(rows):
-        rows = rows.reshape(X * C, seq_rows, rows.shape[-1])
-        return unxor(rows, here_x * C + here_c).reshape(X * C * seq_rows, rows.shape[-1])
-
-    packets = reorder(packets)
-    ge_all = packets[:, :feature_dim]
-    extra = packets[:, feature_dim : feature_dim + 4].astype(F32)
-    pull_all = (extra[:, 0:1] + extra[:, 1:2]) * (1.0 / width)
-    inv_all = extra[:, 2:3] + extra[:, 3:4]
-
-    head_rows = colbert_head.shape[0]
-    mine = (here_x * C + here_c) * head_rows
+    packets, summed_all, proj_full = lax.optimization_barrier(
+        (packets, summed.astype(BF16), proj_full)
+    )
+    summed_all = lax.all_gather(summed_all, TENSOR, axis=0, tiled=True)
+
+    share = head_rows // Z
+    lines = width // feature_dim // Z
     head_term = lax.dot_general(
-        lax.dynamic_slice_in_dim(unit_all, mine, head_rows, 1),
-        ge_all,
+        unit_plane,
+        ge_plane.reshape(Y * X * C * seq_rows, feature_dim),
         (((0,), (0,)), ((), ())),
         preferred_element_type=F32,
     )
-    gain_term = jnp.sum(
-        lax.dot_general(
-            ge_all, head_full, (((1,), (1,)), ((), ())), preferred_element_type=F32
-        )
-        * unit_all.astype(F32),
-        axis=0,
-    )
-    share = head_rows // shards
-    lines = width // feature_dim
-
-    def bundle(head_part, gain_part):
-        return jnp.concatenate(
-            [head_part.astype(BF16)] + [piece[:, None, :] for piece in halves(gain_part)], axis=1
-        )
-
-    def unbundle(rows):
-        pair = rows[:, share].astype(F32) + rows[:, share + 1].astype(F32)
-        return rows[:, :share].astype(F32), pair
-
-    gain_term = jnp.concatenate(
-        [gain_term.reshape(lines, feature_dim), jnp.zeros((shards - lines, feature_dim), F32)]
-    )
-    first = bundle(head_term.reshape(shards, share, feature_dim), gain_term)
-    first = unbundle(lax.all_to_all(first, DP, 0, 0, tiled=True))
-    second = bundle(*[jnp.sum(part, axis=0, keepdims=True) for part in first])
+    gain_term = jnp.sum(packets[:, seq_rows:].astype(F32), axis=0)
+    first = jnp.concatenate(
+        [
+            head_term.reshape(Z, share, feature_dim).astype(BF16),
+            gain_term.reshape(Z, lines, feature_dim).astype(BF16),
+        ],
+        axis=1,
+    )
+    first = lax.all_to_all(first, "z", 0, 0, tiled=True)
+    second = jnp.sum(first.astype(F32), axis=0, keepdims=True).astype(BF16)
+    second = lax.all_to_all(
+        jnp.broadcast_to(second, (Z,) + second.shape[1:]), "z", 0, 0, tiled=True
+    )
 
     packet, packets = lax.optimization_barrier((packet, packets))
-    grad_embedded = packet[:, :feature_dim]
+    grad_embedded = packet[:seq_rows]
     grad_normed = lax.dot_general(
         grad_embedded, head_full, (((1,), (1,)), ((), ())), preferred_element_type=F32
     )
@@ -344,28 +328,30 @@
     residual_grad = (
         inv_rms * scaled - summed * inv_rms**3 * jnp.mean(summed * scaled, axis=-1, keepdims=True)
     ).astype(BF16)
+    ge_all = lax.dynamic_slice_in_dim(ge_plane, here_y * (X * C), X * C, 0)
+    ge_all = ge_all.reshape(X * C * seq_rows, feature_dim)
     gained_head = (head_full.astype(F32) * norm_gain[:, None]).astype(BF16)
     mixed_head = jnp.dot(proj_full, gained_head, preferred_element_type=F32).astype(BF16)
     pulled = lax.dot_general(
-        unit_all, proj_full, (((1,), (1,)), ((), ())), preferred_element_type=F32
-    )
+        summed_all, proj_full, (((1,), (1,)), ((), ())), preferred_element_type=F32
+    )
+    wide = summed_all.astype(F32)
+    inv_all = lax.rsqrt(jnp.mean(wide * wide, axis=-1, keepdims=True) + EPS)
+    embedded_all = jnp.dot(summed_all, gained_head, preferred_element_type=F32)
+    pull_all = jnp.sum(ge_all.astype(F32) * embedded_all, axis=-1, keepdims=True) * (1.0 / width)
     context_grad = (
         inv_all
         * lax.dot_general(
             ge_all, mixed_head, (((1,), (1,)), ((), ())), preferred_element_type=F32
         )
-        - pull_all * pulled
+        - inv_all**3 * pull_all * pulled
     ).astype(BF16)
-    context_grad = reorder(context_grad)
+
     second, context_grad = lax.optimization_barrier((second, context_grad))
-
-    second = lax.all_to_all(
-        jnp.broadcast_to(second, (shards,) + second.shape[1:]), DP, 0, 0, tiled=True
-    )
-    head_got, gain_got = unbundle(second)
+    mine = (here_x * C + here_c) * head_rows
     gain_blk = lax.dynamic_slice_in_dim(norm_gain, mine, head_rows, 0)
-    head_grad = head_got.reshape(head_rows, feature_dim) * gain_blk[:, None]
-    gain_grad = gain_got[:lines].reshape(width)
+    head_grad = second[:, :share].astype(F32).reshape(head_rows, feature_dim) * gain_blk[:, None]
+    gain_grad = second[:, share:].astype(F32).reshape(width)
     return (scores, context_grad, residual_grad, head_grad, gain_grad)
 
 

time: 312 us -> 292 us (0.936)
  waiting for transfers between devices: 62.4 us -> 42.3 us
  blocking collectives: 0 us -> 17.3 us
  starting transfers between devices: 131 us -> 115 us
  local copies, waits for them, and re-layouts: 36.1 us -> 42.4 us
  matrix products: 25.6 us -> 20.8 us
    all_to_all x0 -> x1, blocking collectives: none -> 17.3 us  [local(): lax.all_to_all(jnp.broadcast_to(packet, (Y * X * C,) + packet.shape), PLA...]
    ppermute x18 -> x14, starting transfers between devices: 70.1 us -> 54.9 us  [swap(): return lax.ppermute(values, axis, [(i, i ^ step) for i in range(size)])]
    ppermute x18 -> x14, waiting for transfers between devices: 36.1 us -> 24.8 us  [swap(): return lax.ppermute(values, axis, [(i, i ^ step) for i in range(size)])]
    all_to_all x3, waiting for transfers between devices: 23.4 us -> 14.9 us  [the longest x1 9.25 us: local(): first = lax.all_to_all(first, 'z', 0, 0, tiled=True)]
    another operation x2 -> x0, other arithmetic: 5.05 us -> none  [the longest x1 3.12 us: local(): unit_all = jnp.stack(units).reshape(X * C * seq_rows, width)]
    unnamed x26 -> x50, local copies, waits for them, and re-layouts: 0.07 us -> 4.99 us
    gather x7 -> x5, local copies, waits for them, and re-layouts: 23 us -> 21.9 us  [rows_of(): return values.at[index].get(mode='promise_in_bounds')]
  transfers between devices with their start and end apart: 25 -> 22, of which waited for: 12 -> 11; matrix products, arithmetic and copies ran while one was open for 22% -> 26% of each run, Pallas kernels for 5% -> 5%
where the time goes in v5:
time: 292 us; the launch traced here: 290 us
  starting transfers between devices  115 us (39%)
  local copies, waits for them, and re-layouts  42.4 us (15%)
  waiting for transfers between devices  42.3 us (14%)
  other arithmetic  22.7 us (8%)
  matrix products  20.8 us (7%)
  blocking collectives  17.3 us (6%)
  Pallas kernels  14.6 us (5%)
  between operations  14.4 us (5%)
    ppermute x14, starting transfers between devices, swap(): return lax.ppermute(values, axis, [(i, i ^ step) for i in range(size)])  54.9 us
    ppermute x14, waiting for transfers between devices, swap(): return lax.ppermute(values, axis, [(i, i ^ step) for i in range(size)])  24.8 us
    gather x5, local copies, waits for them, and re-layouts, rows_of(): return values.at[index].get(mode='promise_in_bounds')  21.9 us
    all_to_all x1, starting transfers between devices, local(): notes = lax.all_to_all(note, DP, 0, 0, tiled=True)  19.3 us
    all_to_all x1, blocking collectives, local(): lax.all_to_all(jnp.broadcast_to(packet, (Y * X * C,) + packet.shape), PLA...  17.3 us
    all_to_all x1, starting transfers between devices, local(): lax.all_to_all(chosen.reshape(shards, cap * doc_len, feature_dim), DP, 0,...  14.9 us
    all_to_all x1, starting transfers between devices, local(): first = lax.all_to_all(first, 'z', 0, 0, tiled=True)  9.33 us
    all_to_all x1, waiting for transfers between devices, local(): first = lax.all_to_all(first, 'z', 0, 0, tiled=True)  9.25 us
  transfers between devices with their start and end apart: 22, of which 11 were waited for; matrix products, arithmetic and copies ran while one was open for 26% of the time, Pallas kernels for 5%

profile of v5, /device:TPU:1, one launch (start us, length us, event | category | flops | bytes accessed | tf_op | source)
XLA Modules:
  0.0 289.9 jit_solution(11606618518785778733)
XLA Ops:
  10.8 19.3 %all-to-all-start = ((s32[64,1,128]{2,1,0:T(1,128)}), s32[64,1,128]{2,1,0:T(1,128)S(1)}, u32[]{:S(2)}, u32[]{:S(2)}) async-start(s32[64,1,128]{2,1,0:T(1,128)} %bitcast.7), calls=%async_computation | async-start | bytes 65536 | tf_op jit(solution)/shard_map/all_to_all | solution.py:225
  31.7 3.0 %reshape.322.packed = s32[4096,16]{1,0:T(8,128)} reshape(s32[64,1024]{1,0:T(8,128)} %param.19) | data formatting | bytes 524288 | tf_op jit(solution)/shard_map/reshape | solution.py:70
  34.7 14.9 %gather_fusion = bf16[4096,128]{1,0:T(8,128)(2,1)} fusion(bf16[8192,128]{1,0:T(8,128)(2,1)S(1)} %copy-done, s32[4096]{0:T(1024)S(1)} %broadcast_clamp_fusion), kind=kCustom, calls=%fused_computation | custom fusion | bytes 2113536 | tf_op jit(solution)/shard_map/gather | solution.py:29
  49.6 1.6 copy-done.1
  51.3 1.2 copy-done.3
  52.5 5.4 %decode.1 = bf16[4096,128]{1,0:T(8,128)(2,1)S(1)} custom-call(f32[4]{0:T(128)S(1)} %copy-done.4, s32[4096,16]{1,0:T(8,128)S(1)} %copy-done.1, bf16[4096,128]{1,0:T(8,128)(2,1)S(1)} %copy-done.3), custom_call_target="tpu_custom_call" | custom-call | tf_op jit(solution)/shard_map/decode/pallas_call | solution.py:72
  58.2 2.2 gather_fusion.1
  60.4 14.9 %all-to-all-start.1 = ((bf16[64,128,128]{2,1,0:T(8,128)(2,1)}), bf16[64,128,128]{2,1,0:T(8,128)(2,1)}, u32[]{:S(2)}, u32[]{:S(2)}) async-start(bf16[64,128,128]{2,1,0:T(8,128)(2,1)} %bitcast.116), calls=%async_computation.1 | async-start | bytes 4194304 | tf_op jit(solution)/shard_map/all_to_all | solution.py:229
  76.1 4.3 %collective-permute-start.2 = (bf16[2,4,32,640]{3,2,0,1:T(8,128)(2,1)S(1)}, bf16[2,4,32,640]{3,2,0,1:T(8,128)(2,1)S(1)}, u32[]{:S(2)}, u32[]{:S(2)}) collective-permute-start(bf16[2,4,32,640]{3,2,0,1:T(8,128)(2,1)S(1)} %bitcast.122), channel_id=1, source_target_pairs={{0,384},{128,256},{256,128},{384,0},{1,385},{129,257},{257,129},{3... | collective-permute-start | bytes 983048 | tf_op jit(solution)/shard_map/ppermute | solution.py:25
  80.4 4.0 %collective-permute-start.3 = (bf16[512,128]{1,0:T(8,128)(2,1)S(1)}, bf16[512,128]{1,0:T(8,128)(2,1)S(1)}, u32[]{:S(2)}, u32[]{:S(2)}) collective-permute-start(bf16[512,128]{1,0:T(8,128)(2,1)S(1)} %copy-done.12), channel_id=1, source_target_pairs={{0,1},{1,0},{2,3},{3,2},{4,5},{5,4},{6,7},{7,6},{8,9},{9,8},{10,11... | collective-permute-start | bytes 393224 | tf_op jit(solution)/shard_map/ppermute | solution.py:25
  84.4 2.3 collective-permute-start.1
  86.7 2.1 collective-permute-start
  88.9 4.4 %collective-permute-start.6 = (bf16[2,512,128]{2,1,0:T(8,128)(2,1)S(1)}, bf16[2,512,128]{2,1,0:T(8,128)(2,1)S(1)}, u32[]{:S(2)}, u32[]{:S(2)}) collective-permute-start(bf16[2,512,128]{2,1,0:T(8,128)(2,1)S(1)} %maximum_select_fusion.1), channel_id=1, source_target_pairs={{0,6},{2,4},{4,2},{6,0},{1,7},{3,5},{5,3},{7,1},{8,14},{10,12},{12... | collective-permute-start | bytes 786440 | tf_op jit(solution)/shard_map/ppermute | solution.py:25
  93.3 2.4 collective-permute-start.5
  95.7 2.2 collective-permute-start.4
  97.9 0.9 collective-permute-done.1
  98.9 7.5 %collective-permute-done = bf16[2,4,32,640]{3,2,0,1:T(8,128)(2,1)S(1)} collective-permute-done((bf16[2,4,32,640]{3,2,0,1:T(8,128)(2,1)S(1)}, bf16[2,4,32,640]{3,2,0,1:T(8,128)(2,1)S(1)}, u32[]{:S(2)}, u32[]{:S(2)}) %collective-permute-start) | collective-permute-done | bytes 327712 | tf_op jit(solution)/shard_map/ppermute | solution.py:25
  106.6 1.2 copy.46
  107.8 1.1 pad_maximum_fusion.1
  108.9 2.0 gather_fusion.3
  110.9 1.9 all-gather.4.cloned.1.call-done
  112.9 2.7 convolution_convert_fusion
  115.6 14.1 %collective-permute-start.7 = (bf16[512,1024]{1,0:T(8,128)(2,1)S(1)}, bf16[512,1024]{1,0:T(8,128)(2,1)S(1)}, u32[]{:S(2)}, u32[]{:S(2)}) collective-permute-start(bf16[512,1024]{1,0:T(8,128)(2,1)S(1)} %convolution_convert_fusion), channel_id=1, source_target_pairs={{0,1},{1,0},{2,3},{3,2},{4,5},{5,4},{6,7},{7,6},{8,9},{9,8},{10,11... | collective-permute-start | bytes 3145736 | tf_op jit(solution)/shard_map/ppermute | solution.py:25
  129.7 1.0 convolution_convert_fusion.1
  130.7 1.2 collective-permute-done.7
  131.9 1.8 convert_add_fusion
  134.6 5.6 %collective-permute-start.10 = (bf16[4,32,1024]{2,1,0:T(8,128)(2,1)}, bf16[4,32,1024]{2,1,0:T(8,128)(2,1)}, u32[]{:S(2)}, u32[]{:S(2)}) collective-permute-start(bf16[4,32,1024]{2,1,0:T(8,128)(2,1)} %bitcast.31), channel_id=1, source_target_pairs={{0,6},{2,4},{4,2},{6,0},{1,7},{3,5},{5,3},{7,1},{8,14},{10,12},{12... | collective-permute-start | bytes 786440 | tf_op jit(solution)/shard_map/ppermute | solution.py:25
  140.1 1.9 collective-permute-start.9
  142.1 2.5 collective-permute-start.8
  144.6 1.1 slice.90
  145.7 5.8 %collective-permute-done.10 = bf16[4,32,1024]{2,1,0:T(8,128)(2,1)} collective-permute-done((bf16[4,32,1024]{2,1,0:T(8,128)(2,1)}, bf16[4,32,1024]{2,1,0:T(8,128)(2,1)}, u32[]{:S(2)}, u32[]{:S(2)}) %collective-permute-start.10) | collective-permute-done | bytes 262176 | tf_op jit(solution)/shard_map/ppermute | solution.py:25
  151.6 3.1 %collective-permute-done.8 = bf16[4,32,1024]{2,1,0:T(8,128)(2,1)} collective-permute-done((bf16[4,32,1024]{2,1,0:T(8,128)(2,1)S(1)}, bf16[4,32,1024]{2,1,0:T(8,128)(2,1)}, u32[]{:S(2)}, u32[]{:S(2)}) %collective-permute-start.8) | collective-permute-done | bytes 262176 | tf_op jit(solution)/shard_map/ppermute | solution.py:25
  154.7 1.3 add_convert_fusion
  156.0 3.5 %collective-permute-start.13 = (bf16[32,1024]{1,0:T(8,128)(2,1)S(1)}, bf16[32,1024]{1,0:T(8,128)(2,1)S(1)}, u32[]{:S(2)}, u32[]{:S(2)}) collective-permute-start(bf16[32,1024]{1,0:T(8,128)(2,1)S(1)} %get-tuple-element.52), channel_id=1, source_target_pairs={{0,384},{128,256},{256,128},{384,0},{1,385},{129,257},{257,129},{3... | collective-permute-start | bytes 196616 | tf_op jit(solution)/shard_map/ppermute | solution.py:25
  159.5 2.7 collective-permute-start.12
  162.3 2.8 collective-permute-start.11
  165.4 2.4 collective-permute-done.12
  167.8 3.4 %collective-permute-done.11 = bf16[32,1024]{1,0:T(8,128)(2,1)S(1)} collective-permute-done((bf16[32,1024]{1,0:T(8,128)(2,1)S(1)}, bf16[32,1024]{1,0:T(8,128)(2,1)S(1)}, u32[]{:S(2)}, u32[]{:S(2)}) %collective-permute-start.11) | collective-permute-done | bytes 65568 | tf_op jit(solution)/shard_map/ppermute | solution.py:25
  172.0 2.2 gather_fusion.4
  174.2 1.0 convert_bitcast_fusion
  176.0 1.0 fusion.19
  177.8 2.6 pad_maximum_fusion.2
  180.3 9.2 %all-to-all-start.2 = ((bf16[32,32,512]{2,1,0:T(8,128)(2,1)}), bf16[32,32,512]{2,1,0:T(8,128)(2,1)}, u32[]{:S(2)}, u32[]{:S(2)}) async-start(bf16[32,32,512]{2,1,0:T(8,128)(2,1)} %pad_maximum_fusion.2), calls=%async_computation.2 | async-start | bytes 2097152 | tf_op jit(solution)/shard_map/all_to_all | solution.py:282
  190.3 1.3 fusion.7.embedded_ref
  191.8 1.0 copy-done.2
  192.8 9.2 %score.1 = (f32[128,1]{1,0:T(8,128)S(1)}, bf16[64,128]{1,0:T(8,128)(2,1)S(1)}) custom-call(bf16[8192,128]{1,0:T(8,128)(2,1)} %bitcast.42.docs, f32[32,128]{1,0:T(8,128)S(1)} %fusion.7.embedded_ref, s32[128,32]{1,0:T(8,128)S(1)} %broadcast_in_dim.98.spans, s32[128,2]{1,0:T(8,128)S(1)} %copy.51.flags, f32[32,4096]{1,0:T(8,128)S(1)} %copy-done.2, ...), custom_call_target="tpu_custom_call" | custom-call | flops 134217728 | bytes 30000000 | tf_op jit(solution)/shard_map/score/pallas_call | solution.py:159
  202.0 5.6 %all-to-all-done.2 = bf16[32,32,512]{2,1,0:T(8,128)(2,1)} async-done(((bf16[32,32,512]{2,1,0:T(8,128)(2,1)}), bf16[32,32,512]{2,1,0:T(8,128)(2,1)}, u32[]{:S(2)}, u32[]{:S(2)}) %all-to-all-start.2) | async-done | bytes 1048608 | tf_op jit(solution)/shard_map/all_to_all | solution.py:282
  207.7 17.3 %all_to_all.37 = bf16[32,64,128]{2,1,0:T(8,128)(2,1)} all-to-all(bf16[32,64,128]{2,1,0:T(8,128)(2,1)S(1)} %broadcast_in_dim.103), channel_id=1, replica_groups=mesh['y'=4,'z'=16,'x'=4,'c'=2] {'y','x','c'}, dimensions={0} | all-to-all | bytes 1048576 | tf_op jit(solution)/shard_map/all_to_all | solution.py:289
  225.1 1.4 dynamic_slice.7
  226.6 1.4 select_reduce_fusion.1
  227.9 2.3 copy.52
  230.2 1.0 slice.99
  232.6 1.7 convolution_convert_fusion.3
  234.3 1.0 slice_reduce_fusion
  236.0 9.3 %all-to-all-start.4 = ((bf16[16,34,128]{2,1,0:T(8,128)(2,1)}), bf16[16,34,128]{2,1,0:T(8,128)(2,1)}, u32[]{:S(2)}, u32[]{:S(2)}) async-start(bf16[16,34,128]{2,1,0:T(8,128)(2,1)} %pad_maximum_fusion.4), calls=%async_computation.4 | async-start | bytes 327680 | tf_op jit(solution)/shard_map/all_to_all | solution.py:316
  245.4 1.7 multiply_reduce_fusion.1
  247.1 1.5 subtract_convert_fusion
  248.6 9.3 %all-to-all-done.4 = bf16[16,34,128]{2,1,0:T(8,128)(2,1)} async-done(((bf16[16,34,128]{2,1,0:T(8,128)(2,1)}), bf16[16,34,128]{2,1,0:T(8,128)(2,1)}, u32[]{:S(2)}, u32[]{:S(2)}) %all-to-all-start.4) | async-done | bytes 139296 | tf_op jit(solution)/shard_map/all_to_all | solution.py:316
  257.9 0.9 reduce_sum.105
  259.5 7.6 %all-to-all-start.5 = ((bf16[16,34,128]{2,1,0:T(8,128)(2,1)}), bf16[16,34,128]{2,1,0:T(8,128)(2,1)S(1)}, u32[]{:S(2)}, u32[]{:S(2)}) async-start(bf16[16,34,128]{2,1,0:T(8,128)(2,1)} %broadcast_in_dim.104), calls=%async_computation.5 | async-start | bytes 327680 | tf_op jit(solution)/shard_map/all_to_all | solution.py:318
  267.1 2.2 multiply_reduce_fusion
  269.4 1.5 fusion.2
  270.9 5.2 %convolution_multiply_fusion.1 = f32[256,640]{1,0:T(8,128)} fusion(bf16[256,4096]{1,0:T(8,128)(2,1)S(1)} %copy-done.7, bf16[640,4096]{0,1:T(8,128)(2,1)} %all-gather.6.cloned.1.call-done, f32[256]{0:T(256)S(1)} %get-tuple-element.56), kind=kOutput, calls=%fused_computation.12 | convolution fusion | flops 1342341120 | bytes 7996416 | tf_op jit(solution)/shard_map/dot_general | solution.py:335
  276.1 5.7 %fusion.1 = bf16[256,640]{1,0:T(8,128)(2,1)} fusion(f32[256,640]{1,0:T(8,128)} %convolution_multiply_fusion.1, bf16[256,128]{1,0:T(8,128)(2,1)S(1)} %bitcast.139, bf16[640,4096]{0,1:T(8,128)(2,1)} %all-gather.6.cloned.1.call-done, bf16[4096,128]{1,0:T(8,128)(2,1)S(1)} %bitcast.110, f32[4096]{0:T(1024)S(1)} %copy-done.17, f32[256]{0:T(256)S(1)} %get-tuple-element.55), kind=kOutput, calls=%fused_computation.15 | convolution fusion | flops 715177984 | bytes 7357440 | tf_op jit(solution)/shard_map/dot_general | solution.py:344
  (120 shorter events, 15.3 us)
Async XLA Ops:
  7.2 27.6 %copy-start = (bf16[8192,128]{1,0:T(8,128)(2,1)S(1)}, bf16[8192,128]{1,0:T(8,128)(2,1)}, u32[]{:S(2)}) copy-start(bf16[8192,128]{1,0:T(8,128)(2,1)} %param.20) | copy-start | bytes 6291460
  8.8 0.5 copy-start.23
  8.9 0.5 copy-start.21
  10.8 47.1 %all-to-all-start = ((s32[64,1,128]{2,1,0:T(1,128)}), s32[64,1,128]{2,1,0:T(1,128)S(1)}, u32[]{:S(2)}, u32[]{:S(2)}) async-start(s32[64,1,128]{2,1,0:T(1,128)} %bitcast.7), calls=%async_computation | async-start | bytes 65536 | tf_op jit(solution)/shard_map/all_to_all | solution.py:225
  30.1 82.7 %all-gather.4.cloned.1.call-start = ((), (), s32[]{:S(2)}) async-start(), calls=%async_computation.6 | async-start | bytes 1392640 | tf_op jit(solution)/shard_map/all_gather | solution.py:223
  34.7 14.9 %copy-start.4 = (f32[4]{0:T(128)S(1)}, f32[4]{0:T(128)}, u32[]{:S(2)}) copy-start(f32[4]{0:T(128)} %buckets.1) | copy-start | bytes 52
  49.6 1.6 copy-start.1
  51.3 1.2 copy-start.3
  60.4 15.0 %copy-start.13 = (bf16[256,640]{1,0:T(8,128)(2,1)S(1)}, bf16[256,640]{1,0:T(8,128)(2,1)}, u32[]{:S(2)}) copy-start(bf16[256,640]{1,0:T(8,128)(2,1)} %param.12) | copy-start | bytes 983044
  60.4 20.0 %copy-start.12 = (bf16[512,128]{1,0:T(8,128)(2,1)S(1)}, bf16[512,128]{1,0:T(8,128)(2,1)}, u32[]{:S(2)}) copy-start(bf16[512,128]{1,0:T(8,128)(2,1)} %param.15) | copy-start | bytes 393220
  60.4 117.4 %all-to-all-start.1 = ((bf16[64,128,128]{2,1,0:T(8,128)(2,1)}), bf16[64,128,128]{2,1,0:T(8,128)(2,1)}, u32[]{:S(2)}, u32[]{:S(2)}) async-start(bf16[64,128,128]{2,1,0:T(8,128)(2,1)} %bitcast.116), calls=%async_computation.1 | async-start | bytes 4194304 | tf_op jit(solution)/shard_map/all_to_all | solution.py:229
  75.3 149.8 %all-gather.6.cloned.1.call-start = ((), (), s32[]{:S(2)}) async-start(), calls=%async_computation.7 | async-start | bytes 6553600 | tf_op jit(solution)/shard_map/all_gather | solution.py:294
  76.1 19.6 %collective-permute-start.2 = (bf16[2,4,32,640]{3,2,0,1:T(8,128)(2,1)S(1)}, bf16[2,4,32,640]{3,2,0,1:T(8,128)(2,1)S(1)}, u32[]{:S(2)}, u32[]{:S(2)}) collective-permute-start(bf16[2,4,32,640]{3,2,0,1:T(8,128)(2,1)S(1)} %bitcast.122), channel_id=1, source_target_pairs={{0,384},{128,256},{256,128},{384,0},{1,385},{129,257},{257,129},{3... | collective-permute-start | bytes 983048 | tf_op jit(solution)/shard_map/ppermute | solution.py:25
  80.4 8.5 %collective-permute-start.3 = (bf16[512,128]{1,0:T(8,128)(2,1)S(1)}, bf16[512,128]{1,0:T(8,128)(2,1)S(1)}, u32[]{:S(2)}, u32[]{:S(2)}) collective-permute-start(bf16[512,128]{1,0:T(8,128)(2,1)S(1)} %copy-done.12), channel_id=1, source_target_pairs={{0,1},{1,0},{2,3},{3,2},{4,5},{5,4},{6,7},{7,6},{8,9},{9,8},{10,11... | collective-permute-start | bytes 393224 | tf_op jit(solution)/shard_map/ppermute | solution.py:25
  84.4 14.5 %collective-permute-start.1 = (bf16[2,4,32,640]{3,2,0,1:T(8,128)(2,1)S(1)}, bf16[2,4,32,640]{3,2,0,1:T(8,128)(2,1)S(1)}, u32[]{:S(2)}, u32[]{:S(2)}) collective-permute-start(bf16[2,4,32,640]{3,2,0,1:T(8,128)(2,1)S(1)} %bitcast.123), channel_id=1, source_target_pairs={{0,256},{128,384},{256,0},{384,128},{1,257},{129,385},{257,1},{385... | collective-permute-start | bytes 983048 | tf_op jit(solution)/shard_map/ppermute | solution.py:25
  86.7 19.7 %collective-permute-start = (bf16[2,4,32,640]{3,2,0,1:T(8,128)(2,1)S(1)}, bf16[2,4,32,640]{3,2,0,1:T(8,128)(2,1)S(1)}, u32[]{:S(2)}, u32[]{:S(2)}) collective-permute-start(bf16[2,4,32,640]{3,2,0,1:T(8,128)(2,1)S(1)} %bitcast.124), channel_id=1, source_target_pairs={{0,128},{128,0},{256,384},{384,256},{1,129},{129,1},{257,385},{385... | collective-permute-start | bytes 983048 | tf_op jit(solution)/shard_map/ppermute | solution.py:25
  88.9 18.9 %collective-permute-start.6 = (bf16[2,512,128]{2,1,0:T(8,128)(2,1)S(1)}, bf16[2,512,128]{2,1,0:T(8,128)(2,1)S(1)}, u32[]{:S(2)}, u32[]{:S(2)}) collective-permute-start(bf16[2,512,128]{2,1,0:T(8,128)(2,1)S(1)} %maximum_select_fusion.1), channel_id=1, source_target_pairs={{0,6},{2,4},{4,2},{6,0},{1,7},{3,5},{5,3},{7,1},{8,14},{10,12},{12... | collective-permute-start | bytes 786440 | tf_op jit(solution)/shard_map/ppermute | solution.py:25
  93.3 14.5 %collective-permute-start.5 = (bf16[2,512,128]{2,1,0:T(8,128)(2,1)S(1)}, bf16[2,512,128]{2,1,0:T(8,128)(2,1)S(1)}, u32[]{:S(2)}, u32[]{:S(2)}) collective-permute-start(bf16[2,512,128]{2,1,0:T(8,128)(2,1)S(1)} %maximum_select_fusion.1), channel_id=1, source_target_pairs={{0,4},{2,6},{4,0},{6,2},{1,5},{3,7},{5,1},{7,3},{8,12},{10,14},{12... | collective-permute-start | bytes 786440 | tf_op jit(solution)/shard_map/ppermute | solution.py:25
  95.7 12.1 %collective-permute-start.4 = (bf16[2,512,128]{2,1,0:T(8,128)(2,1)S(1)}, bf16[2,512,128]{2,1,0:T(8,128)(2,1)S(1)}, u32[]{:S(2)}, u32[]{:S(2)}) collective-permute-start(bf16[2,512,128]{2,1,0:T(8,128)(2,1)S(1)} %maximum_select_fusion.1), channel_id=1, source_target_pairs={{0,2},{2,0},{4,6},{6,4},{1,3},{3,1},{5,7},{7,5},{8,10},{10,8},{12,... | collective-permute-start | bytes 786440 | tf_op jit(solution)/shard_map/ppermute | solution.py:25
  112.9 16.8 %copy-start.10 = (bf16[640,1024]{0,1:T(8,128)(2,1)S(1)}, bf16[640,1024]{0,1:T(8,128)(2,1)}, u32[]{:S(2)}) copy-start(bf16[640,1024]{0,1:T(8,128)(2,1)} %all-gather.4.cloned.1.call-done) | copy-start | bytes 3932164
  112.9 16.8 %copy-start.11 = (bf16[2,4,4,32,640]{4,3,2,1,0:T(8,128)(2,1)S(1)}, bf16[2,4,4,32,640]{4,3,2,1,0:T(8,128)(2,1)}, u32[]{:S(2)}) copy-start(bf16[2,4,4,32,640]{4,3,2,1,0:T(8,128)(2,1)} %copy.46) | copy-start | bytes 3932164
  115.6 16.4 %collective-permute-start.7 = (bf16[512,1024]{1,0:T(8,128)(2,1)S(1)}, bf16[512,1024]{1,0:T(8,128)(2,1)S(1)}, u32[]{:S(2)}, u32[]{:S(2)}) collective-permute-start(bf16[512,1024]{1,0:T(8,128)(2,1)S(1)} %convolution_convert_fusion), channel_id=1, source_target_pairs={{0,1},{1,0},{2,3},{3,2},{4,5},{5,4},{6,7},{7,6},{8,9},{9,8},{10,11... | collective-permute-start | bytes 3145736 | tf_op jit(solution)/shard_map/ppermute | solution.py:25
  134.6 17.0 %collective-permute-start.10 = (bf16[4,32,1024]{2,1,0:T(8,128)(2,1)}, bf16[4,32,1024]{2,1,0:T(8,128)(2,1)}, u32[]{:S(2)}, u32[]{:S(2)}) collective-permute-start(bf16[4,32,1024]{2,1,0:T(8,128)(2,1)} %bitcast.31), channel_id=1, source_target_pairs={{0,6},{2,4},{4,2},{6,0},{1,7},{3,5},{5,3},{7,1},{8,14},{10,12},{12... | collective-permute-start | bytes 786440 | tf_op jit(solution)/shard_map/ppermute | solution.py:25
  140.1 11.4 %collective-permute-start.9 = (bf16[4,32,1024]{2,1,0:T(8,128)(2,1)}, bf16[4,32,1024]{2,1,0:T(8,128)(2,1)}, u32[]{:S(2)}, u32[]{:S(2)}) collective-permute-start(bf16[4,32,1024]{2,1,0:T(8,128)(2,1)} %bitcast.30), channel_id=1, source_target_pairs={{0,4},{2,6},{4,0},{6,2},{1,5},{3,7},{5,1},{7,3},{8,12},{10,14},{12... | collective-permute-start | bytes 786440 | tf_op jit(solution)/shard_map/ppermute | solution.py:25
  142.1 12.6 %collective-permute-start.8 = (bf16[4,32,1024]{2,1,0:T(8,128)(2,1)S(1)}, bf16[4,32,1024]{2,1,0:T(8,128)(2,1)}, u32[]{:S(2)}, u32[]{:S(2)}) collective-permute-start(bf16[4,32,1024]{2,1,0:T(8,128)(2,1)S(1)} %bitcast.140), channel_id=1, source_target_pairs={{0,2},{2,0},{4,6},{6,4},{1,3},{3,1},{5,7},{7,5},{8,10},{10,8},{12,... | collective-permute-start | bytes 786440 | tf_op jit(solution)/shard_map/ppermute | solution.py:25
  155.9 19.3 %copy-start.8 = (bf16[32,4096]{1,0:T(8,128)(2,1)S(1)}, bf16[32,4096]{1,0:T(8,128)(2,1)}, u32[]{:S(2)}) copy-start(bf16[32,4096]{1,0:T(8,128)(2,1)} %param.11) | copy-start | bytes 786436
  156.0 9.4 %collective-permute-start.13 = (bf16[32,1024]{1,0:T(8,128)(2,1)S(1)}, bf16[32,1024]{1,0:T(8,128)(2,1)S(1)}, u32[]{:S(2)}, u32[]{:S(2)}) collective-permute-start(bf16[32,1024]{1,0:T(8,128)(2,1)S(1)} %get-tuple-element.52), channel_id=1, source_target_pairs={{0,384},{128,256},{256,128},{384,0},{1,385},{129,257},{257,129},{3... | collective-permute-start | bytes 196616 | tf_op jit(solution)/shard_map/ppermute | solution.py:25
  159.5 8.3 %collective-permute-start.12 = (bf16[32,1024]{1,0:T(8,128)(2,1)S(1)}, bf16[32,1024]{1,0:T(8,128)(2,1)S(1)}, u32[]{:S(2)}, u32[]{:S(2)}) collective-permute-start(bf16[32,1024]{1,0:T(8,128)(2,1)S(1)} %get-tuple-element.53), channel_id=1, source_target_pairs={{0,256},{128,384},{256,0},{384,128},{1,257},{129,385},{257,1},{385... | collective-permute-start | bytes 196616 | tf_op jit(solution)/shard_map/ppermute | solution.py:25
  162.3 9.0 %collective-permute-start.11 = (bf16[32,1024]{1,0:T(8,128)(2,1)S(1)}, bf16[32,1024]{1,0:T(8,128)(2,1)S(1)}, u32[]{:S(2)}, u32[]{:S(2)}) collective-permute-start(bf16[32,1024]{1,0:T(8,128)(2,1)S(1)} %get-tuple-element.54), channel_id=1, source_target_pairs={{0,128},{128,0},{256,384},{384,256},{1,129},{129,1},{257,385},{385... | collective-permute-start | bytes 196616 | tf_op jit(solution)/shard_map/ppermute | solution.py:25
  175.2 0.8 copy-start.5
  176.0 4.4 %copy-start.19 = (f32[32]{0:T(128)}, f32[32]{0:T(128)S(1)}, u32[]{:S(2)}) copy-start(f32[32]{0:T(128)S(1)} %get-tuple-element.58) | copy-start | bytes 388
  177.0 12.6 %copy-start.20 = (s32[1,64]{1,0:T(1,128)S(1)}, s32[1,64]{1,0:T(1,128)}, u32[]{:S(2)}) copy-start(s32[1,64]{1,0:T(1,128)} %param.16) | copy-start | bytes 772
  177.0 12.6 %copy-start.24 = (s32[64]{0:T(128)S(1)}, s32[64]{0:T(128)}, u32[]{:S(2)}) copy-start(s32[64]{0:T(128)} %copy-done.23) | copy-start | bytes 772
  177.0 12.7 %copy-start.22 = (s32[64]{0:T(128)S(1)}, s32[64]{0:T(128)}, u32[]{:S(2)}) copy-start(s32[64]{0:T(128)} %copy-done.21) | copy-start | bytes 772
  180.3 27.3 %all-to-all-start.2 = ((bf16[32,32,512]{2,1,0:T(8,128)(2,1)}), bf16[32,32,512]{2,1,0:T(8,128)(2,1)}, u32[]{:S(2)}, u32[]{:S(2)}) async-start(bf16[32,32,512]{2,1,0:T(8,128)(2,1)} %pad_maximum_fusion.2), calls=%async_computation.2 | async-start | bytes 2097152 | tf_op jit(solution)/shard_map/all_to_all | solution.py:282
  189.5 77.6 %all-gather.8.cloned.1.call-start = ((), (), s32[]{:S(2)}) async-start(), calls=%async_computation.8 | async-start | bytes 2359296 | tf_op jit(solution)/shard_map/all_gather | solution.py:298
  191.8 1.1 copy-start.2
  231.2 0.7 copy-start.9
  231.9 0.7 copy-start.15
  236.0 21.8 %all-to-all-start.4 = ((bf16[16,34,128]{2,1,0:T(8,128)(2,1)}), bf16[16,34,128]{2,1,0:T(8,128)(2,1)}, u32[]{:S(2)}, u32[]{:S(2)}) async-start(bf16[16,34,128]{2,1,0:T(8,128)(2,1)} %pad_maximum_fusion.4), calls=%async_computation.4 | async-start | bytes 327680 | tf_op jit(solution)/shard_map/all_to_all | solution.py:316
  245.4 1.7 copy-start.6
  248.6 20.7 %copy-start.14 = (bf16[256,128]{0,1:T(8,128)(2,1)S(1)}, bf16[256,128]{0,1:T(8,128)(2,1)}, u32[]{:S(2)}) copy-start(bf16[256,128]{0,1:T(8,128)(2,1)} %copy.53) | copy-start | bytes 196612
  248.6 20.8 %copy-start.17 = (f32[4096]{0:T(1024)S(1)}, f32[4096]{0:T(1024)}, u32[]{:S(2)}) copy-start(f32[4096]{0:T(1024)} %param.14) | copy-start | bytes 49156
  259.5 22.4 %all-to-all-start.5 = ((bf16[16,34,128]{2,1,0:T(8,128)(2,1)}), bf16[16,34,128]{2,1,0:T(8,128)(2,1)S(1)}, u32[]{:S(2)}, u32[]{:S(2)}) async-start(bf16[16,34,128]{2,1,0:T(8,128)(2,1)} %broadcast_in_dim.104), calls=%async_computation.5 | async-start | bytes 327680 | tf_op jit(solution)/shard_map/all_to_all | solution.py:318
  267.1 2.3 copy-start.7
  270.9 5.2 %copy-start.16 = (bf16[8,32,128]{2,1,0:T(8,128)(2,1)S(1)}, bf16[8,32,128]{2,1,0:T(8,128)(2,1)}, u32[]{:S(2)}) copy-start(bf16[8,32,128]{2,1,0:T(8,128)(2,1)} %copy-done.15) | copy-start | bytes 196612
  276.1 6.4 %copy-start.18 = (f32[512]{0:T(512)S(1)}, f32[512]{0:T(512)}, u32[]{:S(2)}) copy-start(f32[512]{0:T(512)} %dynamic_slice.7) | copy-start | bytes 6148
Sparse Core Ops, SparseCore 0:
  33.0 79.7 all-gather.3
  114.9 97.4 all-gather.5
  225.2 28.1 all-gather.7

commit v6 on v5

--- a/solution.py
+++ b/solution.py
@@ -178,6 +178,40 @@
     )(docs, embedded, spans, flags, unit, head)
 
 
+def bundle_kernel(packets, unit, out, ge):
+    count, tall, features = packets.shape
+    tokens = unit.shape[0] // count
+    shares, _, _ = out.shape
+    total = jnp.zeros((tall - tokens, features), F32)
+    for i in range(count):
+        ge[i * tokens : (i + 1) * tokens, :] = packets[i, 0:tokens, :]
+        total = total + packets[i, tokens:tall, :].astype(F32)
+    head = lax.dot_general(
+        ge[...], unit[...], (((0,), (0,)), ((), ())), preferred_element_type=F32
+    ).T
+    share = head.shape[0] // shares
+    lines = total.shape[0] // shares
+    for i in range(shares):
+        out[i, 0:share, :] = head[i * share : (i + 1) * share].astype(BF16)
+        gain = jnp.concatenate(
+            [total[i * lines : (i + 1) * lines], jnp.zeros((16 - lines, features), F32)]
+        )
+        out[i, share : share + 16, :] = gain.astype(BF16)
+
+
+def bundle(packets, unit, shares):
+    count, tall, features = packets.shape
+    return pl.pallas_call(
+        bundle_kernel,
+        in_specs=[VMEM] * 2,
+        out_specs=VMEM,
+        out_shape=jax.ShapeDtypeStruct((shares, unit.shape[1] // shares + 16, features), BF16),
+        scratch_shapes=[pltpu.VMEM((unit.shape[0], features), BF16)],
+        compiler_params=pltpu.CompilerParams(vmem_limit_bytes=32 * 1024 * 1024),
+        name="bundle",
+    )(packets, unit)
+
+
 def local(
     residual,
     context,
@@ -225,7 +259,8 @@
     notes = lax.all_to_all(note, DP, 0, 0, tiled=True)
     documents = documents.reshape(per_shard, doc_len, feature_dim)
     chosen = rows_of(documents, notes[:, per_shard : per_shard + cap].reshape(slots))
-    chosen, context, colbert_head = lax.optimization_barrier((chosen, context, colbert_head))
+    chosen, colbert_head = lax.optimization_barrier((chosen, colbert_head))
+    proj_z, context = lax.optimization_barrier((proj_z, context))
     got_docs = lax.all_to_all(
         chosen.reshape(shards, cap * doc_len, feature_dim), DP, 0, 0, tiled=True
     ).reshape(slots * doc_len, feature_dim)
@@ -256,7 +291,12 @@
     head_full = unxor(
         jnp.stack([head_pair] + [swap(head_pair, "x", X, step) for step in range(1, X)]), here_x
     ).reshape(width, feature_dim)
-    by_y, head_full, proj_z = lax.optimization_barrier((by_y, head_full, proj_z))
+    head_rows = colbert_head.shape[0]
+    mine = (here_x * C + here_c) * head_rows
+    gain_blk = lax.dynamic_slice_in_dim(norm_gain, mine, head_rows, 0)
+    by_y, head_full, proj_z, gain_blk = lax.optimization_barrier(
+        (by_y, head_full, proj_z, gain_blk)
+    )
 
     away = jnp.dot(by_y[1], proj_z, preferred_element_type=F32).astype(BF16)
     away = swap(away, "c", C, 1)
@@ -276,15 +316,17 @@
     normed = (scaled_sum * norm_gain).astype(BF16)
     embedded = jnp.dot(normed, head_full, preferred_element_type=F32)
 
-    head_rows = colbert_head.shape[0]
     unit = scaled_sum.astype(BF16).reshape(seq_rows, X * C, head_rows).transpose(1, 0, 2)
     unit, got_docs = lax.optimization_barrier((unit, got_docs))
     unit_plane = lax.all_to_all(
-        jnp.concatenate([unit] * Y), PLANE, 0, 0, tiled=True
+        jnp.broadcast_to(unit, (Y,) + unit.shape).reshape((-1,) + unit.shape[1:]),
+        PLANE,
+        0,
+        0,
+        tiled=True,
     ).reshape(Y * X * C * seq_rows, head_rows)
 
     slot_scores, packet = score(got_docs, embedded, spans, flags, scaled_sum, head_full)
-    scores = jnp.sum(jnp.where(placed, slot_scores, 0.0), axis=0)[None, :]
     packet, unit_plane = lax.optimization_barrier((packet, unit_plane))
     packets = lax.all_to_all(
         jnp.broadcast_to(packet, (Y * X * C,) + packet.shape), PLANE, 0, 0, tiled=True
@@ -299,26 +341,11 @@
 
     share = head_rows // Z
     lines = width // feature_dim // Z
-    head_term = lax.dot_general(
-        unit_plane,
-        ge_plane.reshape(Y * X * C * seq_rows, feature_dim),
-        (((0,), (0,)), ((), ())),
-        preferred_element_type=F32,
-    )
-    gain_term = jnp.sum(packets[:, seq_rows:].astype(F32), axis=0)
-    first = jnp.concatenate(
-        [
-            head_term.reshape(Z, share, feature_dim).astype(BF16),
-            gain_term.reshape(Z, lines, feature_dim).astype(BF16),
-        ],
-        axis=1,
-    )
+    first = bundle(packets, unit_plane, Z)
+    first, slot_scores, ge_plane = lax.optimization_barrier((first, slot_scores, ge_plane))
+    scores = jnp.sum(jnp.where(placed, slot_scores, 0.0), axis=0)[None, :]
     first = lax.all_to_all(first, "z", 0, 0, tiled=True)
     second = jnp.sum(first.astype(F32), axis=0, keepdims=True).astype(BF16)
-    second = lax.all_to_all(
-        jnp.broadcast_to(second, (Z,) + second.shape[1:]), "z", 0, 0, tiled=True
-    )
-
     packet, packets = lax.optimization_barrier((packet, packets))
     grad_embedded = packet[:seq_rows]
     grad_normed = lax.dot_general(
@@ -332,6 +359,12 @@
     ge_all = ge_all.reshape(X * C * seq_rows, feature_dim)
     gained_head = (head_full.astype(F32) * norm_gain[:, None]).astype(BF16)
     mixed_head = jnp.dot(proj_full, gained_head, preferred_element_type=F32).astype(BF16)
+    second, mixed_head, residual_grad = lax.optimization_barrier(
+        (second, mixed_head, residual_grad)
+    )
+    second = lax.all_to_all(
+        jnp.broadcast_to(second, (Z,) + second.shape[1:]), "z", 0, 0, tiled=True
+    )
     pulled = lax.dot_general(
         summed_all, proj_full, (((1,), (1,)), ((), ())), preferred_element_type=F32
     )
@@ -348,10 +381,8 @@
     ).astype(BF16)
 
     second, context_grad = lax.optimization_barrier((second, context_grad))
-    mine = (here_x * C + here_c) * head_rows
-    gain_blk = lax.dynamic_slice_in_dim(norm_gain, mine, head_rows, 0)
     head_grad = second[:, :share].astype(F32).reshape(head_rows, feature_dim) * gain_blk[:, None]
-    gain_grad = second[:, share:].astype(F32).reshape(width)
+    gain_grad = second[:, share : share + lines].astype(F32).reshape(width)
     return (scores, context_grad, residual_grad, head_grad, gain_grad)
 
 

time: 292 us -> 279 us (0.955)
  waiting for transfers between devices: 42.3 us -> 33.9 us
  local copies, waits for them, and re-layouts: 42.4 us -> 38.8 us
    all_to_all x1, waiting for transfers between devices: 9.25 us -> 2.81 us  [local(): first = lax.all_to_all(first, 'z', 0, 0, tiled=True)]
    ppermute x14, starting transfers between devices: 54.9 us -> 49.4 us  [swap(): return lax.ppermute(values, axis, [(i, i ^ step) for i in range(size)])]
    dot_general x1, matrix products: 5.74 us -> 0.98 us  [local(): lax.dot_general(ge_all, mixed_head, (((1,), (1,)), ((), ())), preferred_e...]
    dot_general x1, matrix products: 1.7 us -> 5.48 us  [local(): jnp.dot(proj_full, gained_head, preferred_element_type=F32).astype(BF16)]
    concatenate x2 -> x0, other arithmetic: 3.25 us -> none  [the longest x1 2.56 us: local(): jnp.concatenate([unit] * Y)]
    ppermute x14, waiting for transfers between devices: 24.8 us -> 21.5 us  [swap(): return lax.ppermute(values, axis, [(i, i ^ step) for i in range(size)])]
    all_to_all x1, waiting for transfers between devices: 0.01 us -> 3.17 us  [local(): lax.all_to_all(jnp.broadcast_to(second, (Z,) + second.shape[1:]), 'z', 0,...]
    unnamed x50 -> x61, local copies, waits for them, and re-layouts: 4.99 us -> 5.88 us
  transfers between devices with their start and end apart: 22 -> 22, of which waited for: 11 -> 12; matrix products, arithmetic and copies ran while one was open for 26% -> 26% of each run, Pallas kernels for 5% -> 6%
where the time goes in v6:
time: 279 us; the launch traced here: 275 us
  starting transfers between devices  114 us (41%)
  local copies, waits for them, and re-layouts  38.8 us (14%)
  waiting for transfers between devices  33.9 us (12%)
  other arithmetic  21.2 us (8%)
  matrix products  19.1 us (7%)
  blocking collectives  17.3 us (6%)
  Pallas kernels  16.2 us (6%)
  between operations  14.6 us (5%)
    ppermute x14, starting transfers between devices, swap(): return lax.ppermute(values, axis, [(i, i ^ step) for i in range(size)])  49.4 us
    gather x5, local copies, waits for them, and re-layouts, rows_of(): return values.at[index].get(mode='promise_in_bounds')  22.1 us
    ppermute x14, waiting for transfers between devices, swap(): return lax.ppermute(values, axis, [(i, i ^ step) for i in range(size)])  21.5 us
    all_to_all x1, starting transfers between devices, local(): notes = lax.all_to_all(note, DP, 0, 0, tiled=True)  19.3 us
    all_to_all x1, blocking collectives, local(): lax.all_to_all(jnp.broadcast_to(packet, (Y * X * C,) + packet.shape), PLA...  17.3 us
    all_to_all x1, starting transfers between devices, local(): lax.all_to_all(chosen.reshape(shards, cap * doc_len, feature_dim), DP, 0,...  15 us
    all_to_all x1, starting transfers between devices, local(): first = lax.all_to_all(first, 'z', 0, 0, tiled=True)  11.8 us
    all_to_all x1, starting transfers between devices, local(): lax.all_to_all(jnp.broadcast_to(unit, (Y,) + unit.shape).reshape((-1,) +...  9.46 us
  transfers between devices with their start and end apart: 22, of which 12 were waited for; matrix products, arithmetic and copies ran while one was open for 26% of the time, Pallas kernels for 6%

profile of v6, /device:TPU:1, one launch (start us, length us, event | category | flops | bytes accessed | tf_op | source)
XLA Modules:
  0.0 274.9 jit_solution(4501943113533116848)
XLA Ops:
  11.1 19.3 %all-to-all-start = ((s32[64,1,128]{2,1,0:T(1,128)}), s32[64,1,128]{2,1,0:T(1,128)S(1)}, u32[]{:S(2)}, u32[]{:S(2)}) async-start(s32[64,1,128]{2,1,0:T(1,128)} %bitcast.15), calls=%async_computation | async-start | bytes 65536 | tf_op jit(solution)/shard_map/all_to_all | solution.py:259
  30.5 3.0 %reshape.325.packed = s32[4096,16]{1,0:T(8,128)} reshape(s32[64,1024]{1,0:T(8,128)} %param.19) | data formatting | bytes 524288 | tf_op jit(solution)/shard_map/reshape | solution.py:70
  33.6 14.9 %gather_fusion.1 = bf16[4096,128]{1,0:T(8,128)(2,1)} fusion(bf16[8192,128]{1,0:T(8,128)(2,1)S(1)} %copy-done, s32[4096]{0:T(1024)S(1)} %broadcast_clamp_fusion), kind=kCustom, calls=%fused_computation.1 | custom fusion | bytes 2113536 | tf_op jit(solution)/shard_map/gather | solution.py:29
  48.5 1.6 copy-done.1
  50.1 1.2 copy-done.3
  51.4 5.4 %decode.1 = bf16[4096,128]{1,0:T(8,128)(2,1)S(1)} custom-call(f32[4]{0:T(128)S(1)} %copy-done.6, s32[4096,16]{1,0:T(8,128)S(1)} %copy-done.1, bf16[4096,128]{1,0:T(8,128)(2,1)S(1)} %copy-done.3), custom_call_target="tpu_custom_call" | custom-call | tf_op jit(solution)/shard_map/decode/pallas_call | solution.py:72
  57.0 2.2 gather_fusion.2
  59.2 15.0 %all-to-all-start.1 = ((bf16[64,128,128]{2,1,0:T(8,128)(2,1)}), bf16[64,128,128]{2,1,0:T(8,128)(2,1)}, u32[]{:S(2)}, u32[]{:S(2)}) async-start(bf16[64,128,128]{2,1,0:T(8,128)(2,1)} %bitcast.109), calls=%async_computation.1 | async-start | bytes 4194304 | tf_op jit(solution)/shard_map/all_to_all | solution.py:264
  74.3 3.4 %collective-permute-start.3 = (bf16[512,128]{1,0:T(8,128)(2,1)S(1)}, bf16[512,128]{1,0:T(8,128)(2,1)S(1)}, u32[]{:S(2)}, u32[]{:S(2)}) collective-permute-start(bf16[512,128]{1,0:T(8,128)(2,1)S(1)} %copy-done.14), channel_id=1, source_target_pairs={{0,1},{1,0},{2,3},{3,2},{4,5},{5,4},{6,7},{7,6},{8,9},{9,8},{10,11... | collective-permute-start | bytes 393224 | tf_op jit(solution)/shard_map/ppermute | solution.py:25
  77.7 0.9 collective-permute-done.3
  79.4 4.4 %collective-permute-start.6 = (bf16[2,512,128]{2,1,0:T(8,128)(2,1)}, bf16[2,512,128]{2,1,0:T(8,128)(2,1)}, u32[]{:S(2)}, u32[]{:S(2)}) collective-permute-start(bf16[2,512,128]{2,1,0:T(8,128)(2,1)} %maximum_select_fusion.1), channel_id=1, source_target_pairs={{0,6},{2,4},{4,2},{6,0},{1,7},{3,5},{5,3},{7,1},{8,14},{10,12},{12... | collective-permute-start | bytes 786440 | tf_op jit(solution)/shard_map/ppermute | solution.py:25
  83.8 2.4 collective-permute-start.5
  86.2 2.2 collective-permute-start.4
  89.1 4.5 %collective-permute-start.2 = (bf16[2,4,32,640]{3,2,0,1:T(8,128)(2,1)S(1)}, bf16[2,4,32,640]{3,2,0,1:T(8,128)(2,1)}, u32[]{:S(2)}, u32[]{:S(2)}) collective-permute-start(bf16[2,4,32,640]{3,2,0,1:T(8,128)(2,1)S(1)} %bitcast.114), channel_id=1, source_target_pairs={{0,384},{128,256},{256,128},{384,0},{1,385},{129,257},{257,129},{3... | collective-permute-start | bytes 983048 | tf_op jit(solution)/shard_map/ppermute | solution.py:25
  93.7 2.3 collective-permute-start.1
  96.0 2.2 collective-permute-start
  98.9 2.2 pad_maximum_fusion.1
  101.1 2.1 gather_fusion.3
  103.2 2.8 %collective-permute-done.2 = bf16[2,4,32,640]{3,2,0,1:T(8,128)(2,1)} collective-permute-done((bf16[2,4,32,640]{3,2,0,1:T(8,128)(2,1)S(1)}, bf16[2,4,32,640]{3,2,0,1:T(8,128)(2,1)}, u32[]{:S(2)}, u32[]{:S(2)}) %collective-permute-start.2) | collective-permute-done | bytes 327712 | tf_op jit(solution)/shard_map/ppermute | solution.py:25
  106.1 2.1 collective-permute-done
  108.1 1.4 pad_maximum_fusion
  109.5 1.2 copy.42
  110.7 2.7 convolution_convert_fusion
  113.4 9.5 %collective-permute-start.7 = (bf16[512,1024]{1,0:T(8,128)(2,1)S(1)}, bf16[512,1024]{1,0:T(8,128)(2,1)S(1)}, u32[]{:S(2)}, u32[]{:S(2)}) collective-permute-start(bf16[512,1024]{1,0:T(8,128)(2,1)S(1)} %convolution_convert_fusion), channel_id=1, source_target_pairs={{0,1},{1,0},{2,3},{3,2},{4,5},{5,4},{6,7},{7,6},{8,9},{9,8},{10,11... | collective-permute-start | bytes 3145736 | tf_op jit(solution)/shard_map/ppermute | solution.py:25
  123.0 1.0 convolution_convert_fusion.1
  124.0 1.2 collective-permute-done.7
  125.2 1.8 convert_add_fusion
  127.9 4.3 %collective-permute-start.10 = (bf16[4,32,1024]{2,1,0:T(8,128)(2,1)}, bf16[4,32,1024]{2,1,0:T(8,128)(2,1)}, u32[]{:S(2)}, u32[]{:S(2)}) collective-permute-start(bf16[4,32,1024]{2,1,0:T(8,128)(2,1)} %bitcast.31), channel_id=1, source_target_pairs={{0,6},{2,4},{4,2},{6,0},{1,7},{3,5},{5,3},{7,1},{8,14},{10,12},{12... | collective-permute-start | bytes 786440 | tf_op jit(solution)/shard_map/ppermute | solution.py:25
  132.1 2.4 collective-permute-start.9
  134.5 2.3 collective-permute-start.8
  136.9 1.1 slice.86
  138.0 5.5 %collective-permute-done.10 = bf16[4,32,1024]{2,1,0:T(8,128)(2,1)} collective-permute-done((bf16[4,32,1024]{2,1,0:T(8,128)(2,1)}, bf16[4,32,1024]{2,1,0:T(8,128)(2,1)}, u32[]{:S(2)}, u32[]{:S(2)}) %collective-permute-start.10) | collective-permute-done | bytes 262176 | tf_op jit(solution)/shard_map/ppermute | solution.py:25
  143.5 3.2 %collective-permute-done.8 = bf16[4,32,1024]{2,1,0:T(8,128)(2,1)} collective-permute-done((bf16[4,32,1024]{2,1,0:T(8,128)(2,1)S(1)}, bf16[4,32,1024]{2,1,0:T(8,128)(2,1)}, u32[]{:S(2)}, u32[]{:S(2)}) %collective-permute-start.8) | collective-permute-done | bytes 262176 | tf_op jit(solution)/shard_map/ppermute | solution.py:25
  146.7 1.3 add_convert_fusion
  148.0 5.1 %collective-permute-start.13 = (bf16[32,1024]{1,0:T(8,128)(2,1)S(1)}, bf16[32,1024]{1,0:T(8,128)(2,1)S(1)}, u32[]{:S(2)}, u32[]{:S(2)}) collective-permute-start(bf16[32,1024]{1,0:T(8,128)(2,1)S(1)} %get-tuple-element.68), channel_id=1, source_target_pairs={{0,384},{128,256},{256,128},{384,0},{1,385},{129,257},{257,129},{3... | collective-permute-start | bytes 196616 | tf_op jit(solution)/shard_map/ppermute | solution.py:25
  153.1 2.4 collective-permute-start.12
  155.5 2.0 collective-permute-start.11
  158.7 3.0 %collective-permute-done.12 = bf16[32,1024]{1,0:T(8,128)(2,1)S(1)} collective-permute-done((bf16[32,1024]{1,0:T(8,128)(2,1)S(1)}, bf16[32,1024]{1,0:T(8,128)(2,1)S(1)}, u32[]{:S(2)}, u32[]{:S(2)}) %collective-permute-start.12) | collective-permute-done | bytes 65568 | tf_op jit(solution)/shard_map/ppermute | solution.py:25
  161.7 2.2 collective-permute-done.11
  164.7 2.3 gather_fusion.4
  167.0 1.0 convert_bitcast_fusion
  168.8 1.0 fusion.19
  170.0 1.1 broadcast_in_dim.104
  171.1 9.5 %all-to-all-start.2 = ((bf16[32,32,512]{2,1,0:T(8,128)(2,1)}), bf16[32,32,512]{2,1,0:T(8,128)(2,1)}, u32[]{:S(2)}, u32[]{:S(2)}) async-start(bf16[32,32,512]{2,1,0:T(8,128)(2,1)} %bitcast.110), calls=%async_computation.2 | async-start | bytes 2097152 | tf_op jit(solution)/shard_map/all_to_all | solution.py:321
  181.4 1.3 fusion.7.embedded_ref
  182.9 1.0 copy-done.2
  183.9 9.2 %score.1 = (f32[128,1]{1,0:T(8,128)S(1)}, bf16[64,128]{1,0:T(8,128)(2,1)S(1)}) custom-call(bf16[8192,128]{1,0:T(8,128)(2,1)} %bitcast.42.docs, f32[32,128]{1,0:T(8,128)S(1)} %fusion.7.embedded_ref, s32[128,32]{1,0:T(8,128)S(1)} %broadcast_in_dim.103.spans, s32[128,2]{1,0:T(8,128)S(1)} %copy.46.flags, f32[32,4096]{1,0:T(8,128)S(1)} %copy-done.2, ...), custom_call_target="tpu_custom_call" | custom-call | flops 134217728 | bytes 30000000 | tf_op jit(solution)/shard_map/score/pallas_call | solution.py:159
  193.1 5.6 %all-to-all-done.2 = bf16[32,32,512]{2,1,0:T(8,128)(2,1)} async-done(((bf16[32,32,512]{2,1,0:T(8,128)(2,1)}), bf16[32,32,512]{2,1,0:T(8,128)(2,1)}, u32[]{:S(2)}, u32[]{:S(2)}) %all-to-all-start.2) | async-done | bytes 1048608 | tf_op jit(solution)/shard_map/all_to_all | solution.py:321
  198.8 17.3 %all_to_all.37.packets = bf16[32,64,128]{2,1,0:T(8,128)(2,1)} all-to-all(bf16[32,64,128]{2,1,0:T(8,128)(2,1)S(1)} %broadcast_in_dim.105), channel_id=1, replica_groups=mesh['y'=4,'z'=16,'x'=4,'c'=2] {'y','x','c'}, dimensions={0} | all-to-all | bytes 1048576 | tf_op jit(solution)/shard_map/all_to_all | solution.py:331
  216.2 1.1 copy-done.4
  217.3 1.6 bundle.1
  219.6 11.8 %all-to-all-start.4 = ((bf16[16,48,128]{2,1,0:T(8,128)(2,1)}), bf16[16,48,128]{2,1,0:T(8,128)(2,1)}, u32[]{:S(2)}, u32[]{:S(2)}) async-start(bf16[16,48,128]{2,1,0:T(8,128)(2,1)} %copy-done.5), calls=%async_computation.4 | async-start | bytes 393216 | tf_op jit(solution)/shard_map/all_to_all | solution.py:347
  231.7 1.4 select_reduce_fusion.1
  233.1 1.7 multiply_reduce_fusion.1
  234.8 5.5 %convolution_convert_fusion.2 = bf16[640,128]{1,0:T(8,128)(2,1)} fusion(bf16[640,4096]{0,1:T(8,128)(2,1)} %all-gather.6.cloned.1.call-done, bf16[4096,128]{1,0:T(8,128)(2,1)S(1)} %bitcast.102, f32[4096]{0:T(1024)} %param.14), kind=kOutput, calls=%fused_computation.16 | convolution fusion | flops 672743424 | bytes 6471680 | tf_op jit(solution)/shard_map/dot_general | solution.py:361
  240.4 0.9 subtract_convert_fusion
  241.2 2.8 %all-to-all-done.4 = bf16[16,48,128]{2,1,0:T(8,128)(2,1)} async-done(((bf16[16,48,128]{2,1,0:T(8,128)(2,1)}), bf16[16,48,128]{2,1,0:T(8,128)(2,1)}, u32[]{:S(2)}, u32[]{:S(2)}) %all-to-all-start.4) | async-done | bytes 196640 | tf_op jit(solution)/shard_map/all_to_all | solution.py:347
  244.0 1.0 reduce_sum.92
  245.7 8.8 %all-to-all-start.5 = ((bf16[16,48,128]{2,1,0:T(8,128)(2,1)}), bf16[16,48,128]{2,1,0:T(8,128)(2,1)S(1)}, u32[]{:S(2)}, u32[]{:S(2)}) async-start(bf16[16,48,128]{2,1,0:T(8,128)(2,1)} %broadcast_in_dim.111), calls=%async_computation.5 | async-start | bytes 393216 | tf_op jit(solution)/shard_map/all_to_all | solution.py:365
  254.6 2.2 multiply_reduce_fusion
  256.8 1.5 fusion.2
  258.4 4.4 %convolution_multiply_fusion.1 = f32[256,640]{1,0:T(8,128)S(1)} fusion(bf16[256,4096]{1,0:T(8,128)(2,1)S(1)} %copy-done.9, bf16[640,4096]{0,1:T(8,128)(2,1)} %all-gather.6.cloned.1.call-done, f32[256]{0:T(256)S(1)} %get-tuple-element.72), kind=kOutput, calls=%fused_computation.12 | convolution fusion | flops 1342341120 | bytes 7996416 | tf_op jit(solution)/shard_map/dot_general | solution.py:368
  262.8 1.0 fusion.1
  263.7 3.2 %all-to-all-done.5 = bf16[16,48,128]{2,1,0:T(8,128)(2,1)S(1)} async-done(((bf16[16,48,128]{2,1,0:T(8,128)(2,1)}), bf16[16,48,128]{2,1,0:T(8,128)(2,1)S(1)}, u32[]{:S(2)}, u32[]{:S(2)}) %all-to-all-start.5) | async-done | bytes 196640 | tf_op jit(solution)/shard_map/all_to_all | solution.py:365
  (130 shorter events, 14.5 us)
Async XLA Ops:
  7.2 26.5 %copy-start = (bf16[8192,128]{1,0:T(8,128)(2,1)S(1)}, bf16[8192,128]{1,0:T(8,128)(2,1)}, u32[]{:S(2)}) copy-start(bf16[8192,128]{1,0:T(8,128)(2,1)} %param.20) | copy-start | bytes 6291460
  7.2 26.3 %copy-start.19 = (s32[64,64]{1,0:T(8,128)S(1)}, s32[64,64]{1,0:T(8,128)}, u32[]{:S(2)}) copy-start(s32[64,64]{1,0:T(8,128)} %param.18) | copy-start | bytes 49156
  7.2 81.3 %all-gather.4.cloned.1.call-start = ((), (), s32[]{:S(2)}) async-start(), calls=%async_computation.6 | async-start | bytes 1392640 | tf_op jit(solution)/shard_map/all_gather | solution.py:257
  9.4 21.0 %copy-start.28 = (s32[64]{0:T(128)}, s32[64]{0:T(128)S(1)}, u32[]{:S(2)}) copy-start(s32[64]{0:T(128)S(1)} %convert_reduce_fusion) | copy-start | bytes 772
  9.5 21.0 %copy-start.26 = (s32[64]{0:T(128)}, s32[64]{0:T(128)S(1)}, u32[]{:S(2)}) copy-start(s32[64]{0:T(128)S(1)} %fusion.16) | copy-start | bytes 772
  11.1 45.6 %all-to-all-start = ((s32[64,1,128]{2,1,0:T(1,128)}), s32[64,1,128]{2,1,0:T(1,128)S(1)}, u32[]{:S(2)}, u32[]{:S(2)}) async-start(s32[64,1,128]{2,1,0:T(1,128)} %bitcast.15), calls=%async_computation | async-start | bytes 65536 | tf_op jit(solution)/shard_map/all_to_all | solution.py:259
  33.6 14.9 %copy-start.6 = (f32[4]{0:T(128)S(1)}, f32[4]{0:T(128)}, u32[]{:S(2)}) copy-start(f32[4]{0:T(128)} %buckets.1) | copy-start | bytes 52
  48.5 1.6 copy-start.1
  50.1 1.2 copy-start.3
  59.2 15.0 %copy-start.14 = (bf16[512,128]{1,0:T(8,128)(2,1)S(1)}, bf16[512,128]{1,0:T(8,128)(2,1)}, u32[]{:S(2)}) copy-start(bf16[512,128]{1,0:T(8,128)(2,1)} %param.15) | copy-start | bytes 393220
  59.2 29.2 %copy-start.15 = (bf16[256,640]{1,0:T(8,128)(2,1)S(1)}, bf16[256,640]{1,0:T(8,128)(2,1)}, u32[]{:S(2)}) copy-start(bf16[256,640]{1,0:T(8,128)(2,1)} %param.12) | copy-start | bytes 983044
  59.2 38.9 %copy-start.17 = (f32[4096]{0:T(1024)S(1)}, f32[4096]{0:T(1024)}, u32[]{:S(2)}) copy-start(f32[4096]{0:T(1024)} %param.14) | copy-start | bytes 49156
  59.2 110.7 %all-to-all-start.1 = ((bf16[64,128,128]{2,1,0:T(8,128)(2,1)}), bf16[64,128,128]{2,1,0:T(8,128)(2,1)}, u32[]{:S(2)}, u32[]{:S(2)}) async-start(bf16[64,128,128]{2,1,0:T(8,128)(2,1)} %bitcast.109), calls=%async_computation.1 | async-start | bytes 4194304 | tf_op jit(solution)/shard_map/all_to_all | solution.py:264
  74.2 142.0 %all-gather.6.cloned.1.call-start = ((), (), s32[]{:S(2)}) async-start(), calls=%async_computation.7 | async-start | bytes 6553600 | tf_op jit(solution)/shard_map/all_gather | solution.py:336
  74.3 4.4 %collective-permute-start.3 = (bf16[512,128]{1,0:T(8,128)(2,1)S(1)}, bf16[512,128]{1,0:T(8,128)(2,1)S(1)}, u32[]{:S(2)}, u32[]{:S(2)}) collective-permute-start(bf16[512,128]{1,0:T(8,128)(2,1)S(1)} %copy-done.14), channel_id=1, source_target_pairs={{0,1},{1,0},{2,3},{3,2},{4,5},{5,4},{6,7},{7,6},{8,9},{9,8},{10,11... | collective-permute-start | bytes 393224 | tf_op jit(solution)/shard_map/ppermute | solution.py:25
  79.4 16.6 %collective-permute-start.6 = (bf16[2,512,128]{2,1,0:T(8,128)(2,1)}, bf16[2,512,128]{2,1,0:T(8,128)(2,1)}, u32[]{:S(2)}, u32[]{:S(2)}) collective-permute-start(bf16[2,512,128]{2,1,0:T(8,128)(2,1)} %maximum_select_fusion.1), channel_id=1, source_target_pairs={{0,6},{2,4},{4,2},{6,0},{1,7},{3,5},{5,3},{7,1},{8,14},{10,12},{12... | collective-permute-start | bytes 786440 | tf_op jit(solution)/shard_map/ppermute | solution.py:25
  83.8 15.1 %copy-start.21 = (s32[1024]{0:T(1024)}, s32[1024]{0:T(1024)S(1)}, u32[]{:S(2)}) copy-start(s32[1024]{0:T(1024)S(1)} %pad_clamp_fusion.2) | copy-start | bytes 12292
  83.8 15.1 %collective-permute-start.5 = (bf16[2,512,128]{2,1,0:T(8,128)(2,1)}, bf16[2,512,128]{2,1,0:T(8,128)(2,1)}, u32[]{:S(2)}, u32[]{:S(2)}) collective-permute-start(bf16[2,512,128]{2,1,0:T(8,128)(2,1)} %maximum_select_fusion.1), channel_id=1, source_target_pairs={{0,4},{2,6},{4,0},{6,2},{1,5},{3,7},{5,1},{7,3},{8,12},{10,14},{12... | collective-permute-start | bytes 786440 | tf_op jit(solution)/shard_map/ppermute | solution.py:25
  86.2 12.6 %collective-permute-start.4 = (bf16[2,512,128]{2,1,0:T(8,128)(2,1)}, bf16[2,512,128]{2,1,0:T(8,128)(2,1)}, u32[]{:S(2)}, u32[]{:S(2)}) collective-permute-start(bf16[2,512,128]{2,1,0:T(8,128)(2,1)} %maximum_select_fusion.1), channel_id=1, source_target_pairs={{0,2},{2,0},{4,6},{6,4},{1,3},{3,1},{5,7},{7,5},{8,10},{10,8},{12,... | collective-permute-start | bytes 786440 | tf_op jit(solution)/shard_map/ppermute | solution.py:25
  89.1 16.9 %collective-permute-start.2 = (bf16[2,4,32,640]{3,2,0,1:T(8,128)(2,1)S(1)}, bf16[2,4,32,640]{3,2,0,1:T(8,128)(2,1)}, u32[]{:S(2)}, u32[]{:S(2)}) collective-permute-start(bf16[2,4,32,640]{3,2,0,1:T(8,128)(2,1)S(1)} %bitcast.114), channel_id=1, source_target_pairs={{0,384},{128,256},{256,128},{384,0},{1,385},{129,257},{257,129},{3... | collective-permute-start | bytes 983048 | tf_op jit(solution)/shard_map/ppermute | solution.py:25
  93.7 12.4 %collective-permute-start.1 = (bf16[2,4,32,640]{3,2,0,1:T(8,128)(2,1)S(1)}, bf16[2,4,32,640]{3,2,0,1:T(8,128)(2,1)}, u32[]{:S(2)}, u32[]{:S(2)}) collective-permute-start(bf16[2,4,32,640]{3,2,0,1:T(8,128)(2,1)S(1)} %bitcast.115), channel_id=1, source_target_pairs={{0,256},{128,384},{256,0},{384,128},{1,257},{129,385},{257,1},{385... | collective-permute-start | bytes 983048 | tf_op jit(solution)/shard_map/ppermute | solution.py:25
  96.0 12.1 %collective-permute-start = (bf16[2,4,32,640]{3,2,0,1:T(8,128)(2,1)S(1)}, bf16[2,4,32,640]{3,2,0,1:T(8,128)(2,1)}, u32[]{:S(2)}, u32[]{:S(2)}) collective-permute-start(bf16[2,4,32,640]{3,2,0,1:T(8,128)(2,1)S(1)} %bitcast.116), channel_id=1, source_target_pairs={{0,128},{128,0},{256,384},{384,256},{1,129},{129,1},{257,385},{385... | collective-permute-start | bytes 983048 | tf_op jit(solution)/shard_map/ppermute | solution.py:25
  110.7 12.2 %copy-start.12 = (bf16[640,1024]{0,1:T(8,128)(2,1)S(1)}, bf16[640,1024]{0,1:T(8,128)(2,1)}, u32[]{:S(2)}) copy-start(bf16[640,1024]{0,1:T(8,128)(2,1)} %all-gather.4.cloned.1.call-done) | copy-start | bytes 3932164
  110.7 12.2 %copy-start.13 = (bf16[2,4,4,32,640]{4,3,2,1,0:T(8,128)(2,1)S(1)}, bf16[2,4,4,32,640]{4,3,2,1,0:T(8,128)(2,1)}, u32[]{:S(2)}) copy-start(bf16[2,4,4,32,640]{4,3,2,1,0:T(8,128)(2,1)} %copy.42) | copy-start | bytes 3932164
  113.4 11.8 %collective-permute-start.7 = (bf16[512,1024]{1,0:T(8,128)(2,1)S(1)}, bf16[512,1024]{1,0:T(8,128)(2,1)S(1)}, u32[]{:S(2)}, u32[]{:S(2)}) collective-permute-start(bf16[512,1024]{1,0:T(8,128)(2,1)S(1)} %convolution_convert_fusion), channel_id=1, source_target_pairs={{0,1},{1,0},{2,3},{3,2},{4,5},{5,4},{6,7},{7,6},{8,9},{9,8},{10,11... | collective-permute-start | bytes 3145736 | tf_op jit(solution)/shard_map/ppermute | solution.py:25
  127.9 15.6 %collective-permute-start.10 = (bf16[4,32,1024]{2,1,0:T(8,128)(2,1)}, bf16[4,32,1024]{2,1,0:T(8,128)(2,1)}, u32[]{:S(2)}, u32[]{:S(2)}) collective-permute-start(bf16[4,32,1024]{2,1,0:T(8,128)(2,1)} %bitcast.31), channel_id=1, source_target_pairs={{0,6},{2,4},{4,2},{6,0},{1,7},{3,5},{5,3},{7,1},{8,14},{10,12},{12... | collective-permute-start | bytes 786440 | tf_op jit(solution)/shard_map/ppermute | solution.py:25
  132.1 11.4 %collective-permute-start.9 = (bf16[4,32,1024]{2,1,0:T(8,128)(2,1)}, bf16[4,32,1024]{2,1,0:T(8,128)(2,1)}, u32[]{:S(2)}, u32[]{:S(2)}) collective-permute-start(bf16[4,32,1024]{2,1,0:T(8,128)(2,1)} %bitcast.30), channel_id=1, source_target_pairs={{0,4},{2,6},{4,0},{6,2},{1,5},{3,7},{5,1},{7,3},{8,12},{10,14},{12... | collective-permute-start | bytes 786440 | tf_op jit(solution)/shard_map/ppermute | solution.py:25
  134.5 12.1 %collective-permute-start.8 = (bf16[4,32,1024]{2,1,0:T(8,128)(2,1)S(1)}, bf16[4,32,1024]{2,1,0:T(8,128)(2,1)}, u32[]{:S(2)}, u32[]{:S(2)}) collective-permute-start(bf16[4,32,1024]{2,1,0:T(8,128)(2,1)S(1)} %bitcast.129), channel_id=1, source_target_pairs={{0,2},{2,0},{4,6},{6,4},{1,3},{3,1},{5,7},{7,5},{8,10},{10,8},{12,... | collective-permute-start | bytes 786440 | tf_op jit(solution)/shard_map/ppermute | solution.py:25
  147.9 20.1 %copy-start.10 = (bf16[32,4096]{1,0:T(8,128)(2,1)S(1)}, bf16[32,4096]{1,0:T(8,128)(2,1)}, u32[]{:S(2)}) copy-start(bf16[32,4096]{1,0:T(8,128)(2,1)} %param.11) | copy-start | bytes 786436
  148.0 10.8 %collective-permute-start.13 = (bf16[32,1024]{1,0:T(8,128)(2,1)S(1)}, bf16[32,1024]{1,0:T(8,128)(2,1)S(1)}, u32[]{:S(2)}, u32[]{:S(2)}) collective-permute-start(bf16[32,1024]{1,0:T(8,128)(2,1)S(1)} %get-tuple-element.68), channel_id=1, source_target_pairs={{0,384},{128,256},{256,128},{384,0},{1,385},{129,257},{257,129},{3... | collective-permute-start | bytes 196616 | tf_op jit(solution)/shard_map/ppermute | solution.py:25
  153.1 8.7 %collective-permute-start.12 = (bf16[32,1024]{1,0:T(8,128)(2,1)S(1)}, bf16[32,1024]{1,0:T(8,128)(2,1)S(1)}, u32[]{:S(2)}, u32[]{:S(2)}) collective-permute-start(bf16[32,1024]{1,0:T(8,128)(2,1)S(1)} %get-tuple-element.69), channel_id=1, source_target_pairs={{0,256},{128,384},{256,0},{384,128},{1,257},{129,385},{257,1},{385... | collective-permute-start | bytes 196616 | tf_op jit(solution)/shard_map/ppermute | solution.py:25
  155.5 8.5 %collective-permute-start.11 = (bf16[32,1024]{1,0:T(8,128)(2,1)S(1)}, bf16[32,1024]{1,0:T(8,128)(2,1)S(1)}, u32[]{:S(2)}, u32[]{:S(2)}) collective-permute-start(bf16[32,1024]{1,0:T(8,128)(2,1)S(1)} %get-tuple-element.70), channel_id=1, source_target_pairs={{0,128},{128,0},{256,384},{384,256},{1,129},{129,1},{257,385},{385... | collective-permute-start | bytes 196616 | tf_op jit(solution)/shard_map/ppermute | solution.py:25
  168.0 0.8 copy-start.7
  168.8 2.3 copy-start.22
  169.9 10.8 %copy-start.25 = (s32[1,64]{1,0:T(1,128)S(1)}, s32[1,64]{1,0:T(1,128)}, u32[]{:S(2)}) copy-start(s32[1,64]{1,0:T(1,128)} %param.16) | copy-start | bytes 772
  169.9 10.8 %copy-start.29 = (s32[64]{0:T(128)S(1)}, s32[64]{0:T(128)}, u32[]{:S(2)}) copy-start(s32[64]{0:T(128)} %copy-done.28) | copy-start | bytes 772
  169.9 10.9 %copy-start.27 = (s32[64]{0:T(128)S(1)}, s32[64]{0:T(128)}, u32[]{:S(2)}) copy-start(s32[64]{0:T(128)} %copy-done.26) | copy-start | bytes 772
  171.1 27.6 %all-to-all-start.2 = ((bf16[32,32,512]{2,1,0:T(8,128)(2,1)}), bf16[32,32,512]{2,1,0:T(8,128)(2,1)}, u32[]{:S(2)}, u32[]{:S(2)}) async-start(bf16[32,32,512]{2,1,0:T(8,128)(2,1)} %bitcast.110), calls=%async_computation.2 | async-start | bytes 2097152 | tf_op jit(solution)/shard_map/all_to_all | solution.py:321
  180.6 74.0 %all-gather.8.cloned.1.call-start = ((), (), s32[]{:S(2)}) async-start(), calls=%async_computation.8 | async-start | bytes 2359296 | tf_op jit(solution)/shard_map/all_gather | solution.py:340
  182.9 1.1 copy-start.2
  216.2 15.3 %slice-start = ((bf16[32,64,128]{2,1,0:T(8,128)(2,1)}), bf16[32,32,128]{2,1,0:T(8,128)(2,1)S(1)}, s32[]{:S(2)}) async-start(bf16[32,64,128]{2,1,0:T(8,128)(2,1)} %all_to_all.37.packets), calls=%async_computation.9 | async-start | bytes 524288 | tf_op jit(solution)/shard_map/slice | solution.py:334
  216.2 1.1 copy-start.4
  218.9 0.7 copy-start.5
  219.6 24.4 %all-to-all-start.4 = ((bf16[16,48,128]{2,1,0:T(8,128)(2,1)}), bf16[16,48,128]{2,1,0:T(8,128)(2,1)}, u32[]{:S(2)}, u32[]{:S(2)}) async-start(bf16[16,48,128]{2,1,0:T(8,128)(2,1)} %copy-done.5), calls=%async_computation.4 | async-start | bytes 393216 | tf_op jit(solution)/shard_map/all_to_all | solution.py:347
  234.8 5.5 %copy-start.8 = (f32[4,4,8,1024]{3,2,0,1:T(8,128)S(1)}, f32[4,4,8,1024]{3,2,0,1:T(8,128)}, u32[]{:S(2)}) copy-start(f32[4,4,8,1024]{3,2,0,1:T(8,128)} %copy-done.7) | copy-start | bytes 1572868
  234.8 5.5 %copy-start.11 = (bf16[32,4096]{1,0:T(8,128)(2,1)S(1)}, bf16[32,4096]{1,0:T(8,128)(2,1)}, u32[]{:S(2)}) copy-start(bf16[32,4096]{1,0:T(8,128)(2,1)} %param.11) | copy-start | bytes 786436
  234.8 5.5 %copy-start.23 = (f32[32]{0:T(128)S(1)}, f32[32]{0:T(128)}, u32[]{:S(2)}) copy-start(f32[32]{0:T(128)} %copy-done.22) | copy-start | bytes 388
  234.8 5.5 %copy-start.24 = (f32[32]{0:T(128)S(1)}, f32[32]{0:T(128)}, u32[]{:S(2)}) copy-start(f32[32]{0:T(128)} %get-tuple-element.73) | copy-start | bytes 388
  240.4 16.5 %copy-start.18 = (f32[4096]{0:T(1024)S(1)}, f32[4096]{0:T(1024)}, u32[]{:S(2)}) copy-start(f32[4096]{0:T(1024)} %param.14) | copy-start | bytes 49156
  245.7 21.2 %all-to-all-start.5 = ((bf16[16,48,128]{2,1,0:T(8,128)(2,1)}), bf16[16,48,128]{2,1,0:T(8,128)(2,1)S(1)}, u32[]{:S(2)}, u32[]{:S(2)}) async-start(bf16[16,48,128]{2,1,0:T(8,128)(2,1)} %broadcast_in_dim.111), calls=%async_computation.5 | async-start | bytes 393216 | tf_op jit(solution)/shard_map/all_to_all | solution.py:365
  254.6 2.2 copy-start.9
  258.4 4.4 %copy-start.16 = (bf16[640,128]{1,0:T(8,128)(2,1)S(1)}, bf16[640,128]{1,0:T(8,128)(2,1)}, u32[]{:S(2)}) copy-start(bf16[640,128]{1,0:T(8,128)(2,1)} %convolution_convert_fusion.2) | copy-start | bytes 491524
  258.4 9.2 %copy-start.20 = (f32[512]{0:T(512)S(1)}, f32[512]{0:T(512)}, u32[]{:S(2)}) copy-start(f32[512]{0:T(512)} %dynamic_slice.6) | copy-start | bytes 6148
Sparse Core Ops, SparseCore 0:
  10.1 68.3 all-gather.3
  110.8 95.0 all-gather.5
  216.3 30.6 all-gather.7

commit v7 on v6

--- a/solution.py
+++ b/solution.py
@@ -178,17 +178,25 @@
     )(docs, embedded, spans, flags, unit, head)
 
 
-def bundle_kernel(packets, unit, out, ge):
+def bundle_kernel(here, packets, *refs):
+    *units, out, ge = refs
     count, tall, features = packets.shape
-    tokens = unit.shape[0] // count
+    rows = units[0].shape[0]
+    tokens = len(units) * rows // count
     shares, _, _ = out.shape
     total = jnp.zeros((tall - tokens, features), F32)
     for i in range(count):
-        ge[i * tokens : (i + 1) * tokens, :] = packets[i, 0:tokens, :]
+        ge[i * tokens : (i + 1) * tokens, :] = packets[here[0] ^ i, 0:tokens, :]
         total = total + packets[i, tokens:tall, :].astype(F32)
-    head = lax.dot_general(
-        ge[...], unit[...], (((0,), (0,)), ((), ())), preferred_element_type=F32
-    ).T
+    head = jnp.zeros((features, units[0].shape[1]), F32)
+    for i, unit in enumerate(units):
+        head = head + lax.dot_general(
+            ge[i * rows : (i + 1) * rows, :],
+            unit[...],
+            (((0,), (0,)), ((), ())),
+            preferred_element_type=F32,
+        )
+    head = head.T
     share = head.shape[0] // shares
     lines = total.shape[0] // shares
     for i in range(shares):
@@ -199,17 +207,17 @@
         out[i, share : share + 16, :] = gain.astype(BF16)
 
 
-def bundle(packets, unit, shares):
+def bundle(here, packets, units, shares):
     count, tall, features = packets.shape
     return pl.pallas_call(
         bundle_kernel,
-        in_specs=[VMEM] * 2,
+        in_specs=[SMEM] + [VMEM] * (1 + len(units)),
         out_specs=VMEM,
-        out_shape=jax.ShapeDtypeStruct((shares, unit.shape[1] // shares + 16, features), BF16),
-        scratch_shapes=[pltpu.VMEM((unit.shape[0], features), BF16)],
+        out_shape=jax.ShapeDtypeStruct((shares, units[0].shape[1] // shares + 16, features), BF16),
+        scratch_shapes=[pltpu.VMEM((len(units) * units[0].shape[0], features), BF16)],
         compiler_params=pltpu.CompilerParams(vmem_limit_bytes=32 * 1024 * 1024),
         name="bundle",
-    )(packets, unit)
+    )(here, packets, *units)
 
 
 def local(
@@ -259,8 +267,7 @@
     notes = lax.all_to_all(note, DP, 0, 0, tiled=True)
     documents = documents.reshape(per_shard, doc_len, feature_dim)
     chosen = rows_of(documents, notes[:, per_shard : per_shard + cap].reshape(slots))
-    chosen, colbert_head = lax.optimization_barrier((chosen, colbert_head))
-    proj_z, context = lax.optimization_barrier((proj_z, context))
+    chosen, context = lax.optimization_barrier((chosen, context))
     got_docs = lax.all_to_all(
         chosen.reshape(shards, cap * doc_len, feature_dim), DP, 0, 0, tiled=True
     ).reshape(slots * doc_len, feature_dim)
@@ -282,21 +289,13 @@
     by_y = jnp.stack([blocks] + [swap(blocks, "y", Y, step) for step in range(1, Y)], axis=2)
     by_y = by_y.reshape(C, X * Y * seq_rows, context.shape[1])
 
-    head_pair = swap(colbert_head, "c", C, 1)
-    head_pair = jnp.where(
-        here_c == 0,
-        jnp.stack([colbert_head, head_pair]),
-        jnp.stack([head_pair, colbert_head]),
-    )
-    head_full = unxor(
-        jnp.stack([head_pair] + [swap(head_pair, "x", X, step) for step in range(1, X)]), here_x
-    ).reshape(width, feature_dim)
     head_rows = colbert_head.shape[0]
     mine = (here_x * C + here_c) * head_rows
     gain_blk = lax.dynamic_slice_in_dim(norm_gain, mine, head_rows, 0)
-    by_y, head_full, proj_z, gain_blk = lax.optimization_barrier(
-        (by_y, head_full, proj_z, gain_blk)
-    )
+    by_y, proj_z, gain_blk, colbert_head = lax.optimization_barrier(
+        (by_y, proj_z, gain_blk, colbert_head)
+    )
+    head_full = lax.all_gather(colbert_head, TENSOR, axis=0, tiled=True)
 
     away = jnp.dot(by_y[1], proj_z, preferred_element_type=F32).astype(BF16)
     away = swap(away, "c", C, 1)
@@ -314,36 +313,34 @@
     inv_rms = lax.rsqrt(jnp.mean(summed * summed, axis=-1, keepdims=True) + EPS)
     scaled_sum = summed * inv_rms
     normed = (scaled_sum * norm_gain).astype(BF16)
+
+    unit = scaled_sum.astype(BF16).reshape(seq_rows, X, C, head_rows).transpose(1, 2, 0, 3)
+    unit = unxor(jnp.where(here_c == 0, unit, unit[:, ::-1]), here_x)
+    unit = jnp.stack([unit[:, 0], swap(unit[:, 1], "c", C, 1)], axis=1)
+    unit = jnp.stack([unit[0]] + [swap(unit[step], "x", X, step) for step in range(1, X)])
+    unit, normed, got_docs = lax.optimization_barrier((unit, normed, got_docs))
+    unit = unit.reshape(X * C * seq_rows, head_rows)
+    units = [unit] + [swap(unit, "y", Y, step) for step in range(1, Y)]
+
     embedded = jnp.dot(normed, head_full, preferred_element_type=F32)
-
-    unit = scaled_sum.astype(BF16).reshape(seq_rows, X * C, head_rows).transpose(1, 0, 2)
-    unit, got_docs = lax.optimization_barrier((unit, got_docs))
-    unit_plane = lax.all_to_all(
-        jnp.broadcast_to(unit, (Y,) + unit.shape).reshape((-1,) + unit.shape[1:]),
-        PLANE,
-        0,
-        0,
-        tiled=True,
-    ).reshape(Y * X * C * seq_rows, head_rows)
-
     slot_scores, packet = score(got_docs, embedded, spans, flags, scaled_sum, head_full)
-    packet, unit_plane = lax.optimization_barrier((packet, unit_plane))
     packets = lax.all_to_all(
         jnp.broadcast_to(packet, (Y * X * C,) + packet.shape), PLANE, 0, 0, tiled=True
     )
     ge_plane = packets[:, :seq_rows]
 
-    proj_full = lax.all_gather(proj_z, "y", axis=1, tiled=True)
-    packets, summed_all, proj_full = lax.optimization_barrier(
-        (packets, summed.astype(BF16), proj_full)
-    )
-    summed_all = lax.all_gather(summed_all, TENSOR, axis=0, tiled=True)
 
     share = head_rows // Z
     lines = width // feature_dim // Z
-    first = bundle(packets, unit_plane, Z)
+    here = ((here_y * X + here_x) * C + here_c).reshape(1)
+    first = bundle(here, packets, units, Z)
     first, slot_scores, ge_plane = lax.optimization_barrier((first, slot_scores, ge_plane))
     scores = jnp.sum(jnp.where(placed, slot_scores, 0.0), axis=0)[None, :]
+    proj_full = lax.all_gather(proj_z, "y", axis=1, tiled=True)
+    marker, summed_all, proj_full = lax.optimization_barrier(
+        (first, summed.astype(BF16), proj_full)
+    )
+    summed_all = lax.all_gather(summed_all, TENSOR, axis=0, tiled=True)
     first = lax.all_to_all(first, "z", 0, 0, tiled=True)
     second = jnp.sum(first.astype(F32), axis=0, keepdims=True).astype(BF16)
     packet, packets = lax.optimization_barrier((packet, packets))

time: 279 us -> 296 us (1.061)
  waiting for transfers between devices: 33.9 us -> 69 us
  blocking collectives: 17.3 us -> 0 us
  other arithmetic: 21.2 us -> 13.2 us
  starting transfers between devices: 114 us -> 121 us
  local copies, waits for them, and re-layouts: 38.8 us -> 35.8 us
    ppermute x14 -> x17, waiting for transfers between devices: 21.5 us -> 52.7 us  [swap(): return lax.ppermute(values, axis, [(i, i ^ step) for i in range(size)])]
    all_to_all x1 -> x0, blocking collectives: 17.3 us -> none  [local(): lax.all_to_all(jnp.broadcast_to(packet, (Y * X * C,) + packet.shape), PLA...]
    all_to_all x1, waiting for transfers between devices: 2.81 us -> 9.6 us  [local(): first = lax.all_to_all(first, 'z', 0, 0, tiled=True)]
    ppermute x14 -> x17, starting transfers between devices: 49.4 us -> 55.5 us  [swap(): return lax.ppermute(values, axis, [(i, i ^ step) for i in range(size)])]
    all_to_all x1, waiting for transfers between devices: 5.6 us -> 1.93 us  [local(): lax.all_to_all(jnp.broadcast_to(packet, (Y * X * C,) + packet.shape), PLA...]
    gather x5, local copies, waits for them, and re-layouts: 22.1 us -> 18.9 us  [rows_of(): return values.at[index].get(mode='promise_in_bounds')]
  transfers between devices with their start and end apart: 22 -> 26, of which waited for: 12 -> 15; matrix products, arithmetic and copies ran while one was open for 26% -> 22% of each run, Pallas kernels for 6% -> 6%
where the time goes in v7:
time: 296 us; the launch traced here: 291 us
  starting transfers between devices  121 us (41%)
  waiting for transfers between devices  69 us (23%)
  local copies, waits for them, and re-layouts  35.8 us (12%)
  matrix products  20.3 us (7%)
  Pallas kernels  17 us (6%)
  between operations  14.6 us (5%)
  other arithmetic  13.2 us (4%)
    ppermute x17, starting transfers between devices, swap(): return lax.ppermute(values, axis, [(i, i ^ step) for i in range(size)])  55.5 us
    ppermute x17, waiting for transfers between devices, swap(): return lax.ppermute(values, axis, [(i, i ^ step) for i in range(size)])  52.7 us
    all_to_all x1, starting transfers between devices, local(): notes = lax.all_to_all(note, DP, 0, 0, tiled=True)  19.3 us
    gather x5, local copies, waits for them, and re-layouts, rows_of(): return values.at[index].get(mode='promise_in_bounds')  18.9 us
    all_to_all x1, starting transfers between devices, local(): lax.all_to_all(chosen.reshape(shards, cap * doc_len, feature_dim), DP, 0,...  15 us
    all_to_all x1, starting transfers between devices, local(): first = lax.all_to_all(first, 'z', 0, 0, tiled=True)  11.6 us
    all_to_all x1, starting transfers between devices, local(): lax.all_to_all(jnp.broadcast_to(packet, (Y * X * C,) + packet.shape), PLA...  10.5 us
    all_to_all x1, waiting for transfers between devices, local(): first = lax.all_to_all(first, 'z', 0, 0, tiled=True)  9.6 us
  transfers between devices with their start and end apart: 26, of which 15 were waited for; matrix products, arithmetic and copies ran while one was open for 22% of the time, Pallas kernels for 6%

profile of v7, /device:TPU:1, one launch (start us, length us, event | category | flops | bytes accessed | tf_op | source)
XLA Modules:
  0.0 290.7 jit_solution(5043791368841600693)
XLA Ops:
  11.1 19.3 %all-to-all-start = ((s32[64,1,128]{2,1,0:T(1,128)}), s32[64,1,128]{2,1,0:T(1,128)S(1)}, u32[]{:S(2)}, u32[]{:S(2)}) async-start(s32[64,1,128]{2,1,0:T(1,128)} %bitcast.8), calls=%async_computation | async-start | bytes 65536 | tf_op jit(solution)/shard_map/all_to_all | solution.py:267
  30.4 0.8 reshape.263
  31.3 3.0 %reshape.262.packed = s32[4096,16]{1,0:T(8,128)} reshape(s32[64,1024]{1,0:T(8,128)} %param.19) | data formatting | bytes 524288 | tf_op jit(solution)/shard_map/reshape | solution.py:70
  34.4 15.0 %gather_fusion = bf16[4096,128]{1,0:T(8,128)(2,1)} fusion(bf16[8192,128]{1,0:T(8,128)(2,1)S(1)} %copy-done, s32[4096]{0:T(1024)S(1)} %broadcast_clamp_fusion), kind=kCustom, calls=%fused_computation | custom fusion | bytes 2113536 | tf_op jit(solution)/shard_map/gather | solution.py:29
  49.3 1.6 copy-done.2
  50.9 1.2 copy-done.5
  52.2 5.4 %decode.1 = bf16[4096,128]{1,0:T(8,128)(2,1)S(1)} custom-call(f32[4]{0:T(128)S(1)} %copy-done.6, s32[4096,16]{1,0:T(8,128)S(1)} %copy-done.2, bf16[4096,128]{1,0:T(8,128)(2,1)S(1)} %copy-done.5), custom_call_target="tpu_custom_call" | custom-call | tf_op jit(solution)/shard_map/decode/pallas_call | solution.py:72
  57.9 2.2 gather_fusion.1
  60.1 15.0 %all-to-all-start.1 = ((bf16[64,128,128]{2,1,0:T(8,128)(2,1)}), bf16[64,128,128]{2,1,0:T(8,128)(2,1)}, u32[]{:S(2)}, u32[]{:S(2)}) async-start(bf16[64,128,128]{2,1,0:T(8,128)(2,1)} %bitcast.114), calls=%async_computation.1 | async-start | bytes 4194304 | tf_op jit(solution)/shard_map/all_to_all | solution.py:271
  75.8 4.3 %collective-permute-start.2 = (bf16[2,4,32,640]{3,2,0,1:T(8,128)(2,1)S(1)}, bf16[2,4,32,640]{3,2,0,1:T(8,128)(2,1)S(1)}, u32[]{:S(2)}, u32[]{:S(2)}) collective-permute-start(bf16[2,4,32,640]{3,2,0,1:T(8,128)(2,1)S(1)} %bitcast.118), channel_id=1, source_target_pairs={{0,384},{128,256},{256,128},{384,0},{1,385},{129,257},{257,129},{3... | collective-permute-start | bytes 983048 | tf_op jit(solution)/shard_map/ppermute | solution.py:25
  80.1 2.3 collective-permute-start.1
  82.3 2.4 collective-permute-start
  85.4 10.5 %collective-permute-done.2 = bf16[2,4,32,640]{3,2,0,1:T(8,128)(2,1)S(1)} collective-permute-done((bf16[2,4,32,640]{3,2,0,1:T(8,128)(2,1)S(1)}, bf16[2,4,32,640]{3,2,0,1:T(8,128)(2,1)S(1)}, u32[]{:S(2)}, u32[]{:S(2)}) %collective-permute-start.2) | collective-permute-done | bytes 327712 | tf_op jit(solution)/shard_map/ppermute | solution.py:25
  95.9 3.4 %collective-permute-done = bf16[2,4,32,640]{3,2,0,1:T(8,128)(2,1)S(1)} collective-permute-done((bf16[2,4,32,640]{3,2,0,1:T(8,128)(2,1)S(1)}, bf16[2,4,32,640]{3,2,0,1:T(8,128)(2,1)S(1)}, u32[]{:S(2)}, u32[]{:S(2)}) %collective-permute-start) | collective-permute-done | bytes 327712 | tf_op jit(solution)/shard_map/ppermute | solution.py:25
  99.5 1.2 copy.46
  101.5 3.6 %convolution_convert_fusion = bf16[512,1024]{1,0:T(8,128)(2,1)} fusion(bf16[640,1024]{0,1:T(8,128)(2,1)} %all-gather.5.cloned.1.call-done, bf16[2,512,640]{2,1,0:T(8,128)(2,1)} %bitcast.116), kind=kOutput, calls=%fused_computation.9 | convolution fusion | flops 671612928 | bytes 3014656 | tf_op jit(solution)/shard_map/dot_general | solution.py:300
  105.2 5.5 %collective-permute-start.3 = (bf16[512,1024]{1,0:T(8,128)(2,1)}, bf16[512,1024]{1,0:T(8,128)(2,1)}, u32[]{:S(2)}, u32[]{:S(2)}) collective-permute-start(bf16[512,1024]{1,0:T(8,128)(2,1)} %convolution_convert_fusion), channel_id=1, source_target_pairs={{0,1},{1,0},{2,3},{3,2},{4,5},{5,4},{6,7},{7,6},{8,9},{9,8},{10,11... | collective-permute-start | bytes 3145736 | tf_op jit(solution)/shard_map/ppermute | solution.py:25
  110.8 2.1 convolution_convert_fusion.1
  113.3 1.7 convert_add_fusion
  115.0 4.4 %collective-permute-start.6 = (bf16[4,32,1024]{2,1,0:T(8,128)(2,1)S(1)}, bf16[4,32,1024]{2,1,0:T(8,128)(2,1)S(1)}, u32[]{:S(2)}, u32[]{:S(2)}) collective-permute-start(bf16[4,32,1024]{2,1,0:T(8,128)(2,1)S(1)} %bitcast.133), channel_id=1, source_target_pairs={{0,6},{2,4},{4,2},{6,0},{1,7},{3,5},{5,3},{7,1},{8,14},{10,12},{12... | collective-permute-start | bytes 786440 | tf_op jit(solution)/shard_map/ppermute | solution.py:25
  119.4 2.5 collective-permute-start.5
  121.9 2.1 collective-permute-start.4
  124.1 7.9 %collective-permute-done.6 = bf16[4,32,1024]{2,1,0:T(8,128)(2,1)S(1)} collective-permute-done((bf16[4,32,1024]{2,1,0:T(8,128)(2,1)S(1)}, bf16[4,32,1024]{2,1,0:T(8,128)(2,1)S(1)}, u32[]{:S(2)}, u32[]{:S(2)}) %collective-permute-start.6) | collective-permute-done | bytes 262176 | tf_op jit(solution)/shard_map/ppermute | solution.py:25
  132.0 5.1 %collective-permute-done.4 = bf16[4,32,1024]{2,1,0:T(8,128)(2,1)S(1)} collective-permute-done((bf16[4,32,1024]{2,1,0:T(8,128)(2,1)S(1)}, bf16[4,32,1024]{2,1,0:T(8,128)(2,1)S(1)}, u32[]{:S(2)}, u32[]{:S(2)}) %collective-permute-start.4) | collective-permute-done | bytes 262176 | tf_op jit(solution)/shard_map/ppermute | solution.py:25
  137.3 3.0 %collective-permute-start.9 = (bf16[32,1024]{1,0:T(8,128)(2,1)S(1)}, bf16[32,1024]{1,0:T(8,128)(2,1)S(1)}, u32[]{:S(2)}, u32[]{:S(2)}) collective-permute-start(bf16[32,1024]{1,0:T(8,128)(2,1)S(1)} %get-tuple-element.67), channel_id=1, source_target_pairs={{0,384},{128,256},{256,128},{384,0},{1,385},{129,257},{257,129},{3... | collective-permute-start | bytes 196616 | tf_op jit(solution)/shard_map/ppermute | solution.py:25
  140.3 3.5 %collective-permute-start.8 = (bf16[32,1024]{1,0:T(8,128)(2,1)S(1)}, bf16[32,1024]{1,0:T(8,128)(2,1)S(1)}, u32[]{:S(2)}, u32[]{:S(2)}) collective-permute-start(bf16[32,1024]{1,0:T(8,128)(2,1)S(1)} %get-tuple-element.68), channel_id=1, source_target_pairs={{0,256},{128,384},{256,0},{384,128},{1,257},{129,385},{257,1},{385... | collective-permute-start | bytes 196616 | tf_op jit(solution)/shard_map/ppermute | solution.py:25
  143.9 2.6 collective-permute-start.7
  146.5 0.9 collective-permute-done.8
  147.4 2.7 collective-permute-done.7
  151.6 0.8 multiply_convert_fusion.1
  152.4 0.8 copy-done.3
  154.1 4.3 %collective-permute-start.10 = (bf16[4,32,512]{2,1,0:T(8,128)(2,1)S(1)}, bf16[4,32,512]{2,1,0:T(8,128)(2,1)S(1)}, u32[]{:S(2)}, u32[]{:S(2)}) collective-permute-start(bf16[4,32,512]{2,1,0:T(8,128)(2,1)S(1)} %get-tuple-element.65), channel_id=1, source_target_pairs={{0,1},{1,0},{2,3},{3,2},{4,5},{5,4},{6,7},{7,6},{8,9},{9,8},{10,11... | collective-permute-start | bytes 393224 | tf_op jit(solution)/shard_map/ppermute | solution.py:25
  158.8 0.7 collective-permute-done.10
  159.5 4.6 %collective-permute-start.13 = (bf16[2,32,512]{2,1,0:T(8,128)(2,1)S(1)}, bf16[2,32,512]{2,1,0:T(8,128)(2,1)S(1)}, u32[]{:S(2)}, u32[]{:S(2)}) collective-permute-start(bf16[2,32,512]{2,1,0:T(8,128)(2,1)S(1)} %get-tuple-element.62), channel_id=1, source_target_pairs={{0,6},{2,4},{4,2},{6,0},{1,7},{3,5},{5,3},{7,1},{8,14},{10,12},{12... | collective-permute-start | bytes 196616 | tf_op jit(solution)/shard_map/ppermute | solution.py:25
  164.1 2.3 collective-permute-start.12
  166.4 2.1 collective-permute-start.11
  168.9 2.1 collective-permute-done.12
  171.0 0.8 collective-permute-done.11
  171.9 1.7 fusion.26.embedded_ref
  173.7 1.0 copy-done.4
  174.8 9.2 %score.1 = (f32[128,1]{1,0:T(8,128)S(1)}, bf16[64,128]{1,0:T(8,128)(2,1)S(1)}) custom-call(bf16[8192,128]{1,0:T(8,128)(2,1)} %bitcast.43.docs, f32[32,128]{1,0:T(8,128)S(1)} %fusion.26.embedded_ref, s32[128,32]{1,0:T(8,128)S(1)} %broadcast_in_dim.100.spans, s32[128,2]{1,0:T(8,128)S(1)} %copy.52.flags, f32[32,4096]{1,0:T(8,128)S(1)} %copy-done.4, ...), custom_call_target="tpu_custom_call" | custom-call | flops 134217728 | bytes 30000000 | tf_op jit(solution)/shard_map/score/pallas_call | solution.py:159
  184.0 0.9 broadcast_in_dim.101
  184.9 10.5 %all-to-all-start.2 = ((bf16[32,64,128]{2,1,0:T(8,128)(2,1)}), bf16[32,64,128]{2,1,0:T(8,128)(2,1)}, u32[]{:S(2)}, u32[]{:S(2)}) async-start(bf16[32,64,128]{2,1,0:T(8,128)(2,1)} %broadcast_in_dim.101), calls=%async_computation.2 | async-start | bytes 1048576 | tf_op jit(solution)/shard_map/all_to_all | solution.py:327
  195.4 3.3 %collective-permute-start.14 = (bf16[256,512]{1,0:T(8,128)(2,1)S(1)}, bf16[256,512]{1,0:T(8,128)(2,1)}, u32[]{:S(2)}, u32[]{:S(2)}) collective-permute-start(bf16[256,512]{1,0:T(8,128)(2,1)S(1)} %bitcast.106), channel_id=1, source_target_pairs={{0,128},{128,0},{256,384},{384,256},{1,129},{129,1},{257,385},{385... | collective-permute-start | bytes 786440 | tf_op jit(solution)/shard_map/ppermute | solution.py:25
  198.7 4.3 %collective-permute-start.15 = (bf16[256,512]{1,0:T(8,128)(2,1)S(1)}, bf16[256,512]{1,0:T(8,128)(2,1)}, u32[]{:S(2)}, u32[]{:S(2)}) collective-permute-start(bf16[256,512]{1,0:T(8,128)(2,1)S(1)} %bitcast.107), channel_id=1, source_target_pairs={{0,256},{128,384},{256,0},{384,128},{1,257},{129,385},{257,1},{385... | collective-permute-start | bytes 786440 | tf_op jit(solution)/shard_map/ppermute | solution.py:25
  203.1 1.9 collective-permute-start.16
  205.1 1.9 all-to-all-done.2.packets
  207.0 1.7 slice.127
  208.7 7.5 %collective-permute-done.14.refs_1_ = bf16[256,512]{1,0:T(8,128)(2,1)} collective-permute-done((bf16[256,512]{1,0:T(8,128)(2,1)S(1)}, bf16[256,512]{1,0:T(8,128)(2,1)}, u32[]{:S(2)}, u32[]{:S(2)}) %collective-permute-start.14) | collective-permute-done | bytes 262176 | tf_op jit(solution)/shard_map/ppermute | solution.py:25
  216.2 10.7 %collective-permute-done.15.refs_2_ = bf16[256,512]{1,0:T(8,128)(2,1)} collective-permute-done((bf16[256,512]{1,0:T(8,128)(2,1)S(1)}, bf16[256,512]{1,0:T(8,128)(2,1)}, u32[]{:S(2)}, u32[]{:S(2)}) %collective-permute-start.15) | collective-permute-done | bytes 262176 | tf_op jit(solution)/shard_map/ppermute | solution.py:25
  226.9 2.4 bundle.1
  229.9 0.9 subtract_convert_fusion
  230.9 11.6 %all-to-all-start.3 = ((bf16[16,48,128]{2,1,0:T(8,128)(2,1)}), bf16[16,48,128]{2,1,0:T(8,128)(2,1)S(1)}, u32[]{:S(2)}, u32[]{:S(2)}) async-start(bf16[16,48,128]{2,1,0:T(8,128)(2,1)} %bundle.1), calls=%async_computation.3 | async-start | bytes 393216 | tf_op jit(solution)/shard_map/all_to_all | solution.py:344
  242.5 0.8 constant_dynamic-slice_fusion
  244.1 1.4 select_reduce_fusion.1
  245.4 9.6 %all-to-all-done.3 = bf16[16,48,128]{2,1,0:T(8,128)(2,1)S(1)} async-done(((bf16[16,48,128]{2,1,0:T(8,128)(2,1)}), bf16[16,48,128]{2,1,0:T(8,128)(2,1)S(1)}, u32[]{:S(2)}, u32[]{:S(2)}) %all-to-all-start.3) | async-done | bytes 196640 | tf_op jit(solution)/shard_map/all_to_all | solution.py:344
  255.1 5.5 %convolution_convert_fusion.2 = bf16[640,128]{1,0:T(8,128)(2,1)} fusion(bf16[640,4096]{0,1:T(8,128)(2,1)} %all-gather.9.cloned.1.call-done, bf16[4096,128]{1,0:T(8,128)(2,1)S(1)} %copy-done.1, f32[4096]{0:T(1024)S(1)} %copy-done.17), kind=kOutput, calls=%fused_computation.16 | convolution fusion | flops 672743424 | bytes 6471680 | tf_op jit(solution)/shard_map/dot_general | solution.py:358
  261.2 8.9 %all-to-all-start.4 = ((bf16[16,48,128]{2,1,0:T(8,128)(2,1)}), bf16[16,48,128]{2,1,0:T(8,128)(2,1)S(1)}, u32[]{:S(2)}, u32[]{:S(2)}) async-start(bf16[16,48,128]{2,1,0:T(8,128)(2,1)} %broadcast_in_dim.107), calls=%async_computation.4 | async-start | bytes 393216 | tf_op jit(solution)/shard_map/all_to_all | solution.py:362
  270.2 2.2 multiply_reduce_fusion
  272.4 1.5 fusion.2
  274.0 4.4 %convolution_multiply_fusion.1 = f32[256,640]{1,0:T(8,128)S(1)} fusion(bf16[256,4096]{1,0:T(8,128)(2,1)S(1)} %copy-done.9, bf16[640,4096]{0,1:T(8,128)(2,1)} %all-gather.9.cloned.1.call-done, f32[256]{0:T(256)S(1)} %get-tuple-element.71), kind=kOutput, calls=%fused_computation.12 | convolution fusion | flops 1342341120 | bytes 7996416 | tf_op jit(solution)/shard_map/dot_general | solution.py:365
  278.4 1.0 fusion.1
  279.4 3.4 %all-to-all-done.4 = bf16[16,48,128]{2,1,0:T(8,128)(2,1)S(1)} async-done(((bf16[16,48,128]{2,1,0:T(8,128)(2,1)}), bf16[16,48,128]{2,1,0:T(8,128)(2,1)S(1)}, u32[]{:S(2)}, u32[]{:S(2)}) %all-to-all-start.4) | async-done | bytes 196640 | tf_op jit(solution)/shard_map/all_to_all | solution.py:362
  283.4 0.8 convert_multiply_fusion
  (126 shorter events, 13.2 us)
Async XLA Ops:
  7.2 27.2 %copy-start = (bf16[8192,128]{1,0:T(8,128)(2,1)S(1)}, bf16[8192,128]{1,0:T(8,128)(2,1)}, u32[]{:S(2)}) copy-start(bf16[8192,128]{1,0:T(8,128)(2,1)} %param.20) | copy-start | bytes 6291460
  7.2 93.6 %all-gather.5.cloned.1.call-start = ((), (), s32[]{:S(2)}) async-start(), calls=%async_computation.5 | async-start | bytes 1392640 | tf_op jit(solution)/shard_map/all_gather | solution.py:265
  9.4 101.3 %copy-start.23 = (s32[64]{0:T(128)}, s32[64]{0:T(128)S(1)}, u32[]{:S(2)}) copy-start(s32[64]{0:T(128)S(1)} %fusion.20) | copy-start | bytes 772
  11.1 46.5 %all-to-all-start = ((s32[64,1,128]{2,1,0:T(1,128)}), s32[64,1,128]{2,1,0:T(1,128)S(1)}, u32[]{:S(2)}, u32[]{:S(2)}) async-start(s32[64,1,128]{2,1,0:T(1,128)} %bitcast.8), calls=%async_computation | async-start | bytes 65536 | tf_op jit(solution)/shard_map/all_to_all | solution.py:267
  34.4 15.0 %copy-start.6 = (f32[4]{0:T(128)S(1)}, f32[4]{0:T(128)}, u32[]{:S(2)}) copy-start(f32[4]{0:T(128)} %buckets.1) | copy-start | bytes 52
  49.3 1.6 copy-start.2
  50.9 1.2 copy-start.5
  60.1 15.0 %copy-start.13 = (bf16[256,640]{1,0:T(8,128)(2,1)S(1)}, bf16[256,640]{1,0:T(8,128)(2,1)}, u32[]{:S(2)}) copy-start(bf16[256,640]{1,0:T(8,128)(2,1)} %param.12) | copy-start | bytes 983044
  60.1 24.7 %copy-start.15 = (f32[4096]{0:T(1024)S(1)}, f32[4096]{0:T(1024)}, u32[]{:S(2)}) copy-start(f32[4096]{0:T(1024)} %param.14) | copy-start | bytes 49156
  60.1 111.8 %all-to-all-start.1 = ((bf16[64,128,128]{2,1,0:T(8,128)(2,1)}), bf16[64,128,128]{2,1,0:T(8,128)(2,1)}, u32[]{:S(2)}, u32[]{:S(2)}) async-start(bf16[64,128,128]{2,1,0:T(8,128)(2,1)} %bitcast.114), calls=%async_computation.1 | async-start | bytes 4194304 | tf_op jit(solution)/shard_map/all_to_all | solution.py:271
  75.0 96.9 %all-gather.7.cloned.1.call-start = ((), (), s32[]{:S(2)}) async-start(), calls=%async_computation.6 | async-start | bytes 1179648 | tf_op jit(solution)/shard_map/all_gather | solution.py:298
  75.8 20.1 %collective-permute-start.2 = (bf16[2,4,32,640]{3,2,0,1:T(8,128)(2,1)S(1)}, bf16[2,4,32,640]{3,2,0,1:T(8,128)(2,1)S(1)}, u32[]{:S(2)}, u32[]{:S(2)}) collective-permute-start(bf16[2,4,32,640]{3,2,0,1:T(8,128)(2,1)S(1)} %bitcast.118), channel_id=1, source_target_pairs={{0,384},{128,256},{256,128},{384,0},{1,385},{129,257},{257,129},{3... | collective-permute-start | bytes 983048 | tf_op jit(solution)/shard_map/ppermute | solution.py:25
  80.1 15.8 %collective-permute-start.1 = (bf16[2,4,32,640]{3,2,0,1:T(8,128)(2,1)S(1)}, bf16[2,4,32,640]{3,2,0,1:T(8,128)(2,1)S(1)}, u32[]{:S(2)}, u32[]{:S(2)}) collective-permute-start(bf16[2,4,32,640]{3,2,0,1:T(8,128)(2,1)S(1)} %bitcast.119), channel_id=1, source_target_pairs={{0,256},{128,384},{256,0},{384,128},{1,257},{129,385},{257,1},{385... | collective-permute-start | bytes 983048 | tf_op jit(solution)/shard_map/ppermute | solution.py:25
  82.3 17.0 %collective-permute-start = (bf16[2,4,32,640]{3,2,0,1:T(8,128)(2,1)S(1)}, bf16[2,4,32,640]{3,2,0,1:T(8,128)(2,1)S(1)}, u32[]{:S(2)}, u32[]{:S(2)}) collective-permute-start(bf16[2,4,32,640]{3,2,0,1:T(8,128)(2,1)S(1)} %bitcast.120), channel_id=1, source_target_pairs={{0,128},{128,0},{256,384},{384,256},{1,129},{129,1},{257,385},{385... | collective-permute-start | bytes 983048 | tf_op jit(solution)/shard_map/ppermute | solution.py:25
  100.8 130.1 %all-gather.9.cloned.1.call-start = ((), (), s32[]{:S(2)}) async-start(), calls=%async_computation.7 | async-start | bytes 6553600 | tf_op jit(solution)/shard_map/all_gather | solution.py:339
  101.5 9.3 %copy-start.12 = (bf16[640,1024]{0,1:T(8,128)(2,1)S(1)}, bf16[640,1024]{0,1:T(8,128)(2,1)}, u32[]{:S(2)}) copy-start(bf16[640,1024]{0,1:T(8,128)(2,1)} %all-gather.5.cloned.1.call-done) | copy-start | bytes 3932164
  105.2 8.1 %collective-permute-start.3 = (bf16[512,1024]{1,0:T(8,128)(2,1)}, bf16[512,1024]{1,0:T(8,128)(2,1)}, u32[]{:S(2)}, u32[]{:S(2)}) collective-permute-start(bf16[512,1024]{1,0:T(8,128)(2,1)} %convolution_convert_fusion), channel_id=1, source_target_pairs={{0,1},{1,0},{2,3},{3,2},{4,5},{5,4},{6,7},{7,6},{8,9},{9,8},{10,11... | collective-permute-start | bytes 3145736 | tf_op jit(solution)/shard_map/ppermute | solution.py:25
  112.9 11.2 %copy-start.22 = (s32[1,64]{1,0:T(1,128)S(1)}, s32[1,64]{1,0:T(1,128)}, u32[]{:S(2)}) copy-start(s32[1,64]{1,0:T(1,128)} %param.16) | copy-start | bytes 772
  115.0 17.0 %collective-permute-start.6 = (bf16[4,32,1024]{2,1,0:T(8,128)(2,1)S(1)}, bf16[4,32,1024]{2,1,0:T(8,128)(2,1)S(1)}, u32[]{:S(2)}, u32[]{:S(2)}) collective-permute-start(bf16[4,32,1024]{2,1,0:T(8,128)(2,1)S(1)} %bitcast.133), channel_id=1, source_target_pairs={{0,6},{2,4},{4,2},{6,0},{1,7},{3,5},{5,3},{7,1},{8,14},{10,12},{12... | collective-permute-start | bytes 786440 | tf_op jit(solution)/shard_map/ppermute | solution.py:25
  119.4 12.6 %collective-permute-start.5 = (bf16[4,32,1024]{2,1,0:T(8,128)(2,1)S(1)}, bf16[4,32,1024]{2,1,0:T(8,128)(2,1)S(1)}, u32[]{:S(2)}, u32[]{:S(2)}) collective-permute-start(bf16[4,32,1024]{2,1,0:T(8,128)(2,1)S(1)} %bitcast.132), channel_id=1, source_target_pairs={{0,4},{2,6},{4,0},{6,2},{1,5},{3,7},{5,1},{7,3},{8,12},{10,14},{12... | collective-permute-start | bytes 786440 | tf_op jit(solution)/shard_map/ppermute | solution.py:25
  121.9 15.2 %collective-permute-start.4 = (bf16[4,32,1024]{2,1,0:T(8,128)(2,1)S(1)}, bf16[4,32,1024]{2,1,0:T(8,128)(2,1)S(1)}, u32[]{:S(2)}, u32[]{:S(2)}) collective-permute-start(bf16[4,32,1024]{2,1,0:T(8,128)(2,1)S(1)} %bitcast.131), channel_id=1, source_target_pairs={{0,2},{2,0},{4,6},{6,4},{1,3},{3,1},{5,7},{7,5},{8,10},{10,8},{12,... | collective-permute-start | bytes 786440 | tf_op jit(solution)/shard_map/ppermute | solution.py:25
  137.3 13.5 %copy-start.10 = (bf16[32,4096]{1,0:T(8,128)(2,1)S(1)}, bf16[32,4096]{1,0:T(8,128)(2,1)}, u32[]{:S(2)}) copy-start(bf16[32,4096]{1,0:T(8,128)(2,1)} %param.11) | copy-start | bytes 786436
  137.3 9.2 %collective-permute-start.9 = (bf16[32,1024]{1,0:T(8,128)(2,1)S(1)}, bf16[32,1024]{1,0:T(8,128)(2,1)S(1)}, u32[]{:S(2)}, u32[]{:S(2)}) collective-permute-start(bf16[32,1024]{1,0:T(8,128)(2,1)S(1)} %get-tuple-element.67), channel_id=1, source_target_pairs={{0,384},{128,256},{256,128},{384,0},{1,385},{129,257},{257,129},{3... | collective-permute-start | bytes 196616 | tf_op jit(solution)/shard_map/ppermute | solution.py:25
  140.3 7.0 %collective-permute-start.8 = (bf16[32,1024]{1,0:T(8,128)(2,1)S(1)}, bf16[32,1024]{1,0:T(8,128)(2,1)S(1)}, u32[]{:S(2)}, u32[]{:S(2)}) collective-permute-start(bf16[32,1024]{1,0:T(8,128)(2,1)S(1)} %get-tuple-element.68), channel_id=1, source_target_pairs={{0,256},{128,384},{256,0},{384,128},{1,257},{129,385},{257,1},{385... | collective-permute-start | bytes 196616 | tf_op jit(solution)/shard_map/ppermute | solution.py:25
  143.9 6.2 %collective-permute-start.7 = (bf16[32,1024]{1,0:T(8,128)(2,1)S(1)}, bf16[32,1024]{1,0:T(8,128)(2,1)S(1)}, u32[]{:S(2)}, u32[]{:S(2)}) collective-permute-start(bf16[32,1024]{1,0:T(8,128)(2,1)S(1)} %get-tuple-element.69), channel_id=1, source_target_pairs={{0,128},{128,0},{256,384},{384,256},{1,129},{129,1},{257,385},{385... | collective-permute-start | bytes 196616 | tf_op jit(solution)/shard_map/ppermute | solution.py:25
  150.8 0.8 copy-start.7
  151.5 0.9 copy-start.19
  152.4 0.8 copy-start.3
  154.1 5.3 %collective-permute-start.10 = (bf16[4,32,512]{2,1,0:T(8,128)(2,1)S(1)}, bf16[4,32,512]{2,1,0:T(8,128)(2,1)S(1)}, u32[]{:S(2)}, u32[]{:S(2)}) collective-permute-start(bf16[4,32,512]{2,1,0:T(8,128)(2,1)S(1)} %get-tuple-element.65), channel_id=1, source_target_pairs={{0,1},{1,0},{2,3},{3,2},{4,5},{5,4},{6,7},{7,6},{8,9},{9,8},{10,11... | collective-permute-start | bytes 393224 | tf_op jit(solution)/shard_map/ppermute | solution.py:25
  159.5 9.4 %collective-permute-start.13 = (bf16[2,32,512]{2,1,0:T(8,128)(2,1)S(1)}, bf16[2,32,512]{2,1,0:T(8,128)(2,1)S(1)}, u32[]{:S(2)}, u32[]{:S(2)}) collective-permute-start(bf16[2,32,512]{2,1,0:T(8,128)(2,1)S(1)} %get-tuple-element.62), channel_id=1, source_target_pairs={{0,6},{2,4},{4,2},{6,0},{1,7},{3,5},{5,3},{7,1},{8,14},{10,12},{12... | collective-permute-start | bytes 196616 | tf_op jit(solution)/shard_map/ppermute | solution.py:25
  164.1 6.9 %collective-permute-start.12 = (bf16[2,32,512]{2,1,0:T(8,128)(2,1)S(1)}, bf16[2,32,512]{2,1,0:T(8,128)(2,1)S(1)}, u32[]{:S(2)}, u32[]{:S(2)}) collective-permute-start(bf16[2,32,512]{2,1,0:T(8,128)(2,1)S(1)} %get-tuple-element.63), channel_id=1, source_target_pairs={{0,4},{2,6},{4,0},{6,2},{1,5},{3,7},{5,1},{7,3},{8,12},{10,14},{12... | collective-permute-start | bytes 196616 | tf_op jit(solution)/shard_map/ppermute | solution.py:25
  166.4 5.4 %collective-permute-start.11 = (bf16[2,32,512]{2,1,0:T(8,128)(2,1)S(1)}, bf16[2,32,512]{2,1,0:T(8,128)(2,1)S(1)}, u32[]{:S(2)}, u32[]{:S(2)}) collective-permute-start(bf16[2,32,512]{2,1,0:T(8,128)(2,1)S(1)} %get-tuple-element.61), channel_id=1, source_target_pairs={{0,2},{2,0},{4,6},{6,4},{1,3},{3,1},{5,7},{7,5},{8,10},{10,8},{12,... | collective-permute-start | bytes 196616 | tf_op jit(solution)/shard_map/ppermute | solution.py:25
  171.9 1.8 copy-start.1
  173.7 1.0 copy-start.4
  184.0 45.3 %copy-start.16 = (f32[4096]{0:T(1024)S(1)}, f32[4096]{0:T(1024)}, u32[]{:S(2)}) copy-start(f32[4096]{0:T(1024)} %param.14) | copy-start | bytes 49156
  184.9 22.1 %all-to-all-start.2 = ((bf16[32,64,128]{2,1,0:T(8,128)(2,1)}), bf16[32,64,128]{2,1,0:T(8,128)(2,1)}, u32[]{:S(2)}, u32[]{:S(2)}) async-start(bf16[32,64,128]{2,1,0:T(8,128)(2,1)} %broadcast_in_dim.101), calls=%async_computation.2 | async-start | bytes 1048576 | tf_op jit(solution)/shard_map/all_to_all | solution.py:327
  195.4 74.8 %all-gather.11.cloned.1.call-start = ((), (), s32[]{:S(2)}) async-start(), calls=%async_computation.8 | async-start | bytes 2359296 | tf_op jit(solution)/shard_map/all_gather | solution.py:343
  195.4 20.8 %collective-permute-start.14 = (bf16[256,512]{1,0:T(8,128)(2,1)S(1)}, bf16[256,512]{1,0:T(8,128)(2,1)}, u32[]{:S(2)}, u32[]{:S(2)}) collective-permute-start(bf16[256,512]{1,0:T(8,128)(2,1)S(1)} %bitcast.106), channel_id=1, source_target_pairs={{0,128},{128,0},{256,384},{384,256},{1,129},{129,1},{257,385},{385... | collective-permute-start | bytes 786440 | tf_op jit(solution)/shard_map/ppermute | solution.py:25
  198.7 28.2 %collective-permute-start.15 = (bf16[256,512]{1,0:T(8,128)(2,1)S(1)}, bf16[256,512]{1,0:T(8,128)(2,1)}, u32[]{:S(2)}, u32[]{:S(2)}) collective-permute-start(bf16[256,512]{1,0:T(8,128)(2,1)S(1)} %bitcast.107), channel_id=1, source_target_pairs={{0,256},{128,384},{256,0},{384,128},{1,257},{129,385},{257,1},{385... | collective-permute-start | bytes 786440 | tf_op jit(solution)/shard_map/ppermute | solution.py:25
  203.1 23.8 %collective-permute-start.16 = (bf16[256,512]{1,0:T(8,128)(2,1)S(1)}, bf16[256,512]{1,0:T(8,128)(2,1)}, u32[]{:S(2)}, u32[]{:S(2)}) collective-permute-start(bf16[256,512]{1,0:T(8,128)(2,1)S(1)} %bitcast.108), channel_id=1, source_target_pairs={{0,384},{128,256},{256,128},{384,0},{1,385},{129,257},{257,129},{3... | collective-permute-start | bytes 786440 | tf_op jit(solution)/shard_map/ppermute | solution.py:25
  207.0 22.3 %copy-start.8 = (f32[4,4,8,1024]{3,2,0,1:T(8,128)S(1)}, f32[4,4,8,1024]{3,2,0,1:T(8,128)}, u32[]{:S(2)}) copy-start(f32[4,4,8,1024]{3,2,0,1:T(8,128)} %copy-done.7) | copy-start | bytes 1572868
  207.0 22.3 %copy-start.11 = (bf16[32,4096]{1,0:T(8,128)(2,1)S(1)}, bf16[32,4096]{1,0:T(8,128)(2,1)}, u32[]{:S(2)}) copy-start(bf16[32,4096]{1,0:T(8,128)(2,1)} %param.11) | copy-start | bytes 786436
  208.7 21.2 %copy-start.20 = (f32[32]{0:T(128)S(1)}, f32[32]{0:T(128)}, u32[]{:S(2)}) copy-start(f32[32]{0:T(128)} %copy-done.19) | copy-start | bytes 388
  208.7 21.2 %copy-start.21 = (f32[32]{0:T(128)S(1)}, f32[32]{0:T(128)}, u32[]{:S(2)}) copy-start(f32[32]{0:T(128)} %get-tuple-element.72) | copy-start | bytes 388
  229.9 25.2 %copy-start.17 = (f32[4096]{0:T(1024)S(1)}, f32[4096]{0:T(1024)}, u32[]{:S(2)}) copy-start(f32[4096]{0:T(1024)} %param.14) | copy-start | bytes 49156
  230.9 24.1 %all-to-all-start.3 = ((bf16[16,48,128]{2,1,0:T(8,128)(2,1)}), bf16[16,48,128]{2,1,0:T(8,128)(2,1)S(1)}, u32[]{:S(2)}, u32[]{:S(2)}) async-start(bf16[16,48,128]{2,1,0:T(8,128)(2,1)} %bundle.1), calls=%async_computation.3 | async-start | bytes 393216 | tf_op jit(solution)/shard_map/all_to_all | solution.py:344
  261.2 21.5 %all-to-all-start.4 = ((bf16[16,48,128]{2,1,0:T(8,128)(2,1)}), bf16[16,48,128]{2,1,0:T(8,128)(2,1)S(1)}, u32[]{:S(2)}, u32[]{:S(2)}) async-start(bf16[16,48,128]{2,1,0:T(8,128)(2,1)} %broadcast_in_dim.107), calls=%async_computation.4 | async-start | bytes 393216 | tf_op jit(solution)/shard_map/all_to_all | solution.py:362
  270.2 2.2 copy-start.9
  274.0 4.4 %copy-start.14 = (bf16[640,128]{1,0:T(8,128)(2,1)S(1)}, bf16[640,128]{1,0:T(8,128)(2,1)}, u32[]{:S(2)}) copy-start(bf16[640,128]{1,0:T(8,128)(2,1)} %convolution_convert_fusion.2) | copy-start | bytes 491524
  274.0 9.4 %copy-start.18 = (f32[512]{0:T(512)S(1)}, f32[512]{0:T(512)}, u32[]{:S(2)}) copy-start(f32[512]{0:T(512)} %dynamic_slice.6) | copy-start | bytes 6148
Sparse Core Ops, SparseCore 0:
  10.1 68.1 all-gather.4
  100.9 40.2 all-gather.6
  143.4 81.2 all-gather.8
  231.0 32.3 all-gather.10

commit v8 on v6

--- a/solution.py
+++ b/solution.py
@@ -79,7 +79,7 @@
     )(buckets, packed, rows)
 
 
-def score_kernel(docs, embedded_ref, spans, flags, unit, head, scores, packet, weights, totals):
+def score_kernel(docs, embedded_ref, spans, flags, unit, head, scores, packets, weights, totals):
     slots, queries_n = totals.shape
     tokens = docs.shape[0] // slots
     features = docs.shape[1]
@@ -137,9 +137,12 @@
     grad_q = lax.fori_loop(0, slots // group, add, jnp.zeros((queries_n, features), F32))
     along = jnp.sum(embedded * grad_q, axis=1, keepdims=True)
     grad_embedded = (inverse * grad_q - inverse * inverse * inverse * embedded * along).astype(BF16)
-    packet[0:queries_n, :] = grad_embedded
+    copies = packets.shape[0]
+    for k in range(copies):
+        packets[k, 0:queries_n, :] = grad_embedded
 
     block = 8
+    lines = []
     for i in range(head.shape[0] // (block * features)):
         sums = []
         for k in range(i * block, (i + 1) * block):
@@ -148,21 +151,36 @@
                 grad_embedded, head[at, :], (((1,), (1,)), ((), ())), preferred_element_type=F32
             )
             sums.append(jnp.sum(grad_normed * unit[:, at], axis=0, keepdims=True))
-        line = queries_n + i * block
-        packet[line : line + block, :] = jnp.concatenate(sums, axis=0).astype(BF16)
-
-
-def score(docs, embedded, spans, flags, unit, head):
+        lines.append(jnp.concatenate(sums, axis=0))
+    gain = jnp.concatenate(lines, axis=0).astype(BF16)
+    base = queries_n + gain.shape[0]
+    for k in range(copies):
+        packets[k, queries_n:base, :] = gain
+
+    parts = (packets.shape[1] - base) // queries_n
+    sets = head.shape[0] // (parts * features)
+    for j in range(sets):
+        for part in range(parts):
+            at = (j * parts + part) * features
+            piece = unit[:, at : at + features].astype(BF16)
+            row = base + part * queries_n
+            for k in range(j, copies, sets):
+                packets[k, row : row + queries_n, :] = piece
+
+
+def score(docs, embedded, spans, flags, unit, head, copies, sets):
     slots = flags.shape[0]
     queries_n, features = embedded.shape
     count = docs.shape[0]
+    lines = head.shape[0] // features
+    tall = queries_n + lines + lines // sets * queries_n
     return pl.pallas_call(
         score_kernel,
         in_specs=[VMEM] * 6,
         out_specs=[VMEM] * 2,
         out_shape=[
             jax.ShapeDtypeStruct((slots, 1), F32),
-            jax.ShapeDtypeStruct((queries_n + head.shape[0] // features, features), BF16),
+            jax.ShapeDtypeStruct((copies, tall, features), BF16),
         ],
         scratch_shapes=[
             pltpu.VMEM((count, queries_n), F32),
@@ -178,38 +196,47 @@
     )(docs, embedded, spans, flags, unit, head)
 
 
-def bundle_kernel(packets, unit, out, ge):
-    count, tall, features = packets.shape
-    tokens = unit.shape[0] // count
-    shares, _, _ = out.shape
-    total = jnp.zeros((tall - tokens, features), F32)
+def bundle_kernel(packets, out, sides):
+    count, _, features = packets.shape
+    shares, tall, _ = out.shape
+    share = tall - 16
+    parts = sides.shape[0] - 1
+    tokens = sides.shape[1] // count
+    base = packets.shape[1] - parts * tokens
+    total = jnp.zeros((base - tokens, features), F32)
     for i in range(count):
-        ge[i * tokens : (i + 1) * tokens, :] = packets[i, 0:tokens, :]
-        total = total + packets[i, tokens:tall, :].astype(F32)
-    head = lax.dot_general(
-        ge[...], unit[...], (((0,), (0,)), ((), ())), preferred_element_type=F32
-    ).T
-    share = head.shape[0] // shares
+        sides[0, i * tokens : (i + 1) * tokens, :] = packets[i, 0:tokens, :]
+        total = total + packets[i, tokens:base, :].astype(F32)
+        for part in range(parts):
+            row = base + part * tokens
+            sides[part + 1, i * tokens : (i + 1) * tokens, :] = packets[i, row : row + tokens, :]
     lines = total.shape[0] // shares
+    each = features // share
+    for part in range(parts):
+        head = lax.dot_general(
+            sides[0], sides[part + 1], (((0,), (0,)), ((), ())), preferred_element_type=F32
+        ).T
+        for k in range(each):
+            out[part * each + k, 0:share, :] = head[k * share : (k + 1) * share].astype(BF16)
     for i in range(shares):
-        out[i, 0:share, :] = head[i * share : (i + 1) * share].astype(BF16)
         gain = jnp.concatenate(
             [total[i * lines : (i + 1) * lines], jnp.zeros((16 - lines, features), F32)]
         )
         out[i, share : share + 16, :] = gain.astype(BF16)
 
 
-def bundle(packets, unit, shares):
+def bundle(packets, tokens, lines, shares):
     count, tall, features = packets.shape
+    parts = (tall - tokens - lines) // tokens
     return pl.pallas_call(
         bundle_kernel,
-        in_specs=[VMEM] * 2,
+        in_specs=[VMEM],
         out_specs=VMEM,
-        out_shape=jax.ShapeDtypeStruct((shares, unit.shape[1] // shares + 16, features), BF16),
-        scratch_shapes=[pltpu.VMEM((unit.shape[0], features), BF16)],
+        out_shape=jax.ShapeDtypeStruct((shares, parts * features // shares + 16, features), BF16),
+        scratch_shapes=[pltpu.VMEM((parts + 1, count * tokens, features), BF16)],
         compiler_params=pltpu.CompilerParams(vmem_limit_bytes=32 * 1024 * 1024),
         name="bundle",
-    )(packets, unit)
+    )(packets)
 
 
 def local(
@@ -316,21 +343,12 @@
     normed = (scaled_sum * norm_gain).astype(BF16)
     embedded = jnp.dot(normed, head_full, preferred_element_type=F32)
 
-    unit = scaled_sum.astype(BF16).reshape(seq_rows, X * C, head_rows).transpose(1, 0, 2)
-    unit, got_docs = lax.optimization_barrier((unit, got_docs))
-    unit_plane = lax.all_to_all(
-        jnp.broadcast_to(unit, (Y,) + unit.shape).reshape((-1,) + unit.shape[1:]),
-        PLANE,
-        0,
-        0,
-        tiled=True,
-    ).reshape(Y * X * C * seq_rows, head_rows)
-
-    slot_scores, packet = score(got_docs, embedded, spans, flags, scaled_sum, head_full)
-    packet, unit_plane = lax.optimization_barrier((packet, unit_plane))
-    packets = lax.all_to_all(
-        jnp.broadcast_to(packet, (Y * X * C,) + packet.shape), PLANE, 0, 0, tiled=True
-    )
+    scaled_sum, got_docs = lax.optimization_barrier((scaled_sum, got_docs))
+    slot_scores, packets = score(
+        got_docs, embedded, spans, flags, scaled_sum, head_full, Y * X * C, X * C
+    )
+    grad_embedded = packets[0, :seq_rows]
+    packets = lax.all_to_all(packets, PLANE, 0, 0, tiled=True)
     ge_plane = packets[:, :seq_rows]
 
     proj_full = lax.all_gather(proj_z, "y", axis=1, tiled=True)
@@ -341,13 +359,13 @@
 
     share = head_rows // Z
     lines = width // feature_dim // Z
-    first = bundle(packets, unit_plane, Z)
+    first = bundle(packets, seq_rows, width // feature_dim, Z)
     first, slot_scores, ge_plane = lax.optimization_barrier((first, slot_scores, ge_plane))
     scores = jnp.sum(jnp.where(placed, slot_scores, 0.0), axis=0)[None, :]
     first = lax.all_to_all(first, "z", 0, 0, tiled=True)
     second = jnp.sum(first.astype(F32), axis=0, keepdims=True).astype(BF16)
-    packet, packets = lax.optimization_barrier((packet, packets))
-    grad_embedded = packet[:seq_rows]
+
+    grad_embedded, packets = lax.optimization_barrier((grad_embedded, packets))
     grad_normed = lax.dot_general(
         grad_embedded, head_full, (((1,), (1,)), ((), ())), preferred_element_type=F32
     )

time: 279 us -> 280 us (level)
  blocking collectives: 17.3 us -> 31.5 us
  starting transfers between devices: 114 us -> 105 us
  waiting for transfers between devices: 33.9 us -> 27 us
  local copies, waits for them, and re-layouts: 38.8 us -> 42.7 us
    all_to_all x1, blocking collectives: 17.3 us -> 31.5 us  [local(): packets = lax.all_to_all(packets, PLANE, 0, 0, tiled=True)]
    all_to_all x1 -> x0, starting transfers between devices: 9.46 us -> none  [local(): lax.all_to_all(jnp.broadcast_to(unit, (Y,) + unit.shape).reshape((-1,) +...]
    all_to_all x1 -> x0, waiting for transfers between devices: 5.6 us -> none  [local(): lax.all_to_all(jnp.broadcast_to(unit, (Y,) + unit.shape).reshape((-1,) +...]
    unnamed x61 -> x64, local copies, waits for them, and re-layouts: 5.88 us -> 8.01 us
  transfers between devices with their start and end apart: 22 -> 21, of which waited for: 12 -> 11; matrix products, arithmetic and copies ran while one was open for 26% -> 27% of each run, Pallas kernels for 6% -> 6%
where the time goes in v8:
time: 280 us; the launch traced here: 276 us
  starting transfers between devices  105 us (38%)
  local copies, waits for them, and re-layouts  42.7 us (15%)
  blocking collectives  31.5 us (11%)
  waiting for transfers between devices  27 us (10%)
  other arithmetic  21.9 us (8%)
  matrix products  18 us (6%)
  Pallas kernels  15.3 us (5%)
  between operations  14.6 us (5%)
    ppermute x14, starting transfers between devices, swap(): return lax.ppermute(values, axis, [(i, i ^ step) for i in range(size)])  48.9 us
    all_to_all x1, blocking collectives, local(): packets = lax.all_to_all(packets, PLANE, 0, 0, tiled=True)  31.5 us
    gather x5, local copies, waits for them, and re-layouts, rows_of(): return values.at[index].get(mode='promise_in_bounds')  22 us
    ppermute x14, waiting for transfers between devices, swap(): return lax.ppermute(values, axis, [(i, i ^ step) for i in range(size)])  20.2 us
    all_to_all x1, starting transfers between devices, local(): notes = lax.all_to_all(note, DP, 0, 0, tiled=True)  19.3 us
    all_to_all x1, starting transfers between devices, local(): lax.all_to_all(chosen.reshape(shards, cap * doc_len, feature_dim), DP, 0,...  15 us
    all_to_all x1, starting transfers between devices, local(): first = lax.all_to_all(first, 'z', 0, 0, tiled=True)  12.6 us
    pallas_call x1, Pallas kernels, score(): pl.pallas_call(score_kernel, in_specs=[VMEM] * 6, out_specs=[VMEM] * 2, o...  9.23 us
  transfers between devices with their start and end apart: 21, of which 11 were waited for; matrix products, arithmetic and copies ran while one was open for 27% of the time, Pallas kernels for 6%

profile of v8, /device:TPU:1, one launch (start us, length us, event | category | flops | bytes accessed | tf_op | source)
XLA Modules:
  0.0 275.6 jit_solution(9315335082326143952)
XLA Ops:
  11.1 19.3 %all-to-all-start = ((s32[64,1,128]{2,1,0:T(1,128)}), s32[64,1,128]{2,1,0:T(1,128)S(1)}, u32[]{:S(2)}, u32[]{:S(2)}) async-start(s32[64,1,128]{2,1,0:T(1,128)} %bitcast.15), calls=%async_computation | async-start | bytes 65536 | tf_op jit(solution)/shard_map/all_to_all | solution.py:286
  30.5 3.0 %reshape.316.packed = s32[4096,16]{1,0:T(8,128)} reshape(s32[64,1024]{1,0:T(8,128)} %param.19) | data formatting | bytes 524288 | tf_op jit(solution)/shard_map/reshape | solution.py:70
  33.6 14.9 %gather_fusion.1 = bf16[4096,128]{1,0:T(8,128)(2,1)} fusion(bf16[8192,128]{1,0:T(8,128)(2,1)S(1)} %copy-done, s32[4096]{0:T(1024)S(1)} %broadcast_clamp_fusion), kind=kCustom, calls=%fused_computation.1 | custom fusion | bytes 2113536 | tf_op jit(solution)/shard_map/gather | solution.py:29
  48.5 1.6 copy-done.1
  50.1 1.2 copy-done.5
  51.4 5.4 %decode.1 = bf16[4096,128]{1,0:T(8,128)(2,1)S(1)} custom-call(f32[4]{0:T(128)S(1)} %copy-done.8, s32[4096,16]{1,0:T(8,128)S(1)} %copy-done.1, bf16[4096,128]{1,0:T(8,128)(2,1)S(1)} %copy-done.5), custom_call_target="tpu_custom_call" | custom-call | tf_op jit(solution)/shard_map/decode/pallas_call | solution.py:72
  57.0 2.2 gather_fusion.2
  59.2 15.0 %all-to-all-start.1 = ((bf16[64,128,128]{2,1,0:T(8,128)(2,1)}), bf16[64,128,128]{2,1,0:T(8,128)(2,1)}, u32[]{:S(2)}, u32[]{:S(2)}) async-start(bf16[64,128,128]{2,1,0:T(8,128)(2,1)} %bitcast.106), calls=%async_computation.1 | async-start | bytes 4194304 | tf_op jit(solution)/shard_map/all_to_all | solution.py:291
  74.3 3.4 %collective-permute-start.3 = (bf16[512,128]{1,0:T(8,128)(2,1)S(1)}, bf16[512,128]{1,0:T(8,128)(2,1)S(1)}, u32[]{:S(2)}, u32[]{:S(2)}) collective-permute-start(bf16[512,128]{1,0:T(8,128)(2,1)S(1)} %copy-done.16), channel_id=1, source_target_pairs={{0,1},{1,0},{2,3},{3,2},{4,5},{5,4},{6,7},{7,6},{8,9},{9,8},{10,11... | collective-permute-start | bytes 393224 | tf_op jit(solution)/shard_map/ppermute | solution.py:25
  77.7 0.9 collective-permute-done.3
  79.4 4.4 %collective-permute-start.6 = (bf16[2,512,128]{2,1,0:T(8,128)(2,1)}, bf16[2,512,128]{2,1,0:T(8,128)(2,1)}, u32[]{:S(2)}, u32[]{:S(2)}) collective-permute-start(bf16[2,512,128]{2,1,0:T(8,128)(2,1)} %maximum_select_fusion.1), channel_id=1, source_target_pairs={{0,6},{2,4},{4,2},{6,0},{1,7},{3,5},{5,3},{7,1},{8,14},{10,12},{12... | collective-permute-start | bytes 786440 | tf_op jit(solution)/shard_map/ppermute | solution.py:25
  83.8 2.4 collective-permute-start.5
  86.2 2.2 collective-permute-start.4
  89.1 4.5 %collective-permute-start.2 = (bf16[2,4,32,640]{3,2,0,1:T(8,128)(2,1)S(1)}, bf16[2,4,32,640]{3,2,0,1:T(8,128)(2,1)}, u32[]{:S(2)}, u32[]{:S(2)}) collective-permute-start(bf16[2,4,32,640]{3,2,0,1:T(8,128)(2,1)S(1)} %bitcast.110), channel_id=1, source_target_pairs={{0,384},{128,256},{256,128},{384,0},{1,385},{129,257},{257,129},{3... | collective-permute-start | bytes 983048 | tf_op jit(solution)/shard_map/ppermute | solution.py:25
  93.7 2.3 collective-permute-start.1
  96.0 2.2 collective-permute-start
  98.9 2.2 pad_maximum_fusion.1
  101.1 2.1 gather_fusion.3
  103.2 3.4 %collective-permute-done.2 = bf16[2,4,32,640]{3,2,0,1:T(8,128)(2,1)} collective-permute-done((bf16[2,4,32,640]{3,2,0,1:T(8,128)(2,1)S(1)}, bf16[2,4,32,640]{3,2,0,1:T(8,128)(2,1)}, u32[]{:S(2)}, u32[]{:S(2)}) %collective-permute-start.2) | collective-permute-done | bytes 327712 | tf_op jit(solution)/shard_map/ppermute | solution.py:25
  106.7 2.0 collective-permute-done
  108.7 1.4 pad_maximum_fusion
  110.0 1.2 copy.37
  111.4 2.7 convolution_convert_fusion
  114.0 9.0 %collective-permute-start.7 = (bf16[512,1024]{1,0:T(8,128)(2,1)S(1)}, bf16[512,1024]{1,0:T(8,128)(2,1)S(1)}, u32[]{:S(2)}, u32[]{:S(2)}) collective-permute-start(bf16[512,1024]{1,0:T(8,128)(2,1)S(1)} %convolution_convert_fusion), channel_id=1, source_target_pairs={{0,1},{1,0},{2,3},{3,2},{4,5},{5,4},{6,7},{7,6},{8,9},{9,8},{10,11... | collective-permute-start | bytes 3145736 | tf_op jit(solution)/shard_map/ppermute | solution.py:25
  123.2 1.0 convolution_convert_fusion.1
  124.2 1.0 collective-permute-done.7
  125.3 1.8 convert_add_fusion
  127.1 0.8 fusion.18
  127.9 4.3 %collective-permute-start.10 = (bf16[4,32,1024]{2,1,0:T(8,128)(2,1)}, bf16[4,32,1024]{2,1,0:T(8,128)(2,1)}, u32[]{:S(2)}, u32[]{:S(2)}) collective-permute-start(bf16[4,32,1024]{2,1,0:T(8,128)(2,1)} %bitcast.31), channel_id=1, source_target_pairs={{0,6},{2,4},{4,2},{6,0},{1,7},{3,5},{5,3},{7,1},{8,14},{10,12},{12... | collective-permute-start | bytes 786440 | tf_op jit(solution)/shard_map/ppermute | solution.py:25
  132.2 2.3 collective-permute-start.9
  134.6 2.3 collective-permute-start.8
  138.9 1.1 slice.86
  140.1 3.4 %collective-permute-done.10 = bf16[4,32,1024]{2,1,0:T(8,128)(2,1)} collective-permute-done((bf16[4,32,1024]{2,1,0:T(8,128)(2,1)}, bf16[4,32,1024]{2,1,0:T(8,128)(2,1)}, u32[]{:S(2)}, u32[]{:S(2)}) %collective-permute-start.10) | collective-permute-done | bytes 262176 | tf_op jit(solution)/shard_map/ppermute | solution.py:25
  143.5 3.2 %collective-permute-done.8 = bf16[4,32,1024]{2,1,0:T(8,128)(2,1)} collective-permute-done((bf16[4,32,1024]{2,1,0:T(8,128)(2,1)S(1)}, bf16[4,32,1024]{2,1,0:T(8,128)(2,1)}, u32[]{:S(2)}, u32[]{:S(2)}) %collective-permute-start.8) | collective-permute-done | bytes 262176 | tf_op jit(solution)/shard_map/ppermute | solution.py:25
  146.7 1.3 add_convert_fusion
  148.7 5.1 %collective-permute-start.13 = (bf16[32,1024]{1,0:T(8,128)(2,1)}, bf16[32,1024]{1,0:T(8,128)(2,1)}, u32[]{:S(2)}, u32[]{:S(2)}) collective-permute-start(bf16[32,1024]{1,0:T(8,128)(2,1)} %get-tuple-element.63), channel_id=1, source_target_pairs={{0,384},{128,256},{256,128},{384,0},{1,385},{129,257},{257,129},{3... | collective-permute-start | bytes 196616 | tf_op jit(solution)/shard_map/ppermute | solution.py:25
  153.8 2.3 collective-permute-start.12
  156.2 2.1 collective-permute-start.11
  158.7 0.9 collective-permute-done.13
  159.6 3.2 %collective-permute-done.12 = bf16[32,1024]{1,0:T(8,128)(2,1)} collective-permute-done((bf16[32,1024]{1,0:T(8,128)(2,1)}, bf16[32,1024]{1,0:T(8,128)(2,1)}, u32[]{:S(2)}, u32[]{:S(2)}) %collective-permute-start.12) | collective-permute-done | bytes 65568 | tf_op jit(solution)/shard_map/ppermute | solution.py:25
  162.8 2.1 collective-permute-done.11
  164.8 1.7 pad_maximum_fusion.2
  166.5 2.2 gather_fusion.4
  168.7 1.0 convert_bitcast_fusion
  172.5 1.0 copy-done.4
  173.5 9.2 %score.1 = (f32[128,1]{1,0:T(8,128)S(1)}, bf16[32,192,128]{2,1,0:T(8,128)(2,1)S(1)}) custom-call(bf16[8192,128]{1,0:T(8,128)(2,1)} %bitcast.41.docs, f32[32,128]{1,0:T(8,128)S(1)} %fusion.7.embedded_ref, s32[128,32]{1,0:T(8,128)S(1)} %broadcast_in_dim.97.spans, s32[128,2]{1,0:T(8,128)S(1)} %copy.41.flags, f32[32,4096]{1,0:T(8,128)S(1)} %copy-done.4, ...), custom_call_target="tpu_custom_call" | custom-call | flops 134217728 | bytes 30000000 | tf_op jit(solution)/shard_map/score/pallas_call | solution.py:177
  182.8 1.1 copy-done.6
  183.9 31.5 %all_to_all.32.packets = bf16[32,192,128]{2,1,0:T(8,128)(2,1)} all-to-all(bf16[32,192,128]{2,1,0:T(8,128)(2,1)S(1)} %get-tuple-element.38), channel_id=1, replica_groups=mesh['y'=4,'z'=16,'x'=4,'c'=2] {'y','x','c'}, dimensions={0} | all-to-all | bytes 3145728 | tf_op jit(solution)/shard_map/all_to_all | solution.py:351
  215.4 1.3 slice_bitcast_fusion.3
  216.7 1.4 copy-done.2
  219.5 12.6 %all-to-all-start.3 = ((bf16[16,48,128]{2,1,0:T(8,128)(2,1)}), bf16[16,48,128]{2,1,0:T(8,128)(2,1)}, u32[]{:S(2)}, u32[]{:S(2)}) async-start(bf16[16,48,128]{2,1,0:T(8,128)(2,1)} %copy-done.7), calls=%async_computation.3 | async-start | bytes 393216 | tf_op jit(solution)/shard_map/all_to_all | solution.py:365
  232.4 1.4 select_reduce_fusion.1
  233.7 1.7 multiply_reduce_fusion.1
  235.5 5.5 %convolution_convert_fusion.2 = bf16[640,128]{1,0:T(8,128)(2,1)} fusion(bf16[640,4096]{0,1:T(8,128)(2,1)} %all-gather.6.cloned.1.call-done, bf16[4096,128]{1,0:T(8,128)(2,1)S(1)} %bitcast.99, f32[4096]{0:T(1024)S(1)} %copy-done.19), kind=kOutput, calls=%fused_computation.16 | convolution fusion | flops 672743424 | bytes 6471680 | tf_op jit(solution)/shard_map/dot_general | solution.py:379
  241.0 0.9 subtract_convert_fusion
  241.9 2.8 %all-to-all-done.3 = bf16[16,48,128]{2,1,0:T(8,128)(2,1)} async-done(((bf16[16,48,128]{2,1,0:T(8,128)(2,1)}), bf16[16,48,128]{2,1,0:T(8,128)(2,1)}, u32[]{:S(2)}, u32[]{:S(2)}) %all-to-all-start.3) | async-done | bytes 196640 | tf_op jit(solution)/shard_map/all_to_all | solution.py:365
  244.7 1.0 reduce_sum.92
  246.4 8.8 %all-to-all-start.4 = ((bf16[16,48,128]{2,1,0:T(8,128)(2,1)}), bf16[16,48,128]{2,1,0:T(8,128)(2,1)S(1)}, u32[]{:S(2)}, u32[]{:S(2)}) async-start(bf16[16,48,128]{2,1,0:T(8,128)(2,1)} %broadcast_in_dim.103), calls=%async_computation.4 | async-start | bytes 393216 | tf_op jit(solution)/shard_map/all_to_all | solution.py:383
  255.2 2.2 multiply_reduce_fusion
  257.4 1.5 fusion.2
  259.0 4.4 %convolution_multiply_fusion.1 = f32[256,640]{1,0:T(8,128)S(1)} fusion(bf16[256,4096]{1,0:T(8,128)(2,1)S(1)} %copy-done.11, bf16[640,4096]{0,1:T(8,128)(2,1)} %all-gather.6.cloned.1.call-done, f32[256]{0:T(256)S(1)} %get-tuple-element.67), kind=kOutput, calls=%fused_computation.12 | convolution fusion | flops 1342341120 | bytes 7996416 | tf_op jit(solution)/shard_map/dot_general | solution.py:386
  263.4 1.0 fusion.1
  264.4 3.2 %all-to-all-done.4 = bf16[16,48,128]{2,1,0:T(8,128)(2,1)S(1)} async-done(((bf16[16,48,128]{2,1,0:T(8,128)(2,1)}), bf16[16,48,128]{2,1,0:T(8,128)(2,1)S(1)}, u32[]{:S(2)}, u32[]{:S(2)}) %all-to-all-start.4) | async-done | bytes 196640 | tf_op jit(solution)/shard_map/all_to_all | solution.py:383
  268.2 0.8 convert_multiply_fusion
  (129 shorter events, 15.5 us)
Async XLA Ops:
  7.2 26.5 %copy-start = (bf16[8192,128]{1,0:T(8,128)(2,1)S(1)}, bf16[8192,128]{1,0:T(8,128)(2,1)}, u32[]{:S(2)}) copy-start(bf16[8192,128]{1,0:T(8,128)(2,1)} %param.20) | copy-start | bytes 6291460
  7.2 26.3 %copy-start.20 = (s32[64,64]{1,0:T(8,128)S(1)}, s32[64,64]{1,0:T(8,128)}, u32[]{:S(2)}) copy-start(s32[64,64]{1,0:T(8,128)} %param.18) | copy-start | bytes 49156
  7.2 81.3 %all-gather.4.cloned.1.call-start = ((), (), s32[]{:S(2)}) async-start(), calls=%async_computation.5 | async-start | bytes 1392640 | tf_op jit(solution)/shard_map/all_gather | solution.py:284
  9.4 21.0 %copy-start.30 = (s32[64]{0:T(128)}, s32[64]{0:T(128)S(1)}, u32[]{:S(2)}) copy-start(s32[64]{0:T(128)S(1)} %convert_reduce_fusion) | copy-start | bytes 772
  9.5 21.0 %copy-start.28 = (s32[64]{0:T(128)}, s32[64]{0:T(128)S(1)}, u32[]{:S(2)}) copy-start(s32[64]{0:T(128)S(1)} %fusion.15) | copy-start | bytes 772
  11.1 45.6 %all-to-all-start = ((s32[64,1,128]{2,1,0:T(1,128)}), s32[64,1,128]{2,1,0:T(1,128)S(1)}, u32[]{:S(2)}, u32[]{:S(2)}) async-start(s32[64,1,128]{2,1,0:T(1,128)} %bitcast.15), calls=%async_computation | async-start | bytes 65536 | tf_op jit(solution)/shard_map/all_to_all | solution.py:286
  33.6 14.9 %copy-start.8 = (f32[4]{0:T(128)S(1)}, f32[4]{0:T(128)}, u32[]{:S(2)}) copy-start(f32[4]{0:T(128)} %buckets.1) | copy-start | bytes 52
  48.5 1.6 copy-start.1
  50.1 1.2 copy-start.5
  59.2 15.0 %copy-start.16 = (bf16[512,128]{1,0:T(8,128)(2,1)S(1)}, bf16[512,128]{1,0:T(8,128)(2,1)}, u32[]{:S(2)}) copy-start(bf16[512,128]{1,0:T(8,128)(2,1)} %param.15) | copy-start | bytes 393220
  59.2 29.2 %copy-start.17 = (bf16[256,640]{1,0:T(8,128)(2,1)S(1)}, bf16[256,640]{1,0:T(8,128)(2,1)}, u32[]{:S(2)}) copy-start(bf16[256,640]{1,0:T(8,128)(2,1)} %param.12) | copy-start | bytes 983044
  59.2 38.9 %copy-start.19 = (f32[4096]{0:T(1024)S(1)}, f32[4096]{0:T(1024)}, u32[]{:S(2)}) copy-start(f32[4096]{0:T(1024)} %param.14) | copy-start | bytes 49156
  59.2 113.1 %all-to-all-start.1 = ((bf16[64,128,128]{2,1,0:T(8,128)(2,1)}), bf16[64,128,128]{2,1,0:T(8,128)(2,1)}, u32[]{:S(2)}, u32[]{:S(2)}) async-start(bf16[64,128,128]{2,1,0:T(8,128)(2,1)} %bitcast.106), calls=%async_computation.1 | async-start | bytes 4194304 | tf_op jit(solution)/shard_map/all_to_all | solution.py:291
  74.2 141.2 %all-gather.6.cloned.1.call-start = ((), (), s32[]{:S(2)}) async-start(), calls=%async_computation.6 | async-start | bytes 6553600 | tf_op jit(solution)/shard_map/all_gather | solution.py:354
  74.3 4.4 %collective-permute-start.3 = (bf16[512,128]{1,0:T(8,128)(2,1)S(1)}, bf16[512,128]{1,0:T(8,128)(2,1)S(1)}, u32[]{:S(2)}, u32[]{:S(2)}) collective-permute-start(bf16[512,128]{1,0:T(8,128)(2,1)S(1)} %copy-done.16), channel_id=1, source_target_pairs={{0,1},{1,0},{2,3},{3,2},{4,5},{5,4},{6,7},{7,6},{8,9},{9,8},{10,11... | collective-permute-start | bytes 393224 | tf_op jit(solution)/shard_map/ppermute | solution.py:25
  79.4 16.6 %collective-permute-start.6 = (bf16[2,512,128]{2,1,0:T(8,128)(2,1)}, bf16[2,512,128]{2,1,0:T(8,128)(2,1)}, u32[]{:S(2)}, u32[]{:S(2)}) collective-permute-start(bf16[2,512,128]{2,1,0:T(8,128)(2,1)} %maximum_select_fusion.1), channel_id=1, source_target_pairs={{0,6},{2,4},{4,2},{6,0},{1,7},{3,5},{5,3},{7,1},{8,14},{10,12},{12... | collective-permute-start | bytes 786440 | tf_op jit(solution)/shard_map/ppermute | solution.py:25
  83.8 15.1 %copy-start.22 = (s32[1024]{0:T(1024)}, s32[1024]{0:T(1024)S(1)}, u32[]{:S(2)}) copy-start(s32[1024]{0:T(1024)S(1)} %pad_clamp_fusion.2) | copy-start | bytes 12292
  83.8 15.1 %collective-permute-start.5 = (bf16[2,512,128]{2,1,0:T(8,128)(2,1)}, bf16[2,512,128]{2,1,0:T(8,128)(2,1)}, u32[]{:S(2)}, u32[]{:S(2)}) collective-permute-start(bf16[2,512,128]{2,1,0:T(8,128)(2,1)} %maximum_select_fusion.1), channel_id=1, source_target_pairs={{0,4},{2,6},{4,0},{6,2},{1,5},{3,7},{5,1},{7,3},{8,12},{10,14},{12... | collective-permute-start | bytes 786440 | tf_op jit(solution)/shard_map/ppermute | solution.py:25
  86.2 12.6 %collective-permute-start.4 = (bf16[2,512,128]{2,1,0:T(8,128)(2,1)}, bf16[2,512,128]{2,1,0:T(8,128)(2,1)}, u32[]{:S(2)}, u32[]{:S(2)}) collective-permute-start(bf16[2,512,128]{2,1,0:T(8,128)(2,1)} %maximum_select_fusion.1), channel_id=1, source_target_pairs={{0,2},{2,0},{4,6},{6,4},{1,3},{3,1},{5,7},{7,5},{8,10},{10,8},{12,... | collective-permute-start | bytes 786440 | tf_op jit(solution)/shard_map/ppermute | solution.py:25
  89.1 17.5 %collective-permute-start.2 = (bf16[2,4,32,640]{3,2,0,1:T(8,128)(2,1)S(1)}, bf16[2,4,32,640]{3,2,0,1:T(8,128)(2,1)}, u32[]{:S(2)}, u32[]{:S(2)}) collective-permute-start(bf16[2,4,32,640]{3,2,0,1:T(8,128)(2,1)S(1)} %bitcast.110), channel_id=1, source_target_pairs={{0,384},{128,256},{256,128},{384,0},{1,385},{129,257},{257,129},{3... | collective-permute-start | bytes 983048 | tf_op jit(solution)/shard_map/ppermute | solution.py:25
  93.7 13.0 %collective-permute-start.1 = (bf16[2,4,32,640]{3,2,0,1:T(8,128)(2,1)S(1)}, bf16[2,4,32,640]{3,2,0,1:T(8,128)(2,1)}, u32[]{:S(2)}, u32[]{:S(2)}) collective-permute-start(bf16[2,4,32,640]{3,2,0,1:T(8,128)(2,1)S(1)} %bitcast.111), channel_id=1, source_target_pairs={{0,256},{128,384},{256,0},{384,128},{1,257},{129,385},{257,1},{385... | collective-permute-start | bytes 983048 | tf_op jit(solution)/shard_map/ppermute | solution.py:25
  96.0 12.7 %collective-permute-start = (bf16[2,4,32,640]{3,2,0,1:T(8,128)(2,1)S(1)}, bf16[2,4,32,640]{3,2,0,1:T(8,128)(2,1)}, u32[]{:S(2)}, u32[]{:S(2)}) collective-permute-start(bf16[2,4,32,640]{3,2,0,1:T(8,128)(2,1)S(1)} %bitcast.112), channel_id=1, source_target_pairs={{0,128},{128,0},{256,384},{384,256},{1,129},{129,1},{257,385},{385... | collective-permute-start | bytes 983048 | tf_op jit(solution)/shard_map/ppermute | solution.py:25
  111.3 11.8 %copy-start.27 = (s32[1,64]{1,0:T(1,128)S(1)}, s32[1,64]{1,0:T(1,128)}, u32[]{:S(2)}) copy-start(s32[1,64]{1,0:T(1,128)} %param.16) | copy-start | bytes 772
  111.3 11.8 %copy-start.31 = (s32[64]{0:T(128)S(1)}, s32[64]{0:T(128)}, u32[]{:S(2)}) copy-start(s32[64]{0:T(128)} %copy-done.30) | copy-start | bytes 772
  111.3 11.8 %copy-start.29 = (s32[64]{0:T(128)S(1)}, s32[64]{0:T(128)}, u32[]{:S(2)}) copy-start(s32[64]{0:T(128)} %copy-done.28) | copy-start | bytes 772
  111.3 143.9 %all-gather.8.cloned.1.call-start = ((), (), s32[]{:S(2)}) async-start(), calls=%async_computation.7 | async-start | bytes 2359296 | tf_op jit(solution)/shard_map/all_gather | solution.py:358
  111.3 11.9 %copy-start.14 = (bf16[640,1024]{0,1:T(8,128)(2,1)S(1)}, bf16[640,1024]{0,1:T(8,128)(2,1)}, u32[]{:S(2)}) copy-start(bf16[640,1024]{0,1:T(8,128)(2,1)} %all-gather.4.cloned.1.call-done) | copy-start | bytes 3932164
  111.3 11.9 %copy-start.15 = (bf16[2,4,4,32,640]{4,3,2,1,0:T(8,128)(2,1)S(1)}, bf16[2,4,4,32,640]{4,3,2,1,0:T(8,128)(2,1)}, u32[]{:S(2)}) copy-start(bf16[2,4,4,32,640]{4,3,2,1,0:T(8,128)(2,1)} %copy.37) | copy-start | bytes 3932164
  114.0 11.2 %collective-permute-start.7 = (bf16[512,1024]{1,0:T(8,128)(2,1)S(1)}, bf16[512,1024]{1,0:T(8,128)(2,1)S(1)}, u32[]{:S(2)}, u32[]{:S(2)}) collective-permute-start(bf16[512,1024]{1,0:T(8,128)(2,1)S(1)} %convolution_convert_fusion), channel_id=1, source_target_pairs={{0,1},{1,0},{2,3},{3,2},{4,5},{5,4},{6,7},{7,6},{8,9},{9,8},{10,11... | collective-permute-start | bytes 3145736 | tf_op jit(solution)/shard_map/ppermute | solution.py:25
  127.9 15.6 %collective-permute-start.10 = (bf16[4,32,1024]{2,1,0:T(8,128)(2,1)}, bf16[4,32,1024]{2,1,0:T(8,128)(2,1)}, u32[]{:S(2)}, u32[]{:S(2)}) collective-permute-start(bf16[4,32,1024]{2,1,0:T(8,128)(2,1)} %bitcast.31), channel_id=1, source_target_pairs={{0,6},{2,4},{4,2},{6,0},{1,7},{3,5},{5,3},{7,1},{8,14},{10,12},{12... | collective-permute-start | bytes 786440 | tf_op jit(solution)/shard_map/ppermute | solution.py:25
  132.2 11.3 %collective-permute-start.9 = (bf16[4,32,1024]{2,1,0:T(8,128)(2,1)}, bf16[4,32,1024]{2,1,0:T(8,128)(2,1)}, u32[]{:S(2)}, u32[]{:S(2)}) collective-permute-start(bf16[4,32,1024]{2,1,0:T(8,128)(2,1)} %bitcast.30), channel_id=1, source_target_pairs={{0,4},{2,6},{4,0},{6,2},{1,5},{3,7},{5,1},{7,3},{8,12},{10,14},{12... | collective-permute-start | bytes 786440 | tf_op jit(solution)/shard_map/ppermute | solution.py:25
  134.6 12.2 %collective-permute-start.8 = (bf16[4,32,1024]{2,1,0:T(8,128)(2,1)S(1)}, bf16[4,32,1024]{2,1,0:T(8,128)(2,1)}, u32[]{:S(2)}, u32[]{:S(2)}) collective-permute-start(bf16[4,32,1024]{2,1,0:T(8,128)(2,1)S(1)} %bitcast.123), channel_id=1, source_target_pairs={{0,2},{2,0},{4,6},{6,4},{1,3},{3,1},{5,7},{7,5},{8,10},{10,8},{12,... | collective-permute-start | bytes 786440 | tf_op jit(solution)/shard_map/ppermute | solution.py:25
  138.1 20.1 %copy-start.23 = (s32[64,2]{0,1:T(2,128)S(1)}, s32[64,2]{0,1:T(2,128)}, u32[]{:S(2)}) copy-start(s32[64,2]{0,1:T(2,128)} %copy.39) | copy-start | bytes 1540
  148.0 21.8 %copy-start.12 = (bf16[32,4096]{1,0:T(8,128)(2,1)S(1)}, bf16[32,4096]{1,0:T(8,128)(2,1)}, u32[]{:S(2)}) copy-start(bf16[32,4096]{1,0:T(8,128)(2,1)} %param.11) | copy-start | bytes 786436
  148.7 10.9 %collective-permute-start.13 = (bf16[32,1024]{1,0:T(8,128)(2,1)}, bf16[32,1024]{1,0:T(8,128)(2,1)}, u32[]{:S(2)}, u32[]{:S(2)}) collective-permute-start(bf16[32,1024]{1,0:T(8,128)(2,1)} %get-tuple-element.63), channel_id=1, source_target_pairs={{0,384},{128,256},{256,128},{384,0},{1,385},{129,257},{257,129},{3... | collective-permute-start | bytes 196616 | tf_op jit(solution)/shard_map/ppermute | solution.py:25
  153.8 8.9 %collective-permute-start.12 = (bf16[32,1024]{1,0:T(8,128)(2,1)}, bf16[32,1024]{1,0:T(8,128)(2,1)}, u32[]{:S(2)}, u32[]{:S(2)}) collective-permute-start(bf16[32,1024]{1,0:T(8,128)(2,1)} %get-tuple-element.64), channel_id=1, source_target_pairs={{0,256},{128,384},{256,0},{384,128},{1,257},{129,385},{257,1},{385... | collective-permute-start | bytes 196616 | tf_op jit(solution)/shard_map/ppermute | solution.py:25
  156.2 8.7 %collective-permute-start.11 = (bf16[32,1024]{1,0:T(8,128)(2,1)}, bf16[32,1024]{1,0:T(8,128)(2,1)}, u32[]{:S(2)}, u32[]{:S(2)}) collective-permute-start(bf16[32,1024]{1,0:T(8,128)(2,1)} %get-tuple-element.65), channel_id=1, source_target_pairs={{0,128},{128,0},{256,384},{384,256},{1,129},{129,1},{257,385},{385... | collective-permute-start | bytes 196616 | tf_op jit(solution)/shard_map/ppermute | solution.py:25
  169.8 1.5 copy-start.9
  170.5 12.2 %copy-start.24 = (f32[32]{0:T(128)}, f32[32]{0:T(128)S(1)}, u32[]{:S(2)}) copy-start(f32[32]{0:T(128)S(1)} %get-tuple-element.69) | copy-start | bytes 388
  171.6 0.8 copy-start.3
  172.5 1.1 copy-start.4
  182.8 1.2 copy-start.6
  215.4 16.7 %slice-start = ((bf16[32,192,128]{2,1,0:T(8,128)(2,1)}), bf16[32,32,128]{2,1,0:T(8,128)(2,1)S(1)}, s32[]{:S(2)}) async-start(bf16[32,192,128]{2,1,0:T(8,128)(2,1)} %all_to_all.32.packets), calls=%async_computation.8 | async-start | bytes 524288 | tf_op jit(solution)/shard_map/slice | solution.py:352
  216.7 1.4 copy-start.2
  218.8 0.7 copy-start.7
  219.5 25.3 %all-to-all-start.3 = ((bf16[16,48,128]{2,1,0:T(8,128)(2,1)}), bf16[16,48,128]{2,1,0:T(8,128)(2,1)}, u32[]{:S(2)}, u32[]{:S(2)}) async-start(bf16[16,48,128]{2,1,0:T(8,128)(2,1)} %copy-done.7), calls=%async_computation.3 | async-start | bytes 393216 | tf_op jit(solution)/shard_map/all_to_all | solution.py:365
  235.4 5.6 %copy-start.10 = (f32[4,4,8,1024]{3,2,0,1:T(8,128)S(1)}, f32[4,4,8,1024]{3,2,0,1:T(8,128)}, u32[]{:S(2)}) copy-start(f32[4,4,8,1024]{3,2,0,1:T(8,128)} %copy-done.9) | copy-start | bytes 1572868
  235.4 5.6 %copy-start.13 = (bf16[32,4096]{1,0:T(8,128)(2,1)S(1)}, bf16[32,4096]{1,0:T(8,128)(2,1)}, u32[]{:S(2)}) copy-start(bf16[32,4096]{1,0:T(8,128)(2,1)} %param.11) | copy-start | bytes 786436
  235.5 5.5 %copy-start.25 = (f32[32]{0:T(128)S(1)}, f32[32]{0:T(128)}, u32[]{:S(2)}) copy-start(f32[32]{0:T(128)} %copy-done.24) | copy-start | bytes 388
  235.5 5.5 %copy-start.26 = (f32[32]{0:T(128)S(1)}, f32[32]{0:T(128)}, u32[]{:S(2)}) copy-start(f32[32]{0:T(128)} %get-tuple-element.68) | copy-start | bytes 388
  246.4 21.1 %all-to-all-start.4 = ((bf16[16,48,128]{2,1,0:T(8,128)(2,1)}), bf16[16,48,128]{2,1,0:T(8,128)(2,1)S(1)}, u32[]{:S(2)}, u32[]{:S(2)}) async-start(bf16[16,48,128]{2,1,0:T(8,128)(2,1)} %broadcast_in_dim.103), calls=%async_computation.4 | async-start | bytes 393216 | tf_op jit(solution)/shard_map/all_to_all | solution.py:383
  255.2 2.2 copy-start.11
  259.0 4.4 %copy-start.18 = (bf16[640,128]{1,0:T(8,128)(2,1)S(1)}, bf16[640,128]{1,0:T(8,128)(2,1)}, u32[]{:S(2)}) copy-start(bf16[640,128]{1,0:T(8,128)(2,1)} %convolution_convert_fusion.2) | copy-start | bytes 491524
  259.0 9.2 %copy-start.21 = (f32[512]{0:T(512)S(1)}, f32[512]{0:T(512)}, u32[]{:S(2)}) copy-start(f32[512]{0:T(512)} %dynamic_slice.6) | copy-start | bytes 6148
Sparse Core Ops, SparseCore 0:
  10.1 68.2 all-gather.3
  111.4 83.5 all-gather.5
  215.5 31.6 all-gather.7

commit v9 on v6

--- a/solution.py
+++ b/solution.py
@@ -30,7 +30,13 @@
 
 
 def unxor(blocks, place):
-    return rows_of(blocks, jnp.arange(blocks.shape[0], dtype=I32) ^ place)
+    blocks = list(blocks)
+    bit = 1
+    while bit < len(blocks):
+        other = (place & bit) != 0
+        blocks = [jnp.where(other, blocks[i ^ bit], block) for i, block in enumerate(blocks)]
+        bit *= 2
+    return blocks
 
 
 def decode_kernel(buckets, packed, rows, out):
@@ -278,7 +284,7 @@
     here_x, here_c, here_y = lax.axis_index("x"), lax.axis_index("c"), lax.axis_index("y")
     blocks = context.reshape(X, C, seq_rows, context.shape[1])
     blocks = jnp.where(here_c == 0, blocks, blocks[:, ::-1])
-    blocks = unxor(blocks, here_x).transpose(1, 0, 2, 3)
+    blocks = jnp.stack(unxor(blocks, here_x)).transpose(1, 0, 2, 3)
     by_y = jnp.stack([blocks] + [swap(blocks, "y", Y, step) for step in range(1, Y)], axis=2)
     by_y = by_y.reshape(C, X * Y * seq_rows, context.shape[1])
 
@@ -288,8 +294,8 @@
         jnp.stack([colbert_head, head_pair]),
         jnp.stack([head_pair, colbert_head]),
     )
-    head_full = unxor(
-        jnp.stack([head_pair] + [swap(head_pair, "x", X, step) for step in range(1, X)]), here_x
+    head_full = jnp.stack(
+        unxor([head_pair] + [swap(head_pair, "x", X, step) for step in range(1, X)], here_x)
     ).reshape(width, feature_dim)
     head_rows = colbert_head.shape[0]
     mine = (here_x * C + here_c) * head_rows
@@ -308,8 +314,7 @@
         row = row + swap(pieces[step - 1], "x", X, step).astype(F32)
     for_y = row.astype(BF16)
     columns = [for_y[0]] + [swap(for_y[step], "y", Y, step) for step in range(1, Y)]
-    columns = unxor(jnp.stack(columns), here_y)
-    attended = columns.transpose(1, 0, 2).reshape(seq_rows, width).astype(F32)
+    attended = jnp.concatenate(unxor(columns, here_y), axis=1).astype(F32)
     summed = residual.astype(F32) + attended
     inv_rms = lax.rsqrt(jnp.mean(summed * summed, axis=-1, keepdims=True) + EPS)
     scaled_sum = summed * inv_rms

time: 279 us -> 275 us (0.986)
  waiting for transfers between devices: 33.9 us -> 41 us
  other arithmetic: 21.2 us -> 15.3 us
  local copies, waits for them, and re-layouts: 38.8 us -> 34.8 us
    all_to_all x1, starting transfers between devices: 11.8 us -> 4.41 us  [local(): first = lax.all_to_all(first, 'z', 0, 0, tiled=True)]
    ppermute x14, waiting for transfers between devices: 21.5 us -> 27.6 us  [swap(): return lax.ppermute(values, axis, [(i, i ^ step) for i in range(size)])]
    gather x5 -> x2, local copies, waits for them, and re-layouts: 22.1 us -> 17.1 us  [rows_of(): return values.at[index].get(mode='promise_in_bounds')]
    all_to_all x1, starting transfers between devices: 9.46 us -> 13.3 us  [local(): lax.all_to_all(jnp.broadcast_to(unit, (Y,) + unit.shape).reshape((-1,) +...]
    unnamed x61 -> x81, local copies, waits for them, and re-layouts: 5.88 us -> 6.83 us
  transfers between devices with their start and end apart: 22 -> 22, of which waited for: 12 -> 14; matrix products, arithmetic and copies ran while one was open for 26% -> 23% of each run, Pallas kernels for 6% -> 6%
where the time goes in v9:
time: 275 us; the launch traced here: 270 us
  starting transfers between devices  112 us (41%)
  waiting for transfers between devices  41 us (15%)
  local copies, waits for them, and re-layouts  34.8 us (13%)
  matrix products  19.1 us (7%)
  blocking collectives  17.3 us (6%)
  Pallas kernels  16.2 us (6%)
  other arithmetic  15.3 us (6%)
  between operations  14.7 us (5%)
    ppermute x14, starting transfers between devices, swap(): return lax.ppermute(values, axis, [(i, i ^ step) for i in range(size)])  49.8 us
    ppermute x14, waiting for transfers between devices, swap(): return lax.ppermute(values, axis, [(i, i ^ step) for i in range(size)])  27.6 us
    all_to_all x1, starting transfers between devices, local(): notes = lax.all_to_all(note, DP, 0, 0, tiled=True)  19.3 us
    all_to_all x1, blocking collectives, local(): lax.all_to_all(jnp.broadcast_to(packet, (Y * X * C,) + packet.shape), PLA...  17.3 us
    gather x2, local copies, waits for them, and re-layouts, rows_of(): return values.at[index].get(mode='promise_in_bounds')  17.1 us
    all_to_all x1, starting transfers between devices, local(): lax.all_to_all(chosen.reshape(shards, cap * doc_len, feature_dim), DP, 0,...  15 us
    all_to_all x1, starting transfers between devices, local(): lax.all_to_all(jnp.broadcast_to(unit, (Y,) + unit.shape).reshape((-1,) +...  13.3 us
    all_to_all x1, starting transfers between devices, local(): lax.all_to_all(jnp.broadcast_to(second, (Z,) + second.shape[1:]), 'z', 0,...  10 us
  transfers between devices with their start and end apart: 22, of which 14 were waited for; matrix products, arithmetic and copies ran while one was open for 23% of the time, Pallas kernels for 6%

profile of v9, /device:TPU:1, one launch (start us, length us, event | category | flops | bytes accessed | tf_op | source)
XLA Modules:
  0.0 270.4 jit_solution(3527287625481077528)
XLA Ops:
  10.7 0.7 add_add_fusion
  11.4 19.3 %all-to-all-start = ((s32[64,1,128]{2,1,0:T(1,128)}), s32[64,1,128]{2,1,0:T(1,128)S(1)}, u32[]{:S(2)}, u32[]{:S(2)}) async-start(s32[64,1,128]{2,1,0:T(1,128)} %bitcast.14), calls=%async_computation | async-start | bytes 65536 | tf_op jit(solution)/shard_map/all_to_all | solution.py:265
  30.7 3.0 %reshape.231.packed = s32[4096,16]{1,0:T(8,128)} reshape(s32[64,1024]{1,0:T(8,128)} %param.19) | data formatting | bytes 524288 | tf_op jit(solution)/shard_map/reshape | solution.py:76
  33.9 14.9 %gather_fusion = bf16[4096,128]{1,0:T(8,128)(2,1)} fusion(bf16[8192,128]{1,0:T(8,128)(2,1)S(1)} %copy-done, s32[4096]{0:T(1024)S(1)} %broadcast_clamp_fusion), kind=kCustom, calls=%fused_computation | custom fusion | bytes 2113536 | tf_op jit(solution)/shard_map/gather | solution.py:29
  48.8 1.6 copy-done.1
  50.4 1.2 copy-done.3
  51.6 5.4 %decode.1 = bf16[4096,128]{1,0:T(8,128)(2,1)S(1)} custom-call(f32[4]{0:T(128)S(1)} %copy-done.6, s32[4096,16]{1,0:T(8,128)S(1)} %copy-done.1, bf16[4096,128]{1,0:T(8,128)(2,1)S(1)} %copy-done.3), custom_call_target="tpu_custom_call" | custom-call | tf_op jit(solution)/shard_map/decode/pallas_call | solution.py:78
  57.3 2.2 gather_fusion.1
  59.5 15.0 %all-to-all-start.1 = ((bf16[64,128,128]{2,1,0:T(8,128)(2,1)}), bf16[64,128,128]{2,1,0:T(8,128)(2,1)}, u32[]{:S(2)}, u32[]{:S(2)}) async-start(bf16[64,128,128]{2,1,0:T(8,128)(2,1)} %bitcast.113), calls=%async_computation.1 | async-start | bytes 4194304 | tf_op jit(solution)/shard_map/all_to_all | solution.py:270
  74.6 3.4 %collective-permute-start.3 = (bf16[512,128]{1,0:T(8,128)(2,1)S(1)}, bf16[512,128]{1,0:T(8,128)(2,1)S(1)}, u32[]{:S(2)}, u32[]{:S(2)}) collective-permute-start(bf16[512,128]{1,0:T(8,128)(2,1)S(1)} %copy-done.20), channel_id=1, source_target_pairs={{0,1},{1,0},{2,3},{3,2},{4,5},{5,4},{6,7},{7,6},{8,9},{9,8},{10,11... | collective-permute-start | bytes 393224 | tf_op jit(solution)/shard_map/ppermute | solution.py:25
  79.0 0.7 maximum_select_fusion
  79.7 4.4 %collective-permute-start.4 = (bf16[2,512,128]{2,1,0:T(8,128)(2,1)}, bf16[2,512,128]{2,1,0:T(8,128)(2,1)S(1)}, u32[]{:S(2)}, u32[]{:S(2)}) collective-permute-start(bf16[2,512,128]{2,1,0:T(8,128)(2,1)} %maximum_select_fusion), channel_id=1, source_target_pairs={{0,6},{2,4},{4,2},{6,0},{1,7},{3,5},{5,3},{7,1},{8,14},{10,12},{12... | collective-permute-start | bytes 786440 | tf_op jit(solution)/shard_map/ppermute | solution.py:25
  84.1 2.4 collective-permute-start.5
  86.5 2.2 collective-permute-start.6
  88.9 4.5 %collective-permute-start.2 = (bf16[2,4,32,640]{3,2,0,1:T(8,128)(2,1)S(1)}, bf16[2,4,32,640]{3,2,0,1:T(8,128)(2,1)S(1)}, u32[]{:S(2)}, u32[]{:S(2)}) collective-permute-start(bf16[2,4,32,640]{3,2,0,1:T(8,128)(2,1)S(1)} %get-tuple-element.76), channel_id=1, source_target_pairs={{0,384},{128,256},{256,128},{384,0},{1,385},{129,257},{257,129},{3... | collective-permute-start | bytes 983048 | tf_op jit(solution)/shard_map/ppermute | solution.py:25
  93.5 2.3 collective-permute-start.1
  95.8 2.6 collective-permute-start
  98.5 1.1 select_bitcast_fusion.3
  99.8 7.4 %collective-permute-done.2 = bf16[2,4,32,640]{3,2,0,1:T(8,128)(2,1)S(1)} collective-permute-done((bf16[2,4,32,640]{3,2,0,1:T(8,128)(2,1)S(1)}, bf16[2,4,32,640]{3,2,0,1:T(8,128)(2,1)S(1)}, u32[]{:S(2)}, u32[]{:S(2)}) %collective-permute-start.2) | collective-permute-done | bytes 327712 | tf_op jit(solution)/shard_map/ppermute | solution.py:25
  107.2 1.8 collective-permute-done
  109.2 1.2 copy.38
  110.4 2.7 convolution_convert_fusion
  113.1 8.6 %collective-permute-start.7 = (bf16[512,1024]{1,0:T(8,128)(2,1)S(1)}, bf16[512,1024]{1,0:T(8,128)(2,1)S(1)}, u32[]{:S(2)}, u32[]{:S(2)}) collective-permute-start(bf16[512,1024]{1,0:T(8,128)(2,1)S(1)} %convolution_convert_fusion), channel_id=1, source_target_pairs={{0,1},{1,0},{2,3},{3,2},{4,5},{5,4},{6,7},{7,6},{8,9},{9,8},{10,11... | collective-permute-start | bytes 3145736 | tf_op jit(solution)/shard_map/ppermute | solution.py:25
  121.8 1.0 convolution_convert_fusion.1
  122.8 1.2 collective-permute-done.7
  124.6 4.5 %collective-permute-start.10 = (bf16[4,32,1024]{2,1,0:T(8,128)(2,1)S(1)}, bf16[4,32,1024]{2,1,0:T(8,128)(2,1)S(1)}, u32[]{:S(2)}, u32[]{:S(2)}) collective-permute-start(bf16[4,32,1024]{2,1,0:T(8,128)(2,1)S(1)} %bitcast.134), channel_id=1, source_target_pairs={{0,6},{2,4},{4,2},{6,0},{1,7},{3,5},{5,3},{7,1},{8,14},{10,12},{12... | collective-permute-start | bytes 786440 | tf_op jit(solution)/shard_map/ppermute | solution.py:25
  129.0 2.3 collective-permute-start.9
  131.4 2.3 collective-permute-start.8
  133.7 6.3 %collective-permute-done.10 = bf16[4,32,1024]{2,1,0:T(8,128)(2,1)S(1)} collective-permute-done((bf16[4,32,1024]{2,1,0:T(8,128)(2,1)S(1)}, bf16[4,32,1024]{2,1,0:T(8,128)(2,1)S(1)}, u32[]{:S(2)}, u32[]{:S(2)}) %collective-permute-start.10) | collective-permute-done | bytes 262176 | tf_op jit(solution)/shard_map/ppermute | solution.py:25
  140.1 3.2 %collective-permute-done.8 = bf16[4,32,1024]{2,1,0:T(8,128)(2,1)S(1)} collective-permute-done((bf16[4,32,1024]{2,1,0:T(8,128)(2,1)S(1)}, bf16[4,32,1024]{2,1,0:T(8,128)(2,1)S(1)}, u32[]{:S(2)}, u32[]{:S(2)}) %collective-permute-start.8) | collective-permute-done | bytes 262176 | tf_op jit(solution)/shard_map/ppermute | solution.py:25
  143.5 0.7 copy-done.18
  144.8 5.9 %collective-permute-start.11 = (bf16[32,1024]{1,0:T(8,128)(2,1)}, bf16[32,1024]{1,0:T(8,128)(2,1)}, u32[]{:S(2)}, u32[]{:S(2)}) collective-permute-start(bf16[32,1024]{1,0:T(8,128)(2,1)} %get-tuple-element.83), channel_id=1, source_target_pairs={{0,384},{128,256},{256,128},{384,0},{1,385},{129,257},{257,129},{3... | collective-permute-start | bytes 196616 | tf_op jit(solution)/shard_map/ppermute | solution.py:25
  150.7 1.9 collective-permute-start.12
  152.6 2.5 collective-permute-start.13
  155.2 4.8 %collective-permute-done.12 = bf16[32,1024]{1,0:T(8,128)(2,1)} collective-permute-done((bf16[32,1024]{1,0:T(8,128)(2,1)S(1)}, bf16[32,1024]{1,0:T(8,128)(2,1)}, u32[]{:S(2)}, u32[]{:S(2)}) %collective-permute-start.12) | collective-permute-done | bytes 65568 | tf_op jit(solution)/shard_map/ppermute | solution.py:25
  160.1 2.2 collective-permute-done.13
  162.3 1.0 broadcast_select_fusion.19
  164.0 1.0 fusion.20
  165.1 2.7 all-to-all-done.1
  167.9 1.1 broadcast_in_dim.101
  169.0 13.3 %all-to-all-start.2 = ((bf16[32,32,512]{2,1,0:T(8,128)(2,1)}), bf16[32,32,512]{2,1,0:T(8,128)(2,1)}, u32[]{:S(2)}, u32[]{:S(2)}) async-start(bf16[32,32,512]{2,1,0:T(8,128)(2,1)} %bitcast.114), calls=%async_computation.2 | async-start | bytes 2097152 | tf_op jit(solution)/shard_map/all_to_all | solution.py:326
  183.2 1.3 fusion.9.embedded_ref
  184.6 1.0 copy-done.2
  185.7 9.2 %score.1 = (f32[128,1]{1,0:T(8,128)S(1)}, bf16[64,128]{1,0:T(8,128)(2,1)S(1)}) custom-call(bf16[8192,128]{1,0:T(8,128)(2,1)} %bitcast.36.docs, f32[32,128]{1,0:T(8,128)S(1)} %fusion.9.embedded_ref, s32[128,32]{1,0:T(8,128)S(1)} %broadcast_in_dim.100.spans, s32[128,2]{1,0:T(8,128)S(1)} %copy.41.flags, f32[32,4096]{1,0:T(8,128)S(1)} %copy-done.2, ...), custom_call_target="tpu_custom_call" | custom-call | flops 134217728 | bytes 30000000 | tf_op jit(solution)/shard_map/score/pallas_call | solution.py:165
  194.9 5.6 %all-to-all-done.2 = bf16[32,32,512]{2,1,0:T(8,128)(2,1)} async-done(((bf16[32,32,512]{2,1,0:T(8,128)(2,1)}), bf16[32,32,512]{2,1,0:T(8,128)(2,1)}, u32[]{:S(2)}, u32[]{:S(2)}) %all-to-all-start.2) | async-done | bytes 1048608 | tf_op jit(solution)/shard_map/all_to_all | solution.py:326
  200.6 17.3 %all_to_all.37.packets = bf16[32,64,128]{2,1,0:T(8,128)(2,1)} all-to-all(bf16[32,64,128]{2,1,0:T(8,128)(2,1)S(1)} %broadcast_in_dim.102), channel_id=1, replica_groups=mesh['y'=4,'z'=16,'x'=4,'c'=2] {'y','x','c'}, dimensions={0} | all-to-all | bytes 1048576 | tf_op jit(solution)/shard_map/all_to_all | solution.py:336
  218.0 1.1 copy-done.4
  219.0 1.6 bundle.1
  221.4 4.4 %all-to-all-start.4 = ((bf16[16,48,128]{2,1,0:T(8,128)(2,1)}), bf16[16,48,128]{2,1,0:T(8,128)(2,1)}, u32[]{:S(2)}, u32[]{:S(2)}) async-start(bf16[16,48,128]{2,1,0:T(8,128)(2,1)} %copy-done.5), calls=%async_computation.4 | async-start | bytes 393216 | tf_op jit(solution)/shard_map/all_to_all | solution.py:352
  226.4 0.9 copy.43
  227.5 1.3 select_reduce_fusion.1
  228.8 1.5 multiply_reduce_fusion.1
  230.5 5.7 %convolution_convert_fusion.2 = bf16[640,128]{1,0:T(8,128)(2,1)} fusion(bf16[640,4096]{0,1:T(8,128)(2,1)} %all-gather.6.cloned.1.call-done, bf16[4096,128]{1,0:T(8,128)(2,1)S(1)} %bitcast.110, f32[4096]{0:T(1024)S(1)} %copy-done.28), kind=kOutput, calls=%fused_computation.13 | convolution fusion | flops 672743424 | bytes 6471680 | tf_op jit(solution)/shard_map/dot_general | solution.py:366
  236.2 0.9 subtract_convert_fusion
  237.0 1.3 all-to-all-done.4
  238.3 1.0 reduce_sum.92
  239.3 0.8 broadcast_in_dim.108
  240.1 10.0 %all-to-all-start.5 = ((bf16[16,48,128]{2,1,0:T(8,128)(2,1)}), bf16[16,48,128]{2,1,0:T(8,128)(2,1)S(1)}, u32[]{:S(2)}, u32[]{:S(2)}) async-start(bf16[16,48,128]{2,1,0:T(8,128)(2,1)} %broadcast_in_dim.108), calls=%async_computation.5 | async-start | bytes 393216 | tf_op jit(solution)/shard_map/all_to_all | solution.py:370
  250.1 2.2 multiply_reduce_fusion
  252.4 1.5 fusion.2
  254.0 4.4 %convolution_multiply_fusion.1 = f32[256,640]{1,0:T(8,128)S(1)} fusion(bf16[256,4096]{1,0:T(8,128)(2,1)S(1)} %copy-done.7, bf16[640,4096]{0,1:T(8,128)(2,1)} %all-gather.6.cloned.1.call-done, f32[256]{0:T(256)S(1)} %get-tuple-element.85), kind=kOutput, calls=%fused_computation.9 | convolution fusion | flops 1342341120 | bytes 7996416 | tf_op jit(solution)/shard_map/dot_general | solution.py:373
  258.3 1.0 fusion.1
  259.3 3.1 %all-to-all-done.5 = bf16[16,48,128]{2,1,0:T(8,128)(2,1)S(1)} async-done(((bf16[16,48,128]{2,1,0:T(8,128)(2,1)}), bf16[16,48,128]{2,1,0:T(8,128)(2,1)S(1)}, u32[]{:S(2)}, u32[]{:S(2)}) %all-to-all-start.5) | async-done | bytes 196640 | tf_op jit(solution)/shard_map/all_to_all | solution.py:370
  263.1 0.8 convert_multiply_fusion
  (143 shorter events, 11.1 us)
Async XLA Ops:
  7.2 26.7 %copy-start = (bf16[8192,128]{1,0:T(8,128)(2,1)S(1)}, bf16[8192,128]{1,0:T(8,128)(2,1)}, u32[]{:S(2)}) copy-start(bf16[8192,128]{1,0:T(8,128)(2,1)} %param.20) | copy-start | bytes 6291460
  7.2 26.6 %copy-start.30 = (s32[64,64]{1,0:T(8,128)S(1)}, s32[64,64]{1,0:T(8,128)}, u32[]{:S(2)}) copy-start(s32[64,64]{1,0:T(8,128)} %param.18) | copy-start | bytes 49156
  7.2 81.5 %all-gather.4.cloned.1.call-start = ((), (), s32[]{:S(2)}) async-start(), calls=%async_computation.6 | async-start | bytes 1392640 | tf_op jit(solution)/shard_map/all_gather | solution.py:263
  9.4 21.3 %copy-start.38 = (s32[64]{0:T(128)}, s32[64]{0:T(128)S(1)}, u32[]{:S(2)}) copy-start(s32[64]{0:T(128)S(1)} %convert_reduce_fusion) | copy-start | bytes 772
  9.5 0.5 copy-start.36
  9.7 24.2 %copy-start.24 = (s32[64,2]{1,0:T(8,128)}, s32[64,2]{1,0:T(8,128)S(1)}, u32[]{:S(2)}) copy-start(s32[64,2]{1,0:T(8,128)S(1)} %reshape.234) | copy-start | bytes 1540
  11.4 45.6 %all-to-all-start = ((s32[64,1,128]{2,1,0:T(1,128)}), s32[64,1,128]{2,1,0:T(1,128)S(1)}, u32[]{:S(2)}, u32[]{:S(2)}) async-start(s32[64,1,128]{2,1,0:T(1,128)} %bitcast.14), calls=%async_computation | async-start | bytes 65536 | tf_op jit(solution)/shard_map/all_to_all | solution.py:265
  33.9 14.9 %copy-start.6 = (f32[4]{0:T(128)S(1)}, f32[4]{0:T(128)}, u32[]{:S(2)}) copy-start(f32[4]{0:T(128)} %buckets.1) | copy-start | bytes 52
  48.8 1.6 copy-start.1
  50.4 1.2 copy-start.3
  57.0 2.5 copy-start.22
  59.5 15.1 %copy-start.20 = (bf16[512,128]{1,0:T(8,128)(2,1)S(1)}, bf16[512,128]{1,0:T(8,128)(2,1)}, u32[]{:S(2)}) copy-start(bf16[512,128]{1,0:T(8,128)(2,1)} %param.15) | copy-start | bytes 393220
  59.5 18.5 %copy-start.27 = (f32[4096]{0:T(1024)S(1)}, f32[4096]{0:T(1024)}, u32[]{:S(2)}) copy-start(f32[4096]{0:T(1024)} %param.14) | copy-start | bytes 49156
  59.5 29.2 %copy-start.21 = (bf16[256,640]{1,0:T(8,128)(2,1)S(1)}, bf16[256,640]{1,0:T(8,128)(2,1)}, u32[]{:S(2)}) copy-start(bf16[256,640]{1,0:T(8,128)(2,1)} %param.12) | copy-start | bytes 983044
  59.5 108.2 %all-to-all-start.1 = ((bf16[64,128,128]{2,1,0:T(8,128)(2,1)}), bf16[64,128,128]{2,1,0:T(8,128)(2,1)}, u32[]{:S(2)}, u32[]{:S(2)}) async-start(bf16[64,128,128]{2,1,0:T(8,128)(2,1)} %bitcast.113), calls=%async_computation.1 | async-start | bytes 4194304 | tf_op jit(solution)/shard_map/all_to_all | solution.py:270
  74.5 143.4 %all-gather.6.cloned.1.call-start = ((), (), s32[]{:S(2)}) async-start(), calls=%async_computation.7 | async-start | bytes 6553600 | tf_op jit(solution)/shard_map/all_gather | solution.py:341
  74.6 4.4 %collective-permute-start.3 = (bf16[512,128]{1,0:T(8,128)(2,1)S(1)}, bf16[512,128]{1,0:T(8,128)(2,1)S(1)}, u32[]{:S(2)}, u32[]{:S(2)}) collective-permute-start(bf16[512,128]{1,0:T(8,128)(2,1)S(1)} %copy-done.20), channel_id=1, source_target_pairs={{0,1},{1,0},{2,3},{3,2},{4,5},{5,4},{6,7},{7,6},{8,9},{9,8},{10,11... | collective-permute-start | bytes 393224 | tf_op jit(solution)/shard_map/ppermute | solution.py:25
  79.7 16.1 %collective-permute-start.4 = (bf16[2,512,128]{2,1,0:T(8,128)(2,1)}, bf16[2,512,128]{2,1,0:T(8,128)(2,1)S(1)}, u32[]{:S(2)}, u32[]{:S(2)}) collective-permute-start(bf16[2,512,128]{2,1,0:T(8,128)(2,1)} %maximum_select_fusion), channel_id=1, source_target_pairs={{0,6},{2,4},{4,2},{6,0},{1,7},{3,5},{5,3},{7,1},{8,14},{10,12},{12... | collective-permute-start | bytes 786440 | tf_op jit(solution)/shard_map/ppermute | solution.py:25
  84.1 14.3 %collective-permute-start.5 = (bf16[2,512,128]{2,1,0:T(8,128)(2,1)}, bf16[2,512,128]{2,1,0:T(8,128)(2,1)}, u32[]{:S(2)}, u32[]{:S(2)}) collective-permute-start(bf16[2,512,128]{2,1,0:T(8,128)(2,1)} %maximum_select_fusion), channel_id=1, source_target_pairs={{0,4},{2,6},{4,0},{6,2},{1,5},{3,7},{5,1},{7,3},{8,12},{10,14},{12... | collective-permute-start | bytes 786440 | tf_op jit(solution)/shard_map/ppermute | solution.py:25
  86.5 12.0 %collective-permute-start.6 = (bf16[2,512,128]{2,1,0:T(8,128)(2,1)}, bf16[2,512,128]{2,1,0:T(8,128)(2,1)}, u32[]{:S(2)}, u32[]{:S(2)}) collective-permute-start(bf16[2,512,128]{2,1,0:T(8,128)(2,1)} %maximum_select_fusion), channel_id=1, source_target_pairs={{0,2},{2,0},{4,6},{6,4},{1,3},{3,1},{5,7},{7,5},{8,10},{10,8},{12,... | collective-permute-start | bytes 786440 | tf_op jit(solution)/shard_map/ppermute | solution.py:25
  88.9 18.2 %collective-permute-start.2 = (bf16[2,4,32,640]{3,2,0,1:T(8,128)(2,1)S(1)}, bf16[2,4,32,640]{3,2,0,1:T(8,128)(2,1)S(1)}, u32[]{:S(2)}, u32[]{:S(2)}) collective-permute-start(bf16[2,4,32,640]{3,2,0,1:T(8,128)(2,1)S(1)} %get-tuple-element.76), channel_id=1, source_target_pairs={{0,384},{128,256},{256,128},{384,0},{1,385},{129,257},{257,129},{3... | collective-permute-start | bytes 983048 | tf_op jit(solution)/shard_map/ppermute | solution.py:25
  93.5 13.7 %collective-permute-start.1 = (bf16[2,4,32,640]{3,2,0,1:T(8,128)(2,1)S(1)}, bf16[2,4,32,640]{3,2,0,1:T(8,128)(2,1)S(1)}, u32[]{:S(2)}, u32[]{:S(2)}) collective-permute-start(bf16[2,4,32,640]{3,2,0,1:T(8,128)(2,1)S(1)} %get-tuple-element.76), channel_id=1, source_target_pairs={{0,256},{128,384},{256,0},{384,128},{1,257},{129,385},{257,1},{385... | collective-permute-start | bytes 983048 | tf_op jit(solution)/shard_map/ppermute | solution.py:25
  95.8 13.2 %collective-permute-start = (bf16[2,4,32,640]{3,2,0,1:T(8,128)(2,1)S(1)}, bf16[2,4,32,640]{3,2,0,1:T(8,128)(2,1)S(1)}, u32[]{:S(2)}, u32[]{:S(2)}) collective-permute-start(bf16[2,4,32,640]{3,2,0,1:T(8,128)(2,1)S(1)} %get-tuple-element.76), channel_id=1, source_target_pairs={{0,128},{128,0},{256,384},{384,256},{1,129},{129,1},{257,385},{385... | collective-permute-start | bytes 983048 | tf_op jit(solution)/shard_map/ppermute | solution.py:25
  110.4 11.3 %copy-start.16 = (bf16[640,1024]{0,1:T(8,128)(2,1)S(1)}, bf16[640,1024]{0,1:T(8,128)(2,1)}, u32[]{:S(2)}) copy-start(bf16[640,1024]{0,1:T(8,128)(2,1)} %all-gather.4.cloned.1.call-done) | copy-start | bytes 3932164
  110.4 11.3 %copy-start.17 = (bf16[2,4,4,32,640]{4,3,2,1,0:T(8,128)(2,1)S(1)}, bf16[2,4,4,32,640]{4,3,2,1,0:T(8,128)(2,1)}, u32[]{:S(2)}) copy-start(bf16[2,4,4,32,640]{4,3,2,1,0:T(8,128)(2,1)} %copy.38) | copy-start | bytes 3932164
  113.1 10.9 %collective-permute-start.7 = (bf16[512,1024]{1,0:T(8,128)(2,1)S(1)}, bf16[512,1024]{1,0:T(8,128)(2,1)S(1)}, u32[]{:S(2)}, u32[]{:S(2)}) collective-permute-start(bf16[512,1024]{1,0:T(8,128)(2,1)S(1)} %convolution_convert_fusion), channel_id=1, source_target_pairs={{0,1},{1,0},{2,3},{3,2},{4,5},{5,4},{6,7},{7,6},{8,9},{9,8},{10,11... | collective-permute-start | bytes 3145736 | tf_op jit(solution)/shard_map/ppermute | solution.py:25
  124.5 38.8 %copy-start.8 = (bf16[32,4096]{1,0:T(8,128)(2,1)S(1)}, bf16[32,4096]{1,0:T(8,128)(2,1)}, u32[]{:S(2)}) copy-start(bf16[32,4096]{1,0:T(8,128)(2,1)} %param.11) | copy-start | bytes 786436
  124.6 15.5 %collective-permute-start.10 = (bf16[4,32,1024]{2,1,0:T(8,128)(2,1)S(1)}, bf16[4,32,1024]{2,1,0:T(8,128)(2,1)S(1)}, u32[]{:S(2)}, u32[]{:S(2)}) collective-permute-start(bf16[4,32,1024]{2,1,0:T(8,128)(2,1)S(1)} %bitcast.134), channel_id=1, source_target_pairs={{0,6},{2,4},{4,2},{6,0},{1,7},{3,5},{5,3},{7,1},{8,14},{10,12},{12... | collective-permute-start | bytes 786440 | tf_op jit(solution)/shard_map/ppermute | solution.py:25
  129.0 11.0 %collective-permute-start.9 = (bf16[4,32,1024]{2,1,0:T(8,128)(2,1)S(1)}, bf16[4,32,1024]{2,1,0:T(8,128)(2,1)S(1)}, u32[]{:S(2)}, u32[]{:S(2)}) collective-permute-start(bf16[4,32,1024]{2,1,0:T(8,128)(2,1)S(1)} %bitcast.133), channel_id=1, source_target_pairs={{0,4},{2,6},{4,0},{6,2},{1,5},{3,7},{5,1},{7,3},{8,12},{10,14},{12... | collective-permute-start | bytes 786440 | tf_op jit(solution)/shard_map/ppermute | solution.py:25
  131.4 11.9 %collective-permute-start.8 = (bf16[4,32,1024]{2,1,0:T(8,128)(2,1)S(1)}, bf16[4,32,1024]{2,1,0:T(8,128)(2,1)S(1)}, u32[]{:S(2)}, u32[]{:S(2)}) collective-permute-start(bf16[4,32,1024]{2,1,0:T(8,128)(2,1)S(1)} %bitcast.132), channel_id=1, source_target_pairs={{0,2},{2,0},{4,6},{6,4},{1,3},{3,1},{5,7},{7,5},{8,10},{10,8},{12,... | collective-permute-start | bytes 786440 | tf_op jit(solution)/shard_map/ppermute | solution.py:25
  143.5 0.7 copy-start.18
  144.8 10.4 %collective-permute-start.11 = (bf16[32,1024]{1,0:T(8,128)(2,1)}, bf16[32,1024]{1,0:T(8,128)(2,1)}, u32[]{:S(2)}, u32[]{:S(2)}) collective-permute-start(bf16[32,1024]{1,0:T(8,128)(2,1)} %get-tuple-element.83), channel_id=1, source_target_pairs={{0,384},{128,256},{256,128},{384,0},{1,385},{129,257},{257,129},{3... | collective-permute-start | bytes 196616 | tf_op jit(solution)/shard_map/ppermute | solution.py:25
  150.7 9.4 %collective-permute-start.12 = (bf16[32,1024]{1,0:T(8,128)(2,1)S(1)}, bf16[32,1024]{1,0:T(8,128)(2,1)}, u32[]{:S(2)}, u32[]{:S(2)}) collective-permute-start(bf16[32,1024]{1,0:T(8,128)(2,1)S(1)} %get-tuple-element.82), channel_id=1, source_target_pairs={{0,256},{128,384},{256,0},{384,128},{1,257},{129,385},{257,1},{385... | collective-permute-start | bytes 196616 | tf_op jit(solution)/shard_map/ppermute | solution.py:25
  152.6 9.7 %collective-permute-start.13 = (bf16[32,1024]{1,0:T(8,128)(2,1)S(1)}, bf16[32,1024]{1,0:T(8,128)(2,1)}, u32[]{:S(2)}, u32[]{:S(2)}) collective-permute-start(bf16[32,1024]{1,0:T(8,128)(2,1)S(1)} %get-tuple-element.81), channel_id=1, source_target_pairs={{0,128},{128,0},{256,384},{384,256},{1,129},{129,1},{257,385},{385... | collective-permute-start | bytes 196616 | tf_op jit(solution)/shard_map/ppermute | solution.py:25
  163.3 1.7 copy-start.12
  163.3 1.7 copy-start.14
  163.3 5.7 %copy-start.10 = (bf16[32,1024]{1,0:T(8,128)(2,1)}, bf16[32,1024]{1,0:T(8,128)(2,1)S(1)}, u32[]{:S(2)}) copy-start(bf16[32,1024]{1,0:T(8,128)(2,1)S(1)} %get-tuple-element.72) | copy-start | bytes 196612
  164.0 1.0 copy-start.32
  167.8 14.5 %copy-start.25 = (s32[64,2]{1,0:T(8,128)S(1)}, s32[64,2]{1,0:T(8,128)}, u32[]{:S(2)}) copy-start(s32[64,2]{1,0:T(8,128)} %copy-done.24) | copy-start | bytes 1540
  167.9 14.6 %copy-start.35 = (s32[1,64]{1,0:T(1,128)S(1)}, s32[1,64]{1,0:T(1,128)}, u32[]{:S(2)}) copy-start(s32[1,64]{1,0:T(1,128)} %param.16) | copy-start | bytes 772
  167.9 14.6 %copy-start.39 = (s32[64]{0:T(128)S(1)}, s32[64]{0:T(128)}, u32[]{:S(2)}) copy-start(s32[64]{0:T(128)} %copy-done.38) | copy-start | bytes 772
  167.9 14.7 %copy-start.37 = (s32[64]{0:T(128)S(1)}, s32[64]{0:T(128)}, u32[]{:S(2)}) copy-start(s32[64]{0:T(128)} %copy-done.36) | copy-start | bytes 772
  167.9 14.9 %copy-start.23 = (s32[64,1,128]{2,1,0:T(1,128)S(1)}, s32[64,1,128]{2,1,0:T(1,128)}, u32[]{:S(2)}) copy-start(s32[64,1,128]{2,1,0:T(1,128)} %copy-done.22) | copy-start | bytes 98308
  169.0 31.5 %all-to-all-start.2 = ((bf16[32,32,512]{2,1,0:T(8,128)(2,1)}), bf16[32,32,512]{2,1,0:T(8,128)(2,1)}, u32[]{:S(2)}, u32[]{:S(2)}) async-start(bf16[32,32,512]{2,1,0:T(8,128)(2,1)} %bitcast.114), calls=%async_computation.2 | async-start | bytes 2097152 | tf_op jit(solution)/shard_map/all_to_all | solution.py:326
  182.3 67.8 %all-gather.8.cloned.1.call-start = ((), (), s32[]{:S(2)}) async-start(), calls=%async_computation.8 | async-start | bytes 2359296 | tf_op jit(solution)/shard_map/all_gather | solution.py:345
  184.6 1.1 copy-start.2
  217.9 7.9 %slice-start = ((bf16[32,64,128]{2,1,0:T(8,128)(2,1)}), bf16[32,32,128]{2,1,0:T(8,128)(2,1)S(1)}, s32[]{:S(2)}) async-start(bf16[32,64,128]{2,1,0:T(8,128)(2,1)} %all_to_all.37.packets), calls=%async_computation.9 | async-start | bytes 524288 | tf_op jit(solution)/shard_map/slice | solution.py:339
  218.0 1.1 copy-start.4
  220.7 0.7 copy-start.5
  221.4 17.0 %all-to-all-start.4 = ((bf16[16,48,128]{2,1,0:T(8,128)(2,1)}), bf16[16,48,128]{2,1,0:T(8,128)(2,1)}, u32[]{:S(2)}, u32[]{:S(2)}) async-start(bf16[16,48,128]{2,1,0:T(8,128)(2,1)} %copy-done.5), calls=%async_computation.4 | async-start | bytes 393216 | tf_op jit(solution)/shard_map/all_to_all | solution.py:352
  226.4 4.0 %copy-start.28 = (f32[4096]{0:T(1024)S(1)}, f32[4096]{0:T(1024)}, u32[]{:S(2)}) copy-start(f32[4096]{0:T(1024)} %param.14) | copy-start | bytes 49156
  230.4 5.7 %copy-start.9 = (bf16[32,4096]{1,0:T(8,128)(2,1)S(1)}, bf16[32,4096]{1,0:T(8,128)(2,1)}, u32[]{:S(2)}) copy-start(bf16[32,4096]{1,0:T(8,128)(2,1)} %param.11) | copy-start | bytes 786436
  230.4 5.7 %copy-start.11 = (bf16[32,1024]{1,0:T(8,128)(2,1)S(1)}, bf16[32,1024]{1,0:T(8,128)(2,1)}, u32[]{:S(2)}) copy-start(bf16[32,1024]{1,0:T(8,128)(2,1)} %copy-done.10) | copy-start | bytes 196612
  230.4 5.7 %copy-start.13 = (bf16[32,1024]{1,0:T(8,128)(2,1)S(1)}, bf16[32,1024]{1,0:T(8,128)(2,1)}, u32[]{:S(2)}) copy-start(bf16[32,1024]{1,0:T(8,128)(2,1)} %copy-done.12) | copy-start | bytes 196612
  230.4 5.7 %copy-start.15 = (bf16[32,1024]{1,0:T(8,128)(2,1)S(1)}, bf16[32,1024]{1,0:T(8,128)(2,1)}, u32[]{:S(2)}) copy-start(bf16[32,1024]{1,0:T(8,128)(2,1)} %copy-done.14) | copy-start | bytes 196612
  230.4 5.7 %copy-start.33 = (f32[32]{0:T(128)S(1)}, f32[32]{0:T(128)}, u32[]{:S(2)}) copy-start(f32[32]{0:T(128)} %copy-done.32) | copy-start | bytes 388
  230.4 5.7 %copy-start.34 = (f32[32]{0:T(128)S(1)}, f32[32]{0:T(128)}, u32[]{:S(2)}) copy-start(f32[32]{0:T(128)} %get-tuple-element.86) | copy-start | bytes 388
  236.2 16.2 %copy-start.29 = (f32[4096]{0:T(1024)S(1)}, f32[4096]{0:T(1024)}, u32[]{:S(2)}) copy-start(f32[4096]{0:T(1024)} %param.14) | copy-start | bytes 49156
  240.1 22.4 %all-to-all-start.5 = ((bf16[16,48,128]{2,1,0:T(8,128)(2,1)}), bf16[16,48,128]{2,1,0:T(8,128)(2,1)S(1)}, u32[]{:S(2)}, u32[]{:S(2)}) async-start(bf16[16,48,128]{2,1,0:T(8,128)(2,1)} %broadcast_in_dim.108), calls=%async_computation.5 | async-start | bytes 393216 | tf_op jit(solution)/shard_map/all_to_all | solution.py:370
  250.1 2.2 copy-start.7
  253.9 4.4 %copy-start.19 = (bf16[8,32,128]{2,1,0:T(8,128)(2,1)S(1)}, bf16[8,32,128]{2,1,0:T(8,128)(2,1)}, u32[]{:S(2)}) copy-start(bf16[8,32,128]{2,1,0:T(8,128)(2,1)} %constant_dynamic-slice_fusion) | copy-start | bytes 196612
  253.9 4.4 %copy-start.26 = (bf16[640,128]{1,0:T(8,128)(2,1)S(1)}, bf16[640,128]{1,0:T(8,128)(2,1)}, u32[]{:S(2)}) copy-start(bf16[640,128]{1,0:T(8,128)(2,1)} %convolution_convert_fusion.2) | copy-start | bytes 491524
  253.9 9.1 %copy-start.31 = (f32[512]{0:T(512)S(1)}, f32[512]{0:T(512)}, u32[]{:S(2)}) copy-start(f32[512]{0:T(512)} %dynamic_slice.6) | copy-start | bytes 6148
Sparse Core Ops, SparseCore 0:
  10.1 67.9 all-gather.3
  110.5 94.3 all-gather.5
  218.1 29.0 all-gather.7
